TPU v7x, 32 devices: a whole 2x2x4 slice. The times are simulated.
32 devices in a mesh: row: 4 (over z), col: 8 (over y, x, core).
Axes of the slice: x: 2, y: 2, z: 4, core: 2. Of those that a mesh axis runs over, the one named last changes fastest.
Arguments:
- val_wave: bfloat16 [8, 64, 64, 128], replicated, may hold values from -6 to 6
- cond_wave: bfloat16 [32, 64, 64, 128], P(('row', 'col')), may hold values from -6 to 6
- val_energy: float32 [8], replicated, may hold values from -12 to -0.5
- cond_energy: float32 [32], replicated, may hold values from 0.5 to 20
- band_owner: int32 [32], P(('row', 'col')), may hold values from 0 to 31, each once
- grid_map: int32 [30720], replicated, may hold values from 0 to 262143, as said below
Outputs:
- chi: float32 [2, 1024, 30720], P(None, 'row', 'col')
Inputs may be any that keep to these rules, and one draw needn't show every extreme that they name: `band_owner`: every one of the 32 band numbers stands in exactly one slot. `grid_map`: 30720 distinct flat grid points: those of the shortest wave vectors, with indices above 32 read as negative frequencies, ordered by length with ties in random order.
All inputs are finite; a program needn't handle non-finite values.
Results may differ from a plain program's by a relative error of at most 0.0041.
Values may be sent and summed in bfloat16 or wider, within the bound.
No kernel may reach another device: no remote copies, remote signals or barrier semaphores. Data moves between devices by JAX's collectives and lax.ppermute only.
A program may use at most 576 MiB of HBM per device.

v0:
```python
import math

import jax
import jax.numpy as jnp
import numpy as np
from jax import lax
from jax.experimental import pallas as pl
from jax.experimental.pallas import tpu as pltpu
from jax.sharding import PartitionSpec as P

ROWS_DEV = 256
LANES = 128
VMEM_BYTES = 56 * 1024 * 1024
HALF = 64
KEEP = 40
ROWS_K = 48
ORIGIN = KEEP // 2


def round_up(value, step):
    return -(-value // step) * step


def length_counts(points):
    freq = np.arange(points) - points // 2
    square = freq * freq
    lengths = square[:, None, None] + square[None, :, None] + square[None, None, :]
    return np.cumsum(np.bincount(lengths.reshape(-1)))


def column_order(top):
    freq = np.arange(KEEP) - ORIGIN
    first, second = np.meshgrid(freq, freq, indexing="ij")
    length = (first * first + second * second).reshape(-1)
    order = np.argsort(length, kind="stable")
    order = order[length[order] <= top]
    return first.reshape(-1)[order], second.reshape(-1)[order], length[order]


class Bucket:
    def __init__(self, low, high, column_length):
        self.pieces = []
        offset = 0
        for index in range(KEEP):
            freq = index - ORIGIN
            start = int(np.searchsorted(column_length, low - freq * freq, side="left"))
            stop = int(np.searchsorted(column_length, high - freq * freq, side="right"))
            if stop > start:
                self.pieces.append((index, start, stop, offset))
                offset += stop - start
        self.size = offset

    def ids(self, column_2, column_3, points, width):
        out = np.full((width,), -1, np.int32)
        for index, start, stop, offset in self.pieces:
            k1 = (index - ORIGIN) % points
            k2 = column_2[start:stop] % points
            k3 = column_3[start:stop] % points
            out[offset : offset + stop - start] = (k1 * points + k2) * points + k3
        return out


def make_plan(points, total, blocks, slab):
    cumulative = length_counts(points)
    width = total // blocks
    top = int(np.searchsorted(cumulative, total, side="left"))
    column_2, column_3, column_length = column_order(top)
    buckets = []
    for block in range(blocks):
        low = int(np.searchsorted(cumulative, block * width, side="right"))
        high = int(np.searchsorted(cumulative, (block + 1) * width, side="left"))
        buckets.append(Bucket(low, high, column_length))
    slab_top = int(np.searchsorted(cumulative, slab, side="left"))
    slab_bucket = Bucket(0, slab_top, column_length)
    slab_columns = int(np.searchsorted(column_length, slab_top, side="right"))
    slab_edge = math.isqrt(slab_top)
    block_lanes = round_up(max(bucket.size for bucket in buckets), LANES)
    slab_lanes = round_up(slab_bucket.size, LANES)
    return dict(
        buckets=buckets,
        slab_bucket=slab_bucket,
        slab_columns=slab_columns,
        slab_edge=slab_edge,
        block_lanes=block_lanes,
        slab_lanes=slab_lanes,
        block_ids=np.stack([b.ids(column_2, column_3, points, block_lanes) for b in buckets]),
        slab_ids=slab_bucket.ids(column_2, column_3, points, slab_lanes),
        column_place=((column_3 + ORIGIN) * KEEP + column_2 + ORIGIN).astype(np.int32),
    )


def dft_table(points):
    n = np.arange(points)
    freq = np.arange(KEEP) - ORIGIN
    angle = (n[:, None] * freq[None, :] % points) * (2.0 * np.pi / points)
    cosine, sine = np.cos(angle), np.sin(angle)
    table = np.zeros((2 * HALF, 2 * HALF))
    table[:points, :KEEP] = cosine
    table[HALF : HALF + points, :KEEP] = sine
    table[:points, HALF : HALF + KEEP] = -sine
    table[HALF : HALF + points, HALF : HALF + KEEP] = cosine
    high = table.astype(jnp.bfloat16)
    low = (table - high.astype(np.float64)).astype(jnp.bfloat16)
    return np.block([[high, low], [high, np.zeros_like(low)]])


def split_parts(value):
    high = value.astype(jnp.bfloat16)
    low = (value - high.astype(jnp.float32)).astype(jnp.bfloat16)
    return high, low


def apply_table(parts, table):
    both = jnp.dot(parts, table, preferred_element_type=jnp.float32)
    return both[:, :LANES] + both[:, LANES:]


def stack_complex(turned, low_lanes):
    real, imag = turned[:KEEP], turned[HALF : HALF + KEEP]
    first = jnp.where(low_lanes, real, pltpu.roll(imag, HALF, 1))
    second = jnp.where(low_lanes, pltpu.roll(real, HALF, 1), imag)
    return jnp.concatenate([first, second], 0)


def pack_pieces(pieces, width, source, rows, lane, out):
    for tile in range(width // LANES):
        left, right = tile * LANES, (tile + 1) * LANES
        value = jnp.zeros((rows, LANES), jnp.float32)
        for index, start, stop, offset in pieces:
            begin, end = max(left, offset), min(right, offset + stop - start)
            while begin < end:
                at = start + begin - offset
                here = min(end, begin + LANES - at % LANES)
                block = source(index, at // LANES)
                shift = (begin - at) % LANES
                if shift:
                    block = pltpu.roll(block, shift, 1)
                inside = (lane >= begin - left) & (lane < here - left)
                value = jnp.where(inside, block, value)
                begin = here
        out(tile, value)


def spectrum_kernel(plan, points, bands, weight_ref, val_ref, cond_ref, table_ref, place_ref, send_ref, slab_ref,
                    cond_a, cond_b, middle, turned, last, sorter, plain_rows, weighted_rows, plain_sorted, weighted_sorted):
    band = pl.program_id(0)
    planes = 8
    lane = lax.broadcasted_iota(jnp.int32, (1, LANES), 1)
    low_lanes = lane < HALF
    depth = last.shape[0]

    @pl.when(band == 0)
    def _():
        scale = 1.0 / float(points) ** 1.5
        sign = jnp.where(low_lanes, scale, -scale)

        @pl.loop(0, points)
        def _(n):
            rows = pl.ds(pl.multiple_of(n * points, points), points)
            wave = cond_ref[0, n].astype(jnp.float32)
            cond_a[rows, :] = wave * scale
            cond_b[rows, :] = pltpu.roll(wave, HALF, 1) * sign

        columns = sorter.shape[1]
        for begin in range(0, depth, LANES):
            at = lax.broadcasted_iota(jnp.int32, (LANES, columns), 0) + begin
            sorter[begin : begin + LANES, :] = jnp.where(at == place_ref[...], 1.0, 0.0).astype(jnp.bfloat16)
        last[KEEP * KEEP :, :] = jnp.zeros((depth - KEEP * KEEP, 2 * LANES), jnp.bfloat16)
        plain_rows[...] = jnp.zeros_like(plain_rows)
        weighted_rows[...] = jnp.zeros_like(weighted_rows)

    table = table_ref[...]

    @pl.loop(0, points // planes)
    def _(block):
        rows = pl.ds(pl.multiple_of(block * planes * points, planes * points), planes * points)
        wave = val_ref[0, pl.ds(block * planes, planes)].reshape(planes * points, LANES).astype(jnp.float32)
        other = pltpu.roll(wave, HALF, 1)
        density = jnp.where(low_lanes, wave, other) * cond_a[rows, :] + jnp.where(low_lanes, other, wave) * cond_b[rows, :]
        high, low = split_parts(density)
        field = apply_table(jnp.concatenate([high, low], 1), table)
        for pair in range(planes // 2):
            both = field[pair * 2 * points : (pair + 1) * 2 * points].T
            high, low = split_parts(stack_complex(both, low_lanes))
            at = pl.ds(pl.multiple_of((block * planes + pair * 2) * KEEP, 2 * KEEP), 2 * KEEP)
            middle[at, :LANES] = high
            middle[at, LANES:] = low

    step = 8 * KEEP

    @pl.loop(0, points // 8)
    def _(block):
        rows = pl.ds(pl.multiple_of(block * step, step), step)
        turned[rows, :] = apply_table(middle[rows, :], table)

    for pair in range(KEEP // 2):
        both = jnp.concatenate(
            [turned[pl.ds(2 * pair, points, stride=KEEP), :], turned[pl.ds(2 * pair + 1, points, stride=KEEP), :]], 0
        ).T
        high, low = split_parts(stack_complex(both, low_lanes))
        at = slice(2 * pair * KEEP, (2 * pair + 2) * KEEP)
        last[at, :LANES] = high
        last[at, LANES:] = low

    weight = weight_ref[band]
    slab_rows = weighted_rows.shape[1]
    slab_first = (ORIGIN - plan["slab_edge"]) * KEEP // LANES
    slab_last = slab_first + weighted_rows.shape[2] // LANES
    for tile in range(depth // LANES):
        rows = slice(tile * LANES, (tile + 1) * LANES)
        field = apply_table(last[rows, :], table).T
        for part in range(2):
            value = field[part * HALF : part * HALF + ROWS_K]
            at = part * bands + band
            plain_rows[at, :, rows] = value.astype(jnp.bfloat16)
            if slab_first <= tile < slab_last:
                lanes = slice((tile - slab_first) * LANES, (tile - slab_first + 1) * LANES)
                weighted_rows[at, :, lanes] = (weight * value).astype(jnp.bfloat16)

    @pl.when(band == bands - 1)
    def _():
        count = 2 * bands
        for begin in range(0, count, 4):
            block = plain_rows[begin : begin + 4].reshape(4 * ROWS_K, depth)
            value = jnp.dot(block, sorter[...], preferred_element_type=jnp.float32)
            for tile in range(plain_sorted.shape[0]):
                rows = slice(begin * ROWS_K, (begin + 4) * ROWS_K)
                plain_sorted[tile, rows, :] = value[:, tile * LANES : (tile + 1) * LANES]
            block = weighted_rows[begin : begin + 4].reshape(4 * slab_rows, weighted_rows.shape[2])
            value = jnp.dot(
                block,
                sorter[slab_first * LANES : slab_last * LANES, : weighted_sorted.shape[0] * LANES],
                preferred_element_type=jnp.float32,
            )
            for tile in range(weighted_sorted.shape[0]):
                rows = slice(begin * slab_rows, (begin + 4) * slab_rows)
                weighted_sorted[tile, rows, :] = value[:, tile * LANES : (tile + 1) * LANES]

        def plain_at(index, tile):
            return plain_sorted[tile, pl.ds(index, count, stride=ROWS_K), :]

        def weighted_at(index, tile):
            return weighted_sorted[tile, pl.ds(index, count, stride=slab_rows), :]

        for block, bucket in enumerate(plan["buckets"]):

            def keep(tile, value):
                send_ref[block, :, tile * LANES : (tile + 1) * LANES] = value.astype(jnp.bfloat16)

            pack_pieces(bucket.pieces, plan["block_lanes"], plain_at, count, lane, keep)

        def keep_slab(tile, value):
            slab_ref[:, tile * LANES : (tile + 1) * LANES] = value.astype(jnp.bfloat16)

        pack_pieces(plan["slab_bucket"].pieces, plan["slab_lanes"], weighted_at, count, lane, keep_slab)


def spectra(plan, val_wave, cond_wave, weight):
    bands, points = val_wave.shape[0], val_wave.shape[1]
    depth = round_up(KEEP * KEEP, LANES)
    columns = round_up(plan["column_place"].shape[0], 256)
    place = np.full((1, columns), -1, np.int32)
    place[0, : plan["column_place"].shape[0]] = plan["column_place"]
    edge = plan["slab_edge"]
    slab_first = (ORIGIN - edge) * KEEP // LANES
    slab_last = round_up((ORIGIN + edge + 1) * KEEP, LANES) // LANES
    slab_depth = (slab_last - slab_first) * LANES
    slab_columns = round_up(plan["slab_columns"], LANES)
    grid_rows = points * points
    kernel = lambda *refs: spectrum_kernel(plan, points, bands, *refs)
    return pl.pallas_call(
        kernel,
        grid=(bands,),
        in_specs=[
            pl.BlockSpec(memory_space=pltpu.SMEM),
            pl.BlockSpec((1, points, points, 2 * points), lambda v: (v, 0, 0, 0)),
            pl.BlockSpec((1, points, points, 2 * points), lambda v: (0, 0, 0, 0)),
            pl.BlockSpec((4 * HALF, 4 * HALF), lambda v: (0, 0)),
            pl.BlockSpec((1, columns), lambda v: (0, 0)),
        ],
        out_specs=[
            pl.BlockSpec((len(plan["buckets"]), 2 * bands, plan["block_lanes"]), lambda v: (0, 0, 0)),
            pl.BlockSpec((2 * bands, plan["slab_lanes"]), lambda v: (0, 0)),
        ],
        out_shape=[
            jax.ShapeDtypeStruct((len(plan["buckets"]), 2 * bands, plan["block_lanes"]), jnp.bfloat16),
            jax.ShapeDtypeStruct((2 * bands, plan["slab_lanes"]), jnp.bfloat16),
        ],
        scratch_shapes=[
            pltpu.VMEM((grid_rows, LANES), jnp.float32),
            pltpu.VMEM((grid_rows, LANES), jnp.float32),
            pltpu.VMEM((points * KEEP, 2 * LANES), jnp.bfloat16),
            pltpu.VMEM((points * KEEP, LANES), jnp.float32),
            pltpu.VMEM((depth, 2 * LANES), jnp.bfloat16),
            pltpu.VMEM((depth, columns), jnp.bfloat16),
            pltpu.VMEM((2 * bands, ROWS_K, depth), jnp.bfloat16),
            pltpu.VMEM((2 * bands, ROWS_K, slab_depth), jnp.bfloat16),
            pltpu.VMEM((columns // LANES, 2 * bands * ROWS_K, LANES), jnp.float32),
            pltpu.VMEM((slab_columns // LANES, 2 * bands * ROWS_K, LANES), jnp.float32),
        ],
        compiler_params=pltpu.CompilerParams(vmem_limit_bytes=VMEM_BYTES, dimension_semantics=("arbitrary",)),
    )(weight, val_wave, cond_wave, jnp.asarray(dft_table(points)), jnp.asarray(place))


def one_hot(ids_ref, wanted):
    blocks = []
    for begin in range(0, ids_ref.shape[1], LANES):
        ids = jnp.broadcast_to(ids_ref[:, begin : begin + LANES], (LANES, LANES)).T
        ids = jnp.concatenate([ids] * (wanted.shape[1] // LANES), 1)
        blocks.append(jnp.where(ids == wanted, 1.0, 0.0).astype(jnp.bfloat16))
    return jnp.concatenate(blocks, 0)


def product_kernel(bands, panels_ref, slab_ref, ids_ref, slab_ids_ref, wanted_ref, slab_wanted_ref, out_ref, left, hot):
    rows = slab_wanted_ref.shape[1]

    @pl.when(pl.program_id(0) == 0)
    def _():
        chosen = jnp.dot(
            slab_ref[...], one_hot(slab_ids_ref, slab_wanted_ref[...]), preferred_element_type=jnp.float32
        )
        parts = chosen.reshape(-1, 2, bands, rows)
        swapped = jnp.concatenate([parts[:, 1:], -parts[:, :1]], 1).reshape(chosen.shape)
        left[:rows, :] = chosen.T.astype(jnp.bfloat16)
        left[rows:, :] = swapped.T.astype(jnp.bfloat16)

    wanted = wanted_ref[...]
    for begin in range(0, ids_ref.shape[1], LANES):
        ids = jnp.broadcast_to(ids_ref[:, begin : begin + LANES], (LANES, LANES)).T
        ids = jnp.concatenate([ids] * (wanted.shape[1] // LANES), 1)
        hot[begin : begin + LANES, :] = jnp.where(ids == wanted, 1.0, 0.0).astype(jnp.bfloat16)
    panel = jnp.dot(panels_ref[...], hot[...], preferred_element_type=jnp.float32).astype(jnp.bfloat16)
    chi = jnp.dot(left[...], panel, preferred_element_type=jnp.float32)
    out_ref[0] = chi[:rows]
    out_ref[1] = chi[rows:]


def product(bands, panels, slab, ids, slab_ids, wanted, slab_wanted):
    columns = wanted.shape[1]
    rows = slab_wanted.shape[1]
    block = 768
    whole = lambda array: pl.BlockSpec(array.shape, lambda n: (0, 0))
    kernel = lambda *refs: product_kernel(bands, *refs)
    return pl.pallas_call(
        kernel,
        grid=(columns // block,),
        in_specs=[
            whole(panels),
            whole(slab),
            whole(ids),
            whole(slab_ids),
            pl.BlockSpec((1, block), lambda n: (0, n)),
            whole(slab_wanted),
        ],
        out_specs=pl.BlockSpec((2, rows, block), lambda n: (0, 0, n)),
        out_shape=jax.ShapeDtypeStruct((2, rows, columns), jnp.float32),
        scratch_shapes=[
            pltpu.VMEM((2 * rows, panels.shape[0]), jnp.bfloat16),
            pltpu.VMEM((panels.shape[1], block), jnp.bfloat16),
        ],
        compiler_params=pltpu.CompilerParams(vmem_limit_bytes=VMEM_BYTES, dimension_semantics=("arbitrary",)),
    )(panels, slab, ids, slab_ids, wanted, slab_wanted)


def on_device(val_wave, cond_wave, val_energy, cond_energy, band_owner, grid_map):
    bands, points = val_wave.shape[0], val_wave.shape[1]
    band_total = cond_energy.shape[0]
    row_count = lax.axis_size("row")
    col_count = lax.axis_size("col")
    plan = make_plan(points, grid_map.shape[0], col_count, ROWS_DEV * row_count)
    energy = jnp.sum(jnp.where(band_owner[0] == jnp.arange(band_total, dtype=jnp.int32), cond_energy, 0.0))
    weight = -2.0 / (math.sqrt(bands * band_total) * (energy - val_energy))
    send, slab = spectra(plan, val_wave, cond_wave, weight)
    slab = lax.all_gather(slab, ("row", "col"), axis=0, tiled=True)
    by_columns = lax.all_to_all(send, "col", split_axis=0, concat_axis=0, tiled=True)
    panels = lax.all_gather(by_columns, "row", axis=0, tiled=True)
    panels = panels.reshape(-1, plan["block_lanes"])
    width = grid_map.shape[0] // col_count
    col, row = lax.axis_index("col"), lax.axis_index("row")
    ids = lax.dynamic_slice(jnp.asarray(plan["block_ids"]), (col, 0), (1, plan["block_lanes"]))
    slab_ids = jnp.asarray(plan["slab_ids"])[None]
    wanted = lax.dynamic_slice(grid_map, (col * width,), (width,))[None]
    slab_wanted = lax.dynamic_slice(grid_map, (row * ROWS_DEV,), (ROWS_DEV,))[None]
    return product(bands, panels, slab, ids, slab_ids, wanted, slab_wanted)


def solution(mesh):
    in_specs = (P(), P(("row", "col"), None, None, None), P(), P(), P(("row", "col")), P())
    out_specs = P(None, "row", "col")
    return jax.shard_map(
        on_device, mesh=mesh, in_specs=in_specs, out_specs=out_specs, check_vma=False
    )
```

profile of v0, /device:TPU:0, one launch (start us, length us, event | category | flops | bytes accessed | tf_op | source)
XLA Modules:
  0.0 249.7 jit_solution(4295223276221506291)
XLA Ops:
  6.5 0.0 all-gather.5.cloned.1.call-start
  7.2 1.3 fusion
  8.4 1.7 multiply_divide_fusion.refs_0_
  10.2 65.2 %shard_map.100 = (bf16[8,16,4224]{2,1,0:T(8,128)(2,1)}, bf16[16,1152]{1,0:T(8,128)(2,1)}) custom-call(f32[8]{0:T(128)} %multiply_divide_fusion.refs_0_, bf16[8,64,64,128]{3,2,1,0:T(8,128)(2,1)} %refs_1_.1, bf16[1,64,64,128]{3,2,1,0:T(8,128)(2,1)} %refs_2_.1, bf16[256,256]{1,0:T(8,128)(2,1)} %constant.32.clone.refs_3_, s32[1,1280]{1,0:T(1,128)} %constant.33.clone.refs_4_), custom_call_target="tpu_custom_call" | custom-call | tf_op jit(solution)/shard_map/pallas_call | solution.py:271
  75.4 0.0 all-gather.5.cloned.1.call-update
  75.4 0.0 all-gather.3.cloned.1.call-start
  75.4 21.3 %all_to_all.5 = bf16[8,16,4224]{2,1,0:T(8,128)(2,1)} all-to-all(bf16[8,16,4224]{2,1,0:T(8,128)(2,1)} %get-tuple-element.7), channel_id=1, replica_groups=mesh['row'=4,'col'=8] {'col'}, dimensions={0} | all-to-all | bytes 2162688 | tf_op jit(solution)/shard_map/all_to_all | solution.py:375
  96.7 0.0 all-gather.3.cloned.1.call-update
  96.7 1.3 dynamic_slice.11
  98.1 0.8 dynamic_slice.10
  98.9 0.6 broadcast_in_dim.15.refs_4_
  99.5 1.5 constant_dynamic-slice_fusion.refs_2_
  101.0 31.7 %all-gather.5.cloned.1.call-done.refs_1_ = bf16[512,1152]{1,0:T(8,128)(2,1)} async-done(((bf16[16,1152]{1,0:T(8,128)(2,1)}), bf16[512,1152]{1,0:T(8,128)(2,1)}) %all-gather.5.cloned.1.call-update) | async-done | bytes 1179664 | tf_op jit(solution)/shard_map/all_gather | solution.py:374
  132.7 83.5 %all-gather.3.cloned.1.call-done = bf16[32,16,4224]{2,1,0:T(8,128)(2,1)} async-done(((bf16[8,16,4224]{2,1,0:T(8,128)(2,1)}), bf16[32,16,4224]{2,1,0:T(8,128)(2,1)}) %all-gather.3.cloned.1.call-update) | async-done | bytes 4325392 | tf_op jit(solution)/shard_map/all_gather | solution.py:376
  216.2 26.6 %shard_map.101 = f32[2,256,3840]{2,1,0:T(8,128)} custom-call(bf16[512,4224]{1,0:T(8,128)(2,1)} %bitcast.4, bf16[512,1152]{1,0:T(8,128)(2,1)} %all-gather.5.cloned.1.call-done.refs_1_, s32[1,4224]{1,0:T(1,128)} %constant_dynamic-slice_fusion.refs_2_, s32[1,1152]{1,0:T(1,128)} %constant.38.refs_3_, s32[1,3840]{1,0:T(1,128)} %broadcast_in_dim.15.refs_4_, ...), custom_call_target="tpu_custom_call" | custom-call | tf_op jit(solution)/shard_map/pallas_call | solution.py:344
Async XLA Ops:
  6.5 126.2 %all-gather.5.cloned.1.call-start = ((), (), s32[]{:S(2)}) async-start(), calls=%async_computation.2 | async-start | bytes 1216512 | tf_op jit(solution)/shard_map/all_gather | solution.py:374
  75.4 140.8 %all-gather.3.cloned.1.call-start = ((), (), s32[]{:S(2)}) async-start(), calls=%async_computation.1 | async-start | bytes 5406720 | tf_op jit(solution)/shard_map/all_gather | solution.py:376
Sparse Core Ops, SparseCore 0:
  75.5 57.1 all-gather.4
  134.3 81.8 all-gather.2
where the time goes:
time: 250 us
  waiting for transfers between devices  115 us (46%)
  Pallas kernels  91.8 us (37%)
  blocking collectives  21.3 us (9%)
  between operations  14.1 us (6%)
  local copies, waits for them, and re-layouts  4.27 us (2%)
  other arithmetic  3 us (1%)
    all_gather x1, waiting for transfers between devices, on_device(): panels = lax.all_gather(by_columns, 'row', axis=0, tiled=True)  83.5 us
    pallas_call x1, Pallas kernels, spectra(): pl.pallas_call(kernel, grid=(bands,), in_specs=[pl.BlockSpec(memory_space...  65.2 us
    all_gather x1, waiting for transfers between devices, on_device(): slab = lax.all_gather(slab, ('row', 'col'), axis=0, tiled=True)  31.7 us
    pallas_call x1, Pallas kernels, product(): pl.pallas_call(kernel, grid=(columns // block,), in_specs=[whole(panels),...  26.6 us
    all_to_all x1, blocking collectives, on_device(): lax.all_to_all(send, 'col', split_axis=0, concat_axis=0, tiled=True)  21.3 us
  transfers between devices with their start and end apart: 2, of which 2 were waited for; matrix products, arithmetic and copies ran while one was open for 2% of the time, Pallas kernels for 0%

commit v1 on v0

v1 whole, which is shorter than its diff:
```python
import math

import jax
import jax.numpy as jnp
import numpy as np
from jax import lax
from jax.experimental import pallas as pl
from jax.experimental.pallas import tpu as pltpu
from jax.sharding import PartitionSpec as P

ROWS_DEV = 256
LANES = 128
VMEM_BYTES = 56 * 1024 * 1024
HALF = 64
KEEP = 40
ROWS_K = 48
ORIGIN = KEEP // 2
PARTS = 3
CHUNKS = 2


def round_up(value, step):
    return -(-value // step) * step


def length_counts(points):
    freq = np.arange(points) - points // 2
    square = freq * freq
    lengths = square[:, None, None] + square[None, :, None] + square[None, None, :]
    return np.cumsum(np.bincount(lengths.reshape(-1)))


def column_order(top):
    freq = np.arange(KEEP) - ORIGIN
    first, second = np.meshgrid(freq, freq, indexing="ij")
    length = (first * first + second * second).reshape(-1)
    order = np.argsort(length, kind="stable")
    order = order[length[order] <= top]
    return first.reshape(-1)[order], second.reshape(-1)[order], length[order]


class Bucket:
    def __init__(self, ranges, column_length):
        self.pieces = []
        self.edges = {}
        offset = 0
        for low, high in ranges:
            begin = offset
            for index in range(KEEP):
                freq = index - ORIGIN
                start = int(np.searchsorted(column_length, low - freq * freq, side="left"))
                stop = int(np.searchsorted(column_length, high - freq * freq, side="right"))
                if stop > start:
                    self.pieces.append((index, start, stop, offset))
                    offset += stop - start
            for length in range(low, high + 1):
                self.edges[length] = (begin, offset)
        self.size = offset

    def ids(self, column_2, column_3, points, width):
        out = np.full((width,), -1, np.int32)
        for index, start, stop, offset in self.pieces:
            k1 = (index - ORIGIN) % points
            k2 = column_2[start:stop] % points
            k3 = column_3[start:stop] % points
            out[offset : offset + stop - start] = (k1 * points + k2) * points + k3
        return out


def length_ranges(cumulative, first, step, count):
    shell = lambda rank: int(np.searchsorted(cumulative, rank, side="right"))
    ranges, low = [], shell(first)
    for part in range(1, count):
        before, after = shell(first + part * step - 1), shell(first + part * step)
        if before == after:
            if low < before:
                ranges.append((low, before - 1))
            if low <= before:
                ranges.append((before, before))
        elif low <= before:
            ranges.append((low, before))
        low = before + 1
    high = shell(first + count * step - 1)
    if low <= high:
        ranges.append((low, high))
    return ranges


def make_plan(points, total, blocks, slab, slab_blocks):
    cumulative = length_counts(points)
    shell = lambda rank: int(np.searchsorted(cumulative, rank, side="right"))
    width, slab_width = total // blocks, slab // slab_blocks
    step = width // PARTS
    column_2, column_3, column_length = column_order(shell(total - 1))
    buckets = [Bucket(length_ranges(cumulative, n * width, step, PARTS), column_length) for n in range(blocks)]
    slabs = [Bucket(length_ranges(cumulative, n * slab_width, slab_width, 1), column_length) for n in range(slab_blocks)]
    slab_top = shell(slab - 1)
    lanes = round_up(max(bucket.size for bucket in buckets), LANES)
    slab_lanes = round_up(max(bucket.size for bucket in slabs), LANES)
    windows = np.zeros((blocks, PARTS, 2), np.int64)
    for n, bucket in enumerate(buckets):
        for part in range(PARTS):
            rank = n * width + part * step
            windows[n, part, 0] = bucket.edges[shell(rank)][0] // LANES * LANES
            windows[n, part, 1] = round_up(bucket.edges[shell(rank + step - 1)][1], LANES)
    window = int((windows[..., 1] - windows[..., 0]).max())
    return dict(
        buckets=buckets,
        slabs=slabs,
        slab_columns=int(np.searchsorted(column_length, slab_top, side="right")),
        slab_edge=math.isqrt(slab_top),
        lanes=lanes,
        slab_lanes=slab_lanes,
        window=window,
        starts=np.minimum(windows[..., 0], lanes - window).astype(np.int32),
        ids=np.stack([bucket.ids(column_2, column_3, points, lanes) for bucket in buckets]),
        slab_ids=np.stack([bucket.ids(column_2, column_3, points, slab_lanes) for bucket in slabs]),
        column_place=((column_3 + ORIGIN) * KEEP + column_2 + ORIGIN).astype(np.int32),
    )


def dft_table(points):
    n = np.arange(points)
    freq = np.arange(KEEP) - ORIGIN
    angle = (n[:, None] * freq[None, :] % points) * (2.0 * np.pi / points)
    cosine, sine = np.cos(angle), np.sin(angle)
    table = np.zeros((2 * HALF, 2 * HALF))
    table[:points, :KEEP] = cosine
    table[HALF : HALF + points, :KEEP] = sine
    table[:points, HALF : HALF + KEEP] = -sine
    table[HALF : HALF + points, HALF : HALF + KEEP] = cosine
    high = table.astype(jnp.bfloat16)
    low = (table - high.astype(np.float64)).astype(jnp.bfloat16)
    return np.block([[high, low], [high, np.zeros_like(low)]])


def split_parts(value):
    high = value.astype(jnp.bfloat16)
    low = (value - high.astype(jnp.float32)).astype(jnp.bfloat16)
    return high, low


def apply_table(parts, table):
    both = jnp.dot(parts, table, preferred_element_type=jnp.float32)
    return both[:, :LANES] + both[:, LANES:]


def stack_complex(turned, low_lanes):
    real, imag = turned[:KEEP], turned[HALF : HALF + KEEP]
    first = jnp.where(low_lanes, real, pltpu.roll(imag, HALF, 1))
    second = jnp.where(low_lanes, pltpu.roll(real, HALF, 1), imag)
    return jnp.concatenate([first, second], 0)


def pack_pieces(pieces, width, source, rows, lane, out):
    for tile in range(width // LANES):
        left, right = tile * LANES, (tile + 1) * LANES
        value = jnp.zeros((rows, LANES), jnp.float32)
        for index, start, stop, offset in pieces:
            begin, end = max(left, offset), min(right, offset + stop - start)
            while begin < end:
                at = start + begin - offset
                block = source(index, at // LANES)
                shift = (begin - at) % LANES
                if shift:
                    block = pltpu.roll(block, shift, 1)
                value = block if begin == left else jnp.where(lane >= begin - left, block, value)
                begin = min(end, begin + LANES - at % LANES)
        out(tile, value)


def slab_tiles(plan):
    first = (ORIGIN - plan["slab_edge"]) * KEEP // LANES
    last = round_up((ORIGIN + plan["slab_edge"] + 1) * KEEP, LANES) // LANES
    return first, last


def spectrum_kernel(plan, points, first_band, weight_ref, val_ref, cond_ref, table_ref, plain_ref, weighted_ref,
                    cond_a, cond_b, middle, turned, last):
    band = pl.program_id(0)
    planes = 8
    lane = lax.broadcasted_iota(jnp.int32, (1, LANES), 1)
    low_lanes = lane < HALF
    depth = last.shape[0]

    @pl.when(band == 0)
    def _():
        scale = 1.0 / float(points) ** 1.5
        sign = jnp.where(low_lanes, scale, -scale)

        @pl.loop(0, points // planes)
        def _(block):
            rows = pl.ds(pl.multiple_of(block * planes * points, planes * points), planes * points)
            wave = cond_ref[0, pl.ds(block * planes, planes)].reshape(planes * points, LANES).astype(jnp.float32)
            cond_a[rows, :] = wave * scale
            cond_b[rows, :] = pltpu.roll(wave, HALF, 1) * sign

        last[KEEP * KEEP :, :] = jnp.zeros((depth - KEEP * KEEP, 2 * LANES), jnp.bfloat16)

    table = table_ref[...]
    step = planes * KEEP

    def first_axis(block):
        rows = pl.ds(pl.multiple_of(block * planes * points, planes * points), planes * points)
        wave = val_ref[0, pl.ds(block * planes, planes)].reshape(planes * points, LANES).astype(jnp.float32)
        other = pltpu.roll(wave, HALF, 1)
        density = jnp.where(low_lanes, wave, other) * cond_a[rows, :] + jnp.where(low_lanes, other, wave) * cond_b[rows, :]
        high, low = split_parts(density)
        field = apply_table(jnp.concatenate([high, low], 1), table)
        for pair in range(planes // 2):
            both = field[pair * 2 * points : (pair + 1) * 2 * points].T
            high, low = split_parts(stack_complex(both, low_lanes))
            at = pl.ds(pl.multiple_of((block * planes + pair * 2) * KEEP, 2 * KEEP), 2 * KEEP)
            middle[at, :LANES] = high
            middle[at, LANES:] = low

    def second_axis(block):
        rows = pl.ds(pl.multiple_of(block * step, step), step)
        turned[rows, :] = apply_table(middle[rows, :], table)

    first_axis(0)

    @pl.loop(1, points // planes)
    def _(block):
        second_axis(block - 1)
        first_axis(block)

    second_axis(points // planes - 1)

    for pair in range(KEEP // 2):
        both = jnp.concatenate(
            [turned[pl.ds(2 * pair, points, stride=KEEP), :], turned[pl.ds(2 * pair + 1, points, stride=KEEP), :]], 0
        ).T
        high, low = split_parts(stack_complex(both, low_lanes))
        at = slice(2 * pair * KEEP, (2 * pair + 2) * KEEP)
        last[at, :LANES] = high
        last[at, LANES:] = low

    weight = weight_ref[first_band + band]
    slab_first, slab_last = slab_tiles(plan)
    for begin in range(0, depth // LANES, 5):
        end = min(begin + 5, depth // LANES)
        field = apply_table(last[begin * LANES : end * LANES, :], table)
        for tile in range(begin, end):
            turn = field[(tile - begin) * LANES : (tile - begin + 1) * LANES].T
            for part in range(2):
                value = turn[part * HALF : part * HALF + ROWS_K]
                plain_ref[part, 0, :, tile * LANES : (tile + 1) * LANES] = value.astype(jnp.bfloat16)
                if slab_first <= tile < slab_last:
                    lanes = slice((tile - slab_first) * LANES, (tile - slab_first + 1) * LANES)
                    weighted_ref[part, 0, :, lanes] = (weight * value).astype(jnp.bfloat16)


def spectra(plan, val_wave, cond_wave, weight, first_band, count):
    points = val_wave.shape[1]
    depth = round_up(KEEP * KEEP, LANES)
    slab_first, slab_last = slab_tiles(plan)
    slab_depth = (slab_last - slab_first) * LANES
    grid_rows = points * points
    kernel = lambda *refs: spectrum_kernel(plan, points, first_band, *refs)
    return pl.pallas_call(
        kernel,
        grid=(count,),
        in_specs=[
            pl.BlockSpec(memory_space=pltpu.SMEM),
            pl.BlockSpec((1, points, points, 2 * points), lambda v: (first_band + v, 0, 0, 0)),
            pl.BlockSpec((1, points, points, 2 * points), lambda v: (0, 0, 0, 0)),
            pl.BlockSpec((4 * HALF, 4 * HALF), lambda v: (0, 0)),
        ],
        out_specs=[
            pl.BlockSpec((2, 1, ROWS_K, depth), lambda v: (0, v, 0, 0)),
            pl.BlockSpec((2, 1, ROWS_K, slab_depth), lambda v: (0, v, 0, 0)),
        ],
        out_shape=[
            jax.ShapeDtypeStruct((2, count, ROWS_K, depth), jnp.bfloat16),
            jax.ShapeDtypeStruct((2, count, ROWS_K, slab_depth), jnp.bfloat16),
        ],
        scratch_shapes=[
            pltpu.VMEM((grid_rows, LANES), jnp.float32),
            pltpu.VMEM((grid_rows, LANES), jnp.float32),
            pltpu.VMEM((points * KEEP, 2 * LANES), jnp.bfloat16),
            pltpu.VMEM((points * KEEP, LANES), jnp.float32),
            pltpu.VMEM((depth, 2 * LANES), jnp.bfloat16),
        ],
        compiler_params=pltpu.CompilerParams(vmem_limit_bytes=VMEM_BYTES, dimension_semantics=("arbitrary",)),
        cost_estimate=pl.CostEstimate(flops=count * 1200000000, bytes_accessed=count * 2000000, transcendentals=0),
        name="spectra",
    )(weight, val_wave, cond_wave, jnp.asarray(dft_table(points)))


def pack_kernel(plan, groups, col_ref, place_ref, *refs):
    plains, weighteds = refs[:groups], refs[groups : 2 * groups]
    slots = len(plan["buckets"])
    outs = refs[2 * groups : 2 * groups + slots]
    slab_ref, sorter, plain_sorted, weighted_sorted, blocks = refs[2 * groups + slots :]
    depth, columns = sorter.shape
    count = 2 * sum(plain.shape[1] for plain in plains)
    lane = lax.broadcasted_iota(jnp.int32, (1, LANES), 1)
    for begin in range(0, depth, LANES):
        at = lax.broadcasted_iota(jnp.int32, (LANES, columns), 0) + begin
        sorter[begin : begin + LANES, :] = jnp.where(at == place_ref[...], 1.0, 0.0).astype(jnp.bfloat16)

    def sort_rows(parts, which, target):
        rows = jnp.concatenate([part[n] for n in range(2) for part in parts], 0)
        rows = rows.reshape(count * ROWS_K, rows.shape[2])
        value = jnp.dot(rows, which, preferred_element_type=jnp.float32)
        for tile in range(target.shape[0]):
            target[tile] = value[:, tile * LANES : (tile + 1) * LANES]

    slab_first, slab_last = slab_tiles(plan)
    sort_rows(plains, sorter[...], plain_sorted)
    sort_rows(weighteds, sorter[slab_first * LANES : slab_last * LANES, : weighted_sorted.shape[0] * LANES], weighted_sorted)

    def plain_at(index, tile):
        return plain_sorted[tile, pl.ds(index, count, stride=ROWS_K), :]

    def weighted_at(index, tile):
        return weighted_sorted[tile, pl.ds(index, count, stride=ROWS_K), :]

    col = col_ref[0]
    for block, bucket in enumerate(plan["buckets"]):
        slot = jnp.bitwise_xor(col, block)

        def keep(tile, value):
            blocks[slot, :, tile * LANES : (tile + 1) * LANES] = value.astype(jnp.bfloat16)

        pack_pieces(bucket.pieces, plan["lanes"], plain_at, count, lane, keep)
    for slot, out in enumerate(outs):
        out[...] = blocks[slot]
    for block, bucket in enumerate(plan["slabs"]):

        def keep_slab(tile, value):
            slab_ref[block, :, tile * LANES : (tile + 1) * LANES] = value.astype(jnp.bfloat16)

        pack_pieces(bucket.pieces, plan["slab_lanes"], weighted_at, count, lane, keep_slab)


def packed(plan, col, plains, weighteds):
    depth = plains[0].shape[3]
    count = 2 * sum(plain.shape[1] for plain in plains)
    columns = round_up(plan["column_place"].shape[0], 256)
    slab_columns = round_up(plan["slab_columns"], LANES)
    place = np.full((1, columns), -1, np.int32)
    place[0, : plan["column_place"].shape[0]] = plan["column_place"]
    slots, lanes = len(plan["buckets"]), plan["lanes"]
    kernel = lambda *refs: pack_kernel(plan, len(plains), *refs)
    vmem = pl.BlockSpec(memory_space=pltpu.VMEM)
    slab_shape = (len(plan["slabs"]), count, plan["slab_lanes"])
    return pl.pallas_call(
        kernel,
        in_specs=[pl.BlockSpec(memory_space=pltpu.SMEM)] + [vmem] * (1 + 2 * len(plains)),
        out_specs=[vmem] * (slots + 1),
        out_shape=[jax.ShapeDtypeStruct((count, lanes), jnp.bfloat16)] * slots
        + [jax.ShapeDtypeStruct(slab_shape, jnp.bfloat16)],
        scratch_shapes=[
            pltpu.VMEM((depth, columns), jnp.bfloat16),
            pltpu.VMEM((columns // LANES, count * ROWS_K, LANES), jnp.float32),
            pltpu.VMEM((slab_columns // LANES, count * ROWS_K, LANES), jnp.float32),
            pltpu.VMEM((slots, count, lanes), jnp.bfloat16),
        ],
        compiler_params=pltpu.CompilerParams(vmem_limit_bytes=VMEM_BYTES),
        cost_estimate=pl.CostEstimate(flops=4000000000, bytes_accessed=4000000, transcendentals=0),
        name="pack",
    )(col, jnp.asarray(place), *plains, *weighteds)


def one_hot(ids_ref, begin, wanted):
    ids = jnp.broadcast_to(ids_ref[:, pl.ds(begin, LANES)], (LANES, LANES)).T
    ids = jnp.concatenate([ids] * (wanted.shape[1] // LANES), 1)
    return jnp.where(ids == wanted, 1.0, 0.0).astype(jnp.bfloat16)


def product_kernel(shape, place_ref, slab_ref, ids_ref, slab_ids_ref, wanted_ref, slab_wanted_ref, *refs):
    rounds, chunks, slots, group = shape
    panels = refs[: chunks * (2 * rounds - 1)]
    out_ref, panel, chosen_rows, left, hot = refs[chunks * (2 * rounds - 1) :]
    rows = slab_wanted_ref.shape[1]
    window = hot.shape[0]

    @pl.when(pl.program_id(0) == 0)
    def _():
        size = slots * group
        col = place_ref[0]
        for chunk in range(chunks):
            own, *others = panels[chunk * (2 * rounds - 1) : (chunk + 1) * (2 * rounds - 1)]
            for turn in range(rounds):
                base = (turn * chunks + chunk) * size
                if turn == 0:
                    panel[base : base + size, :] = own[...]
                else:
                    panel[base : base + size, :] = others[turn - 1][...] + others[2 * rounds - 2 - turn][...]
                for slot in range(slots):
                    chosen_rows[base + slot * group : base + (slot + 1) * group, :] = slab_ref[
                        jnp.bitwise_xor(col, slot), turn, chunk
                    ].astype(jnp.float32)
        choice = jnp.concatenate(
            [one_hot(slab_ids_ref, begin, slab_wanted_ref[...]) for begin in range(0, slab_ids_ref.shape[1], LANES)], 0
        )
        chosen = jnp.dot(chosen_rows[...].astype(jnp.bfloat16), choice, preferred_element_type=jnp.float32)
        lane = lax.broadcasted_iota(jnp.int32, (1, LANES), 1)
        real_lanes = lane % group < group // 2
        for begin in range(0, chosen.shape[0], LANES):
            turned = chosen[begin : begin + LANES].T
            after = pltpu.roll(turned, LANES - group // 2, 1)
            before = pltpu.roll(turned, group // 2, 1)
            left[:rows, begin : begin + LANES] = turned.astype(jnp.bfloat16)
            left[rows:, begin : begin + LANES] = jnp.where(real_lanes, after, -before).astype(jnp.bfloat16)

    start = pl.multiple_of(place_ref[1 + pl.program_id(0)], LANES)
    wanted = wanted_ref[...]
    for begin in range(0, window, LANES):
        hot[begin : begin + LANES, :] = one_hot(ids_ref, pl.multiple_of(start + begin, LANES), wanted)
    ordered = jnp.dot(panel[:, pl.ds(start, window)], hot[...], preferred_element_type=jnp.float32).astype(jnp.bfloat16)
    chi = jnp.dot(left[...], ordered, preferred_element_type=jnp.float32)
    out_ref[0] = chi[:rows]
    out_ref[1] = chi[rows:]


def product(plan, shape, place, slab, ids, slab_ids, wanted, slab_wanted, panels):
    rounds, chunks, slots, group = shape
    columns, rows, pairs = wanted.shape[1], slab_wanted.shape[1], rounds * chunks * slots * group
    block = columns // PARTS
    whole = lambda array: pl.BlockSpec(array.shape, lambda n: (0,) * array.ndim)
    kernel = lambda *refs: product_kernel(shape, *refs)
    return pl.pallas_call(
        kernel,
        grid=(PARTS,),
        in_specs=[
            pl.BlockSpec(memory_space=pltpu.SMEM),
            whole(slab),
            whole(ids),
            whole(slab_ids),
            pl.BlockSpec((1, block), lambda n: (0, n)),
            whole(slab_wanted),
        ]
        + [whole(panel) for panel in panels],
        out_specs=pl.BlockSpec((2, rows, block), lambda n: (0, 0, n)),
        out_shape=jax.ShapeDtypeStruct((2, rows, columns), jnp.float32),
        scratch_shapes=[
            pltpu.VMEM((pairs, plan["lanes"]), jnp.bfloat16),
            pltpu.VMEM((pairs, plan["slab_lanes"]), jnp.float32),
            pltpu.VMEM((2 * rows, pairs), jnp.bfloat16),
            pltpu.VMEM((plan["window"], block), jnp.bfloat16),
        ],
        compiler_params=pltpu.CompilerParams(vmem_limit_bytes=VMEM_BYTES, dimension_semantics=("arbitrary",)),
        cost_estimate=pl.CostEstimate(flops=12000000000, bytes_accessed=16000000, transcendentals=0),
        name="product",
    )(place, slab, ids, slab_ids, wanted, slab_wanted, *panels)


def shifted(value, axis, step):
    size = lax.axis_size(axis)
    return lax.ppermute(value, axis, [(n, n + step) for n in range(size) if 0 <= n + step < size])


def from_planes(own):
    size = lax.axis_size("row")
    further, back = [], []
    for step in range(1, size):
        if step < 3:
            further.append(shifted(own, "row", -step))
            back.append(shifted(own, "row", step))
        else:
            further.append(shifted(further[-1], "row", -1))
            back.append(shifted(back[-1], "row", 1))
    return further, back


def within_plane(blocks):
    size = lax.axis_size("col")
    parts = [blocks[0]]
    for slot in range(1, size):
        parts.append(lax.ppermute(blocks[slot], "col", [(n, n ^ slot) for n in range(size)]))
    return jnp.concatenate(parts, 0)


def slab_to_rows(slab):
    size = lax.axis_size("row")
    row = lax.axis_index("row")
    out = [lax.dynamic_index_in_dim(slab, row, 0, keepdims=False)]
    sent = {}
    for step in range(1 - size, size):
        if step:
            block = lax.dynamic_index_in_dim(slab, jnp.clip(row + step, 0, size - 1), 0, keepdims=False)
            sent[step] = shifted(block, "row", step)
    for turn in range(1, size):
        out.append(sent[-turn] + sent[size - turn])
    return jnp.stack(out)


def on_device(val_wave, cond_wave, val_energy, cond_energy, band_owner, grid_map):
    bands, points = val_wave.shape[0], val_wave.shape[1]
    band_total = cond_energy.shape[0]
    row_count = lax.axis_size("row")
    col_count = lax.axis_size("col")
    col, row = lax.axis_index("col"), lax.axis_index("row")
    plan = make_plan(points, grid_map.shape[0], col_count, ROWS_DEV * row_count, row_count)
    energy = jnp.sum(jnp.where(band_owner[0] == jnp.arange(band_total, dtype=jnp.int32), cond_energy, 0.0))
    weight = -2.0 / (math.sqrt(bands * band_total) * (energy - val_energy))
    chunk = bands // CHUNKS
    panels, slabs = [], []
    for part in range(CHUNKS):
        pieces = []
        split = 1 if part == 0 else 2
        for piece in range(split):
            count = chunk // split
            pieces.append(spectra(plan, val_wave, cond_wave, weight, part * chunk + piece * count, count))
        *blocks, slab = packed(plan, col[None], [p[0] for p in pieces], [p[1] for p in pieces])
        own = within_plane(blocks)
        further, back = from_planes(own)
        panels += [own] + further + back
        slabs.append(slab)
    slab = slab_to_rows(jnp.stack(slabs, 1))
    slab = lax.all_gather(slab, "col", axis=0)
    width = grid_map.shape[0] // col_count
    place = jnp.concatenate([col[None], lax.dynamic_index_in_dim(jnp.asarray(plan["starts"]), col, 0, keepdims=False)])
    ids = lax.dynamic_slice(jnp.asarray(plan["ids"]), (col, 0), (1, plan["lanes"]))
    slab_ids = lax.dynamic_slice(jnp.asarray(plan["slab_ids"]), (row, 0), (1, plan["slab_lanes"]))
    wanted = lax.dynamic_slice(grid_map, (col * width,), (width,))[None]
    slab_wanted = lax.dynamic_slice(grid_map, (row * ROWS_DEV,), (ROWS_DEV,))[None]
    shape = (row_count, CHUNKS, col_count, 2 * chunk)
    return product(plan, shape, place, slab, ids, slab_ids, wanted, slab_wanted, panels)


def solution(mesh):
    in_specs = (P(), P(("row", "col"), None, None, None), P(), P(), P(("row", "col")), P())
    out_specs = P(None, "row", "col")
    return jax.shard_map(
        on_device, mesh=mesh, in_specs=in_specs, out_specs=out_specs, check_vma=False
    )
```

time: 250 us -> 253 us (1.012)
  the two profiles are of different devices: /device:TPU:0 before, /device:TPU:8 now
where the time goes in v1:
time: 253 us; the launch traced here: 252 us
  waiting for transfers between devices  81.1 us (32%)
  Pallas kernels  77.9 us (31%)
  starting transfers between devices  68.4 us (27%)
  blocking collectives  8.93 us (4%)
  local copies, waits for them, and re-layouts  8.92 us (4%)
  other arithmetic  5.3 us (2%)
    ppermute x18, waiting for transfers between devices, shifted(): lax.ppermute(value, axis, [(n, n + step) for n in range(size) if 0 <= n +...  60.5 us
    ppermute x18, starting transfers between devices, shifted(): lax.ppermute(value, axis, [(n, n + step) for n in range(size) if 0 <= n +...  57.6 us
    pallas_call x3, Pallas kernels, spectra(): pl.pallas_call(kernel, grid=(count,), in_specs=[pl.BlockSpec(memory_space...  51.7 us
    ppermute x14, waiting for transfers between devices, within_plane(): lax.ppermute(blocks[slot], 'col', [(n, n ^ slot) for n in range(size)])  20.6 us
    pallas_call x1, Pallas kernels, product(): pl.pallas_call(kernel, grid=(PARTS,), in_specs=[pl.BlockSpec(memory_space...  16.2 us
    ppermute x14, starting transfers between devices, within_plane(): lax.ppermute(blocks[slot], 'col', [(n, n ^ slot) for n in range(size)])  10.8 us
    pallas_call x2, Pallas kernels, packed(): pl.pallas_call(kernel, in_specs=[pl.BlockSpec(memory_space=pltpu.SMEM)] +...  9.95 us
    all_gather x1, blocking collectives, on_device(): slab = lax.all_gather(slab, 'col', axis=0)  8.93 us
  transfers between devices with their start and end apart: 32, of which 12 were waited for; matrix products, arithmetic and copies ran while one was open for 4% of the time, Pallas kernels for 12%

profile of v1, /device:TPU:8, one launch (start us, length us, event | category | flops | bytes accessed | tf_op | source)
XLA Modules:
  0.0 251.8 jit_solution(16550036270761356780)
XLA Ops:
  0.7 1.3 fusion.13
  1.9 1.8 multiply_divide_fusion.refs_0_
  3.7 13.7 %spectra.5 = (bf16[2,2,48,1664]{3,2,1,0:T(8,128)(2,1)}, bf16[2,2,48,640]{3,2,1,0:T(8,128)(2,1)}) custom-call(f32[8]{0:T(128)} %multiply_divide_fusion.refs_0_, bf16[8,64,64,128]{3,2,1,0:T(8,128)(2,1)} %refs_1_.7, bf16[1,64,64,128]{3,2,1,0:T(8,128)(2,1)} %refs_2_.5, bf16[256,256]{1,0:T(8,128)(2,1)} %constant.74.clone.refs_3_), custom_call_target="tpu_custom_call" | custom-call | flops 2400000000 | bytes 4000000 | tf_op jit(solution)/shard_map/spectra/pallas_call | solution.py:261
  17.4 13.7 %spectra.4 = (bf16[2,2,48,1664]{3,2,1,0:T(8,128)(2,1)}, bf16[2,2,48,640]{3,2,1,0:T(8,128)(2,1)}) custom-call(f32[8]{0:T(128)} %multiply_divide_fusion.refs_0_, bf16[8,64,64,128]{3,2,1,0:T(8,128)(2,1)} %refs_1_.7, bf16[1,64,64,128]{3,2,1,0:T(8,128)(2,1)} %refs_2_.5, bf16[256,256]{1,0:T(8,128)(2,1)} %constant.74.clone.refs_3_), custom_call_target="tpu_custom_call" | custom-call | flops 2400000000 | bytes 4000000 | tf_op jit(solution)/shard_map/spectra/pallas_call | solution.py:261
  31.1 5.0 %pack.3 = (bf16[8,4224]{1,0:T(8,128)(2,1)}, bf16[8,4224]{1,0:T(8,128)(2,1)}, bf16[8,4224]{1,0:T(8,128)(2,1)}, bf16[8,4224]{1,0:T(8,128)(2,1)}, bf16[8,4224]{1,0:...) custom-call(s32[1]{0:T(128)} %bitcast.refs_0_, ...), custom_call_target="tpu_custom_call" | custom-call | flops 4000000000 | bytes 4000000 | tf_op jit(solution)/shard_map/pack/pallas_call | solution.py:349
  36.1 1.6 collective-permute-start.20
  38.0 1.5 collective-permute-start.22
  39.7 24.3 %spectra.3 = (bf16[2,4,48,1664]{3,2,1,0:T(8,128)(2,1)}, bf16[2,4,48,640]{3,2,1,0:T(8,128)(2,1)}) custom-call(f32[8]{0:T(128)} %multiply_divide_fusion.refs_0_, bf16[8,64,64,128]{3,2,1,0:T(8,128)(2,1)} %refs_1_.7, bf16[1,64,64,128]{3,2,1,0:T(8,128)(2,1)} %refs_2_.5, bf16[256,256]{1,0:T(8,128)(2,1)} %constant.74.clone.refs_3_), custom_call_target="tpu_custom_call" | custom-call | flops 4800000000 | bytes 8000000 | tf_op jit(solution)/shard_map/spectra/pallas_call | solution.py:261
  64.0 1.4 dynamic_slice.49
  66.8 5.0 %pack.2 = (bf16[8,4224]{1,0:T(8,128)(2,1)}, bf16[8,4224]{1,0:T(8,128)(2,1)}, bf16[8,4224]{1,0:T(8,128)(2,1)}, bf16[8,4224]{1,0:T(8,128)(2,1)}, bf16[8,4224]{1,0:...) custom-call(s32[1]{0:T(128)} %bitcast.refs_0_, ...), custom_call_target="tpu_custom_call" | custom-call | flops 4000000000 | bytes 4000000 | tf_op jit(solution)/shard_map/pack/pallas_call | solution.py:349
  71.8 0.9 constant_dynamic-update-slice_fusion.7
  72.7 1.5 constant_dynamic-slice_fusion.1.refs_2_
  74.9 0.9 fusion.2
  75.8 2.5 collective-permute-start.24
  78.7 3.4 %collective-permute-start.5 = (bf16[2,8,384]{2,1,0:T(8,128)(2,1)S(1)}, bf16[2,8,384]{2,1,0:T(8,128)(2,1)S(1)}, u32[]{:S(2)}, u32[]{:S(2)}) collective-permute-start(bf16[2,8,384]{2,1,0:T(8,128)(2,1)S(1)} %fusion.1), channel_id=1, source_target_pairs={{0,8},{8,16},{16,24},{1,9},{9,17},{17,25},{2,10},{10,18},{18,26},{... | collective-permute-start | bytes 36872 | tf_op jit(solution)/shard_map/ppermute | solution.py:453
  82.1 2.4 collective-permute-start
  85.3 1.5 collective-permute-start.2
  86.9 1.4 collective-permute-done.6
  88.3 1.5 collective-permute-start.7
  89.8 3.0 %collective-permute-done.7 = bf16[8,4224]{1,0:T(8,128)(2,1)S(1)} collective-permute-done((bf16[8,4224]{1,0:T(8,128)(2,1)}, bf16[8,4224]{1,0:T(8,128)(2,1)S(1)}, u32[]{:S(2)}, u32[]{:S(2)}) %collective-permute-start.7) | collective-permute-done | bytes 67616 | tf_op jit(solution)/shard_map/ppermute | solution.py:473
  93.0 4.4 %collective-permute-done.8 = bf16[8,4224]{1,0:T(8,128)(2,1)S(1)} collective-permute-done((bf16[8,4224]{1,0:T(8,128)(2,1)}, bf16[8,4224]{1,0:T(8,128)(2,1)S(1)}, u32[]{:S(2)}, u32[]{:S(2)}) %collective-permute-start.8) | collective-permute-done | bytes 67616 | tf_op jit(solution)/shard_map/ppermute | solution.py:473
  97.4 1.5 collective-permute-start.9
  98.9 3.0 %collective-permute-done.9 = bf16[8,4224]{1,0:T(8,128)(2,1)S(1)} collective-permute-done((bf16[8,4224]{1,0:T(8,128)(2,1)}, bf16[8,4224]{1,0:T(8,128)(2,1)S(1)}, u32[]{:S(2)}, u32[]{:S(2)}) %collective-permute-start.9) | collective-permute-done | bytes 67616 | tf_op jit(solution)/shard_map/ppermute | solution.py:473
  102.0 4.5 %collective-permute-done.10 = bf16[8,4224]{1,0:T(8,128)(2,1)S(1)} collective-permute-done((bf16[8,4224]{1,0:T(8,128)(2,1)}, bf16[8,4224]{1,0:T(8,128)(2,1)S(1)}, u32[]{:S(2)}, u32[]{:S(2)}) %collective-permute-start.10) | collective-permute-done | bytes 67616 | tf_op jit(solution)/shard_map/ppermute | solution.py:473
  106.5 1.1 collective-permute-start.11
  107.6 4.3 %collective-permute-done.11 = bf16[8,4224]{1,0:T(8,128)(2,1)S(1)} collective-permute-done((bf16[8,4224]{1,0:T(8,128)(2,1)}, bf16[8,4224]{1,0:T(8,128)(2,1)S(1)}, u32[]{:S(2)}, u32[]{:S(2)}) %collective-permute-start.11) | collective-permute-done | bytes 67616 | tf_op jit(solution)/shard_map/ppermute | solution.py:473
  111.9 5.4 %collective-permute-start.3 = (bf16[2,8,384]{2,1,0:T(8,128)(2,1)S(1)}, bf16[2,8,384]{2,1,0:T(8,128)(2,1)S(1)}, u32[]{:S(2)}, u32[]{:S(2)}) collective-permute-start(bf16[2,8,384]{2,1,0:T(8,128)(2,1)S(1)} %get-tuple-element.57), channel_id=1, source_target_pairs={{0,16},{8,24},{1,17},{9,25},{2,18},{10,26},{3,19},{11,27},{4,20},{... | collective-permute-start | bytes 36872 | tf_op jit(solution)/shard_map/ppermute | solution.py:453
  118.1 10.8 %collective-permute-start.30 = (bf16[64,4224]{1,0:T(8,128)(2,1)S(1)}, bf16[64,4224]{1,0:T(8,128)(2,1)S(1)}, u32[]{:S(2)}, u32[]{:S(2)}) collective-permute-start(bf16[64,4224]{1,0:T(8,128)(2,1)S(1)} %constant_dynamic-update-slice_fusion.8.refs_13_), channel_id=1, source_target_pairs={{0,16},{8,24},{1,17},{9,25},{2,18},{10,26},{3,19},{11,27},{4,20},{... | collective-permute-start | bytes 1622024 | tf_op jit(solution)/shard_map/ppermute | solution.py:453
  128.9 1.9 collective-permute-start.29
  130.8 1.3 collective-permute-start.27
  132.1 4.0 %collective-permute-start.26 = (bf16[64,4224]{1,0:T(8,128)(2,1)S(1)}, bf16[64,4224]{1,0:T(8,128)(2,1)S(1)}, u32[]{:S(2)}, u32[]{:S(2)}) collective-permute-start(bf16[64,4224]{1,0:T(8,128)(2,1)S(1)} %constant_dynamic-update-slice_fusion.8.refs_13_), channel_id=1, source_target_pairs={{8,0},{16,8},{24,16},{9,1},{17,9},{25,17},{10,2},{18,10},{26,18},{... | collective-permute-start | bytes 1622024 | tf_op jit(solution)/shard_map/ppermute | solution.py:453
  136.1 5.5 %collective-permute-start.17 = (bf16[64,4224]{1,0:T(8,128)(2,1)S(1)}, bf16[64,4224]{1,0:T(8,128)(2,1)S(1)}, u32[]{:S(2)}, u32[]{:S(2)}) collective-permute-start(bf16[64,4224]{1,0:T(8,128)(2,1)S(1)} %constant_dynamic-update-slice_fusion.refs_6_), channel_id=1, source_target_pairs={{0,16},{8,24},{1,17},{9,25},{2,18},{10,26},{3,19},{11,27},{4,20},{... | collective-permute-start | bytes 1622024 | tf_op jit(solution)/shard_map/ppermute | solution.py:453
  141.7 7.4 %collective-permute-done.30.refs_18_ = bf16[64,4224]{1,0:T(8,128)(2,1)S(1)} collective-permute-done((bf16[64,4224]{1,0:T(8,128)(2,1)S(1)}, bf16[64,4224]{1,0:T(8,128)(2,1)S(1)}, u32[]{:S(2)}, u32[]{:S(2)}) %collective-permute-start.30) | collective-permute-done | bytes 540704 | tf_op jit(solution)/shard_map/ppermute | solution.py:453
  149.1 1.9 collective-permute-start.16
  151.0 21.2 %collective-permute-done.29.refs_17_ = bf16[64,4224]{1,0:T(8,128)(2,1)S(1)} collective-permute-done((bf16[64,4224]{1,0:T(8,128)(2,1)S(1)}, bf16[64,4224]{1,0:T(8,128)(2,1)S(1)}, u32[]{:S(2)}, u32[]{:S(2)}) %collective-permute-start.29) | collective-permute-done | bytes 540704 | tf_op jit(solution)/shard_map/ppermute | solution.py:453
  172.2 1.3 collective-permute-start.14
  174.8 1.3 constant_dynamic-slice_fusion.refs_3_
  176.1 1.9 collective-permute-start.13
  178.0 4.4 %collective-permute-start.31 = (bf16[64,4224]{1,0:T(8,128)(2,1)S(1)}, bf16[64,4224]{1,0:T(8,128)(2,1)S(1)}, u32[]{:S(2)}, u32[]{:S(2)}) collective-permute-start(bf16[64,4224]{1,0:T(8,128)(2,1)S(1)} %collective-permute-done.30.refs_18_), channel_id=1, source_target_pairs={{0,8},{8,16},{16,24},{1,9},{9,17},{17,25},{2,10},{10,18},{18,26},{... | collective-permute-start | bytes 1622024 | tf_op jit(solution)/shard_map/ppermute | solution.py:453
  182.5 1.3 collective-permute-done.17.refs_11_
  183.7 1.9 collective-permute-start.28
  185.7 9.7 %collective-permute-done.16.refs_10_ = bf16[64,4224]{1,0:T(8,128)(2,1)S(1)} collective-permute-done((bf16[64,4224]{1,0:T(8,128)(2,1)S(1)}, bf16[64,4224]{1,0:T(8,128)(2,1)S(1)}, u32[]{:S(2)}, u32[]{:S(2)}) %collective-permute-start.16) | collective-permute-done | bytes 540704 | tf_op jit(solution)/shard_map/ppermute | solution.py:453
  195.3 4.4 %collective-permute-start.18 = (bf16[64,4224]{1,0:T(8,128)(2,1)S(1)}, bf16[64,4224]{1,0:T(8,128)(2,1)S(1)}, u32[]{:S(2)}, u32[]{:S(2)}) collective-permute-start(bf16[64,4224]{1,0:T(8,128)(2,1)S(1)} %collective-permute-done.17.refs_11_), channel_id=1, source_target_pairs={{0,8},{8,16},{16,24},{1,9},{9,17},{17,25},{2,10},{10,18},{18,26},{... | collective-permute-start | bytes 1622024 | tf_op jit(solution)/shard_map/ppermute | solution.py:453
  199.7 4.2 %collective-permute-start.15 = (bf16[64,4224]{1,0:T(8,128)(2,1)S(1)}, bf16[64,4224]{1,0:T(8,128)(2,1)S(1)}, u32[]{:S(2)}, u32[]{:S(2)}) collective-permute-start(bf16[64,4224]{1,0:T(8,128)(2,1)S(1)} %collective-permute-done.14.refs_8_), channel_id=1, source_target_pairs={{8,0},{16,8},{24,16},{9,1},{17,9},{25,17},{10,2},{18,10},{26,18},{... | collective-permute-start | bytes 1622024 | tf_op jit(solution)/shard_map/ppermute | solution.py:453
  204.0 8.9 %all-gather = bf16[32,2,8,384]{3,2,0,1:T(8,128)(2,1)S(1)} all-gather(bf16[4,2,8,384]{3,2,0,1:T(8,128)(2,1)S(1)} %pad_maximum_fusion), channel_id=2, replica_groups=mesh['row'=4,'col'=8] {'col'}, dimensions={0}, use_global_device_ids=true | all-gather | bytes 442368 | tf_op jit(solution)/shard_map/all_gather | solution.py:514
  213.8 10.0 %collective-permute-done.28.refs_16_ = bf16[64,4224]{1,0:T(8,128)(2,1)S(1)} collective-permute-done((bf16[64,4224]{1,0:T(8,128)(2,1)S(1)}, bf16[64,4224]{1,0:T(8,128)(2,1)S(1)}, u32[]{:S(2)}, u32[]{:S(2)}) %collective-permute-start.28) | collective-permute-done | bytes 540704 | tf_op jit(solution)/shard_map/ppermute | solution.py:453
  223.8 11.0 %collective-permute-done.15.refs_9_ = bf16[64,4224]{1,0:T(8,128)(2,1)S(1)} collective-permute-done((bf16[64,4224]{1,0:T(8,128)(2,1)S(1)}, bf16[64,4224]{1,0:T(8,128)(2,1)S(1)}, u32[]{:S(2)}, u32[]{:S(2)}) %collective-permute-start.15) | collective-permute-done | bytes 540704 | tf_op jit(solution)/shard_map/ppermute | solution.py:453
  235.6 16.2 %product.1 = f32[2,256,3840]{2,1,0:T(8,128)} custom-call(s32[4]{0:T(128)} %pad_add_fusion.refs_0_, bf16[8,4,2,8,384]{4,3,2,1,0:T(8,128)(2,1)} %bitcast.27, s32[1,4224]{1,0:T(1,128)} %constant_dynamic-slice_fusion.1.refs_2_, s32[1,384]{1,0:T(1,128)} %constant_dynamic-slice_fusion.refs_3_, s32[1,3840]{1,0:T(1,128)} %broadcast_in_dim.17.refs_4_, ...), custom_call_target="tpu_custom_call" | custom-call | flops 12000000000 | bytes 16000000 | tf_op jit(solution)/shard_map/product/pallas_call | solution.py:425
  (91 shorter events, 7.7 us)
Async XLA Ops:
  36.1 39.7 %collective-permute-start.19 = (bf16[8,4224]{1,0:T(8,128)(2,1)}, bf16[8,4224]{1,0:T(8,128)(2,1)S(1)}, u32[]{:S(2)}, u32[]{:S(2)}) collective-permute-start(bf16[8,4224]{1,0:T(8,128)(2,1)} %get-tuple-element.46), channel_id=1, source_target_pairs={{0,1},{1,0},{2,3},{3,2},{4,5},{5,4},{6,7},{7,6},{8,9},{9,8},{10,11... | collective-permute-start | bytes 202760 | tf_op jit(solution)/shard_map/ppermute | solution.py:473
  36.1 42.2 %collective-permute-start.20 = (bf16[8,4224]{1,0:T(8,128)(2,1)}, bf16[8,4224]{1,0:T(8,128)(2,1)S(1)}, u32[]{:S(2)}, u32[]{:S(2)}) collective-permute-start(bf16[8,4224]{1,0:T(8,128)(2,1)} %get-tuple-element.47), channel_id=1, source_target_pairs={{0,2},{1,3},{2,0},{3,1},{4,6},{5,7},{6,4},{7,5},{8,10},{9,11},{10,... | collective-permute-start | bytes 202760 | tf_op jit(solution)/shard_map/ppermute | solution.py:473
  37.7 41.0 %collective-permute-start.21 = (bf16[8,4224]{1,0:T(8,128)(2,1)}, bf16[8,4224]{1,0:T(8,128)(2,1)S(1)}, u32[]{:S(2)}, u32[]{:S(2)}) collective-permute-start(bf16[8,4224]{1,0:T(8,128)(2,1)} %get-tuple-element.48), channel_id=1, source_target_pairs={{0,3},{1,2},{2,1},{3,0},{4,7},{5,6},{6,5},{7,4},{8,11},{9,10},{10,... | collective-permute-start | bytes 202760 | tf_op jit(solution)/shard_map/ppermute | solution.py:473
  38.0 44.1 %collective-permute-start.22 = (bf16[8,4224]{1,0:T(8,128)(2,1)}, bf16[8,4224]{1,0:T(8,128)(2,1)S(1)}, u32[]{:S(2)}, u32[]{:S(2)}) collective-permute-start(bf16[8,4224]{1,0:T(8,128)(2,1)} %get-tuple-element.49), channel_id=1, source_target_pairs={{0,4},{1,5},{2,6},{3,7},{4,0},{5,1},{6,2},{7,3},{8,12},{9,13},{10,... | collective-permute-start | bytes 202760 | tf_op jit(solution)/shard_map/ppermute | solution.py:473
  39.5 45.1 %collective-permute-start.23 = (bf16[8,4224]{1,0:T(8,128)(2,1)}, bf16[8,4224]{1,0:T(8,128)(2,1)S(1)}, u32[]{:S(2)}, u32[]{:S(2)}) collective-permute-start(bf16[8,4224]{1,0:T(8,128)(2,1)} %get-tuple-element.50), channel_id=1, source_target_pairs={{0,5},{1,4},{2,7},{3,6},{4,1},{5,0},{6,3},{7,2},{8,13},{9,12},{10,... | collective-permute-start | bytes 202760 | tf_op jit(solution)/shard_map/ppermute | solution.py:473
  39.7 27.1 %copy-start.1 = (bf16[8,4224]{1,0:T(8,128)(2,1)S(1)}, bf16[8,4224]{1,0:T(8,128)(2,1)}, u32[]{:S(2)}) copy-start(bf16[8,4224]{1,0:T(8,128)(2,1)} %get-tuple-element.45) | copy-start | bytes 202756
  64.0 11.8 %copy-start.17 = (bf16[8,4224]{1,0:T(8,128)(2,1)S(1)}, bf16[8,4224]{1,0:T(8,128)(2,1)}, u32[]{:S(2)}) copy-start(bf16[8,4224]{1,0:T(8,128)(2,1)} %get-tuple-element.51) | copy-start | bytes 202756
  64.0 14.3 %copy-start.16 = (bf16[8,4224]{1,0:T(8,128)(2,1)S(1)}, bf16[8,4224]{1,0:T(8,128)(2,1)}, u32[]{:S(2)}) copy-start(bf16[8,4224]{1,0:T(8,128)(2,1)} %get-tuple-element.52) | copy-start | bytes 202756
  75.8 9.5 %collective-permute-start.24 = (bf16[8,4224]{1,0:T(8,128)(2,1)S(1)}, bf16[8,4224]{1,0:T(8,128)(2,1)S(1)}, u32[]{:S(2)}, u32[]{:S(2)}) collective-permute-start(bf16[8,4224]{1,0:T(8,128)(2,1)S(1)} %copy-done.17), channel_id=1, source_target_pairs={{0,6},{1,7},{2,4},{3,5},{4,2},{5,3},{6,0},{7,1},{8,14},{9,15},{10,... | collective-permute-start | bytes 202760 | tf_op jit(solution)/shard_map/ppermute | solution.py:473
  78.3 8.4 %collective-permute-start.25 = (bf16[8,4224]{1,0:T(8,128)(2,1)S(1)}, bf16[8,4224]{1,0:T(8,128)(2,1)S(1)}, u32[]{:S(2)}, u32[]{:S(2)}) collective-permute-start(bf16[8,4224]{1,0:T(8,128)(2,1)S(1)} %copy-done.16), channel_id=1, source_target_pairs={{0,7},{1,6},{2,5},{3,4},{4,3},{5,2},{6,1},{7,0},{8,15},{9,14},{10,... | collective-permute-start | bytes 202760 | tf_op jit(solution)/shard_map/ppermute | solution.py:473
  78.7 33.2 %collective-permute-start.5 = (bf16[2,8,384]{2,1,0:T(8,128)(2,1)S(1)}, bf16[2,8,384]{2,1,0:T(8,128)(2,1)S(1)}, u32[]{:S(2)}, u32[]{:S(2)}) collective-permute-start(bf16[2,8,384]{2,1,0:T(8,128)(2,1)S(1)} %fusion.1), channel_id=1, source_target_pairs={{0,8},{8,16},{16,24},{1,9},{9,17},{17,25},{2,10},{10,18},{18,26},{... | collective-permute-start | bytes 36872 | tf_op jit(solution)/shard_map/ppermute | solution.py:453
  82.1 35.3 %collective-permute-start = (bf16[2,8,384]{2,1,0:T(8,128)(2,1)S(1)}, bf16[2,8,384]{2,1,0:T(8,128)(2,1)S(1)}, u32[]{:S(2)}, u32[]{:S(2)}) collective-permute-start(bf16[2,8,384]{2,1,0:T(8,128)(2,1)S(1)} %get-tuple-element.54), channel_id=1, source_target_pairs={{8,0},{16,8},{24,16},{9,1},{17,9},{25,17},{10,2},{18,10},{26,18},{... | collective-permute-start | bytes 36872 | tf_op jit(solution)/shard_map/ppermute | solution.py:453
  84.6 33.5 %collective-permute-start.1 = (bf16[2,8,384]{2,1,0:T(8,128)(2,1)S(1)}, bf16[2,8,384]{2,1,0:T(8,128)(2,1)S(1)}, u32[]{:S(2)}, u32[]{:S(2)}) collective-permute-start(bf16[2,8,384]{2,1,0:T(8,128)(2,1)S(1)} %get-tuple-element.55), channel_id=1, source_target_pairs={{0,24},{1,25},{2,26},{3,27},{4,28},{5,29},{6,30},{7,31}} | collective-permute-start | bytes 36872 | tf_op jit(solution)/shard_map/ppermute | solution.py:453
  85.3 45.5 %collective-permute-start.2 = (bf16[2,8,384]{2,1,0:T(8,128)(2,1)S(1)}, bf16[2,8,384]{2,1,0:T(8,128)(2,1)S(1)}, u32[]{:S(2)}, u32[]{:S(2)}) collective-permute-start(bf16[2,8,384]{2,1,0:T(8,128)(2,1)S(1)} %get-tuple-element.56), channel_id=1, source_target_pairs={{16,0},{24,8},{17,1},{25,9},{18,2},{26,10},{19,3},{27,11},{20,4},{... | collective-permute-start | bytes 36872 | tf_op jit(solution)/shard_map/ppermute | solution.py:453
  86.8 1.5 collective-permute-start.6
  86.9 147.9 %copy-start.3 = (bf16[64,4224]{1,0:T(8,128)(2,1)}, bf16[64,4224]{1,0:T(8,128)(2,1)S(1)}, u32[]{:S(2)}) copy-start(bf16[64,4224]{1,0:T(8,128)(2,1)S(1)} %constant_dynamic-update-slice_fusion.8.refs_13_) | copy-start | bytes 1622020
  88.3 4.5 %collective-permute-start.7 = (bf16[8,4224]{1,0:T(8,128)(2,1)}, bf16[8,4224]{1,0:T(8,128)(2,1)S(1)}, u32[]{:S(2)}, u32[]{:S(2)}) collective-permute-start(bf16[8,4224]{1,0:T(8,128)(2,1)} %get-tuple-element.39), channel_id=1, source_target_pairs={{0,2},{1,3},{2,0},{3,1},{4,6},{5,7},{6,4},{7,5},{8,10},{9,11},{10,... | collective-permute-start | bytes 202760 | tf_op jit(solution)/shard_map/ppermute | solution.py:473
  92.8 4.6 %collective-permute-start.8 = (bf16[8,4224]{1,0:T(8,128)(2,1)}, bf16[8,4224]{1,0:T(8,128)(2,1)S(1)}, u32[]{:S(2)}, u32[]{:S(2)}) collective-permute-start(bf16[8,4224]{1,0:T(8,128)(2,1)} %get-tuple-element.40), channel_id=1, source_target_pairs={{0,3},{1,2},{2,1},{3,0},{4,7},{5,6},{6,5},{7,4},{8,11},{9,10},{10,... | collective-permute-start | bytes 202760 | tf_op jit(solution)/shard_map/ppermute | solution.py:473
  97.4 4.5 %collective-permute-start.9 = (bf16[8,4224]{1,0:T(8,128)(2,1)}, bf16[8,4224]{1,0:T(8,128)(2,1)S(1)}, u32[]{:S(2)}, u32[]{:S(2)}) collective-permute-start(bf16[8,4224]{1,0:T(8,128)(2,1)} %get-tuple-element.41), channel_id=1, source_target_pairs={{0,4},{1,5},{2,6},{3,7},{4,0},{5,1},{6,2},{7,3},{8,12},{9,13},{10,... | collective-permute-start | bytes 202760 | tf_op jit(solution)/shard_map/ppermute | solution.py:473
  101.9 4.6 %collective-permute-start.10 = (bf16[8,4224]{1,0:T(8,128)(2,1)}, bf16[8,4224]{1,0:T(8,128)(2,1)S(1)}, u32[]{:S(2)}, u32[]{:S(2)}) collective-permute-start(bf16[8,4224]{1,0:T(8,128)(2,1)} %get-tuple-element.42), channel_id=1, source_target_pairs={{0,5},{1,4},{2,7},{3,6},{4,1},{5,0},{6,3},{7,2},{8,13},{9,12},{10,... | collective-permute-start | bytes 202760 | tf_op jit(solution)/shard_map/ppermute | solution.py:473
  106.5 5.4 %collective-permute-start.11 = (bf16[8,4224]{1,0:T(8,128)(2,1)}, bf16[8,4224]{1,0:T(8,128)(2,1)S(1)}, u32[]{:S(2)}, u32[]{:S(2)}) collective-permute-start(bf16[8,4224]{1,0:T(8,128)(2,1)} %get-tuple-element.43), channel_id=1, source_target_pairs={{0,6},{1,7},{2,4},{3,5},{4,2},{5,3},{6,0},{7,1},{8,14},{9,15},{10,... | collective-permute-start | bytes 202760 | tf_op jit(solution)/shard_map/ppermute | solution.py:473
  111.9 17.0 %collective-permute-start.12 = (bf16[8,4224]{1,0:T(8,128)(2,1)}, bf16[8,4224]{1,0:T(8,128)(2,1)S(1)}, u32[]{:S(2)}, u32[]{:S(2)}) collective-permute-start(bf16[8,4224]{1,0:T(8,128)(2,1)} %get-tuple-element.44), channel_id=1, source_target_pairs={{0,7},{1,6},{2,5},{3,4},{4,3},{5,2},{6,1},{7,0},{8,15},{9,14},{10,... | collective-permute-start | bytes 202760 | tf_op jit(solution)/shard_map/ppermute | solution.py:473
  111.9 20.2 %collective-permute-start.3 = (bf16[2,8,384]{2,1,0:T(8,128)(2,1)S(1)}, bf16[2,8,384]{2,1,0:T(8,128)(2,1)S(1)}, u32[]{:S(2)}, u32[]{:S(2)}) collective-permute-start(bf16[2,8,384]{2,1,0:T(8,128)(2,1)S(1)} %get-tuple-element.57), channel_id=1, source_target_pairs={{0,16},{8,24},{1,17},{9,25},{2,18},{10,26},{3,19},{11,27},{4,20},{... | collective-permute-start | bytes 36872 | tf_op jit(solution)/shard_map/ppermute | solution.py:453
  117.4 18.7 %collective-permute-start.4 = (bf16[2,8,384]{2,1,0:T(8,128)(2,1)S(1)}, bf16[2,8,384]{2,1,0:T(8,128)(2,1)S(1)}, u32[]{:S(2)}, u32[]{:S(2)}) collective-permute-start(bf16[2,8,384]{2,1,0:T(8,128)(2,1)S(1)} %get-tuple-element.58), channel_id=1, source_target_pairs={{24,0},{25,1},{26,2},{27,3},{28,4},{29,5},{30,6},{31,7}} | collective-permute-start | bytes 36872 | tf_op jit(solution)/shard_map/ppermute | solution.py:453
  118.1 31.0 %collective-permute-start.30 = (bf16[64,4224]{1,0:T(8,128)(2,1)S(1)}, bf16[64,4224]{1,0:T(8,128)(2,1)S(1)}, u32[]{:S(2)}, u32[]{:S(2)}) collective-permute-start(bf16[64,4224]{1,0:T(8,128)(2,1)S(1)} %constant_dynamic-update-slice_fusion.8.refs_13_), channel_id=1, source_target_pairs={{0,16},{8,24},{1,17},{9,25},{2,18},{10,26},{3,19},{11,27},{4,20},{... | collective-permute-start | bytes 1622024 | tf_op jit(solution)/shard_map/ppermute | solution.py:453
  128.9 43.3 %collective-permute-start.29 = (bf16[64,4224]{1,0:T(8,128)(2,1)S(1)}, bf16[64,4224]{1,0:T(8,128)(2,1)S(1)}, u32[]{:S(2)}, u32[]{:S(2)}) collective-permute-start(bf16[64,4224]{1,0:T(8,128)(2,1)S(1)} %constant_dynamic-update-slice_fusion.8.refs_13_), channel_id=1, source_target_pairs={{0,8},{8,16},{16,24},{1,9},{9,17},{17,25},{2,10},{10,18},{18,26},{... | collective-permute-start | bytes 1622024 | tf_op jit(solution)/shard_map/ppermute | solution.py:453
  130.8 104.0 %copy-start.2 = (bf16[64,4224]{1,0:T(8,128)(2,1)}, bf16[64,4224]{1,0:T(8,128)(2,1)S(1)}, u32[]{:S(2)}) copy-start(bf16[64,4224]{1,0:T(8,128)(2,1)S(1)} %constant_dynamic-update-slice_fusion.refs_6_) | copy-start | bytes 1622020
  130.8 45.2 %collective-permute-start.27 = (bf16[64,4224]{1,0:T(8,128)(2,1)S(1)}, bf16[64,4224]{1,0:T(8,128)(2,1)S(1)}, u32[]{:S(2)}, u32[]{:S(2)}) collective-permute-start(bf16[64,4224]{1,0:T(8,128)(2,1)S(1)} %constant_dynamic-update-slice_fusion.8.refs_13_), channel_id=1, source_target_pairs={{16,0},{24,8},{17,1},{25,9},{18,2},{26,10},{19,3},{27,11},{20,4},{... | collective-permute-start | bytes 1622024 | tf_op jit(solution)/shard_map/ppermute | solution.py:453
  132.1 45.9 %collective-permute-start.26 = (bf16[64,4224]{1,0:T(8,128)(2,1)S(1)}, bf16[64,4224]{1,0:T(8,128)(2,1)S(1)}, u32[]{:S(2)}, u32[]{:S(2)}) collective-permute-start(bf16[64,4224]{1,0:T(8,128)(2,1)S(1)} %constant_dynamic-update-slice_fusion.8.refs_13_), channel_id=1, source_target_pairs={{8,0},{16,8},{24,16},{9,1},{17,9},{25,17},{10,2},{18,10},{26,18},{... | collective-permute-start | bytes 1622024 | tf_op jit(solution)/shard_map/ppermute | solution.py:453
  136.1 47.6 %collective-permute-start.17 = (bf16[64,4224]{1,0:T(8,128)(2,1)S(1)}, bf16[64,4224]{1,0:T(8,128)(2,1)S(1)}, u32[]{:S(2)}, u32[]{:S(2)}) collective-permute-start(bf16[64,4224]{1,0:T(8,128)(2,1)S(1)} %constant_dynamic-update-slice_fusion.refs_6_), channel_id=1, source_target_pairs={{0,16},{8,24},{1,17},{9,25},{2,18},{10,26},{3,19},{11,27},{4,20},{... | collective-permute-start | bytes 1622024 | tf_op jit(solution)/shard_map/ppermute | solution.py:453
  149.1 85.7 %copy-start.4 = (bf16[64,4224]{1,0:T(8,128)(2,1)}, bf16[64,4224]{1,0:T(8,128)(2,1)S(1)}, u32[]{:S(2)}) copy-start(bf16[64,4224]{1,0:T(8,128)(2,1)S(1)} %collective-permute-done.30.refs_18_) | copy-start | bytes 1622020
  149.1 46.3 %collective-permute-start.16 = (bf16[64,4224]{1,0:T(8,128)(2,1)S(1)}, bf16[64,4224]{1,0:T(8,128)(2,1)S(1)}, u32[]{:S(2)}, u32[]{:S(2)}) collective-permute-start(bf16[64,4224]{1,0:T(8,128)(2,1)S(1)} %constant_dynamic-update-slice_fusion.refs_6_), channel_id=1, source_target_pairs={{0,8},{8,16},{16,24},{1,9},{9,17},{17,25},{2,10},{10,18},{18,26},{... | collective-permute-start | bytes 1622024 | tf_op jit(solution)/shard_map/ppermute | solution.py:453
  172.2 62.7 %copy-start.5 = (bf16[64,4224]{1,0:T(8,128)(2,1)}, bf16[64,4224]{1,0:T(8,128)(2,1)S(1)}, u32[]{:S(2)}) copy-start(bf16[64,4224]{1,0:T(8,128)(2,1)S(1)} %collective-permute-done.29.refs_17_) | copy-start | bytes 1622020
  172.2 27.6 %collective-permute-start.14 = (bf16[64,4224]{1,0:T(8,128)(2,1)S(1)}, bf16[64,4224]{1,0:T(8,128)(2,1)S(1)}, u32[]{:S(2)}, u32[]{:S(2)}) collective-permute-start(bf16[64,4224]{1,0:T(8,128)(2,1)S(1)} %constant_dynamic-update-slice_fusion.refs_6_), channel_id=1, source_target_pairs={{16,0},{24,8},{17,1},{25,9},{18,2},{26,10},{19,3},{27,11},{20,4},{... | collective-permute-start | bytes 1622024 | tf_op jit(solution)/shard_map/ppermute | solution.py:453
  176.1 58.8 %copy-start.6 = (bf16[64,4224]{1,0:T(8,128)(2,1)}, bf16[64,4224]{1,0:T(8,128)(2,1)S(1)}, u32[]{:S(2)}) copy-start(bf16[64,4224]{1,0:T(8,128)(2,1)S(1)} %collective-permute-done.27.refs_15_) | copy-start | bytes 1622020
  176.1 37.7 %collective-permute-start.13 = (bf16[64,4224]{1,0:T(8,128)(2,1)S(1)}, bf16[64,4224]{1,0:T(8,128)(2,1)S(1)}, u32[]{:S(2)}, u32[]{:S(2)}) collective-permute-start(bf16[64,4224]{1,0:T(8,128)(2,1)S(1)} %constant_dynamic-update-slice_fusion.refs_6_), channel_id=1, source_target_pairs={{8,0},{16,8},{24,16},{9,1},{17,9},{25,17},{10,2},{18,10},{26,18},{... | collective-permute-start | bytes 1622024 | tf_op jit(solution)/shard_map/ppermute | solution.py:453
  178.0 56.8 %copy-start.7 = (bf16[64,4224]{1,0:T(8,128)(2,1)}, bf16[64,4224]{1,0:T(8,128)(2,1)S(1)}, u32[]{:S(2)}) copy-start(bf16[64,4224]{1,0:T(8,128)(2,1)S(1)} %collective-permute-done.26.refs_14_) | copy-start | bytes 1622020
  178.0 35.8 %collective-permute-start.31 = (bf16[64,4224]{1,0:T(8,128)(2,1)S(1)}, bf16[64,4224]{1,0:T(8,128)(2,1)S(1)}, u32[]{:S(2)}, u32[]{:S(2)}) collective-permute-start(bf16[64,4224]{1,0:T(8,128)(2,1)S(1)} %collective-permute-done.30.refs_18_), channel_id=1, source_target_pairs={{0,8},{8,16},{16,24},{1,9},{9,17},{17,25},{2,10},{10,18},{18,26},{... | collective-permute-start | bytes 1622024 | tf_op jit(solution)/shard_map/ppermute | solution.py:453
  183.7 51.1 %copy-start.8 = (bf16[64,4224]{1,0:T(8,128)(2,1)}, bf16[64,4224]{1,0:T(8,128)(2,1)S(1)}, u32[]{:S(2)}) copy-start(bf16[64,4224]{1,0:T(8,128)(2,1)S(1)} %collective-permute-done.17.refs_11_) | copy-start | bytes 1622020
  183.7 40.0 %collective-permute-start.28 = (bf16[64,4224]{1,0:T(8,128)(2,1)S(1)}, bf16[64,4224]{1,0:T(8,128)(2,1)S(1)}, u32[]{:S(2)}, u32[]{:S(2)}) collective-permute-start(bf16[64,4224]{1,0:T(8,128)(2,1)S(1)} %collective-permute-done.27.refs_15_), channel_id=1, source_target_pairs={{8,0},{16,8},{24,16},{9,1},{17,9},{25,17},{10,2},{18,10},{26,18},{... | collective-permute-start | bytes 1622024 | tf_op jit(solution)/shard_map/ppermute | solution.py:453
  195.3 39.5 %copy-start.9 = (bf16[64,4224]{1,0:T(8,128)(2,1)}, bf16[64,4224]{1,0:T(8,128)(2,1)S(1)}, u32[]{:S(2)}) copy-start(bf16[64,4224]{1,0:T(8,128)(2,1)S(1)} %collective-permute-done.16.refs_10_) | copy-start | bytes 1622020
  195.3 28.5 %collective-permute-start.18 = (bf16[64,4224]{1,0:T(8,128)(2,1)S(1)}, bf16[64,4224]{1,0:T(8,128)(2,1)S(1)}, u32[]{:S(2)}, u32[]{:S(2)}) collective-permute-start(bf16[64,4224]{1,0:T(8,128)(2,1)S(1)} %collective-permute-done.17.refs_11_), channel_id=1, source_target_pairs={{0,8},{8,16},{16,24},{1,9},{9,17},{17,25},{2,10},{10,18},{18,26},{... | collective-permute-start | bytes 1622024 | tf_op jit(solution)/shard_map/ppermute | solution.py:453
  199.7 35.1 %copy-start.10 = (bf16[64,4224]{1,0:T(8,128)(2,1)}, bf16[64,4224]{1,0:T(8,128)(2,1)S(1)}, u32[]{:S(2)}) copy-start(bf16[64,4224]{1,0:T(8,128)(2,1)S(1)} %collective-permute-done.14.refs_8_) | copy-start | bytes 1622020
  199.7 35.1 %collective-permute-start.15 = (bf16[64,4224]{1,0:T(8,128)(2,1)S(1)}, bf16[64,4224]{1,0:T(8,128)(2,1)S(1)}, u32[]{:S(2)}, u32[]{:S(2)}) collective-permute-start(bf16[64,4224]{1,0:T(8,128)(2,1)S(1)} %collective-permute-done.14.refs_8_), channel_id=1, source_target_pairs={{8,0},{16,8},{24,16},{9,1},{17,9},{25,17},{10,2},{18,10},{26,18},{... | collective-permute-start | bytes 1622024 | tf_op jit(solution)/shard_map/ppermute | solution.py:453
  213.8 21.1 %copy-start.11 = (bf16[64,4224]{1,0:T(8,128)(2,1)}, bf16[64,4224]{1,0:T(8,128)(2,1)S(1)}, u32[]{:S(2)}) copy-start(bf16[64,4224]{1,0:T(8,128)(2,1)S(1)} %collective-permute-done.13.refs_7_) | copy-start | bytes 1622020
  213.8 21.1 %copy-start.12 = (bf16[64,4224]{1,0:T(8,128)(2,1)}, bf16[64,4224]{1,0:T(8,128)(2,1)S(1)}, u32[]{:S(2)}) copy-start(bf16[64,4224]{1,0:T(8,128)(2,1)S(1)} %collective-permute-done.31.refs_19_) | copy-start | bytes 1622020
  223.8 11.1 %copy-start.13 = (bf16[64,4224]{1,0:T(8,128)(2,1)}, bf16[64,4224]{1,0:T(8,128)(2,1)S(1)}, u32[]{:S(2)}) copy-start(bf16[64,4224]{1,0:T(8,128)(2,1)S(1)} %collective-permute-done.28.refs_16_) | copy-start | bytes 1622020
  223.8 11.1 %copy-start.14 = (bf16[64,4224]{1,0:T(8,128)(2,1)}, bf16[64,4224]{1,0:T(8,128)(2,1)S(1)}, u32[]{:S(2)}) copy-start(bf16[64,4224]{1,0:T(8,128)(2,1)S(1)} %collective-permute-done.18.refs_12_) | copy-start | bytes 1622020
  (2 other events, 11.0 us)

commit v2 on v1

--- a/solution.py
+++ b/solution.py
@@ -283,16 +283,14 @@
             pltpu.VMEM((depth, 2 * LANES), jnp.bfloat16),
         ],
         compiler_params=pltpu.CompilerParams(vmem_limit_bytes=VMEM_BYTES, dimension_semantics=("arbitrary",)),
-        cost_estimate=pl.CostEstimate(flops=count * 1200000000, bytes_accessed=count * 2000000, transcendentals=0),
+        cost_estimate=pl.CostEstimate(flops=count, bytes_accessed=count, transcendentals=0),
         name="spectra",
     )(weight, val_wave, cond_wave, jnp.asarray(dft_table(points)))
 
 
-def pack_kernel(plan, groups, col_ref, place_ref, *refs):
+def pack_kernel(plan, groups, place_ref, *refs):
     plains, weighteds = refs[:groups], refs[groups : 2 * groups]
-    slots = len(plan["buckets"])
-    outs = refs[2 * groups : 2 * groups + slots]
-    slab_ref, sorter, plain_sorted, weighted_sorted, blocks = refs[2 * groups + slots :]
+    send_ref, slab_ref, sorter, plain_sorted, weighted_sorted = refs[2 * groups :]
     depth, columns = sorter.shape
     count = 2 * sum(plain.shape[1] for plain in plains)
     lane = lax.broadcasted_iota(jnp.int32, (1, LANES), 1)
@@ -317,16 +315,12 @@
     def weighted_at(index, tile):
         return weighted_sorted[tile, pl.ds(index, count, stride=ROWS_K), :]
 
-    col = col_ref[0]
     for block, bucket in enumerate(plan["buckets"]):
-        slot = jnp.bitwise_xor(col, block)
 
         def keep(tile, value):
-            blocks[slot, :, tile * LANES : (tile + 1) * LANES] = value.astype(jnp.bfloat16)
+            send_ref[block, :, tile * LANES : (tile + 1) * LANES] = value.astype(jnp.bfloat16)
 
         pack_pieces(bucket.pieces, plan["lanes"], plain_at, count, lane, keep)
-    for slot, out in enumerate(outs):
-        out[...] = blocks[slot]
     for block, bucket in enumerate(plan["slabs"]):
 
         def keep_slab(tile, value):
@@ -335,33 +329,31 @@
         pack_pieces(bucket.pieces, plan["slab_lanes"], weighted_at, count, lane, keep_slab)
 
 
-def packed(plan, col, plains, weighteds):
+def packed(plan, plains, weighteds):
     depth = plains[0].shape[3]
     count = 2 * sum(plain.shape[1] for plain in plains)
     columns = round_up(plan["column_place"].shape[0], 256)
     slab_columns = round_up(plan["slab_columns"], LANES)
     place = np.full((1, columns), -1, np.int32)
     place[0, : plan["column_place"].shape[0]] = plan["column_place"]
-    slots, lanes = len(plan["buckets"]), plan["lanes"]
     kernel = lambda *refs: pack_kernel(plan, len(plains), *refs)
     vmem = pl.BlockSpec(memory_space=pltpu.VMEM)
+    send_shape = (len(plan["buckets"]), count, plan["lanes"])
     slab_shape = (len(plan["slabs"]), count, plan["slab_lanes"])
     return pl.pallas_call(
         kernel,
-        in_specs=[pl.BlockSpec(memory_space=pltpu.SMEM)] + [vmem] * (1 + 2 * len(plains)),
-        out_specs=[vmem] * (slots + 1),
-        out_shape=[jax.ShapeDtypeStruct((count, lanes), jnp.bfloat16)] * slots
-        + [jax.ShapeDtypeStruct(slab_shape, jnp.bfloat16)],
+        in_specs=[vmem] * (1 + 2 * len(plains)),
+        out_specs=[vmem] * 2,
+        out_shape=[jax.ShapeDtypeStruct(send_shape, jnp.bfloat16), jax.ShapeDtypeStruct(slab_shape, jnp.bfloat16)],
         scratch_shapes=[
             pltpu.VMEM((depth, columns), jnp.bfloat16),
             pltpu.VMEM((columns // LANES, count * ROWS_K, LANES), jnp.float32),
             pltpu.VMEM((slab_columns // LANES, count * ROWS_K, LANES), jnp.float32),
-            pltpu.VMEM((slots, count, lanes), jnp.bfloat16),
         ],
         compiler_params=pltpu.CompilerParams(vmem_limit_bytes=VMEM_BYTES),
-        cost_estimate=pl.CostEstimate(flops=4000000000, bytes_accessed=4000000, transcendentals=0),
+        cost_estimate=pl.CostEstimate(flops=1, bytes_accessed=1, transcendentals=0),
         name="pack",
-    )(col, jnp.asarray(place), *plains, *weighteds)
+    )(jnp.asarray(place), *plains, *weighteds)
 
 
 def one_hot(ids_ref, begin, wanted):
@@ -370,122 +362,90 @@
     return jnp.where(ids == wanted, 1.0, 0.0).astype(jnp.bfloat16)
 
 
-def product_kernel(shape, place_ref, slab_ref, ids_ref, slab_ids_ref, wanted_ref, slab_wanted_ref, *refs):
-    rounds, chunks, slots, group = shape
-    panels = refs[: chunks * (2 * rounds - 1)]
-    out_ref, panel, chosen_rows, left, hot = refs[chunks * (2 * rounds - 1) :]
+def left_kernel(group, slab_ref, slab_ids_ref, slab_wanted_ref, left_ref):
     rows = slab_wanted_ref.shape[1]
+    choice = jnp.concatenate(
+        [one_hot(slab_ids_ref, begin, slab_wanted_ref[...]) for begin in range(0, slab_ids_ref.shape[1], LANES)], 0
+    )
+    chosen = jnp.dot(slab_ref[...], choice, preferred_element_type=jnp.float32)
+    lane = lax.broadcasted_iota(jnp.int32, (1, LANES), 1)
+    real_lanes = lane % group < group // 2
+    for begin in range(0, chosen.shape[0], LANES):
+        turned = chosen[begin : begin + LANES].T
+        after = pltpu.roll(turned, LANES - group // 2, 1)
+        before = pltpu.roll(turned, group // 2, 1)
+        left_ref[:rows, begin : begin + LANES] = turned.astype(jnp.bfloat16)
+        left_ref[rows:, begin : begin + LANES] = jnp.where(real_lanes, after, -before).astype(jnp.bfloat16)
+
+
+def left_side(group, slab, slab_ids, slab_wanted):
+    vmem = pl.BlockSpec(memory_space=pltpu.VMEM)
+    return pl.pallas_call(
+        lambda *refs: left_kernel(group, *refs),
+        in_specs=[vmem] * 3,
+        out_specs=vmem,
+        out_shape=jax.ShapeDtypeStruct((2 * slab_wanted.shape[1], slab.shape[0]), jnp.bfloat16),
+        compiler_params=pltpu.CompilerParams(vmem_limit_bytes=VMEM_BYTES),
+        cost_estimate=pl.CostEstimate(flops=1, bytes_accessed=1, transcendentals=0),
+        name="left_side",
+    )(slab, slab_ids, slab_wanted)
+
+
+def in_order(start, panel_ref, ids_ref, wanted_ref, hot):
+    wanted = wanted_ref[...]
     window = hot.shape[0]
-
-    @pl.when(pl.program_id(0) == 0)
-    def _():
-        size = slots * group
-        col = place_ref[0]
-        for chunk in range(chunks):
-            own, *others = panels[chunk * (2 * rounds - 1) : (chunk + 1) * (2 * rounds - 1)]
-            for turn in range(rounds):
-                base = (turn * chunks + chunk) * size
-                if turn == 0:
-                    panel[base : base + size, :] = own[...]
-                else:
-                    panel[base : base + size, :] = others[turn - 1][...] + others[2 * rounds - 2 - turn][...]
-                for slot in range(slots):
-                    chosen_rows[base + slot * group : base + (slot + 1) * group, :] = slab_ref[
-                        jnp.bitwise_xor(col, slot), turn, chunk
-                    ].astype(jnp.float32)
-        choice = jnp.concatenate(
-            [one_hot(slab_ids_ref, begin, slab_wanted_ref[...]) for begin in range(0, slab_ids_ref.shape[1], LANES)], 0
-        )
-        chosen = jnp.dot(chosen_rows[...].astype(jnp.bfloat16), choice, preferred_element_type=jnp.float32)
-        lane = lax.broadcasted_iota(jnp.int32, (1, LANES), 1)
-        real_lanes = lane % group < group // 2
-        for begin in range(0, chosen.shape[0], LANES):
-            turned = chosen[begin : begin + LANES].T
-            after = pltpu.roll(turned, LANES - group // 2, 1)
-            before = pltpu.roll(turned, group // 2, 1)
-            left[:rows, begin : begin + LANES] = turned.astype(jnp.bfloat16)
-            left[rows:, begin : begin + LANES] = jnp.where(real_lanes, after, -before).astype(jnp.bfloat16)
-
-    start = pl.multiple_of(place_ref[1 + pl.program_id(0)], LANES)
-    wanted = wanted_ref[...]
     for begin in range(0, window, LANES):
         hot[begin : begin + LANES, :] = one_hot(ids_ref, pl.multiple_of(start + begin, LANES), wanted)
-    ordered = jnp.dot(panel[:, pl.ds(start, window)], hot[...], preferred_element_type=jnp.float32).astype(jnp.bfloat16)
-    chi = jnp.dot(left[...], ordered, preferred_element_type=jnp.float32)
+    return jnp.dot(panel_ref[:, pl.ds(start, window)], hot[...], preferred_element_type=jnp.float32).astype(jnp.bfloat16)
+
+
+def order_kernel(starts_ref, ids_ref, wanted_ref, panel_ref, out_ref, hot):
+    start = pl.multiple_of(starts_ref[pl.program_id(0)], LANES)
+    out_ref[...] = in_order(start, panel_ref, ids_ref, wanted_ref, hot)
+
+
+def product_kernel(starts_ref, ids_ref, wanted_ref, panel_ref, left_ref, *refs):
+    *ordered, out_ref, hot = refs
+    rows = out_ref.shape[1]
+    start = pl.multiple_of(starts_ref[pl.program_id(0)], LANES)
+    last = in_order(start, panel_ref, ids_ref, wanted_ref, hot)
+    right = jnp.concatenate([part[...] for part in ordered] + [last], 0)
+    chi = jnp.dot(left_ref[...], right, preferred_element_type=jnp.float32)
     out_ref[0] = chi[:rows]
     out_ref[1] = chi[rows:]
 
 
-def product(plan, shape, place, slab, ids, slab_ids, wanted, slab_wanted, panels):
-    rounds, chunks, slots, group = shape
-    columns, rows, pairs = wanted.shape[1], slab_wanted.shape[1], rounds * chunks * slots * group
+def put_in_order(plan, starts, ids, wanted, panel, left=None, ordered=()):
+    columns = wanted.shape[1]
     block = columns // PARTS
     whole = lambda array: pl.BlockSpec(array.shape, lambda n: (0,) * array.ndim)
-    kernel = lambda *refs: product_kernel(shape, *refs)
+    in_specs = [
+        pl.BlockSpec(memory_space=pltpu.SMEM),
+        whole(ids),
+        pl.BlockSpec((1, block), lambda n: (0, n)),
+        whole(panel),
+    ]
+    operands = [starts, ids, wanted, panel]
+    if left is None:
+        out_spec = pl.BlockSpec((panel.shape[0], block), lambda n: (0, n))
+        out_shape = jax.ShapeDtypeStruct((panel.shape[0], columns), jnp.bfloat16)
+    else:
+        rows = left.shape[0] // 2
+        in_specs += [whole(left)] + [pl.BlockSpec((part.shape[0], block), lambda n: (0, n)) for part in ordered]
+        operands += [left, *ordered]
+        out_spec = pl.BlockSpec((2, rows, block), lambda n: (0, 0, n))
+        out_shape = jax.ShapeDtypeStruct((2, rows, columns), jnp.float32)
     return pl.pallas_call(
-        kernel,
+        order_kernel if left is None else product_kernel,
         grid=(PARTS,),
-        in_specs=[
-            pl.BlockSpec(memory_space=pltpu.SMEM),
-            whole(slab),
-            whole(ids),
-            whole(slab_ids),
-            pl.BlockSpec((1, block), lambda n: (0, n)),
-            whole(slab_wanted),
-        ]
-        + [whole(panel) for panel in panels],
-        out_specs=pl.BlockSpec((2, rows, block), lambda n: (0, 0, n)),
-        out_shape=jax.ShapeDtypeStruct((2, rows, columns), jnp.float32),
-        scratch_shapes=[
-            pltpu.VMEM((pairs, plan["lanes"]), jnp.bfloat16),
-            pltpu.VMEM((pairs, plan["slab_lanes"]), jnp.float32),
-            pltpu.VMEM((2 * rows, pairs), jnp.bfloat16),
-            pltpu.VMEM((plan["window"], block), jnp.bfloat16),
-        ],
+        in_specs=in_specs,
+        out_specs=out_spec,
+        out_shape=out_shape,
+        scratch_shapes=[pltpu.VMEM((plan["window"], block), jnp.bfloat16)],
         compiler_params=pltpu.CompilerParams(vmem_limit_bytes=VMEM_BYTES, dimension_semantics=("arbitrary",)),
-        cost_estimate=pl.CostEstimate(flops=12000000000, bytes_accessed=16000000, transcendentals=0),
-        name="product",
-    )(place, slab, ids, slab_ids, wanted, slab_wanted, *panels)
-
-
-def shifted(value, axis, step):
-    size = lax.axis_size(axis)
-    return lax.ppermute(value, axis, [(n, n + step) for n in range(size) if 0 <= n + step < size])
-
-
-def from_planes(own):
-    size = lax.axis_size("row")
-    further, back = [], []
-    for step in range(1, size):
-        if step < 3:
-            further.append(shifted(own, "row", -step))
-            back.append(shifted(own, "row", step))
-        else:
-            further.append(shifted(further[-1], "row", -1))
-            back.append(shifted(back[-1], "row", 1))
-    return further, back
-
-
-def within_plane(blocks):
-    size = lax.axis_size("col")
-    parts = [blocks[0]]
-    for slot in range(1, size):
-        parts.append(lax.ppermute(blocks[slot], "col", [(n, n ^ slot) for n in range(size)]))
-    return jnp.concatenate(parts, 0)
-
-
-def slab_to_rows(slab):
-    size = lax.axis_size("row")
-    row = lax.axis_index("row")
-    out = [lax.dynamic_index_in_dim(slab, row, 0, keepdims=False)]
-    sent = {}
-    for step in range(1 - size, size):
-        if step:
-            block = lax.dynamic_index_in_dim(slab, jnp.clip(row + step, 0, size - 1), 0, keepdims=False)
-            sent[step] = shifted(block, "row", step)
-    for turn in range(1, size):
-        out.append(sent[-turn] + sent[size - turn])
-    return jnp.stack(out)
+        cost_estimate=pl.CostEstimate(flops=1, bytes_accessed=1, transcendentals=0),
+        name="in_order" if left is None else "product",
+    )(*operands)
 
 
 def on_device(val_wave, cond_wave, val_energy, cond_energy, band_owner, grid_map):
@@ -497,29 +457,27 @@
     plan = make_plan(points, grid_map.shape[0], col_count, ROWS_DEV * row_count, row_count)
     energy = jnp.sum(jnp.where(band_owner[0] == jnp.arange(band_total, dtype=jnp.int32), cond_energy, 0.0))
     weight = -2.0 / (math.sqrt(bands * band_total) * (energy - val_energy))
-    chunk = bands // CHUNKS
-    panels, slabs = [], []
-    for part in range(CHUNKS):
-        pieces = []
-        split = 1 if part == 0 else 2
-        for piece in range(split):
-            count = chunk // split
-            pieces.append(spectra(plan, val_wave, cond_wave, weight, part * chunk + piece * count, count))
-        *blocks, slab = packed(plan, col[None], [p[0] for p in pieces], [p[1] for p in pieces])
-        own = within_plane(blocks)
-        further, back = from_planes(own)
-        panels += [own] + further + back
-        slabs.append(slab)
-    slab = slab_to_rows(jnp.stack(slabs, 1))
-    slab = lax.all_gather(slab, "col", axis=0)
     width = grid_map.shape[0] // col_count
-    place = jnp.concatenate([col[None], lax.dynamic_index_in_dim(jnp.asarray(plan["starts"]), col, 0, keepdims=False)])
+    starts = lax.dynamic_index_in_dim(jnp.asarray(plan["starts"]), col, 0, keepdims=False)
     ids = lax.dynamic_slice(jnp.asarray(plan["ids"]), (col, 0), (1, plan["lanes"]))
     slab_ids = lax.dynamic_slice(jnp.asarray(plan["slab_ids"]), (row, 0), (1, plan["slab_lanes"]))
     wanted = lax.dynamic_slice(grid_map, (col * width,), (width,))[None]
     slab_wanted = lax.dynamic_slice(grid_map, (row * ROWS_DEV,), (ROWS_DEV,))[None]
-    shape = (row_count, CHUNKS, col_count, 2 * chunk)
-    return product(plan, shape, place, slab, ids, slab_ids, wanted, slab_wanted, panels)
+    chunk = bands // CHUNKS
+    panels, slabs = [], []
+    for part in range(CHUNKS):
+        plain, weighted = spectra(plan, val_wave, cond_wave, weight, part * chunk, chunk)
+        send, slab = packed(plan, [plain], [weighted])
+        mine = lax.all_to_all(send, "col", split_axis=0, concat_axis=0, tiled=True)
+        mine, slab, cond_wave = lax.optimization_barrier((mine, slab, cond_wave))
+        panels.append(lax.all_gather(mine, "row", axis=0, tiled=True).reshape(-1, plan["lanes"]))
+        slabs.append(slab)
+    slab = lax.all_to_all(jnp.stack(slabs, 1), "row", split_axis=0, concat_axis=0, tiled=True)
+    slab = lax.all_to_all(jnp.broadcast_to(slab, (col_count, *slab.shape)), "col", split_axis=0, concat_axis=0)
+    slab = slab.transpose(2, 1, 0, 3, 4).reshape(-1, plan["slab_lanes"])
+    left = left_side(2 * chunk, slab, slab_ids, slab_wanted)
+    ordered = [put_in_order(plan, starts, ids, wanted, panel) for panel in panels[:-1]]
+    return put_in_order(plan, starts, ids, wanted, panels[-1], left, ordered)
 
 
 def solution(mesh):

time: 253 us -> 167 us (0.66)
  the two profiles are of different devices: /device:TPU:8 before, /device:TPU:0 now
where the time goes in v2:
time: 167 us; the launch traced here: 166 us
  Pallas kernels  78.1 us (47%)
  blocking collectives  29.3 us (18%)
  waiting for transfers between devices  23.3 us (14%)
  between operations  14.1 us (8%)
  local copies, waits for them, and re-layouts  8.97 us (5%)
  starting transfers between devices  8.89 us (5%)
  other arithmetic  3.89 us (2%)
    pallas_call x2, Pallas kernels, spectra(): pl.pallas_call(kernel, grid=(count,), in_specs=[pl.BlockSpec(memory_space...  48.6 us
    all_to_all x2, blocking collectives, on_device(): mine = lax.all_to_all(send, 'col', split_axis=0, concat_axis=0, tiled=True)  29.3 us
    pallas_call x2, Pallas kernels, put_in_order(): pl.pallas_call(order_kernel if left is None else product_kernel, grid=(PA...  17.1 us
    all_gather x2, waiting for transfers between devices, on_device(): lax.all_gather(mine, 'row', axis=0, tiled=True).reshape(-1, plan['lanes'])  12.1 us
    pallas_call x2, Pallas kernels, packed(): pl.pallas_call(kernel, in_specs=[vmem] * (1 + 2 * len(plains)), out_specs...  9.82 us
    all_to_all x1, waiting for transfers between devices, on_device(): lax.all_to_all(jnp.broadcast_to(slab, (col_count, *slab.shape)), 'col', s...  6.57 us
    all_to_all x1, starting transfers between devices, on_device(): lax.all_to_all(jnp.stack(slabs, 1), 'row', split_axis=0, concat_axis=0, t...  5.21 us
    all_to_all x1, waiting for transfers between devices, on_device(): lax.all_to_all(jnp.stack(slabs, 1), 'row', split_axis=0, concat_axis=0, t...  4.59 us
  transfers between devices with their start and end apart: 4, of which 3 were waited for; matrix products, arithmetic and copies ran while one was open for 6% of the time, Pallas kernels for 23%

profile of v2, /device:TPU:0, one launch (start us, length us, event | category | flops | bytes accessed | tf_op | source)
XLA Modules:
  0.0 166.4 jit_solution(13501088052291703062)
XLA Ops:
  6.5 0.0 all-gather.5.cloned.1.call-start
  7.2 1.3 fusion.1
  8.5 1.9 %multiply_divide_fusion.refs_0_ = f32[8]{0:T(128)} fusion(f32[8]{0:T(128)} %param.15, f32[]{:T(128)} %fusion.1), kind=kLoop, calls=%fused_computation.7 | loop fusion | flops 24 | bytes 68 | tf_op jit(solution)/shard_map/div | solution.py:459
  10.3 24.3 %spectra.2 = (bf16[2,4,48,1664]{3,2,1,0:T(8,128)(2,1)}, bf16[2,4,48,640]{3,2,1,0:T(8,128)(2,1)}) custom-call(f32[8]{0:T(128)} %multiply_divide_fusion.refs_0_, bf16[8,64,64,128]{3,2,1,0:T(8,128)(2,1)} %refs_1_.3, bf16[1,64,64,128]{3,2,1,0:T(8,128)(2,1)} %refs_2_.2, bf16[256,256]{1,0:T(8,128)(2,1)} %constant.43.clone.refs_3_), custom_call_target="tpu_custom_call" | custom-call | flops 4 | bytes 4 | tf_op jit(solution)/shard_map/spectra/pallas_call | solution.py:261
  34.6 4.9 %pack.2 = (bf16[8,8,4224]{2,1,0:T(8,128)(2,1)}, bf16[4,8,384]{2,1,0:T(8,128)(2,1)}) custom-call(s32[1,1280]{1,0:T(1,128)} %constant.44.clone.refs_0_, bf16[2,4,48,1664]{3,2,1,0:T(8,128)(2,1)} %get-tuple-element.18.refs_1_, bf16[2,4,48,640]{3,2,1,0:T(8,128)(2,1)} %get-tuple-element.19.refs_2_), custom_call_target="tpu_custom_call" | custom-call | flops 1 | bytes 1 | tf_op jit(solution)/shard_map/pack/pallas_call | solution.py:343
  39.5 15.2 %all_to_all.20 = bf16[8,8,4224]{2,1,0:T(8,128)(2,1)} all-to-all(bf16[8,8,4224]{2,1,0:T(8,128)(2,1)} %get-tuple-element.20), channel_id=1, replica_groups=mesh['row'=4,'col'=8] {'col'}, dimensions={0} | all-to-all | bytes 1081344 | tf_op jit(solution)/shard_map/all_to_all | solution.py:471
  54.7 0.0 all-gather.5.cloned.1.call-update
  54.7 0.0 all-gather.3.cloned.1.call-start
  54.8 24.3 %spectra.3 = (bf16[2,4,48,1664]{3,2,1,0:T(8,128)(2,1)}, bf16[2,4,48,640]{3,2,1,0:T(8,128)(2,1)}) custom-call(f32[8]{0:T(128)} %multiply_divide_fusion.refs_0_, bf16[8,64,64,128]{3,2,1,0:T(8,128)(2,1)} %refs_1_.3, bf16[1,64,64,128]{3,2,1,0:T(8,128)(2,1)} %refs_2_.2, bf16[256,256]{1,0:T(8,128)(2,1)} %constant.43.clone.refs_3_), custom_call_target="tpu_custom_call" | custom-call | flops 4 | bytes 4 | tf_op jit(solution)/shard_map/spectra/pallas_call | solution.py:261
  79.1 0.0 copy-start
  79.1 4.9 %pack.3 = (bf16[8,8,4224]{2,1,0:T(8,128)(2,1)}, bf16[4,8,384]{2,1,0:T(8,128)(2,1)}) custom-call(s32[1,1280]{1,0:T(1,128)} %constant.44.clone.refs_0_, bf16[2,4,48,1664]{3,2,1,0:T(8,128)(2,1)} %get-tuple-element.23.refs_1_, bf16[2,4,48,640]{3,2,1,0:T(8,128)(2,1)} %get-tuple-element.24.refs_2_), custom_call_target="tpu_custom_call" | custom-call | flops 1 | bytes 1 | tf_op jit(solution)/shard_map/pack/pallas_call | solution.py:343
  84.0 14.1 %all_to_all.21 = bf16[8,8,4224]{2,1,0:T(8,128)(2,1)} all-to-all(bf16[8,8,4224]{2,1,0:T(8,128)(2,1)} %get-tuple-element.25), channel_id=1, replica_groups=mesh['row'=4,'col'=8] {'col'}, dimensions={0} | all-to-all | bytes 1081344 | tf_op jit(solution)/shard_map/all_to_all | solution.py:471
  98.1 0.0 all-gather.3.cloned.1.call-update
  98.2 1.3 dynamic_slice.20
  99.5 0.8 dynamic_slice.18
  100.3 0.6 broadcast_in_dim.13.wanted_ref
  100.9 1.3 constant_dynamic-slice_fusion.refs_1_
  102.2 0.0 copy-done
  102.2 0.7 pad_maximum_fusion
  102.9 0.6 copy.14
  103.5 5.2 %all-to-all-start.2 = ((bf16[4,2,8,384]{3,2,1,0:T(8,128)(2,1)}), bf16[4,2,8,384]{3,2,1,0:T(8,128)(2,1)S(1)}, u32[]{:S(2)}, u32[]{:S(2)}) async-start(bf16[4,2,8,384]{3,2,1,0:T(8,128)(2,1)} %copy.14), calls=%async_computation.2 | async-start | bytes 98304 | tf_op jit(solution)/shard_map/all_to_all | solution.py:475
  108.7 1.3 fusion.starts_ref
  110.0 4.6 %all-to-all-done.2 = bf16[4,2,8,384]{3,2,1,0:T(8,128)(2,1)S(1)} async-done(((bf16[4,2,8,384]{3,2,1,0:T(8,128)(2,1)}), bf16[4,2,8,384]{3,2,1,0:T(8,128)(2,1)S(1)}, u32[]{:S(2)}, u32[]{:S(2)}) %all-to-all-start.2) | async-done | bytes 49184 | tf_op jit(solution)/shard_map/all_to_all | solution.py:475
  114.6 0.8 broadcast_in_dim.15
  115.4 3.6 %all-to-all-start.3 = ((bf16[8,4,2,8,384]{4,3,1,2,0:T(8,128)(2,1)}), bf16[8,4,2,8,384]{4,3,1,2,0:T(8,128)(2,1)S(1)}, u32[]{:S(2)}, u32[]{:S(2)}) async-start(bf16[8,4,2,8,384]{4,3,1,2,0:T(8,128)(2,1)} %broadcast_in_dim.15), calls=%async_computation.3 | async-start | bytes 786432 | tf_op jit(solution)/shard_map/all_to_all | solution.py:476
  119.0 1.5 constant_dynamic-slice_fusion.1.ids_ref
  120.6 6.6 %all-to-all-done.3 = bf16[8,4,2,8,384]{4,3,1,2,0:T(8,128)(2,1)S(1)} async-done(((bf16[8,4,2,8,384]{4,3,1,2,0:T(8,128)(2,1)}), bf16[8,4,2,8,384]{4,3,1,2,0:T(8,128)(2,1)S(1)}, u32[]{:S(2)}, u32[]{:S(2)}) %all-to-all-start.3) | async-done | bytes 393248 | tf_op jit(solution)/shard_map/all_to_all | solution.py:476
  127.1 0.8 copy.16
  127.9 2.5 %left_side.1.left_ref = bf16[512,512]{1,0:T(8,128)(2,1)} custom-call(bf16[512,384]{1,0:T(8,128)(2,1)} %bitcast.14, s32[1,384]{1,0:T(1,128)} %constant_dynamic-slice_fusion.refs_1_, s32[1,256]{1,0:T(1,128)} %bitcast.17), custom_call_target="tpu_custom_call" | custom-call | flops 1 | bytes 1 | tf_op jit(solution)/shard_map/left_side/pallas_call | solution.py:383
  130.5 0.0 all-gather.5.cloned.1.call-done
  130.5 7.1 %in_order.1.refs_0_ = bf16[256,3840]{1,0:T(8,128)(2,1)} custom-call(s32[3]{0:T(128)} %fusion.starts_ref, s32[1,4224]{1,0:T(1,128)} %constant_dynamic-slice_fusion.1.ids_ref, s32[1,3840]{1,0:T(1,128)} %broadcast_in_dim.13.wanted_ref, bf16[256,4224]{1,0:T(8,128)(2,1)} %bitcast.11), custom_call_target="tpu_custom_call" | custom-call | flops 1 | bytes 1 | tf_op jit(solution)/shard_map/in_order/pallas_call | solution.py:438
  137.6 12.1 %all-gather.3.cloned.1.call-done = bf16[32,8,4224]{2,1,0:T(8,128)(2,1)} async-done(((bf16[8,8,4224]{2,1,0:T(8,128)(2,1)}), bf16[32,8,4224]{2,1,0:T(8,128)(2,1)}) %all-gather.3.cloned.1.call-update) | async-done | bytes 2162704 | tf_op jit(solution)/shard_map/all_gather | solution.py:473
  149.7 9.9 %product.1 = f32[2,256,3840]{2,1,0:T(8,128)} custom-call(s32[3]{0:T(128)} %fusion.starts_ref, s32[1,4224]{1,0:T(1,128)} %constant_dynamic-slice_fusion.1.ids_ref, s32[1,3840]{1,0:T(1,128)} %broadcast_in_dim.13.wanted_ref, bf16[256,4224]{1,0:T(8,128)(2,1)} %bitcast.12, bf16[512,512]{1,0:T(8,128)(2,1)} %left_side.1.left_ref, bf16[256,3840]{1,0:T(8,128)(2,1)} %in_order.1.refs_0_), custom_call_target="tpu_custom_call" | custom-call | flops 1 | bytes 1 | tf_op jit(solution)/shard_map/product/pallas_call | solution.py:438
  (1 shorter events, 0.0 us)
Async XLA Ops:
  6.5 123.9 %all-gather.5.cloned.1.call-start = ((), (), s32[]{:S(2)}) async-start(), calls=%async_computation.5 | async-start | bytes 2703360 | tf_op jit(solution)/shard_map/all_gather | solution.py:473
  54.7 94.9 %all-gather.3.cloned.1.call-start = ((), (), s32[]{:S(2)}) async-start(), calls=%async_computation.4 | async-start | bytes 2703360 | tf_op jit(solution)/shard_map/all_gather | solution.py:473
  79.1 23.0 %copy-start = (bf16[4,8,384]{2,1,0:T(8,128)(2,1)S(1)}, bf16[4,8,384]{2,1,0:T(8,128)(2,1)}, u32[]{:S(2)}) copy-start(bf16[4,8,384]{2,1,0:T(8,128)(2,1)} %get-tuple-element.28) | copy-start | bytes 73732
  103.5 11.1 %all-to-all-start.2 = ((bf16[4,2,8,384]{3,2,1,0:T(8,128)(2,1)}), bf16[4,2,8,384]{3,2,1,0:T(8,128)(2,1)S(1)}, u32[]{:S(2)}, u32[]{:S(2)}) async-start(bf16[4,2,8,384]{3,2,1,0:T(8,128)(2,1)} %copy.14), calls=%async_computation.2 | async-start | bytes 98304 | tf_op jit(solution)/shard_map/all_to_all | solution.py:475
  115.4 11.7 %all-to-all-start.3 = ((bf16[8,4,2,8,384]{4,3,1,2,0:T(8,128)(2,1)}), bf16[8,4,2,8,384]{4,3,1,2,0:T(8,128)(2,1)S(1)}, u32[]{:S(2)}, u32[]{:S(2)}) async-start(bf16[8,4,2,8,384]{4,3,1,2,0:T(8,128)(2,1)} %broadcast_in_dim.15), calls=%async_computation.3 | async-start | bytes 786432 | tf_op jit(solution)/shard_map/all_to_all | solution.py:476
Sparse Core Ops, SparseCore 0:
  54.8 47.0 all-gather.4
  103.5 46.1 all-gather.2

commit v3 on v2

--- a/solution.py
+++ b/solution.py
@@ -175,7 +175,7 @@
     return first, last
 
 
-def spectrum_kernel(plan, points, first_band, weight_ref, val_ref, cond_ref, table_ref, plain_ref, weighted_ref,
+def spectrum_kernel(plan, points, first_band, owner_ref, cond_energy_ref, val_energy_ref, val_ref, cond_ref, table_ref, plain_ref, weighted_ref,
                     cond_a, cond_b, middle, turned, last):
     band = pl.program_id(0)
     planes = 8
@@ -219,12 +219,16 @@
         turned[rows, :] = apply_table(middle[rows, :], table)
 
     first_axis(0)
-
-    @pl.loop(1, points // planes)
+    first_axis(1)
+
+    @pl.loop(1, points // planes // 2)
     def _(block):
-        second_axis(block - 1)
-        first_axis(block)
-
+        for part in range(2):
+            second_axis(2 * block - 2 + part)
+        for part in range(2):
+            first_axis(2 * block + part)
+
+    second_axis(points // planes - 2)
     second_axis(points // planes - 1)
 
     for pair in range(KEEP // 2):
@@ -236,7 +240,9 @@
         last[at, :LANES] = high
         last[at, LANES:] = low
 
-    weight = weight_ref[first_band + band]
+    pairs = val_energy_ref.shape[0] * cond_energy_ref.shape[0]
+    gap = cond_energy_ref[owner_ref[0]] - val_energy_ref[first_band + band]
+    weight = -2.0 / (math.sqrt(pairs) * jnp.full((1, LANES), gap, jnp.float32))
     slab_first, slab_last = slab_tiles(plan)
     for begin in range(0, depth // LANES, 5):
         end = min(begin + 5, depth // LANES)
@@ -251,7 +257,7 @@
                     weighted_ref[part, 0, :, lanes] = (weight * value).astype(jnp.bfloat16)
 
 
-def spectra(plan, val_wave, cond_wave, weight, first_band, count):
+def spectra(plan, val_wave, cond_wave, energies, first_band, count):
     points = val_wave.shape[1]
     depth = round_up(KEEP * KEEP, LANES)
     slab_first, slab_last = slab_tiles(plan)
@@ -262,6 +268,8 @@
         kernel,
         grid=(count,),
         in_specs=[
+            pl.BlockSpec(memory_space=pltpu.SMEM),
+            pl.BlockSpec(memory_space=pltpu.SMEM),
             pl.BlockSpec(memory_space=pltpu.SMEM),
             pl.BlockSpec((1, points, points, 2 * points), lambda v: (first_band + v, 0, 0, 0)),
             pl.BlockSpec((1, points, points, 2 * points), lambda v: (0, 0, 0, 0)),
@@ -285,7 +293,7 @@
         compiler_params=pltpu.CompilerParams(vmem_limit_bytes=VMEM_BYTES, dimension_semantics=("arbitrary",)),
         cost_estimate=pl.CostEstimate(flops=count, bytes_accessed=count, transcendentals=0),
         name="spectra",
-    )(weight, val_wave, cond_wave, jnp.asarray(dft_table(points)))
+    )(*energies, val_wave, cond_wave, jnp.asarray(dft_table(points)))
 
 
 def pack_kernel(plan, groups, place_ref, *refs):
@@ -450,13 +458,10 @@
 
 def on_device(val_wave, cond_wave, val_energy, cond_energy, band_owner, grid_map):
     bands, points = val_wave.shape[0], val_wave.shape[1]
-    band_total = cond_energy.shape[0]
     row_count = lax.axis_size("row")
     col_count = lax.axis_size("col")
     col, row = lax.axis_index("col"), lax.axis_index("row")
     plan = make_plan(points, grid_map.shape[0], col_count, ROWS_DEV * row_count, row_count)
-    energy = jnp.sum(jnp.where(band_owner[0] == jnp.arange(band_total, dtype=jnp.int32), cond_energy, 0.0))
-    weight = -2.0 / (math.sqrt(bands * band_total) * (energy - val_energy))
     width = grid_map.shape[0] // col_count
     starts = lax.dynamic_index_in_dim(jnp.asarray(plan["starts"]), col, 0, keepdims=False)
     ids = lax.dynamic_slice(jnp.asarray(plan["ids"]), (col, 0), (1, plan["lanes"]))
@@ -464,17 +469,27 @@
     wanted = lax.dynamic_slice(grid_map, (col * width,), (width,))[None]
     slab_wanted = lax.dynamic_slice(grid_map, (row * ROWS_DEV,), (ROWS_DEV,))[None]
     chunk = bands // CHUNKS
+    energies = (band_owner, cond_energy, val_energy)
     panels, slabs = [], []
     for part in range(CHUNKS):
-        plain, weighted = spectra(plan, val_wave, cond_wave, weight, part * chunk, chunk)
+        plain, weighted = spectra(plan, val_wave, cond_wave, energies, part * chunk, chunk)
         send, slab = packed(plan, [plain], [weighted])
-        mine = lax.all_to_all(send, "col", split_axis=0, concat_axis=0, tiled=True)
-        mine, slab, cond_wave = lax.optimization_barrier((mine, slab, cond_wave))
-        panels.append(lax.all_gather(mine, "row", axis=0, tiled=True).reshape(-1, plan["lanes"]))
         slabs.append(slab)
-    slab = lax.all_to_all(jnp.stack(slabs, 1), "row", split_axis=0, concat_axis=0, tiled=True)
+        if part < CHUNKS - 1:
+            send, cond_wave = lax.optimization_barrier((send, cond_wave))
+            panels.append(lax.all_gather(send, "row", axis=1))
+        else:
+            mine = lax.all_to_all(send, "col", split_axis=0, concat_axis=0, tiled=True)
+            panels.append(lax.all_gather(mine, "row", axis=0, tiled=True).reshape(-1, plan["lanes"]))
+    *early, slab, _ = lax.optimization_barrier((*panels[:-1], jnp.stack(slabs, 1), mine))
+    for part, panel in enumerate(early):
+        panel = lax.all_to_all(panel, "col", split_axis=0, concat_axis=0, tiled=True)
+        panels[part] = panel.reshape(-1, plan["lanes"])
+    slab = lax.all_to_all(slab, "row", split_axis=0, concat_axis=0, tiled=True)
     slab = lax.all_to_all(jnp.broadcast_to(slab, (col_count, *slab.shape)), "col", split_axis=0, concat_axis=0)
-    slab = slab.transpose(2, 1, 0, 3, 4).reshape(-1, plan["slab_lanes"])
+    slab = [slab[:, :, part] for part in range(CHUNKS)]
+    slab[-1] = slab[-1].transpose(1, 0, 2, 3)
+    slab = jnp.stack([part.reshape(-1, plan["slab_lanes"]) for part in slab]).reshape(-1, plan["slab_lanes"])
     left = left_side(2 * chunk, slab, slab_ids, slab_wanted)
     ordered = [put_in_order(plan, starts, ids, wanted, panel) for panel in panels[:-1]]
     return put_in_order(plan, starts, ids, wanted, panels[-1], left, ordered)

time: 167 us -> 158 us (0.946)
  Pallas kernels: 78.1 us -> 67.6 us
  blocking collectives: 29.3 us -> 35 us
  starting transfers between devices: 8.89 us -> 3.83 us
  waiting for transfers between devices: 23.3 us -> 26.8 us
  other arithmetic: 3.89 us -> 1.54 us
    all_to_all x0 -> x2, blocking collectives: none -> 19.9 us  [the longest x1 11.8 us: on_device(): lax.all_to_all(jnp.broadcast_to(slab, (col_count, *slab.shape)), 'col', s...]
    all_to_all x2 -> x1, blocking collectives: 29.3 us -> 15.2 us  [on_device(): mine = lax.all_to_all(send, 'col', split_axis=0, concat_axis=0, tiled=True)]
    all_gather x2 -> x1, waiting for transfers between devices: 12.1 us -> 0.01 us  [on_device(): lax.all_gather(mine, 'row', axis=0, tiled=True).reshape(-1, plan['lanes'])]
    pallas_call x2, Pallas kernels: 48.6 us -> 38.2 us  [spectra(): pl.pallas_call(kernel, grid=(count,), in_specs=[pl.BlockSpec(memory_space...]
    all_gather x0 -> x1, waiting for transfers between devices: none -> 9.94 us  [on_device(): panels.append(lax.all_gather(send, 'row', axis=1))]
    all_to_all x2 -> x1, waiting for transfers between devices: 11.2 us -> 16.8 us  [on_device(): lax.all_to_all(panel, 'col', split_axis=0, concat_axis=0, tiled=True)]
    all_to_all x2 -> x1, starting transfers between devices: 8.85 us -> 3.79 us  [on_device(): lax.all_to_all(panel, 'col', split_axis=0, concat_axis=0, tiled=True)]
    div x1 -> x0, other arithmetic: 1.86 us -> none  [on_device(): weight = -2.0 / (math.sqrt(bands * band_total) * (energy - val_energy))]
  transfers between devices with their start and end apart: 4 -> 3, of which waited for: 3 -> 2; matrix products, arithmetic and copies ran while one was open for 6% -> 5% of each run, Pallas kernels for 23% -> 21%
where the time goes in v3:
time: 158 us; the launch traced here: 157 us
  Pallas kernels  67.6 us (43%)
  blocking collectives  35 us (22%)
  waiting for transfers between devices  26.8 us (17%)
  between operations  14.1 us (9%)
  local copies, waits for them, and re-layouts  8.3 us (5%)
  starting transfers between devices  3.83 us (2%)
    pallas_call x2, Pallas kernels, spectra(): pl.pallas_call(kernel, grid=(count,), in_specs=[pl.BlockSpec(memory_space...  38.2 us
    pallas_call x2, Pallas kernels, put_in_order(): pl.pallas_call(order_kernel if left is None else product_kernel, grid=(PA...  17.1 us
    all_to_all x1, waiting for transfers between devices, on_device(): lax.all_to_all(panel, 'col', split_axis=0, concat_axis=0, tiled=True)  16.8 us
    all_to_all x1, blocking collectives, on_device(): mine = lax.all_to_all(send, 'col', split_axis=0, concat_axis=0, tiled=True)  15.2 us
    all_to_all x1, blocking collectives, on_device(): lax.all_to_all(jnp.broadcast_to(slab, (col_count, *slab.shape)), 'col', s...  11.8 us
    all_gather x1, waiting for transfers between devices, on_device(): panels.append(lax.all_gather(send, 'row', axis=1))  9.94 us
    pallas_call x2, Pallas kernels, packed(): pl.pallas_call(kernel, in_specs=[vmem] * (1 + 2 * len(plains)), out_specs...  9.82 us
    all_to_all x1, blocking collectives, on_device(): slab = lax.all_to_all(slab, 'row', split_axis=0, concat_axis=0, tiled=True)  8.05 us
  transfers between devices with their start and end apart: 3, of which 2 were waited for; matrix products, arithmetic and copies ran while one was open for 5% of the time, Pallas kernels for 21%

profile of v3, /device:TPU:0, one launch (start us, length us, event | category | flops | bytes accessed | tf_op | source)
XLA Modules:
  0.0 157.3 jit_solution(9654464902883182118)
XLA Ops:
  6.5 0.0 all-gather.6.cloned.1.call-start
  7.2 19.1 %spectra.2 = (bf16[2,4,48,1664]{3,2,1,0:T(8,128)(2,1)}, bf16[2,4,48,640]{3,2,1,0:T(8,128)(2,1)}) custom-call(s32[1]{0:T(128)S(6)} %copy.21.refs_0_, f32[32]{0:T(128)} %refs_1_.3, f32[8]{0:T(128)} %refs_2_.3, bf16[8,64,64,128]{3,2,1,0:T(8,128)(2,1)} %refs_3_.3, bf16[1,64,64,128]{3,2,1,0:T(8,128)(2,1)} %refs_4_.2, bf16[256,256]{1,0:T(8,128)(2,1)} %constant.37.clone.refs_5_), custom_call_target="tpu_custom_call" | custom-call | flops 4 | bytes 4 | tf_op jit(solution)/shard_map/spectra/pallas_call | solution.py:267
  26.3 4.9 %pack.2 = (bf16[8,8,4224]{2,1,0:T(8,128)(2,1)}, bf16[4,8,384]{2,1,0:T(8,128)(2,1)}) custom-call(s32[1,1280]{1,0:T(1,128)} %constant.38.clone.refs_0_, bf16[2,4,48,1664]{3,2,1,0:T(8,128)(2,1)} %get-tuple-element.17.refs_1_, bf16[2,4,48,640]{3,2,1,0:T(8,128)(2,1)} %get-tuple-element.18.refs_2_), custom_call_target="tpu_custom_call" | custom-call | flops 1 | bytes 1 | tf_op jit(solution)/shard_map/pack/pallas_call | solution.py:351
  31.2 0.0 all-gather.6.cloned.1.call-update
  31.2 0.0 all-gather.4.cloned.1.call-start
  31.3 19.1 %spectra.3 = (bf16[2,4,48,1664]{3,2,1,0:T(8,128)(2,1)}, bf16[2,4,48,640]{3,2,1,0:T(8,128)(2,1)}) custom-call(s32[1]{0:T(128)S(6)} %copy.21.refs_0_, f32[32]{0:T(128)} %refs_1_.3, f32[8]{0:T(128)} %refs_2_.3, bf16[8,64,64,128]{3,2,1,0:T(8,128)(2,1)} %refs_3_.3, bf16[1,64,64,128]{3,2,1,0:T(8,128)(2,1)} %refs_4_.2, bf16[256,256]{1,0:T(8,128)(2,1)} %constant.37.clone.refs_5_), custom_call_target="tpu_custom_call" | custom-call | flops 4 | bytes 4 | tf_op jit(solution)/shard_map/spectra/pallas_call | solution.py:267
  50.4 0.0 copy-start.1
  50.4 4.9 %pack.3 = (bf16[8,8,4224]{2,1,0:T(8,128)(2,1)}, bf16[4,8,384]{2,1,0:T(8,128)(2,1)}) custom-call(s32[1,1280]{1,0:T(1,128)} %constant.38.clone.refs_0_, bf16[2,4,48,1664]{3,2,1,0:T(8,128)(2,1)} %get-tuple-element.21.refs_1_, bf16[2,4,48,640]{3,2,1,0:T(8,128)(2,1)} %get-tuple-element.22.refs_2_), custom_call_target="tpu_custom_call" | custom-call | flops 1 | bytes 1 | tf_op jit(solution)/shard_map/pack/pallas_call | solution.py:351
  55.3 15.2 %all_to_all.20 = bf16[8,8,4224]{2,1,0:T(8,128)(2,1)} all-to-all(bf16[8,8,4224]{2,1,0:T(8,128)(2,1)} %get-tuple-element.23), channel_id=1, replica_groups=mesh['row'=4,'col'=8] {'col'}, dimensions={0} | all-to-all | bytes 1081344 | tf_op jit(solution)/shard_map/all_to_all | solution.py:482
  70.5 0.0 all-gather.4.cloned.1.call-update
  70.5 0.0 copy-done.1
  70.5 0.7 pad_maximum_fusion.1
  71.3 9.9 %all-gather.6.cloned.1.call-done = bf16[8,32,4224]{2,1,0:T(8,128)(2,1)} async-done(((bf16[8,8,4224]{2,1,0:T(8,128)(2,1)}), bf16[8,32,4224]{2,1,0:T(8,128)(2,1)}) %all-gather.6.cloned.1.call-update) | async-done | bytes 2162704 | tf_op jit(solution)/shard_map/all_gather | solution.py:480
  81.2 8.0 %all_to_all.21 = bf16[4,2,8,384]{3,2,1,0:T(8,128)(2,1)S(1)} all-to-all(bf16[4,2,8,384]{3,2,1,0:T(8,128)(2,1)S(1)} %copy.17), channel_id=1, replica_groups=mesh['row'=4,'col'=8] {'row'}, dimensions={0} | all-to-all | bytes 98304 | tf_op jit(solution)/shard_map/all_to_all | solution.py:488
  89.3 11.8 %all_to_all.22 = bf16[8,4,2,8,384]{4,3,1,2,0:T(8,128)(2,1)S(1)} all-to-all(bf16[8,4,2,8,384]{4,3,1,2,0:T(8,128)(2,1)S(1)} %broadcast_in_dim.10), channel_id=1, replica_groups=mesh['row'=4,'col'=8] {'col'}, dimensions={0} | all-to-all | bytes 786432 | tf_op jit(solution)/shard_map/all_to_all | solution.py:489
  101.1 3.8 %all-to-all-start.3 = ((bf16[8,4,8,4224]{3,2,1,0:T(8,128)(2,1)}), bf16[8,4,8,4224]{3,2,1,0:T(8,128)(2,1)S(1)}, u32[]{:S(2)}, u32[]{:S(2)}) async-start(bf16[8,4,8,4224]{3,2,1,0:T(8,128)(2,1)} %bitcast.16), calls=%async_computation.3 | async-start | bytes 4325376 | tf_op jit(solution)/shard_map/all_to_all | solution.py:486
  104.9 1.4 dynamic_slice.20
  106.3 0.8 dynamic_slice.18
  107.1 0.6 broadcast_in_dim.9.wanted_ref
  107.7 1.3 fusion.starts_ref
  109.0 1.3 constant_dynamic-slice_fusion.refs_1_
  110.2 1.5 constant_dynamic-slice_fusion.1.ids_ref
  111.9 0.8 pad_maximum_fusion
  112.6 2.5 %left_side.1.left_ref = bf16[512,512]{1,0:T(8,128)(2,1)} custom-call(bf16[512,384]{1,0:T(8,128)(2,1)} %bitcast.18, s32[1,384]{1,0:T(1,128)} %constant_dynamic-slice_fusion.refs_1_, s32[1,256]{1,0:T(1,128)} %bitcast.23), custom_call_target="tpu_custom_call" | custom-call | flops 1 | bytes 1 | tf_op jit(solution)/shard_map/left_side/pallas_call | solution.py:391
  115.2 16.8 %all-to-all-done.3 = bf16[8,4,8,4224]{3,2,1,0:T(8,128)(2,1)S(1)} async-done(((bf16[8,4,8,4224]{3,2,1,0:T(8,128)(2,1)}), bf16[8,4,8,4224]{3,2,1,0:T(8,128)(2,1)S(1)}, u32[]{:S(2)}, u32[]{:S(2)}) %all-to-all-start.3) | async-done | bytes 2162720 | tf_op jit(solution)/shard_map/all_to_all | solution.py:486
  132.0 0.0 copy-start
  132.0 1.3 copy-done
  133.4 7.1 %in_order.1.refs_0_ = bf16[256,3840]{1,0:T(8,128)(2,1)} custom-call(s32[3]{0:T(128)} %fusion.starts_ref, s32[1,4224]{1,0:T(1,128)} %constant_dynamic-slice_fusion.1.ids_ref, s32[1,3840]{1,0:T(1,128)} %broadcast_in_dim.9.wanted_ref, bf16[256,4224]{1,0:T(8,128)(2,1)} %bitcast.15), custom_call_target="tpu_custom_call" | custom-call | flops 1 | bytes 1 | tf_op jit(solution)/shard_map/in_order/pallas_call | solution.py:446
  140.5 0.0 all-gather.4.cloned.1.call-done
  140.5 9.9 %product.1 = f32[2,256,3840]{2,1,0:T(8,128)} custom-call(s32[3]{0:T(128)} %fusion.starts_ref, s32[1,4224]{1,0:T(1,128)} %constant_dynamic-slice_fusion.1.ids_ref, s32[1,3840]{1,0:T(1,128)} %broadcast_in_dim.9.wanted_ref, bf16[256,4224]{1,0:T(8,128)(2,1)} %bitcast.17, bf16[512,512]{1,0:T(8,128)(2,1)} %left_side.1.left_ref, bf16[256,3840]{1,0:T(8,128)(2,1)} %in_order.1.refs_0_), custom_call_target="tpu_custom_call" | custom-call | flops 1 | bytes 1 | tf_op jit(solution)/shard_map/product/pallas_call | solution.py:446
  (5 shorter events, 0.1 us)
Async XLA Ops:
  6.5 74.7 %all-gather.6.cloned.1.call-start = ((), (), s32[]{:S(2)}) async-start(), calls=%async_computation.5 | async-start | bytes 2703360 | tf_op jit(solution)/shard_map/all_gather | solution.py:480
  31.2 109.3 %all-gather.4.cloned.1.call-start = ((), (), s32[]{:S(2)}) async-start(), calls=%async_computation.4 | async-start | bytes 2703360 | tf_op jit(solution)/shard_map/all_gather | solution.py:483
  50.4 20.1 %copy-start.1 = (bf16[4,8,384]{2,1,0:T(8,128)(2,1)S(1)}, bf16[4,8,384]{2,1,0:T(8,128)(2,1)}, u32[]{:S(2)}) copy-start(bf16[4,8,384]{2,1,0:T(8,128)(2,1)} %get-tuple-element.25) | copy-start | bytes 73732
  101.1 30.9 %all-to-all-start.3 = ((bf16[8,4,8,4224]{3,2,1,0:T(8,128)(2,1)}), bf16[8,4,8,4224]{3,2,1,0:T(8,128)(2,1)S(1)}, u32[]{:S(2)}, u32[]{:S(2)}) async-start(bf16[8,4,8,4224]{3,2,1,0:T(8,128)(2,1)} %bitcast.16), calls=%async_computation.3 | async-start | bytes 4325376 | tf_op jit(solution)/shard_map/all_to_all | solution.py:486
  132.0 1.3 copy-start
Sparse Core Ops, SparseCore 0:
  31.3 49.8 all-gather.5
  82.8 46.0 all-gather.3

commit v4 on v3

--- a/solution.py
+++ b/solution.py
@@ -201,8 +201,8 @@
     step = planes * KEEP
 
     def first_axis(block):
-        rows = pl.ds(pl.multiple_of(block * planes * points, planes * points), planes * points)
-        wave = val_ref[0, pl.ds(block * planes, planes)].reshape(planes * points, LANES).astype(jnp.float32)
+        rows = slice(block * planes * points, (block + 1) * planes * points)
+        wave = val_ref[0, block * planes : (block + 1) * planes].reshape(planes * points, LANES).astype(jnp.float32)
         other = pltpu.roll(wave, HALF, 1)
         density = jnp.where(low_lanes, wave, other) * cond_a[rows, :] + jnp.where(low_lanes, other, wave) * cond_b[rows, :]
         high, low = split_parts(density)
@@ -210,25 +210,18 @@
         for pair in range(planes // 2):
             both = field[pair * 2 * points : (pair + 1) * 2 * points].T
             high, low = split_parts(stack_complex(both, low_lanes))
-            at = pl.ds(pl.multiple_of((block * planes + pair * 2) * KEEP, 2 * KEEP), 2 * KEEP)
+            at = slice((block * planes + pair * 2) * KEEP, (block * planes + pair * 2 + 2) * KEEP)
             middle[at, :LANES] = high
             middle[at, LANES:] = low
 
     def second_axis(block):
-        rows = pl.ds(pl.multiple_of(block * step, step), step)
+        rows = slice(block * step, (block + 1) * step)
         turned[rows, :] = apply_table(middle[rows, :], table)
 
-    first_axis(0)
-    first_axis(1)
-
-    @pl.loop(1, points // planes // 2)
-    def _(block):
-        for part in range(2):
-            second_axis(2 * block - 2 + part)
-        for part in range(2):
-            first_axis(2 * block + part)
-
-    second_axis(points // planes - 2)
+    for block in range(points // planes):
+        first_axis(block)
+        if block:
+            second_axis(block - 1)
     second_axis(points // planes - 1)
 
     for pair in range(KEEP // 2):
@@ -399,61 +392,61 @@
     )(slab, slab_ids, slab_wanted)
 
 
-def in_order(start, panel_ref, ids_ref, wanted_ref, hot):
+def order_kernel(starts_ref, ids_ref, wanted_ref, panel_ref, out_ref, hot):
+    start = pl.multiple_of(starts_ref[pl.program_id(0)], LANES)
     wanted = wanted_ref[...]
     window = hot.shape[0]
     for begin in range(0, window, LANES):
         hot[begin : begin + LANES, :] = one_hot(ids_ref, pl.multiple_of(start + begin, LANES), wanted)
-    return jnp.dot(panel_ref[:, pl.ds(start, window)], hot[...], preferred_element_type=jnp.float32).astype(jnp.bfloat16)
-
-
-def order_kernel(starts_ref, ids_ref, wanted_ref, panel_ref, out_ref, hot):
-    start = pl.multiple_of(starts_ref[pl.program_id(0)], LANES)
-    out_ref[...] = in_order(start, panel_ref, ids_ref, wanted_ref, hot)
-
-
-def product_kernel(starts_ref, ids_ref, wanted_ref, panel_ref, left_ref, *refs):
-    *ordered, out_ref, hot = refs
+    ordered = jnp.dot(panel_ref[:, pl.ds(start, window)], hot[...], preferred_element_type=jnp.float32)
+    out_ref[...] = ordered.astype(jnp.bfloat16)
+
+
+def put_in_order(plan, starts, ids, wanted, panel):
+    columns = wanted.shape[1]
+    block = columns // PARTS
+    whole = lambda array: pl.BlockSpec(array.shape, lambda n: (0,) * array.ndim)
+    return pl.pallas_call(
+        order_kernel,
+        grid=(PARTS,),
+        in_specs=[
+            pl.BlockSpec(memory_space=pltpu.SMEM),
+            whole(ids),
+            pl.BlockSpec((1, block), lambda n: (0, n)),
+            whole(panel),
+        ],
+        out_specs=pl.BlockSpec((panel.shape[0], block), lambda n: (0, n)),
+        out_shape=jax.ShapeDtypeStruct((panel.shape[0], columns), jnp.bfloat16),
+        scratch_shapes=[pltpu.VMEM((plan["window"], block), jnp.bfloat16)],
+        compiler_params=pltpu.CompilerParams(vmem_limit_bytes=VMEM_BYTES, dimension_semantics=("arbitrary",)),
+        cost_estimate=pl.CostEstimate(flops=1, bytes_accessed=1, transcendentals=0),
+        name="in_order",
+    )(starts, ids, wanted, panel)
+
+
+def product_kernel(left_ref, *refs):
+    *ordered, out_ref = refs
     rows = out_ref.shape[1]
-    start = pl.multiple_of(starts_ref[pl.program_id(0)], LANES)
-    last = in_order(start, panel_ref, ids_ref, wanted_ref, hot)
-    right = jnp.concatenate([part[...] for part in ordered] + [last], 0)
+    right = jnp.concatenate([part[...] for part in ordered], 0)
     chi = jnp.dot(left_ref[...], right, preferred_element_type=jnp.float32)
     out_ref[0] = chi[:rows]
     out_ref[1] = chi[rows:]
 
 
-def put_in_order(plan, starts, ids, wanted, panel, left=None, ordered=()):
-    columns = wanted.shape[1]
-    block = columns // PARTS
-    whole = lambda array: pl.BlockSpec(array.shape, lambda n: (0,) * array.ndim)
-    in_specs = [
-        pl.BlockSpec(memory_space=pltpu.SMEM),
-        whole(ids),
-        pl.BlockSpec((1, block), lambda n: (0, n)),
-        whole(panel),
-    ]
-    operands = [starts, ids, wanted, panel]
-    if left is None:
-        out_spec = pl.BlockSpec((panel.shape[0], block), lambda n: (0, n))
-        out_shape = jax.ShapeDtypeStruct((panel.shape[0], columns), jnp.bfloat16)
-    else:
-        rows = left.shape[0] // 2
-        in_specs += [whole(left)] + [pl.BlockSpec((part.shape[0], block), lambda n: (0, n)) for part in ordered]
-        operands += [left, *ordered]
-        out_spec = pl.BlockSpec((2, rows, block), lambda n: (0, 0, n))
-        out_shape = jax.ShapeDtypeStruct((2, rows, columns), jnp.float32)
+def product(left, ordered):
+    rows, columns = left.shape[0] // 2, ordered[0].shape[1]
+    block = columns // (2 * PARTS) // LANES * LANES
     return pl.pallas_call(
-        order_kernel if left is None else product_kernel,
-        grid=(PARTS,),
-        in_specs=in_specs,
-        out_specs=out_spec,
-        out_shape=out_shape,
-        scratch_shapes=[pltpu.VMEM((plan["window"], block), jnp.bfloat16)],
+        product_kernel,
+        grid=(pl.cdiv(columns, block),),
+        in_specs=[pl.BlockSpec(left.shape, lambda n: (0, 0))]
+        + [pl.BlockSpec((part.shape[0], block), lambda n: (0, n)) for part in ordered],
+        out_specs=pl.BlockSpec((2, rows, block), lambda n: (0, 0, n)),
+        out_shape=jax.ShapeDtypeStruct((2, rows, columns), jnp.float32),
         compiler_params=pltpu.CompilerParams(vmem_limit_bytes=VMEM_BYTES, dimension_semantics=("arbitrary",)),
         cost_estimate=pl.CostEstimate(flops=1, bytes_accessed=1, transcendentals=0),
-        name="in_order" if left is None else "product",
-    )(*operands)
+        name="product",
+    )(left, *ordered)
 
 
 def on_device(val_wave, cond_wave, val_energy, cond_energy, band_owner, grid_map):
@@ -479,20 +472,22 @@
             send, cond_wave = lax.optimization_barrier((send, cond_wave))
             panels.append(lax.all_gather(send, "row", axis=1))
         else:
-            mine = lax.all_to_all(send, "col", split_axis=0, concat_axis=0, tiled=True)
-            panels.append(lax.all_gather(mine, "row", axis=0, tiled=True).reshape(-1, plan["lanes"]))
-    *early, slab, _ = lax.optimization_barrier((*panels[:-1], jnp.stack(slabs, 1), mine))
-    for part, panel in enumerate(early):
-        panel = lax.all_to_all(panel, "col", split_axis=0, concat_axis=0, tiled=True)
-        panels[part] = panel.reshape(-1, plan["lanes"])
+            mine = lax.all_to_all(send, "col", split_axis=0, concat_axis=0, tiled=True).reshape(-1, plan["lanes"])
+            mine = put_in_order(plan, starts, ids, wanted, mine)
+            last = lax.all_gather(mine, "row", axis=0, tiled=True)
+    slab, _ = lax.optimization_barrier((jnp.stack(slabs, 1), mine))
     slab = lax.all_to_all(slab, "row", split_axis=0, concat_axis=0, tiled=True)
     slab = lax.all_to_all(jnp.broadcast_to(slab, (col_count, *slab.shape)), "col", split_axis=0, concat_axis=0)
+    *panels, slab = lax.optimization_barrier((*panels, slab))
     slab = [slab[:, :, part] for part in range(CHUNKS)]
     slab[-1] = slab[-1].transpose(1, 0, 2, 3)
     slab = jnp.stack([part.reshape(-1, plan["slab_lanes"]) for part in slab]).reshape(-1, plan["slab_lanes"])
     left = left_side(2 * chunk, slab, slab_ids, slab_wanted)
-    ordered = [put_in_order(plan, starts, ids, wanted, panel) for panel in panels[:-1]]
-    return put_in_order(plan, starts, ids, wanted, panels[-1], left, ordered)
+    ordered = []
+    for panel in panels:
+        panel = lax.all_to_all(panel, "col", split_axis=0, concat_axis=0, tiled=True)
+        ordered.append(put_in_order(plan, starts, ids, wanted, panel.reshape(-1, plan["lanes"])))
+    return product(left, [*ordered, last])
 
 
 def solution(mesh):

time: 158 us -> 165 us (1.044)
  Pallas kernels: 67.6 us -> 83.1 us
  blocking collectives: 35 us -> 21.2 us
  starting transfers between devices: 3.83 us -> 8.97 us
    all_to_all x1 -> x0, blocking collectives: 15.2 us -> none  [on_device(): mine = lax.all_to_all(send, 'col', split_axis=0, concat_axis=0, tiled=True)]
    pallas_call x2, Pallas kernels: 38.2 us -> 51.1 us  [spectra(): pl.pallas_call(kernel, grid=(count,), in_specs=[pl.BlockSpec(memory_space...]
    all_gather x1, waiting for transfers between devices: 9.94 us -> 0.01 us  [on_device(): panels.append(lax.all_gather(send, 'row', axis=1))]
    all_to_all x0 -> x1, waiting for transfers between devices: none -> 5.63 us  [on_device(): lax.all_to_all(send, 'col', split_axis=0, concat_axis=0, tiled=True)]
    all_to_all x0 -> x1, starting transfers between devices: none -> 5.33 us  [on_device(): lax.all_to_all(send, 'col', split_axis=0, concat_axis=0, tiled=True)]
    all_to_all x1, waiting for transfers between devices: 16.8 us -> 21.2 us  [on_device(): lax.all_to_all(panel, 'col', split_axis=0, concat_axis=0, tiled=True)]
    pallas_call x2 -> x3, Pallas kernels: 17.1 us -> 19.7 us  [the longest x2 11.8 us: put_in_order(): pl.pallas_call(order_kernel, grid=(PARTS,), in_specs=[pl.BlockSpec(memory...]
    all_to_all x1, blocking collectives: 8.05 us -> 10.5 us  [on_device(): slab = lax.all_to_all(slab, 'row', split_axis=0, concat_axis=0, tiled=True)]
  transfers between devices with their start and end apart: 3 -> 4, of which waited for: 2 -> 2; matrix products, arithmetic and copies ran while one was open for 5% -> 5% of each run, Pallas kernels for 21% -> 27%
where the time goes in v4:
time: 165 us; the launch traced here: 164 us
  Pallas kernels  83.1 us (50%)
  waiting for transfers between devices  26.9 us (16%)
  blocking collectives  21.2 us (13%)
  between operations  14.1 us (9%)
  local copies, waits for them, and re-layouts  9.1 us (6%)
  starting transfers between devices  8.97 us (5%)
    pallas_call x2, Pallas kernels, spectra(): pl.pallas_call(kernel, grid=(count,), in_specs=[pl.BlockSpec(memory_space...  51.1 us
    all_to_all x1, waiting for transfers between devices, on_device(): lax.all_to_all(panel, 'col', split_axis=0, concat_axis=0, tiled=True)  21.2 us
    pallas_call x2, Pallas kernels, put_in_order(): pl.pallas_call(order_kernel, grid=(PARTS,), in_specs=[pl.BlockSpec(memory...  11.8 us
    all_to_all x1, blocking collectives, on_device(): lax.all_to_all(jnp.broadcast_to(slab, (col_count, *slab.shape)), 'col', s...  10.7 us
    all_to_all x1, blocking collectives, on_device(): slab = lax.all_to_all(slab, 'row', split_axis=0, concat_axis=0, tiled=True)  10.5 us
    pallas_call x2, Pallas kernels, packed(): pl.pallas_call(kernel, in_specs=[vmem] * (1 + 2 * len(plains)), out_specs...  9.78 us
    pallas_call x1, Pallas kernels, product(): pl.pallas_call(product_kernel, grid=(pl.cdiv(columns, block),), in_specs=...  7.88 us
    all_to_all x1, waiting for transfers between devices, on_device(): lax.all_to_all(send, 'col', split_axis=0, concat_axis=0, tiled=True)  5.63 us
  transfers between devices with their start and end apart: 4, of which 2 were waited for; matrix products, arithmetic and copies ran while one was open for 5% of the time, Pallas kernels for 27%

profile of v4, /device:TPU:0, one launch (start us, length us, event | category | flops | bytes accessed | tf_op | source)
XLA Modules:
  0.0 164.2 jit_solution(15684546293670652845)
XLA Ops:
  6.5 0.0 all-gather.6.cloned.1.call-start
  7.2 25.5 %spectra.2 = (bf16[2,4,48,1664]{3,2,1,0:T(8,128)(2,1)}, bf16[2,4,48,640]{3,2,1,0:T(8,128)(2,1)}) custom-call(s32[1]{0:T(128)S(6)} %copy.20.refs_0_, f32[32]{0:T(128)} %refs_1_.3, f32[8]{0:T(128)} %refs_2_.3, bf16[8,64,64,128]{3,2,1,0:T(8,128)(2,1)} %refs_3_.3, bf16[1,64,64,128]{3,2,1,0:T(8,128)(2,1)} %refs_4_.2, bf16[256,256]{1,0:T(8,128)(2,1)} %constant.37.clone.refs_5_), custom_call_target="tpu_custom_call" | custom-call | flops 4 | bytes 4 | tf_op jit(solution)/shard_map/spectra/pallas_call | solution.py:260
  32.7 4.9 %pack.2 = (bf16[8,8,4224]{2,1,0:T(8,128)(2,1)}, bf16[4,8,384]{2,1,0:T(8,128)(2,1)}) custom-call(s32[1,1280]{1,0:T(1,128)} %constant.38.clone.refs_0_, bf16[2,4,48,1664]{3,2,1,0:T(8,128)(2,1)} %get-tuple-element.18.refs_1_, bf16[2,4,48,640]{3,2,1,0:T(8,128)(2,1)} %get-tuple-element.19.refs_2_), custom_call_target="tpu_custom_call" | custom-call | flops 1 | bytes 1 | tf_op jit(solution)/shard_map/pack/pallas_call | solution.py:344
  37.6 0.0 all-gather.6.cloned.1.call-update
  37.6 25.6 %spectra.3 = (bf16[2,4,48,1664]{3,2,1,0:T(8,128)(2,1)}, bf16[2,4,48,640]{3,2,1,0:T(8,128)(2,1)}) custom-call(s32[1]{0:T(128)S(6)} %copy.20.refs_0_, f32[32]{0:T(128)} %refs_1_.3, f32[8]{0:T(128)} %refs_2_.3, bf16[8,64,64,128]{3,2,1,0:T(8,128)(2,1)} %refs_3_.3, bf16[1,64,64,128]{3,2,1,0:T(8,128)(2,1)} %refs_4_.2, bf16[256,256]{1,0:T(8,128)(2,1)} %constant.37.clone.refs_5_), custom_call_target="tpu_custom_call" | custom-call | flops 4 | bytes 4 | tf_op jit(solution)/shard_map/spectra/pallas_call | solution.py:260
  63.2 0.0 copy-start.2
  63.2 4.9 %pack.3 = (bf16[8,8,4224]{2,1,0:T(8,128)(2,1)}, bf16[4,8,384]{2,1,0:T(8,128)(2,1)}) custom-call(s32[1,1280]{1,0:T(1,128)} %constant.38.clone.refs_0_, bf16[2,4,48,1664]{3,2,1,0:T(8,128)(2,1)} %get-tuple-element.24.refs_1_, bf16[2,4,48,640]{3,2,1,0:T(8,128)(2,1)} %get-tuple-element.25.refs_2_), custom_call_target="tpu_custom_call" | custom-call | flops 1 | bytes 1 | tf_op jit(solution)/shard_map/pack/pallas_call | solution.py:344
  68.1 0.0 copy-start.3
  68.1 5.3 %all-to-all-start = ((bf16[8,8,4224]{2,1,0:T(8,128)(2,1)}), bf16[8,8,4224]{2,1,0:T(8,128)(2,1)S(1)}, u32[]{:S(2)}, u32[]{:S(2)}) async-start(bf16[8,8,4224]{2,1,0:T(8,128)(2,1)} %get-tuple-element.27), calls=%async_computation | async-start | bytes 1081344 | tf_op jit(solution)/shard_map/all_to_all | solution.py:475
  73.4 0.0 all-gather.4.cloned.1.call-start
  73.5 0.8 dynamic_slice.18
  74.3 0.6 broadcast_in_dim.9.wanted_ref
  74.9 1.3 fusion.starts_ref
  76.2 1.5 constant_dynamic-slice_fusion.1.ids_ref
  77.7 5.6 %all-to-all-done = bf16[8,8,4224]{2,1,0:T(8,128)(2,1)S(1)} async-done(((bf16[8,8,4224]{2,1,0:T(8,128)(2,1)}), bf16[8,8,4224]{2,1,0:T(8,128)(2,1)S(1)}, u32[]{:S(2)}, u32[]{:S(2)}) %all-to-all-start) | async-done | bytes 540704 | tf_op jit(solution)/shard_map/all_to_all | solution.py:475
  83.3 0.0 copy-start.1
  83.3 0.8 copy-done.1
  84.1 4.7 %in_order.2 = bf16[64,3840]{1,0:T(8,128)(2,1)} custom-call(s32[3]{0:T(128)} %fusion.starts_ref, s32[1,4224]{1,0:T(1,128)} %constant_dynamic-slice_fusion.1.ids_ref, s32[1,3840]{1,0:T(1,128)} %broadcast_in_dim.9.wanted_ref, bf16[64,4224]{1,0:T(8,128)(2,1)} %bitcast.17), custom_call_target="tpu_custom_call" | custom-call | flops 1 | bytes 1 | tf_op jit(solution)/shard_map/in_order/pallas_call | solution.py:409
  88.8 0.0 all-gather.4.cloned.1.call-update
  88.9 0.0 copy-done.2
  88.9 0.0 copy-done.3
  88.9 10.5 %all_to_all.20 = bf16[4,2,8,384]{3,2,1,0:T(8,128)(2,1)S(1)} all-to-all(bf16[4,2,8,384]{3,2,1,0:T(8,128)(2,1)S(1)} %copy.17), channel_id=1, replica_groups=mesh['row'=4,'col'=8] {'row'}, dimensions={0} | all-to-all | bytes 98304 | tf_op jit(solution)/shard_map/all_to_all | solution.py:479
  99.5 10.7 %all_to_all.21 = bf16[8,4,2,8,384]{4,3,1,2,0:T(8,128)(2,1)S(1)} all-to-all(bf16[8,4,2,8,384]{4,3,1,2,0:T(8,128)(2,1)S(1)} %broadcast_in_dim.10), channel_id=1, replica_groups=mesh['row'=4,'col'=8] {'col'}, dimensions={0} | all-to-all | bytes 786432 | tf_op jit(solution)/shard_map/all_to_all | solution.py:480
  110.2 0.0 all-gather.6.cloned.1.call-done
  110.2 3.6 %all-to-all-start.3 = ((bf16[8,4,8,4224]{3,2,1,0:T(8,128)(2,1)}), bf16[8,4,8,4224]{3,2,1,0:T(8,128)(2,1)S(1)}, u32[]{:S(2)}, u32[]{:S(2)}) async-start(bf16[8,4,8,4224]{3,2,1,0:T(8,128)(2,1)} %bitcast.16), calls=%async_computation.3 | async-start | bytes 4325376 | tf_op jit(solution)/shard_map/all_to_all | solution.py:488
  113.8 1.3 dynamic_slice.20
  115.2 1.2 constant_dynamic-slice_fusion.refs_1_
  116.5 0.8 pad_maximum_fusion
  117.3 2.6 %left_side.1.left_ref = bf16[512,512]{1,0:T(8,128)(2,1)} custom-call(bf16[512,384]{1,0:T(8,128)(2,1)} %bitcast.18, s32[1,384]{1,0:T(1,128)} %constant_dynamic-slice_fusion.refs_1_, s32[1,256]{1,0:T(1,128)} %bitcast.23), custom_call_target="tpu_custom_call" | custom-call | flops 1 | bytes 1 | tf_op jit(solution)/shard_map/left_side/pallas_call | solution.py:384
  119.8 21.2 %all-to-all-done.3 = bf16[8,4,8,4224]{3,2,1,0:T(8,128)(2,1)S(1)} async-done(((bf16[8,4,8,4224]{3,2,1,0:T(8,128)(2,1)}), bf16[8,4,8,4224]{3,2,1,0:T(8,128)(2,1)S(1)}, u32[]{:S(2)}, u32[]{:S(2)}) %all-to-all-start.3) | async-done | bytes 2162720 | tf_op jit(solution)/shard_map/all_to_all | solution.py:488
  141.1 0.0 copy-start
  141.1 1.3 copy-done
  142.4 7.1 %in_order.3.refs_0_ = bf16[256,3840]{1,0:T(8,128)(2,1)} custom-call(s32[3]{0:T(128)} %fusion.starts_ref, s32[1,4224]{1,0:T(1,128)} %constant_dynamic-slice_fusion.1.ids_ref, s32[1,3840]{1,0:T(1,128)} %broadcast_in_dim.9.wanted_ref, bf16[256,4224]{1,0:T(8,128)(2,1)} %bitcast.15), custom_call_target="tpu_custom_call" | custom-call | flops 1 | bytes 1 | tf_op jit(solution)/shard_map/in_order/pallas_call | solution.py:409
  149.5 0.0 all-gather.4.cloned.1.call-done.refs_1_
  149.5 7.9 %product.1 = f32[2,256,3840]{2,1,0:T(8,128)} custom-call(bf16[512,512]{1,0:T(8,128)(2,1)} %left_side.1.left_ref, bf16[256,3840]{1,0:T(8,128)(2,1)} %in_order.3.refs_0_, bf16[256,3840]{1,0:T(8,128)(2,1)} %all-gather.4.cloned.1.call-done.refs_1_), custom_call_target="tpu_custom_call" | custom-call | flops 1 | bytes 1 | tf_op jit(solution)/shard_map/product/pallas_call | solution.py:439
  (7 shorter events, 0.1 us)
Async XLA Ops:
  6.5 103.7 %all-gather.6.cloned.1.call-start = ((), (), s32[]{:S(2)}) async-start(), calls=%async_computation.5 | async-start | bytes 2703360 | tf_op jit(solution)/shard_map/all_gather | solution.py:473
  63.2 25.7 %copy-start.2 = (bf16[4,8,384]{2,1,0:T(8,128)(2,1)S(1)}, bf16[4,8,384]{2,1,0:T(8,128)(2,1)}, u32[]{:S(2)}) copy-start(bf16[4,8,384]{2,1,0:T(8,128)(2,1)} %get-tuple-element.22) | copy-start | bytes 73732
  68.1 20.8 %copy-start.3 = (bf16[4,8,384]{2,1,0:T(8,128)(2,1)S(1)}, bf16[4,8,384]{2,1,0:T(8,128)(2,1)}, u32[]{:S(2)}) copy-start(bf16[4,8,384]{2,1,0:T(8,128)(2,1)} %get-tuple-element.26) | copy-start | bytes 73732
  68.1 15.2 %all-to-all-start = ((bf16[8,8,4224]{2,1,0:T(8,128)(2,1)}), bf16[8,8,4224]{2,1,0:T(8,128)(2,1)S(1)}, u32[]{:S(2)}, u32[]{:S(2)}) async-start(bf16[8,8,4224]{2,1,0:T(8,128)(2,1)} %get-tuple-element.27), calls=%async_computation | async-start | bytes 1081344 | tf_op jit(solution)/shard_map/all_to_all | solution.py:475
  73.4 76.1 %all-gather.4.cloned.1.call-start = ((), (), s32[]{:S(2)}) async-start(), calls=%async_computation.4 | async-start | bytes 2457600 | tf_op jit(solution)/shard_map/all_gather | solution.py:477
  83.3 0.8 copy-start.1
  110.2 30.9 %all-to-all-start.3 = ((bf16[8,4,8,4224]{3,2,1,0:T(8,128)(2,1)}), bf16[8,4,8,4224]{3,2,1,0:T(8,128)(2,1)S(1)}, u32[]{:S(2)}, u32[]{:S(2)}) async-start(bf16[8,4,8,4224]{3,2,1,0:T(8,128)(2,1)} %bitcast.16), calls=%async_computation.3 | async-start | bytes 4325376 | tf_op jit(solution)/shard_map/all_to_all | solution.py:488
  141.1 1.3 copy-start
Sparse Core Ops, SparseCore 0:
  37.8 49.5 all-gather.5
  89.0 42.9 all-gather.3

commit v5 on v4

--- a/solution.py
+++ b/solution.py
@@ -201,8 +201,8 @@
     step = planes * KEEP
 
     def first_axis(block):
-        rows = slice(block * planes * points, (block + 1) * planes * points)
-        wave = val_ref[0, block * planes : (block + 1) * planes].reshape(planes * points, LANES).astype(jnp.float32)
+        rows = pl.ds(pl.multiple_of(block * planes * points, planes * points), planes * points)
+        wave = val_ref[0, pl.ds(block * planes, planes)].reshape(planes * points, LANES).astype(jnp.float32)
         other = pltpu.roll(wave, HALF, 1)
         density = jnp.where(low_lanes, wave, other) * cond_a[rows, :] + jnp.where(low_lanes, other, wave) * cond_b[rows, :]
         high, low = split_parts(density)
@@ -210,51 +210,58 @@
         for pair in range(planes // 2):
             both = field[pair * 2 * points : (pair + 1) * 2 * points].T
             high, low = split_parts(stack_complex(both, low_lanes))
-            at = slice((block * planes + pair * 2) * KEEP, (block * planes + pair * 2 + 2) * KEEP)
+            at = pl.ds(pl.multiple_of((block * planes + pair * 2) * KEEP, 2 * KEEP), 2 * KEEP)
             middle[at, :LANES] = high
             middle[at, LANES:] = low
 
     def second_axis(block):
-        rows = slice(block * step, (block + 1) * step)
+        rows = pl.ds(pl.multiple_of(block * step, step), step)
         turned[rows, :] = apply_table(middle[rows, :], table)
 
-    for block in range(points // planes):
-        first_axis(block)
-        if block:
-            second_axis(block - 1)
-    second_axis(points // planes - 1)
-
-    for pair in range(KEEP // 2):
-        both = jnp.concatenate(
-            [turned[pl.ds(2 * pair, points, stride=KEEP), :], turned[pl.ds(2 * pair + 1, points, stride=KEEP), :]], 0
-        ).T
-        high, low = split_parts(stack_complex(both, low_lanes))
-        at = slice(2 * pair * KEEP, (2 * pair + 2) * KEEP)
-        last[at, :LANES] = high
-        last[at, LANES:] = low
+    blocks = points // planes
+
+    @pl.loop(0, blocks // 2)
+    def _(turn):
+        for part in range(2):
+            second_axis((2 * turn - 2 + part + blocks) % blocks)
+        for part in range(2):
+            first_axis(2 * turn + part)
+
+    @pl.loop(blocks - 2, blocks)
+    def _(block):
+        second_axis(block)
+
+    @pl.loop(0, KEEP // 8)
+    def _(turn):
+        for part in range(4):
+            pair = turn * 4 + part
+            both = jnp.concatenate(
+                [turned[pl.ds(2 * pair, points, stride=KEEP), :], turned[pl.ds(2 * pair + 1, points, stride=KEEP), :]], 0
+            ).T
+            high, low = split_parts(stack_complex(both, low_lanes))
+            at = pl.ds(pl.multiple_of(pair * 2 * KEEP, 2 * KEEP), 2 * KEEP)
+            last[at, :LANES] = high
+            last[at, LANES:] = low
 
     pairs = val_energy_ref.shape[0] * cond_energy_ref.shape[0]
     gap = cond_energy_ref[owner_ref[0]] - val_energy_ref[first_band + band]
     weight = -2.0 / (math.sqrt(pairs) * jnp.full((1, LANES), gap, jnp.float32))
-    slab_first, slab_last = slab_tiles(plan)
-    for begin in range(0, depth // LANES, 5):
-        end = min(begin + 5, depth // LANES)
-        field = apply_table(last[begin * LANES : end * LANES, :], table)
-        for tile in range(begin, end):
-            turn = field[(tile - begin) * LANES : (tile - begin + 1) * LANES].T
+
+    @pl.loop(0, depth // (2 * LANES))
+    def _(turn):
+        field = apply_table(last[pl.ds(pl.multiple_of(turn * 2 * LANES, 2 * LANES), 2 * LANES), :], table)
+        for half in range(2):
+            turn_lanes = pl.ds(pl.multiple_of(turn * 2 * LANES, 2 * LANES) + half * LANES, LANES)
+            spectrum = field[half * LANES : (half + 1) * LANES].T
             for part in range(2):
-                value = turn[part * HALF : part * HALF + ROWS_K]
-                plain_ref[part, 0, :, tile * LANES : (tile + 1) * LANES] = value.astype(jnp.bfloat16)
-                if slab_first <= tile < slab_last:
-                    lanes = slice((tile - slab_first) * LANES, (tile - slab_first + 1) * LANES)
-                    weighted_ref[part, 0, :, lanes] = (weight * value).astype(jnp.bfloat16)
+                value = spectrum[part * HALF : part * HALF + ROWS_K]
+                plain_ref[part, 0, :, turn_lanes] = value.astype(jnp.bfloat16)
+                weighted_ref[part, 0, :, turn_lanes] = (weight * value).astype(jnp.bfloat16)
 
 
 def spectra(plan, val_wave, cond_wave, energies, first_band, count):
     points = val_wave.shape[1]
-    depth = round_up(KEEP * KEEP, LANES)
-    slab_first, slab_last = slab_tiles(plan)
-    slab_depth = (slab_last - slab_first) * LANES
+    depth = round_up(KEEP * KEEP, 2 * LANES)
     grid_rows = points * points
     kernel = lambda *refs: spectrum_kernel(plan, points, first_band, *refs)
     return pl.pallas_call(
@@ -270,11 +277,11 @@
         ],
         out_specs=[
             pl.BlockSpec((2, 1, ROWS_K, depth), lambda v: (0, v, 0, 0)),
-            pl.BlockSpec((2, 1, ROWS_K, slab_depth), lambda v: (0, v, 0, 0)),
+            pl.BlockSpec((2, 1, ROWS_K, depth), lambda v: (0, v, 0, 0)),
         ],
         out_shape=[
             jax.ShapeDtypeStruct((2, count, ROWS_K, depth), jnp.bfloat16),
-            jax.ShapeDtypeStruct((2, count, ROWS_K, slab_depth), jnp.bfloat16),
+            jax.ShapeDtypeStruct((2, count, ROWS_K, depth), jnp.bfloat16),
         ],
         scratch_shapes=[
             pltpu.VMEM((grid_rows, LANES), jnp.float32),
@@ -289,26 +296,24 @@
     )(*energies, val_wave, cond_wave, jnp.asarray(dft_table(points)))
 
 
-def pack_kernel(plan, groups, place_ref, *refs):
-    plains, weighteds = refs[:groups], refs[groups : 2 * groups]
-    send_ref, slab_ref, sorter, plain_sorted, weighted_sorted = refs[2 * groups :]
+def pack_kernel(plan, place_ref, plain_ref, weighted_ref, *refs):
+    *slab_refs, send_ref, slab_ref, sorter, plain_sorted, weighted_sorted = refs
     depth, columns = sorter.shape
-    count = 2 * sum(plain.shape[1] for plain in plains)
+    count = 2 * plain_ref.shape[1]
     lane = lax.broadcasted_iota(jnp.int32, (1, LANES), 1)
     for begin in range(0, depth, LANES):
         at = lax.broadcasted_iota(jnp.int32, (LANES, columns), 0) + begin
         sorter[begin : begin + LANES, :] = jnp.where(at == place_ref[...], 1.0, 0.0).astype(jnp.bfloat16)
 
-    def sort_rows(parts, which, target):
-        rows = jnp.concatenate([part[n] for n in range(2) for part in parts], 0)
-        rows = rows.reshape(count * ROWS_K, rows.shape[2])
-        value = jnp.dot(rows, which, preferred_element_type=jnp.float32)
+    def sort_rows(rows, which, target):
+        value = jnp.dot(rows.reshape(count * ROWS_K, rows.shape[3]), which, preferred_element_type=jnp.float32)
         for tile in range(target.shape[0]):
             target[tile] = value[:, tile * LANES : (tile + 1) * LANES]
 
     slab_first, slab_last = slab_tiles(plan)
-    sort_rows(plains, sorter[...], plain_sorted)
-    sort_rows(weighteds, sorter[slab_first * LANES : slab_last * LANES, : weighted_sorted.shape[0] * LANES], weighted_sorted)
+    slab_places = slice(slab_first * LANES, slab_last * LANES)
+    sort_rows(plain_ref[...], sorter[...], plain_sorted)
+    sort_rows(weighted_ref[:, :, :, slab_places], sorter[slab_places, : weighted_sorted.shape[0] * LANES], weighted_sorted)
 
     def plain_at(index, tile):
         return plain_sorted[tile, pl.ds(index, count, stride=ROWS_K), :]
@@ -328,22 +333,28 @@
             slab_ref[block, :, tile * LANES : (tile + 1) * LANES] = value.astype(jnp.bfloat16)
 
         pack_pieces(bucket.pieces, plan["slab_lanes"], weighted_at, count, lane, keep_slab)
-
-
-def packed(plan, plains, weighteds):
-    depth = plains[0].shape[3]
-    count = 2 * sum(plain.shape[1] for plain in plains)
+    if slab_refs:
+        lanes = plan["slab_lanes"]
+        for part, ref in enumerate([*slab_refs, slab_ref]):
+            for row in range(len(plan["slabs"])):
+                at = plan["lanes"] + (part * len(plan["slabs"]) + row) * lanes
+                for block in range(len(plan["buckets"])):
+                    send_ref[block, :, at : at + lanes] = ref[row]
+
+
+def packed(plan, plain, weighted, slabs):
+    depth, count = plain.shape[3], 2 * plain.shape[1]
     columns = round_up(plan["column_place"].shape[0], 256)
     slab_columns = round_up(plan["slab_columns"], LANES)
     place = np.full((1, columns), -1, np.int32)
     place[0, : plan["column_place"].shape[0]] = plan["column_place"]
-    kernel = lambda *refs: pack_kernel(plan, len(plains), *refs)
     vmem = pl.BlockSpec(memory_space=pltpu.VMEM)
-    send_shape = (len(plan["buckets"]), count, plan["lanes"])
     slab_shape = (len(plan["slabs"]), count, plan["slab_lanes"])
+    riders = (len(slabs) + 1) * len(plan["slabs"]) * plan["slab_lanes"] if slabs else 0
+    send_shape = (len(plan["buckets"]), count, plan["lanes"] + riders)
     return pl.pallas_call(
-        kernel,
-        in_specs=[vmem] * (1 + 2 * len(plains)),
+        lambda *refs: pack_kernel(plan, *refs),
+        in_specs=[vmem] * (3 + len(slabs)),
         out_specs=[vmem] * 2,
         out_shape=[jax.ShapeDtypeStruct(send_shape, jnp.bfloat16), jax.ShapeDtypeStruct(slab_shape, jnp.bfloat16)],
         scratch_shapes=[
@@ -354,7 +365,7 @@
         compiler_params=pltpu.CompilerParams(vmem_limit_bytes=VMEM_BYTES),
         cost_estimate=pl.CostEstimate(flops=1, bytes_accessed=1, transcendentals=0),
         name="pack",
-    )(jnp.asarray(place), *plains, *weighteds)
+    )(jnp.asarray(place), plain, weighted, *slabs)
 
 
 def one_hot(ids_ref, begin, wanted):
@@ -363,12 +374,16 @@
     return jnp.where(ids == wanted, 1.0, 0.0).astype(jnp.bfloat16)
 
 
-def left_kernel(group, slab_ref, slab_ids_ref, slab_wanted_ref, left_ref):
+def left_kernel(slab_ref, slab_ids_ref, slab_wanted_ref, left_ref):
     rows = slab_wanted_ref.shape[1]
+    row_count, chunks, col_count, group, _ = slab_ref.shape
+    order = [(row, part, col) for part in range(chunks - 1) for col in range(col_count) for row in range(row_count)]
+    order += [(row, chunks - 1, col) for row in range(row_count) for col in range(col_count)]
+    slab = jnp.concatenate([slab_ref[place].astype(jnp.float32) for place in order], 0).astype(jnp.bfloat16)
     choice = jnp.concatenate(
         [one_hot(slab_ids_ref, begin, slab_wanted_ref[...]) for begin in range(0, slab_ids_ref.shape[1], LANES)], 0
     )
-    chosen = jnp.dot(slab_ref[...], choice, preferred_element_type=jnp.float32)
+    chosen = jnp.dot(slab, choice, preferred_element_type=jnp.float32)
     lane = lax.broadcasted_iota(jnp.int32, (1, LANES), 1)
     real_lanes = lane % group < group // 2
     for begin in range(0, chosen.shape[0], LANES):
@@ -379,13 +394,13 @@
         left_ref[rows:, begin : begin + LANES] = jnp.where(real_lanes, after, -before).astype(jnp.bfloat16)
 
 
-def left_side(group, slab, slab_ids, slab_wanted):
+def left_side(slab, slab_ids, slab_wanted):
     vmem = pl.BlockSpec(memory_space=pltpu.VMEM)
     return pl.pallas_call(
-        lambda *refs: left_kernel(group, *refs),
+        left_kernel,
         in_specs=[vmem] * 3,
         out_specs=vmem,
-        out_shape=jax.ShapeDtypeStruct((2 * slab_wanted.shape[1], slab.shape[0]), jnp.bfloat16),
+        out_shape=jax.ShapeDtypeStruct((2 * slab_wanted.shape[1], math.prod(slab.shape[:4])), jnp.bfloat16),
         compiler_params=pltpu.CompilerParams(vmem_limit_bytes=VMEM_BYTES),
         cost_estimate=pl.CostEstimate(flops=1, bytes_accessed=1, transcendentals=0),
         name="left_side",
@@ -466,23 +481,20 @@
     panels, slabs = [], []
     for part in range(CHUNKS):
         plain, weighted = spectra(plan, val_wave, cond_wave, energies, part * chunk, chunk)
-        send, slab = packed(plan, [plain], [weighted])
+        send, slab = packed(plan, plain, weighted, slabs if part == CHUNKS - 1 else [])
         slabs.append(slab)
         if part < CHUNKS - 1:
             send, cond_wave = lax.optimization_barrier((send, cond_wave))
             panels.append(lax.all_gather(send, "row", axis=1))
         else:
-            mine = lax.all_to_all(send, "col", split_axis=0, concat_axis=0, tiled=True).reshape(-1, plan["lanes"])
-            mine = put_in_order(plan, starts, ids, wanted, mine)
-            last = lax.all_gather(mine, "row", axis=0, tiled=True)
-    slab, _ = lax.optimization_barrier((jnp.stack(slabs, 1), mine))
+            mine = lax.all_to_all(send, "col", split_axis=0, concat_axis=0, tiled=True).reshape(-1, send.shape[2])
+            ordered_mine = put_in_order(plan, starts, ids, wanted, mine)
+            last = lax.all_gather(ordered_mine, "row", axis=0, tiled=True)
+    slab, _ = lax.optimization_barrier((mine[:, plan["lanes"] :], ordered_mine))
+    slab = slab.reshape(col_count, 2 * chunk, CHUNKS, row_count, plan["slab_lanes"]).transpose(3, 2, 0, 1, 4)
     slab = lax.all_to_all(slab, "row", split_axis=0, concat_axis=0, tiled=True)
-    slab = lax.all_to_all(jnp.broadcast_to(slab, (col_count, *slab.shape)), "col", split_axis=0, concat_axis=0)
     *panels, slab = lax.optimization_barrier((*panels, slab))
-    slab = [slab[:, :, part] for part in range(CHUNKS)]
-    slab[-1] = slab[-1].transpose(1, 0, 2, 3)
-    slab = jnp.stack([part.reshape(-1, plan["slab_lanes"]) for part in slab]).reshape(-1, plan["slab_lanes"])
-    left = left_side(2 * chunk, slab, slab_ids, slab_wanted)
+    left = left_side(slab, slab_ids, slab_wanted)
     ordered = []
     for panel in panels:
         panel = lax.all_to_all(panel, "col", split_axis=0, concat_axis=0, tiled=True)

time: 165 us -> 179 us (1.085)
  waiting for transfers between devices: 26.9 us -> 32.2 us
  Pallas kernels: 83.1 us -> 88.2 us
  starting transfers between devices: 8.97 us -> 11.8 us
    all_to_all x1, blocking collectives: 10.5 us -> 21.2 us  [on_device(): slab = lax.all_to_all(slab, 'row', split_axis=0, concat_axis=0, tiled=True)]
    all_to_all x1 -> x0, blocking collectives: 10.7 us -> none  [on_device(): lax.all_to_all(jnp.broadcast_to(slab, (col_count, *slab.shape)), 'col', s...]
    all_to_all x1, waiting for transfers between devices: 5.63 us -> 9.94 us  [on_device(): lax.all_to_all(send, 'col', split_axis=0, concat_axis=0, tiled=True)]
    pallas_call x2, Pallas kernels: 51.1 us -> 55.2 us  [spectra(): pl.pallas_call(kernel, grid=(count,), in_specs=[pl.BlockSpec(memory_space...]
    all_to_all x1, starting transfers between devices: 3.61 us -> 6.58 us  [on_device(): lax.all_to_all(panel, 'col', split_axis=0, concat_axis=0, tiled=True)]
where the time goes in v5:
time: 179 us; the launch traced here: 178 us
  Pallas kernels  88.2 us (49%)
  waiting for transfers between devices  32.2 us (18%)
  blocking collectives  21.2 us (12%)
  between operations  14.1 us (8%)
  starting transfers between devices  11.8 us (7%)
  local copies, waits for them, and re-layouts  10.4 us (6%)
    pallas_call x2, Pallas kernels, spectra(): pl.pallas_call(kernel, grid=(count,), in_specs=[pl.BlockSpec(memory_space...  55.2 us
    all_to_all x1, waiting for transfers between devices, on_device(): lax.all_to_all(panel, 'col', split_axis=0, concat_axis=0, tiled=True)  22.2 us
    all_to_all x1, blocking collectives, on_device(): slab = lax.all_to_all(slab, 'row', split_axis=0, concat_axis=0, tiled=True)  21.2 us
    pallas_call x2, Pallas kernels, put_in_order(): pl.pallas_call(order_kernel, grid=(PARTS,), in_specs=[pl.BlockSpec(memory...  11.9 us
    pallas_call x2, Pallas kernels, packed(): pl.pallas_call(lambda *refs: pack_kernel(plan, *refs), in_specs=[vmem] *...  10.7 us
    all_to_all x1, waiting for transfers between devices, on_device(): lax.all_to_all(send, 'col', split_axis=0, concat_axis=0, tiled=True)  9.94 us
    pallas_call x1, Pallas kernels, product(): pl.pallas_call(product_kernel, grid=(pl.cdiv(columns, block),), in_specs=...  7.88 us
    all_to_all x1, starting transfers between devices, on_device(): lax.all_to_all(panel, 'col', split_axis=0, concat_axis=0, tiled=True)  6.58 us
  transfers between devices with their start and end apart: 4, of which 2 were waited for; matrix products, arithmetic and copies ran while one was open for 5% of the time, Pallas kernels for 27%

profile of v5, /device:TPU:0, one launch (start us, length us, event | category | flops | bytes accessed | tf_op | source)
XLA Modules:
  0.0 177.9 jit_solution(4703419581364729558)
XLA Ops:
  6.5 0.0 all-gather.6.cloned.1.call-start
  7.2 27.6 %spectra.2 = (bf16[2,4,48,1792]{3,2,1,0:T(8,128)(2,1)}, bf16[2,4,48,1792]{3,2,1,0:T(8,128)(2,1)}) custom-call(s32[1]{0:T(128)S(6)} %copy.17.refs_0_, f32[32]{0:T(128)} %refs_1_.3, f32[8]{0:T(128)} %refs_2_.3, bf16[8,64,64,128]{3,2,1,0:T(8,128)(2,1)} %refs_3_.3, bf16[1,64,64,128]{3,2,1,0:T(8,128)(2,1)} %refs_4_.2, bf16[256,256]{1,0:T(8,128)(2,1)} %constant.37.clone.refs_5_), custom_call_target="tpu_custom_call" | custom-call | flops 4 | bytes 4 | tf_op jit(solution)/shard_map/spectra/pallas_call | solution.py:267
  34.8 5.2 %pack.2 = (bf16[8,8,4224]{2,1,0:T(8,128)(2,1)}, bf16[4,8,384]{2,1,0:T(8,128)(2,1)}) custom-call(s32[1,1280]{1,0:T(1,128)} %constant.38.clone.refs_0_, bf16[2,4,48,1792]{3,2,1,0:T(8,128)(2,1)} %get-tuple-element.17.refs_1_, bf16[2,4,48,1792]{3,2,1,0:T(8,128)(2,1)} %get-tuple-element.18.refs_2_), custom_call_target="tpu_custom_call" | custom-call | flops 1 | bytes 1 | tf_op jit(solution)/shard_map/pack/pallas_call | solution.py:355
  40.0 0.0 all-gather.6.cloned.1.call-update
  40.0 27.6 %spectra.3 = (bf16[2,4,48,1792]{3,2,1,0:T(8,128)(2,1)}, bf16[2,4,48,1792]{3,2,1,0:T(8,128)(2,1)}) custom-call(s32[1]{0:T(128)S(6)} %copy.17.refs_0_, f32[32]{0:T(128)} %refs_1_.3, f32[8]{0:T(128)} %refs_2_.3, bf16[8,64,64,128]{3,2,1,0:T(8,128)(2,1)} %refs_3_.3, bf16[1,64,64,128]{3,2,1,0:T(8,128)(2,1)} %refs_4_.2, bf16[256,256]{1,0:T(8,128)(2,1)} %constant.37.clone.refs_5_), custom_call_target="tpu_custom_call" | custom-call | flops 4 | bytes 4 | tf_op jit(solution)/shard_map/spectra/pallas_call | solution.py:267
  67.6 5.4 %pack.3 = (bf16[8,8,7296]{2,1,0:T(8,128)(2,1)}, bf16[4,8,384]{2,1,0:T(8,128)(2,1)}) custom-call(s32[1,1280]{1,0:T(1,128)} %constant.38.clone.refs_0_, bf16[2,4,48,1792]{3,2,1,0:T(8,128)(2,1)} %get-tuple-element.22.refs_1_, bf16[2,4,48,1792]{3,2,1,0:T(8,128)(2,1)} %get-tuple-element.23.refs_2_, bf16[4,8,384]{2,1,0:T(8,128)(2,1)} %get-tuple-element.24.refs_3_), custom_call_target="tpu_custom_call" | custom-call | flops 1 | bytes 1 | tf_op jit(solution)/shard_map/pack/pallas_call | solution.py:355
  73.1 5.1 %all-to-all-start = ((bf16[8,8,7296]{2,1,0:T(8,128)(2,1)}), bf16[8,8,7296]{2,1,0:T(8,128)(2,1)S(1)}, u32[]{:S(2)}, u32[]{:S(2)}) async-start(bf16[8,8,7296]{2,1,0:T(8,128)(2,1)} %get-tuple-element.25), calls=%async_computation | async-start | bytes 1867776 | tf_op jit(solution)/shard_map/all_to_all | solution.py:490
  78.2 0.0 all-gather.4.cloned.1.call-start
  78.2 0.8 dynamic_slice.18
  79.0 0.6 broadcast_in_dim.6.wanted_ref
  79.7 1.3 fusion.starts_ref
  80.9 1.5 constant_dynamic-slice_fusion.1.ids_ref
  82.4 9.9 %all-to-all-done = bf16[8,8,7296]{2,1,0:T(8,128)(2,1)S(1)} async-done(((bf16[8,8,7296]{2,1,0:T(8,128)(2,1)}), bf16[8,8,7296]{2,1,0:T(8,128)(2,1)S(1)}, u32[]{:S(2)}, u32[]{:S(2)}) %all-to-all-start) | async-done | bytes 933920 | tf_op jit(solution)/shard_map/all_to_all | solution.py:490
  92.4 0.0 copy-start.1
  92.4 0.9 copy-done.1
  93.3 4.8 %in_order.2 = bf16[64,3840]{1,0:T(8,128)(2,1)} custom-call(s32[3]{0:T(128)} %fusion.starts_ref, s32[1,4224]{1,0:T(1,128)} %constant_dynamic-slice_fusion.1.ids_ref, s32[1,3840]{1,0:T(1,128)} %broadcast_in_dim.6.wanted_ref, bf16[64,7296]{1,0:T(8,128)(2,1)} %bitcast.10), custom_call_target="tpu_custom_call" | custom-call | flops 1 | bytes 1 | tf_op jit(solution)/shard_map/in_order/pallas_call | solution.py:424
  98.1 0.0 all-gather.4.cloned.1.call-update
  98.2 1.0 slice.4
  99.2 0.3 reshape.10
  99.5 21.2 %all_to_all.15.slab_ref = bf16[4,2,8,8,384]{4,3,2,1,0:T(8,128)(2,1)} all-to-all(bf16[4,2,8,8,384]{4,3,2,1,0:T(8,128)(2,1)S(1)} %bitcast.13), channel_id=1, replica_groups=mesh['row'=4,'col'=8] {'row'}, dimensions={0} | all-to-all | bytes 786432 | tf_op jit(solution)/shard_map/all_to_all | solution.py:495
  120.8 0.0 all-gather.6.cloned.1.call-done
  120.8 6.6 %all-to-all-start.2 = ((bf16[8,4,8,4224]{3,2,1,0:T(8,128)(2,1)}), bf16[8,4,8,4224]{3,2,1,0:T(8,128)(2,1)S(1)}, u32[]{:S(2)}, u32[]{:S(2)}) async-start(bf16[8,4,8,4224]{3,2,1,0:T(8,128)(2,1)} %bitcast.12), calls=%async_computation.2 | async-start | bytes 4325376 | tf_op jit(solution)/shard_map/all_to_all | solution.py:500
  127.3 1.3 dynamic_slice.20
  128.6 1.3 constant_dynamic-slice_fusion.slab_ids_ref
  129.9 2.6 %left_side.1.left_ref = bf16[512,512]{1,0:T(8,128)(2,1)} custom-call(bf16[4,2,8,8,384]{4,3,2,1,0:T(8,128)(2,1)} %all_to_all.15.slab_ref, s32[1,384]{1,0:T(1,128)} %constant_dynamic-slice_fusion.slab_ids_ref, s32[1,256]{1,0:T(1,128)} %bitcast.14), custom_call_target="tpu_custom_call" | custom-call | flops 1 | bytes 1 | tf_op jit(solution)/shard_map/left_side/pallas_call | solution.py:399
  132.5 22.2 %all-to-all-done.2 = bf16[8,4,8,4224]{3,2,1,0:T(8,128)(2,1)S(1)} async-done(((bf16[8,4,8,4224]{3,2,1,0:T(8,128)(2,1)}), bf16[8,4,8,4224]{3,2,1,0:T(8,128)(2,1)S(1)}, u32[]{:S(2)}, u32[]{:S(2)}) %all-to-all-start.2) | async-done | bytes 2162720 | tf_op jit(solution)/shard_map/all_to_all | solution.py:500
  154.7 0.0 copy-start
  154.7 1.3 copy-done
  156.0 7.1 %in_order.3.refs_0_ = bf16[256,3840]{1,0:T(8,128)(2,1)} custom-call(s32[3]{0:T(128)} %fusion.starts_ref, s32[1,4224]{1,0:T(1,128)} %constant_dynamic-slice_fusion.1.ids_ref, s32[1,3840]{1,0:T(1,128)} %broadcast_in_dim.6.wanted_ref, bf16[256,4224]{1,0:T(8,128)(2,1)} %bitcast.9), custom_call_target="tpu_custom_call" | custom-call | flops 1 | bytes 1 | tf_op jit(solution)/shard_map/in_order/pallas_call | solution.py:424
  163.1 0.0 all-gather.4.cloned.1.call-done.refs_1_
  163.1 7.9 %product.1 = f32[2,256,3840]{2,1,0:T(8,128)} custom-call(bf16[512,512]{1,0:T(8,128)(2,1)} %left_side.1.left_ref, bf16[256,3840]{1,0:T(8,128)(2,1)} %in_order.3.refs_0_, bf16[256,3840]{1,0:T(8,128)(2,1)} %all-gather.4.cloned.1.call-done.refs_1_), custom_call_target="tpu_custom_call" | custom-call | flops 1 | bytes 1 | tf_op jit(solution)/shard_map/product/pallas_call | solution.py:454
  (1 shorter events, 0.0 us)
Async XLA Ops:
  6.5 114.2 %all-gather.6.cloned.1.call-start = ((), (), s32[]{:S(2)}) async-start(), calls=%async_computation.4 | async-start | bytes 2703360 | tf_op jit(solution)/shard_map/all_gather | solution.py:488
  73.1 19.3 %all-to-all-start = ((bf16[8,8,7296]{2,1,0:T(8,128)(2,1)}), bf16[8,8,7296]{2,1,0:T(8,128)(2,1)S(1)}, u32[]{:S(2)}, u32[]{:S(2)}) async-start(bf16[8,8,7296]{2,1,0:T(8,128)(2,1)} %get-tuple-element.25), calls=%async_computation | async-start | bytes 1867776 | tf_op jit(solution)/shard_map/all_to_all | solution.py:490
  78.2 84.9 %all-gather.4.cloned.1.call-start = ((), (), s32[]{:S(2)}) async-start(), calls=%async_computation.3 | async-start | bytes 2457600 | tf_op jit(solution)/shard_map/all_gather | solution.py:492
  92.4 0.9 copy-start.1
  120.8 33.9 %all-to-all-start.2 = ((bf16[8,4,8,4224]{3,2,1,0:T(8,128)(2,1)}), bf16[8,4,8,4224]{3,2,1,0:T(8,128)(2,1)S(1)}, u32[]{:S(2)}, u32[]{:S(2)}) async-start(bf16[8,4,8,4224]{3,2,1,0:T(8,128)(2,1)} %bitcast.12), calls=%async_computation.2 | async-start | bytes 4325376 | tf_op jit(solution)/shard_map/all_to_all | solution.py:500
  154.7 1.3 copy-start
Sparse Core Ops, SparseCore 0:
  40.1 49.9 all-gather.5
  98.3 47.1 all-gather.3

commit v6 on v3

--- a/solution.py
+++ b/solution.py
@@ -16,7 +16,6 @@
 ROWS_K = 48
 ORIGIN = KEEP // 2
 PARTS = 3
-CHUNKS = 2
 
 
 def round_up(value, step):
@@ -222,11 +221,11 @@
     first_axis(1)
 
     @pl.loop(1, points // planes // 2)
-    def _(block):
+    def _(turn):
         for part in range(2):
-            second_axis(2 * block - 2 + part)
+            second_axis(2 * turn - 2 + part)
         for part in range(2):
-            first_axis(2 * block + part)
+            first_axis(2 * turn + part)
 
     second_axis(points // planes - 2)
     second_axis(points // planes - 1)
@@ -399,7 +398,8 @@
     )(slab, slab_ids, slab_wanted)
 
 
-def in_order(start, panel_ref, ids_ref, wanted_ref, hot):
+def in_order(starts_ref, ids_ref, wanted_ref, panel_ref, hot):
+    start = pl.multiple_of(starts_ref[pl.program_id(0)], LANES)
     wanted = wanted_ref[...]
     window = hot.shape[0]
     for begin in range(0, window, LANES):
@@ -408,22 +408,18 @@
 
 
 def order_kernel(starts_ref, ids_ref, wanted_ref, panel_ref, out_ref, hot):
-    start = pl.multiple_of(starts_ref[pl.program_id(0)], LANES)
-    out_ref[...] = in_order(start, panel_ref, ids_ref, wanted_ref, hot)
-
-
-def product_kernel(starts_ref, ids_ref, wanted_ref, panel_ref, left_ref, *refs):
-    *ordered, out_ref, hot = refs
+    out_ref[...] = in_order(starts_ref, ids_ref, wanted_ref, panel_ref, hot)
+
+
+def product_kernel(starts_ref, ids_ref, wanted_ref, panel_ref, left_ref, last_ref, out_ref, hot):
     rows = out_ref.shape[1]
-    start = pl.multiple_of(starts_ref[pl.program_id(0)], LANES)
-    last = in_order(start, panel_ref, ids_ref, wanted_ref, hot)
-    right = jnp.concatenate([part[...] for part in ordered] + [last], 0)
+    right = jnp.concatenate([in_order(starts_ref, ids_ref, wanted_ref, panel_ref, hot), last_ref[...]], 0)
     chi = jnp.dot(left_ref[...], right, preferred_element_type=jnp.float32)
     out_ref[0] = chi[:rows]
     out_ref[1] = chi[rows:]
 
 
-def put_in_order(plan, starts, ids, wanted, panel, left=None, ordered=()):
+def put_in_order(plan, starts, ids, wanted, panel, left=None, last=None):
     columns = wanted.shape[1]
     block = columns // PARTS
     whole = lambda array: pl.BlockSpec(array.shape, lambda n: (0,) * array.ndim)
@@ -439,8 +435,8 @@
         out_shape = jax.ShapeDtypeStruct((panel.shape[0], columns), jnp.bfloat16)
     else:
         rows = left.shape[0] // 2
-        in_specs += [whole(left)] + [pl.BlockSpec((part.shape[0], block), lambda n: (0, n)) for part in ordered]
-        operands += [left, *ordered]
+        in_specs += [whole(left), pl.BlockSpec((last.shape[0], block), lambda n: (0, n))]
+        operands += [left, last]
         out_spec = pl.BlockSpec((2, rows, block), lambda n: (0, 0, n))
         out_shape = jax.ShapeDtypeStruct((2, rows, columns), jnp.float32)
     return pl.pallas_call(
@@ -468,31 +464,29 @@
     slab_ids = lax.dynamic_slice(jnp.asarray(plan["slab_ids"]), (row, 0), (1, plan["slab_lanes"]))
     wanted = lax.dynamic_slice(grid_map, (col * width,), (width,))[None]
     slab_wanted = lax.dynamic_slice(grid_map, (row * ROWS_DEV,), (ROWS_DEV,))[None]
-    chunk = bands // CHUNKS
+    chunk = bands // 2
     energies = (band_owner, cond_energy, val_energy)
-    panels, slabs = [], []
-    for part in range(CHUNKS):
+    slabs = []
+    for part in range(2):
         plain, weighted = spectra(plan, val_wave, cond_wave, energies, part * chunk, chunk)
         send, slab = packed(plan, [plain], [weighted])
         slabs.append(slab)
-        if part < CHUNKS - 1:
+        if part == 0:
             send, cond_wave = lax.optimization_barrier((send, cond_wave))
-            panels.append(lax.all_gather(send, "row", axis=1))
+            early = lax.all_gather(send, "row", axis=1)
         else:
-            mine = lax.all_to_all(send, "col", split_axis=0, concat_axis=0, tiled=True)
-            panels.append(lax.all_gather(mine, "row", axis=0, tiled=True).reshape(-1, plan["lanes"]))
-    *early, slab, _ = lax.optimization_barrier((*panels[:-1], jnp.stack(slabs, 1), mine))
-    for part, panel in enumerate(early):
-        panel = lax.all_to_all(panel, "col", split_axis=0, concat_axis=0, tiled=True)
-        panels[part] = panel.reshape(-1, plan["lanes"])
+            mine = lax.all_to_all(send, "col", split_axis=0, concat_axis=0, tiled=True).reshape(-1, plan["lanes"])
+            mine = put_in_order(plan, starts, ids, wanted, mine)
+            last = lax.all_gather(mine, "row", axis=0, tiled=True)
+    slab, _ = lax.optimization_barrier((jnp.stack(slabs, 1), mine))
     slab = lax.all_to_all(slab, "row", split_axis=0, concat_axis=0, tiled=True)
     slab = lax.all_to_all(jnp.broadcast_to(slab, (col_count, *slab.shape)), "col", split_axis=0, concat_axis=0)
-    slab = [slab[:, :, part] for part in range(CHUNKS)]
-    slab[-1] = slab[-1].transpose(1, 0, 2, 3)
+    early, slab = lax.optimization_barrier((early, slab))
+    slab = [slab[:, :, 0], slab[:, :, 1].transpose(1, 0, 2, 3)]
     slab = jnp.stack([part.reshape(-1, plan["slab_lanes"]) for part in slab]).reshape(-1, plan["slab_lanes"])
     left = left_side(2 * chunk, slab, slab_ids, slab_wanted)
-    ordered = [put_in_order(plan, starts, ids, wanted, panel) for panel in panels[:-1]]
-    return put_in_order(plan, starts, ids, wanted, panels[-1], left, ordered)
+    early = lax.all_to_all(early, "col", split_axis=0, concat_axis=0, tiled=True).reshape(-1, plan["lanes"])
+    return put_in_order(plan, starts, ids, wanted, early, left, last)
 
 
 def solution(mesh):

time: 158 us -> 147 us (0.930)
  blocking collectives: 35 us -> 21.1 us
  starting transfers between devices: 3.83 us -> 9.11 us
  Pallas kernels: 67.6 us -> 65.2 us
    all_to_all x1 -> x0, blocking collectives: 15.2 us -> none  [on_device(): mine = lax.all_to_all(send, 'col', split_axis=0, concat_axis=0, tiled=True)]
    all_to_all x1 -> x2, waiting for transfers between devices: 16.8 us -> 8.6 us  [the longest x1 5.63 us: on_device(): lax.all_to_all(send, 'col', split_axis=0, concat_axis=0, tiled=True)]
    all_gather x2, waiting for transfers between devices: 9.95 us -> 18.1 us  [the longest x1 18.1 us: on_device(): last = lax.all_gather(mine, 'row', axis=0, tiled=True)]
    all_to_all x1 -> x2, starting transfers between devices: 3.79 us -> 9.07 us  [the longest x1 5.29 us: on_device(): lax.all_to_all(send, 'col', split_axis=0, concat_axis=0, tiled=True)]
    pallas_call x2, Pallas kernels: 17.1 us -> 14.6 us  [put_in_order(): pl.pallas_call(order_kernel if left is None else product_kernel, grid=(PA...]
    all_to_all x1, blocking collectives: 8.05 us -> 10.4 us  [on_device(): slab = lax.all_to_all(slab, 'row', split_axis=0, concat_axis=0, tiled=True)]
  transfers between devices with their start and end apart: 3 -> 4, of which waited for: 2 -> 3; matrix products, arithmetic and copies ran while one was open for 5% -> 5% of each run, Pallas kernels for 21% -> 21%
where the time goes in v6:
time: 147 us; the launch traced here: 146 us
  Pallas kernels  65.2 us (44%)
  waiting for transfers between devices  26.7 us (18%)
  blocking collectives  21.1 us (14%)
  between operations  14.1 us (10%)
  starting transfers between devices  9.11 us (6%)
  local copies, waits for them, and re-layouts  9.11 us (6%)
    pallas_call x2, Pallas kernels, spectra(): pl.pallas_call(kernel, grid=(count,), in_specs=[pl.BlockSpec(memory_space...  38.2 us
    all_gather x1, waiting for transfers between devices, on_device(): last = lax.all_gather(mine, 'row', axis=0, tiled=True)  18.1 us
    pallas_call x2, Pallas kernels, put_in_order(): pl.pallas_call(order_kernel if left is None else product_kernel, grid=(PA...  14.6 us
    all_to_all x1, blocking collectives, on_device(): lax.all_to_all(jnp.broadcast_to(slab, (col_count, *slab.shape)), 'col', s...  10.7 us
    all_to_all x1, blocking collectives, on_device(): slab = lax.all_to_all(slab, 'row', split_axis=0, concat_axis=0, tiled=True)  10.4 us
    pallas_call x2, Pallas kernels, packed(): pl.pallas_call(kernel, in_specs=[vmem] * (1 + 2 * len(plains)), out_specs...  9.81 us
    all_to_all x1, waiting for transfers between devices, on_device(): lax.all_to_all(send, 'col', split_axis=0, concat_axis=0, tiled=True)  5.63 us
    all_to_all x1, starting transfers between devices, on_device(): lax.all_to_all(send, 'col', split_axis=0, concat_axis=0, tiled=True)  5.29 us
  transfers between devices with their start and end apart: 4, of which 3 were waited for; matrix products, arithmetic and copies ran while one was open for 5% of the time, Pallas kernels for 21%

profile of v6, /device:TPU:0, one launch (start us, length us, event | category | flops | bytes accessed | tf_op | source)
XLA Modules:
  0.0 146.2 jit_solution(12859938737416197424)
XLA Ops:
  6.5 0.0 all-gather.6.cloned.1.call-start
  7.2 19.1 %spectra.2 = (bf16[2,4,48,1664]{3,2,1,0:T(8,128)(2,1)}, bf16[2,4,48,640]{3,2,1,0:T(8,128)(2,1)}) custom-call(s32[1]{0:T(128)S(6)} %copy.20.refs_0_, f32[32]{0:T(128)} %refs_1_.3, f32[8]{0:T(128)} %refs_2_.3, bf16[8,64,64,128]{3,2,1,0:T(8,128)(2,1)} %refs_3_.3, bf16[1,64,64,128]{3,2,1,0:T(8,128)(2,1)} %refs_4_.2, bf16[256,256]{1,0:T(8,128)(2,1)} %constant.37.clone.refs_5_), custom_call_target="tpu_custom_call" | custom-call | flops 4 | bytes 4 | tf_op jit(solution)/shard_map/spectra/pallas_call | solution.py:266
  26.3 4.9 %pack.2 = (bf16[8,8,4224]{2,1,0:T(8,128)(2,1)}, bf16[4,8,384]{2,1,0:T(8,128)(2,1)}) custom-call(s32[1,1280]{1,0:T(1,128)} %constant.38.clone.refs_0_, bf16[2,4,48,1664]{3,2,1,0:T(8,128)(2,1)} %get-tuple-element.18.refs_1_, bf16[2,4,48,640]{3,2,1,0:T(8,128)(2,1)} %get-tuple-element.19.refs_2_), custom_call_target="tpu_custom_call" | custom-call | flops 1 | bytes 1 | tf_op jit(solution)/shard_map/pack/pallas_call | solution.py:350
  31.2 0.0 all-gather.6.cloned.1.call-update
  31.2 19.1 %spectra.3 = (bf16[2,4,48,1664]{3,2,1,0:T(8,128)(2,1)}, bf16[2,4,48,640]{3,2,1,0:T(8,128)(2,1)}) custom-call(s32[1]{0:T(128)S(6)} %copy.20.refs_0_, f32[32]{0:T(128)} %refs_1_.3, f32[8]{0:T(128)} %refs_2_.3, bf16[8,64,64,128]{3,2,1,0:T(8,128)(2,1)} %refs_3_.3, bf16[1,64,64,128]{3,2,1,0:T(8,128)(2,1)} %refs_4_.2, bf16[256,256]{1,0:T(8,128)(2,1)} %constant.37.clone.refs_5_), custom_call_target="tpu_custom_call" | custom-call | flops 4 | bytes 4 | tf_op jit(solution)/shard_map/spectra/pallas_call | solution.py:266
  50.3 0.0 copy-start.2
  50.3 4.9 %pack.3 = (bf16[8,8,4224]{2,1,0:T(8,128)(2,1)}, bf16[4,8,384]{2,1,0:T(8,128)(2,1)}) custom-call(s32[1,1280]{1,0:T(1,128)} %constant.38.clone.refs_0_, bf16[2,4,48,1664]{3,2,1,0:T(8,128)(2,1)} %get-tuple-element.24.refs_1_, bf16[2,4,48,640]{3,2,1,0:T(8,128)(2,1)} %get-tuple-element.25.refs_2_), custom_call_target="tpu_custom_call" | custom-call | flops 1 | bytes 1 | tf_op jit(solution)/shard_map/pack/pallas_call | solution.py:350
  55.2 0.0 copy-start.3
  55.2 5.3 %all-to-all-start = ((bf16[8,8,4224]{2,1,0:T(8,128)(2,1)}), bf16[8,8,4224]{2,1,0:T(8,128)(2,1)S(1)}, u32[]{:S(2)}, u32[]{:S(2)}) async-start(bf16[8,8,4224]{2,1,0:T(8,128)(2,1)} %get-tuple-element.27), calls=%async_computation | async-start | bytes 1081344 | tf_op jit(solution)/shard_map/all_to_all | solution.py:478
  60.5 0.0 all-gather.4.cloned.1.call-start
  60.6 0.8 dynamic_slice.18
  61.4 0.6 broadcast_in_dim.9.wanted_ref
  62.0 1.3 fusion.starts_ref
  63.3 1.5 %constant_dynamic-slice_fusion.1.ids_ref = s32[1,4224]{1,0:T(1,128)} fusion(s32[8,4224]{1,0:T(8,128)} %constant.35.clone, s32[]{:T(128)S(6)} %select_n.14), kind=kLoop, calls=%fused_computation.3 | loop fusion | bytes 33796 | tf_op jit(solution)/shard_map/dynamic_slice | solution.py:463
  64.8 5.6 %all-to-all-done = bf16[8,8,4224]{2,1,0:T(8,128)(2,1)S(1)} async-done(((bf16[8,8,4224]{2,1,0:T(8,128)(2,1)}), bf16[8,8,4224]{2,1,0:T(8,128)(2,1)S(1)}, u32[]{:S(2)}, u32[]{:S(2)}) %all-to-all-start) | async-done | bytes 540704 | tf_op jit(solution)/shard_map/all_to_all | solution.py:478
  70.5 0.0 copy-start.1
  70.5 0.8 copy-done.1
  71.3 4.7 %in_order.1 = bf16[64,3840]{1,0:T(8,128)(2,1)} custom-call(s32[3]{0:T(128)} %fusion.starts_ref, s32[1,4224]{1,0:T(1,128)} %constant_dynamic-slice_fusion.1.ids_ref, s32[1,3840]{1,0:T(1,128)} %broadcast_in_dim.9.wanted_ref, bf16[64,4224]{1,0:T(8,128)(2,1)} %bitcast.17), custom_call_target="tpu_custom_call" | custom-call | flops 1 | bytes 1 | tf_op jit(solution)/shard_map/in_order/pallas_call | solution.py:442
  76.0 0.0 all-gather.4.cloned.1.call-update
  76.0 0.0 copy-done.2
  76.0 0.0 copy-done.3
  76.0 10.4 %all_to_all.20 = bf16[4,2,8,384]{3,2,1,0:T(8,128)(2,1)S(1)} all-to-all(bf16[4,2,8,384]{3,2,1,0:T(8,128)(2,1)S(1)} %copy.17), channel_id=1, replica_groups=mesh['row'=4,'col'=8] {'row'}, dimensions={0} | all-to-all | bytes 98304 | tf_op jit(solution)/shard_map/all_to_all | solution.py:482
  86.5 10.7 %all_to_all.21 = bf16[8,4,2,8,384]{4,3,1,2,0:T(8,128)(2,1)S(1)} all-to-all(bf16[8,4,2,8,384]{4,3,1,2,0:T(8,128)(2,1)S(1)} %broadcast_in_dim.10), channel_id=1, replica_groups=mesh['row'=4,'col'=8] {'col'}, dimensions={0} | all-to-all | bytes 786432 | tf_op jit(solution)/shard_map/all_to_all | solution.py:483
  97.2 0.0 all-gather.6.cloned.1.call-done
  97.2 3.8 %all-to-all-start.3 = ((bf16[8,4,8,4224]{3,2,1,0:T(8,128)(2,1)}), bf16[8,4,8,4224]{3,2,1,0:T(8,128)(2,1)S(1)}, u32[]{:S(2)}, u32[]{:S(2)}) async-start(bf16[8,4,8,4224]{3,2,1,0:T(8,128)(2,1)} %bitcast.16), calls=%async_computation.3 | async-start | bytes 4325376 | tf_op jit(solution)/shard_map/all_to_all | solution.py:488
  101.0 1.3 dynamic_slice.20
  102.3 1.2 constant_dynamic-slice_fusion.refs_1_
  103.7 0.8 pad_maximum_fusion
  104.5 2.6 %left_side.1.left_ref = bf16[512,512]{1,0:T(8,128)(2,1)} custom-call(bf16[512,384]{1,0:T(8,128)(2,1)} %bitcast.18, s32[1,384]{1,0:T(1,128)} %constant_dynamic-slice_fusion.refs_1_, s32[1,256]{1,0:T(1,128)} %bitcast.23), custom_call_target="tpu_custom_call" | custom-call | flops 1 | bytes 1 | tf_op jit(solution)/shard_map/left_side/pallas_call | solution.py:390
  107.0 18.1 %all-gather.4.cloned.1.call-done.last_ref = bf16[256,3840]{1,0:T(8,128)(2,1)} async-done(((bf16[64,3840]{1,0:T(8,128)(2,1)}), bf16[256,3840]{1,0:T(8,128)(2,1)}) %all-gather.4.cloned.1.call-update) | async-done | bytes 1966096 | tf_op jit(solution)/shard_map/all_gather | solution.py:480
  125.1 3.0 %all-to-all-done.3 = bf16[8,4,8,4224]{3,2,1,0:T(8,128)(2,1)S(1)} async-done(((bf16[8,4,8,4224]{3,2,1,0:T(8,128)(2,1)}), bf16[8,4,8,4224]{3,2,1,0:T(8,128)(2,1)S(1)}, u32[]{:S(2)}, u32[]{:S(2)}) %all-to-all-start.3) | async-done | bytes 2162720 | tf_op jit(solution)/shard_map/all_to_all | solution.py:488
  128.1 0.0 copy-start
  128.1 1.4 copy-done
  129.4 9.9 %product.1 = f32[2,256,3840]{2,1,0:T(8,128)} custom-call(s32[3]{0:T(128)} %fusion.starts_ref, s32[1,4224]{1,0:T(1,128)} %constant_dynamic-slice_fusion.1.ids_ref, s32[1,3840]{1,0:T(1,128)} %broadcast_in_dim.9.wanted_ref, bf16[256,4224]{1,0:T(8,128)(2,1)} %bitcast.15, bf16[512,512]{1,0:T(8,128)(2,1)} %left_side.1.left_ref, ...), custom_call_target="tpu_custom_call" | custom-call | flops 1 | bytes 1 | tf_op jit(solution)/shard_map/product/pallas_call | solution.py:442
  (7 shorter events, 0.1 us)
Async XLA Ops:
  6.5 90.7 %all-gather.6.cloned.1.call-start = ((), (), s32[]{:S(2)}) async-start(), calls=%async_computation.5 | async-start | bytes 2703360 | tf_op jit(solution)/shard_map/all_gather | solution.py:476
  50.3 25.6 %copy-start.2 = (bf16[4,8,384]{2,1,0:T(8,128)(2,1)S(1)}, bf16[4,8,384]{2,1,0:T(8,128)(2,1)}, u32[]{:S(2)}) copy-start(bf16[4,8,384]{2,1,0:T(8,128)(2,1)} %get-tuple-element.22) | copy-start | bytes 73732
  55.2 20.7 %copy-start.3 = (bf16[4,8,384]{2,1,0:T(8,128)(2,1)S(1)}, bf16[4,8,384]{2,1,0:T(8,128)(2,1)}, u32[]{:S(2)}) copy-start(bf16[4,8,384]{2,1,0:T(8,128)(2,1)} %get-tuple-element.26) | copy-start | bytes 73732
  55.2 15.2 %all-to-all-start = ((bf16[8,8,4224]{2,1,0:T(8,128)(2,1)}), bf16[8,8,4224]{2,1,0:T(8,128)(2,1)S(1)}, u32[]{:S(2)}, u32[]{:S(2)}) async-start(bf16[8,8,4224]{2,1,0:T(8,128)(2,1)} %get-tuple-element.27), calls=%async_computation | async-start | bytes 1081344 | tf_op jit(solution)/shard_map/all_to_all | solution.py:478
  60.5 64.6 %all-gather.4.cloned.1.call-start = ((), (), s32[]{:S(2)}) async-start(), calls=%async_computation.4 | async-start | bytes 2457600 | tf_op jit(solution)/shard_map/all_gather | solution.py:480
  70.5 0.8 copy-start.1
  97.2 30.9 %all-to-all-start.3 = ((bf16[8,4,8,4224]{3,2,1,0:T(8,128)(2,1)}), bf16[8,4,8,4224]{3,2,1,0:T(8,128)(2,1)S(1)}, u32[]{:S(2)}, u32[]{:S(2)}) async-start(bf16[8,4,8,4224]{3,2,1,0:T(8,128)(2,1)} %bitcast.16), calls=%async_computation.3 | async-start | bytes 4325376 | tf_op jit(solution)/shard_map/all_to_all | solution.py:488
  128.1 1.4 copy-start
Sparse Core Ops, SparseCore 0:
  31.3 49.8 all-gather.5
  82.8 42.2 all-gather.3

commit v7 on v6

--- a/solution.py
+++ b/solution.py
@@ -15,6 +15,7 @@
 KEEP = 40
 ROWS_K = 48
 ORIGIN = KEEP // 2
+PARITY_LANES = 896
 PARTS = 3
 
 
@@ -36,6 +37,10 @@
     order = np.argsort(length, kind="stable")
     order = order[length[order] <= top]
     return first.reshape(-1)[order], second.reshape(-1)[order], length[order]
+
+
+def column_place(index_2, index_3):
+    return index_3 % 2 * PARITY_LANES + index_3 // 2 * KEEP + index_2
 
 
 class Bucket:
@@ -114,23 +119,31 @@
         starts=np.minimum(windows[..., 0], lanes - window).astype(np.int32),
         ids=np.stack([bucket.ids(column_2, column_3, points, lanes) for bucket in buckets]),
         slab_ids=np.stack([bucket.ids(column_2, column_3, points, slab_lanes) for bucket in slabs]),
-        column_place=((column_3 + ORIGIN) * KEEP + column_2 + ORIGIN).astype(np.int32),
+        column_place=column_place(column_2 + ORIGIN, column_3 + ORIGIN).astype(np.int32),
     )
 
 
-def dft_table(points):
+def dft_tables(points):
     n = np.arange(points)
     freq = np.arange(KEEP) - ORIGIN
     angle = (n[:, None] * freq[None, :] % points) * (2.0 * np.pi / points)
     cosine, sine = np.cos(angle), np.sin(angle)
-    table = np.zeros((2 * HALF, 2 * HALF))
-    table[:points, :KEEP] = cosine
-    table[HALF : HALF + points, :KEEP] = sine
-    table[:points, HALF : HALF + KEEP] = -sine
-    table[HALF : HALF + points, HALF : HALF + KEEP] = cosine
-    high = table.astype(jnp.bfloat16)
-    low = (table - high.astype(np.float64)).astype(jnp.bfloat16)
-    return np.block([[high, low], [high, np.zeros_like(low)]])
+    table = np.zeros((2, points, 2, 2, 2, HALF))
+    for item in range(2):
+        table[0, :, item, item, 0, :KEEP] = cosine
+        table[1, :, item, item, 0, :KEEP] = sine
+        table[0, :, item, item, 1, :KEEP] = -sine
+        table[1, :, item, item, 1, :KEEP] = cosine
+    table = table.reshape(2, points, 2, 4 * HALF)
+    halves = table.reshape(2, points // 2, 2, 2, 4 * HALF).transpose(0, 3, 2, 1, 4)
+    orders = [table.transpose(2, 0, 1, 3), table.transpose(0, 2, 1, 3), halves]
+    out = []
+    for order in orders:
+        order = order.reshape(4 * points, 4 * HALF)
+        high = order.astype(jnp.bfloat16)
+        low = (order - high.astype(np.float64)).astype(jnp.bfloat16)
+        out.append(np.concatenate([high, low]))
+    return np.stack(out)
 
 
 def split_parts(value):
@@ -139,16 +152,21 @@
     return high, low
 
 
-def apply_table(parts, table):
-    both = jnp.dot(parts, table, preferred_element_type=jnp.float32)
-    return both[:, :LANES] + both[:, LANES:]
-
-
-def stack_complex(turned, low_lanes):
-    real, imag = turned[:KEEP], turned[HALF : HALF + KEEP]
-    first = jnp.where(low_lanes, real, pltpu.roll(imag, HALF, 1))
-    second = jnp.where(low_lanes, pltpu.roll(real, HALF, 1), imag)
-    return jnp.concatenate([first, second], 0)
+def store_split(target, rows, blocks):
+    for part, block in enumerate(blocks):
+        high, low = split_parts(jnp.concatenate(block, 0))
+        target[rows, part * LANES : (part + 1) * LANES] = high
+        target[rows, (part + 2) * LANES : (part + 3) * LANES] = low
+
+
+def apply_table(stored, table):
+    high = table[: 2 * LANES]
+    both = jnp.concatenate([stored, stored[:, : 2 * LANES]], 1)
+    return jnp.dot(both, jnp.concatenate([high, high, table[2 * LANES :]], 0), preferred_element_type=jnp.float32)
+
+
+def parts_of(turned):
+    return turned[:KEEP], turned[HALF : HALF + KEEP]
 
 
 def pack_pieces(pieces, width, source, rows, lane, out):
@@ -169,18 +187,18 @@
 
 
 def slab_tiles(plan):
-    first = (ORIGIN - plan["slab_edge"]) * KEEP // LANES
-    last = round_up((ORIGIN + plan["slab_edge"] + 1) * KEEP, LANES) // LANES
-    return first, last
-
-
-def spectrum_kernel(plan, points, first_band, owner_ref, cond_energy_ref, val_energy_ref, val_ref, cond_ref, table_ref, plain_ref, weighted_ref,
-                    cond_a, cond_b, middle, turned, last):
+    first = (ORIGIN - plan["slab_edge"]) // 2 * KEEP // LANES
+    last = round_up(((ORIGIN + plan["slab_edge"]) // 2 + 1) * KEEP, LANES) // LANES
+    return [odd * PARITY_LANES // LANES + tile for odd in range(2) for tile in range(first, last)]
+
+
+def spectrum_kernel(plan, points, first_band, owner_ref, cond_energy_ref, val_energy_ref, val_ref, cond_ref, table_ref,
+                    plain_ref, weighted_ref, cond_a, cond_b, middle, turned, last):
     band = pl.program_id(0)
     planes = 8
+    pairs = planes // 2
     lane = lax.broadcasted_iota(jnp.int32, (1, LANES), 1)
     low_lanes = lane < HALF
-    depth = last.shape[0]
 
     @pl.when(band == 0)
     def _():
@@ -194,10 +212,7 @@
             cond_a[rows, :] = wave * scale
             cond_b[rows, :] = pltpu.roll(wave, HALF, 1) * sign
 
-        last[KEEP * KEEP :, :] = jnp.zeros((depth - KEEP * KEEP, 2 * LANES), jnp.bfloat16)
-
-    table = table_ref[...]
-    step = planes * KEEP
+        last[KEEP * KEEP // 2 :, :] = jnp.zeros((last.shape[0] - KEEP * KEEP // 2, 4 * LANES), jnp.bfloat16)
 
     def first_axis(block):
         rows = pl.ds(pl.multiple_of(block * planes * points, planes * points), planes * points)
@@ -205,17 +220,22 @@
         other = pltpu.roll(wave, HALF, 1)
         density = jnp.where(low_lanes, wave, other) * cond_a[rows, :] + jnp.where(low_lanes, other, wave) * cond_b[rows, :]
         high, low = split_parts(density)
-        field = apply_table(jnp.concatenate([high, low], 1), table)
-        for pair in range(planes // 2):
-            both = field[pair * 2 * points : (pair + 1) * 2 * points].T
-            high, low = split_parts(stack_complex(both, low_lanes))
-            at = pl.ds(pl.multiple_of((block * planes + pair * 2) * KEEP, 2 * KEEP), 2 * KEEP)
-            middle[at, :LANES] = high
-            middle[at, LANES:] = low
+        half = planes * points // 2
+        stored = jnp.concatenate([high[:half], high[half:], low[:half], low[half:]], 1)
+        field = apply_table(stored, table_ref[0])
+        for item in range(2):
+            both = [
+                parts_of(field[pair * 2 * points : (pair + 1) * 2 * points, item * LANES : (item + 1) * LANES].T)
+                for pair in range(pairs // 2)
+            ]
+            at = pl.ds(pl.multiple_of((block * pairs + item * pairs // 2) * KEEP, 2 * KEEP), 2 * KEEP)
+            store_split(middle, at, list(zip(*both)))
 
     def second_axis(block):
-        rows = pl.ds(pl.multiple_of(block * step, step), step)
-        turned[rows, :] = apply_table(middle[rows, :], table)
+        rows = pl.ds(pl.multiple_of(block * pairs * KEEP, pairs * KEEP), pairs * KEEP)
+        field = apply_table(middle[rows, :], table_ref[1])
+        for item in range(2):
+            turned[item, rows, :] = field[:, item * LANES : (item + 1) * LANES]
 
     first_axis(0)
     first_axis(1)
@@ -230,37 +250,40 @@
     second_axis(points // planes - 2)
     second_axis(points // planes - 1)
 
-    for pair in range(KEEP // 2):
-        both = jnp.concatenate(
-            [turned[pl.ds(2 * pair, points, stride=KEEP), :], turned[pl.ds(2 * pair + 1, points, stride=KEEP), :]], 0
-        ).T
-        high, low = split_parts(stack_complex(both, low_lanes))
-        at = slice(2 * pair * KEEP, (2 * pair + 2) * KEEP)
-        last[at, :LANES] = high
-        last[at, LANES:] = low
-
-    pairs = val_energy_ref.shape[0] * cond_energy_ref.shape[0]
+    for begin in range(0, KEEP, 4):
+        both = []
+        for pair in range(2):
+            items = [
+                turned[item, pl.ds(begin + 2 * pair + k3, points // 2, stride=KEEP), :]
+                for k3 in range(2)
+                for item in range(2)
+            ]
+            both.append(parts_of(jnp.concatenate(items, 0).T))
+        store_split(last, slice(begin // 2 * KEEP, (begin // 2 + 2) * KEEP), list(zip(*both)))
+
+    bands = val_energy_ref.shape[0] * cond_energy_ref.shape[0]
     gap = cond_energy_ref[owner_ref[0]] - val_energy_ref[first_band + band]
-    weight = -2.0 / (math.sqrt(pairs) * jnp.full((1, LANES), gap, jnp.float32))
-    slab_first, slab_last = slab_tiles(plan)
-    for begin in range(0, depth // LANES, 5):
-        end = min(begin + 5, depth // LANES)
-        field = apply_table(last[begin * LANES : end * LANES, :], table)
-        for tile in range(begin, end):
-            turn = field[(tile - begin) * LANES : (tile - begin + 1) * LANES].T
-            for part in range(2):
-                value = turn[part * HALF : part * HALF + ROWS_K]
-                plain_ref[part, 0, :, tile * LANES : (tile + 1) * LANES] = value.astype(jnp.bfloat16)
-                if slab_first <= tile < slab_last:
-                    lanes = slice((tile - slab_first) * LANES, (tile - slab_first + 1) * LANES)
-                    weighted_ref[part, 0, :, lanes] = (weight * value).astype(jnp.bfloat16)
+    weight = -2.0 / (math.sqrt(bands) * jnp.full((1, LANES), gap, jnp.float32))
+    slab = slab_tiles(plan)
+    tiles = PARITY_LANES // LANES
+    for begin, end in ((0, tiles // 2), (tiles // 2, tiles)):
+        field = apply_table(last[begin * LANES : end * LANES, :], table_ref[2])
+        for odd in range(2):
+            for row in range(begin, end):
+                tile = odd * tiles + row
+                turn = field[(row - begin) * LANES : (row - begin + 1) * LANES, odd * LANES : (odd + 1) * LANES].T
+                for part in range(2):
+                    value = turn[part * HALF : part * HALF + ROWS_K]
+                    plain_ref[part, 0, :, tile * LANES : (tile + 1) * LANES] = value.astype(jnp.bfloat16)
+                    if tile in slab:
+                        lanes = slice(slab.index(tile) * LANES, (slab.index(tile) + 1) * LANES)
+                        weighted_ref[part, 0, :, lanes] = (weight * value).astype(jnp.bfloat16)
 
 
 def spectra(plan, val_wave, cond_wave, energies, first_band, count):
     points = val_wave.shape[1]
-    depth = round_up(KEEP * KEEP, LANES)
-    slab_first, slab_last = slab_tiles(plan)
-    slab_depth = (slab_last - slab_first) * LANES
+    depth = 2 * PARITY_LANES
+    slab_depth = len(slab_tiles(plan)) * LANES
     grid_rows = points * points
     kernel = lambda *refs: spectrum_kernel(plan, points, first_band, *refs)
     return pl.pallas_call(
@@ -272,7 +295,7 @@
             pl.BlockSpec(memory_space=pltpu.SMEM),
             pl.BlockSpec((1, points, points, 2 * points), lambda v: (first_band + v, 0, 0, 0)),
             pl.BlockSpec((1, points, points, 2 * points), lambda v: (0, 0, 0, 0)),
-            pl.BlockSpec((4 * HALF, 4 * HALF), lambda v: (0, 0)),
+            pl.BlockSpec((3, 8 * points, 4 * HALF), lambda v: (0, 0, 0)),
         ],
         out_specs=[
             pl.BlockSpec((2, 1, ROWS_K, depth), lambda v: (0, v, 0, 0)),
@@ -285,14 +308,14 @@
         scratch_shapes=[
             pltpu.VMEM((grid_rows, LANES), jnp.float32),
             pltpu.VMEM((grid_rows, LANES), jnp.float32),
-            pltpu.VMEM((points * KEEP, 2 * LANES), jnp.bfloat16),
-            pltpu.VMEM((points * KEEP, LANES), jnp.float32),
-            pltpu.VMEM((depth, 2 * LANES), jnp.bfloat16),
+            pltpu.VMEM((points // 2 * KEEP, 4 * LANES), jnp.bfloat16),
+            pltpu.VMEM((2, points // 2 * KEEP, LANES), jnp.float32),
+            pltpu.VMEM((PARITY_LANES, 4 * LANES), jnp.bfloat16),
         ],
         compiler_params=pltpu.CompilerParams(vmem_limit_bytes=VMEM_BYTES, dimension_semantics=("arbitrary",)),
         cost_estimate=pl.CostEstimate(flops=count, bytes_accessed=count, transcendentals=0),
         name="spectra",
-    )(*energies, val_wave, cond_wave, jnp.asarray(dft_table(points)))
+    )(*energies, val_wave, cond_wave, jnp.asarray(dft_tables(points)))
 
 
 def pack_kernel(plan, groups, place_ref, *refs):
@@ -312,9 +335,9 @@
         for tile in range(target.shape[0]):
             target[tile] = value[:, tile * LANES : (tile + 1) * LANES]
 
-    slab_first, slab_last = slab_tiles(plan)
+    slab = [sorter[tile * LANES : (tile + 1) * LANES, : weighted_sorted.shape[0] * LANES] for tile in slab_tiles(plan)]
     sort_rows(plains, sorter[...], plain_sorted)
-    sort_rows(weighteds, sorter[slab_first * LANES : slab_last * LANES, : weighted_sorted.shape[0] * LANES], weighted_sorted)
+    sort_rows(weighteds, jnp.concatenate(slab, 0), weighted_sorted)
 
     def plain_at(index, tile):
         return plain_sorted[tile, pl.ds(index, count, stride=ROWS_K), :]

time: 147 us -> 147 us (level)
  no operation moved by 1% of the time
where the time goes in v7:
time: 147 us; the launch traced here: 146 us
  Pallas kernels  65.2 us (44%)
  waiting for transfers between devices  26.7 us (18%)
  blocking collectives  21.1 us (14%)
  between operations  14.1 us (10%)
  starting transfers between devices  9.11 us (6%)
  local copies, waits for them, and re-layouts  9.11 us (6%)
    pallas_call x2, Pallas kernels, spectra(): pl.pallas_call(kernel, grid=(count,), in_specs=[pl.BlockSpec(memory_space...  38.1 us
    all_gather x1, waiting for transfers between devices, on_device(): last = lax.all_gather(mine, 'row', axis=0, tiled=True)  18 us
    pallas_call x2, Pallas kernels, put_in_order(): pl.pallas_call(order_kernel if left is None else product_kernel, grid=(PA...  14.6 us
    all_to_all x1, blocking collectives, on_device(): lax.all_to_all(jnp.broadcast_to(slab, (col_count, *slab.shape)), 'col', s...  10.7 us
    all_to_all x1, blocking collectives, on_device(): slab = lax.all_to_all(slab, 'row', split_axis=0, concat_axis=0, tiled=True)  10.4 us
    pallas_call x2, Pallas kernels, packed(): pl.pallas_call(kernel, in_specs=[vmem] * (1 + 2 * len(plains)), out_specs...  9.99 us
    all_to_all x1, waiting for transfers between devices, on_device(): lax.all_to_all(send, 'col', split_axis=0, concat_axis=0, tiled=True)  5.63 us
    all_to_all x1, starting transfers between devices, on_device(): lax.all_to_all(send, 'col', split_axis=0, concat_axis=0, tiled=True)  5.28 us
  transfers between devices with their start and end apart: 4, of which 3 were waited for; matrix products, arithmetic and copies ran while one was open for 5% of the time, Pallas kernels for 21%

profile of v7, /device:TPU:0, one launch (start us, length us, event | category | flops | bytes accessed | tf_op | source)
XLA Modules:
  0.0 146.2 jit_solution(9772795022116487315)
XLA Ops:
  6.5 0.0 all-gather.6.cloned.1.call-start
  7.2 19.0 %spectra.2 = (bf16[2,4,48,1792]{3,2,1,0:T(8,128)(2,1)}, bf16[2,4,48,768]{3,2,1,0:T(8,128)(2,1)}) custom-call(s32[1]{0:T(128)S(6)} %copy.20.refs_0_, f32[32]{0:T(128)} %refs_1_.3, f32[8]{0:T(128)} %refs_2_.3, bf16[8,64,64,128]{3,2,1,0:T(8,128)(2,1)} %refs_3_.3, bf16[1,64,64,128]{3,2,1,0:T(8,128)(2,1)} %refs_4_.2, bf16[3,512,256]{2,1,0:T(8,128)(2,1)} %constant.37.clone.refs_5_), custom_call_target="tpu_custom_call" | custom-call | flops 4 | bytes 4 | tf_op jit(solution)/shard_map/spectra/pallas_call | solution.py:289
  26.2 5.0 %pack.2 = (bf16[8,8,4224]{2,1,0:T(8,128)(2,1)}, bf16[4,8,384]{2,1,0:T(8,128)(2,1)}) custom-call(s32[1,1280]{1,0:T(1,128)} %constant.38.clone.refs_0_, bf16[2,4,48,1792]{3,2,1,0:T(8,128)(2,1)} %get-tuple-element.18.refs_1_, bf16[2,4,48,768]{3,2,1,0:T(8,128)(2,1)} %get-tuple-element.19.refs_2_), custom_call_target="tpu_custom_call" | custom-call | flops 1 | bytes 1 | tf_op jit(solution)/shard_map/pack/pallas_call | solution.py:373
  31.2 0.0 all-gather.6.cloned.1.call-update
  31.2 19.1 %spectra.3 = (bf16[2,4,48,1792]{3,2,1,0:T(8,128)(2,1)}, bf16[2,4,48,768]{3,2,1,0:T(8,128)(2,1)}) custom-call(s32[1]{0:T(128)S(6)} %copy.20.refs_0_, f32[32]{0:T(128)} %refs_1_.3, f32[8]{0:T(128)} %refs_2_.3, bf16[8,64,64,128]{3,2,1,0:T(8,128)(2,1)} %refs_3_.3, bf16[1,64,64,128]{3,2,1,0:T(8,128)(2,1)} %refs_4_.2, bf16[3,512,256]{2,1,0:T(8,128)(2,1)} %constant.37.clone.refs_5_), custom_call_target="tpu_custom_call" | custom-call | flops 4 | bytes 4 | tf_op jit(solution)/shard_map/spectra/pallas_call | solution.py:289
  50.3 0.0 copy-start.2
  50.3 5.0 %pack.3 = (bf16[8,8,4224]{2,1,0:T(8,128)(2,1)}, bf16[4,8,384]{2,1,0:T(8,128)(2,1)}) custom-call(s32[1,1280]{1,0:T(1,128)} %constant.38.clone.refs_0_, bf16[2,4,48,1792]{3,2,1,0:T(8,128)(2,1)} %get-tuple-element.24.refs_1_, bf16[2,4,48,768]{3,2,1,0:T(8,128)(2,1)} %get-tuple-element.25.refs_2_), custom_call_target="tpu_custom_call" | custom-call | flops 1 | bytes 1 | tf_op jit(solution)/shard_map/pack/pallas_call | solution.py:373
  55.3 0.0 copy-start.3
  55.3 5.3 %all-to-all-start = ((bf16[8,8,4224]{2,1,0:T(8,128)(2,1)}), bf16[8,8,4224]{2,1,0:T(8,128)(2,1)S(1)}, u32[]{:S(2)}, u32[]{:S(2)}) async-start(bf16[8,8,4224]{2,1,0:T(8,128)(2,1)} %get-tuple-element.27), calls=%async_computation | async-start | bytes 1081344 | tf_op jit(solution)/shard_map/all_to_all | solution.py:501
  60.6 0.0 all-gather.4.cloned.1.call-start
  60.6 0.8 dynamic_slice.18
  61.4 0.6 broadcast_in_dim.9.wanted_ref
  62.1 1.3 fusion.starts_ref
  63.3 1.5 %constant_dynamic-slice_fusion.1.ids_ref = s32[1,4224]{1,0:T(1,128)} fusion(s32[8,4224]{1,0:T(8,128)} %constant.35.clone, s32[]{:T(128)S(6)} %select_n.14), kind=kLoop, calls=%fused_computation.3 | loop fusion | bytes 33796 | tf_op jit(solution)/shard_map/dynamic_slice | solution.py:486
  64.9 5.6 %all-to-all-done = bf16[8,8,4224]{2,1,0:T(8,128)(2,1)S(1)} async-done(((bf16[8,8,4224]{2,1,0:T(8,128)(2,1)}), bf16[8,8,4224]{2,1,0:T(8,128)(2,1)S(1)}, u32[]{:S(2)}, u32[]{:S(2)}) %all-to-all-start) | async-done | bytes 540704 | tf_op jit(solution)/shard_map/all_to_all | solution.py:501
  70.5 0.0 copy-start.1
  70.5 0.8 copy-done.1
  71.3 4.7 %in_order.1 = bf16[64,3840]{1,0:T(8,128)(2,1)} custom-call(s32[3]{0:T(128)} %fusion.starts_ref, s32[1,4224]{1,0:T(1,128)} %constant_dynamic-slice_fusion.1.ids_ref, s32[1,3840]{1,0:T(1,128)} %broadcast_in_dim.9.wanted_ref, bf16[64,4224]{1,0:T(8,128)(2,1)} %bitcast.17), custom_call_target="tpu_custom_call" | custom-call | flops 1 | bytes 1 | tf_op jit(solution)/shard_map/in_order/pallas_call | solution.py:465
  76.0 0.0 all-gather.4.cloned.1.call-update
  76.0 0.0 copy-done.2
  76.0 0.0 copy-done.3
  76.1 10.4 %all_to_all.20 = bf16[4,2,8,384]{3,2,1,0:T(8,128)(2,1)S(1)} all-to-all(bf16[4,2,8,384]{3,2,1,0:T(8,128)(2,1)S(1)} %copy.17), channel_id=1, replica_groups=mesh['row'=4,'col'=8] {'row'}, dimensions={0} | all-to-all | bytes 98304 | tf_op jit(solution)/shard_map/all_to_all | solution.py:505
  86.5 10.7 %all_to_all.21 = bf16[8,4,2,8,384]{4,3,1,2,0:T(8,128)(2,1)S(1)} all-to-all(bf16[8,4,2,8,384]{4,3,1,2,0:T(8,128)(2,1)S(1)} %broadcast_in_dim.10), channel_id=1, replica_groups=mesh['row'=4,'col'=8] {'col'}, dimensions={0} | all-to-all | bytes 786432 | tf_op jit(solution)/shard_map/all_to_all | solution.py:506
  97.2 0.0 all-gather.6.cloned.1.call-done
  97.2 3.8 %all-to-all-start.3 = ((bf16[8,4,8,4224]{3,2,1,0:T(8,128)(2,1)}), bf16[8,4,8,4224]{3,2,1,0:T(8,128)(2,1)S(1)}, u32[]{:S(2)}, u32[]{:S(2)}) async-start(bf16[8,4,8,4224]{3,2,1,0:T(8,128)(2,1)} %bitcast.16), calls=%async_computation.3 | async-start | bytes 4325376 | tf_op jit(solution)/shard_map/all_to_all | solution.py:511
  101.0 1.3 dynamic_slice.20
  102.4 1.2 constant_dynamic-slice_fusion.refs_1_
  103.7 0.8 pad_maximum_fusion
  104.5 2.6 %left_side.1.left_ref = bf16[512,512]{1,0:T(8,128)(2,1)} custom-call(bf16[512,384]{1,0:T(8,128)(2,1)} %bitcast.18, s32[1,384]{1,0:T(1,128)} %constant_dynamic-slice_fusion.refs_1_, s32[1,256]{1,0:T(1,128)} %bitcast.23), custom_call_target="tpu_custom_call" | custom-call | flops 1 | bytes 1 | tf_op jit(solution)/shard_map/left_side/pallas_call | solution.py:413
  107.1 18.0 %all-gather.4.cloned.1.call-done.last_ref = bf16[256,3840]{1,0:T(8,128)(2,1)} async-done(((bf16[64,3840]{1,0:T(8,128)(2,1)}), bf16[256,3840]{1,0:T(8,128)(2,1)}) %all-gather.4.cloned.1.call-update) | async-done | bytes 1966096 | tf_op jit(solution)/shard_map/all_gather | solution.py:503
  125.1 3.0 %all-to-all-done.3 = bf16[8,4,8,4224]{3,2,1,0:T(8,128)(2,1)S(1)} async-done(((bf16[8,4,8,4224]{3,2,1,0:T(8,128)(2,1)}), bf16[8,4,8,4224]{3,2,1,0:T(8,128)(2,1)S(1)}, u32[]{:S(2)}, u32[]{:S(2)}) %all-to-all-start.3) | async-done | bytes 2162720 | tf_op jit(solution)/shard_map/all_to_all | solution.py:511
  128.1 0.0 copy-start
  128.1 1.4 copy-done
  129.5 9.9 %product.1 = f32[2,256,3840]{2,1,0:T(8,128)} custom-call(s32[3]{0:T(128)} %fusion.starts_ref, s32[1,4224]{1,0:T(1,128)} %constant_dynamic-slice_fusion.1.ids_ref, s32[1,3840]{1,0:T(1,128)} %broadcast_in_dim.9.wanted_ref, bf16[256,4224]{1,0:T(8,128)(2,1)} %bitcast.15, bf16[512,512]{1,0:T(8,128)(2,1)} %left_side.1.left_ref, ...), custom_call_target="tpu_custom_call" | custom-call | flops 1 | bytes 1 | tf_op jit(solution)/shard_map/product/pallas_call | solution.py:465
  (7 shorter events, 0.2 us)
Async XLA Ops:
  6.5 90.7 %all-gather.6.cloned.1.call-start = ((), (), s32[]{:S(2)}) async-start(), calls=%async_computation.5 | async-start | bytes 2703360 | tf_op jit(solution)/shard_map/all_gather | solution.py:499
  50.3 25.7 %copy-start.2 = (bf16[4,8,384]{2,1,0:T(8,128)(2,1)S(1)}, bf16[4,8,384]{2,1,0:T(8,128)(2,1)}, u32[]{:S(2)}) copy-start(bf16[4,8,384]{2,1,0:T(8,128)(2,1)} %get-tuple-element.22) | copy-start | bytes 73732
  55.3 20.7 %copy-start.3 = (bf16[4,8,384]{2,1,0:T(8,128)(2,1)S(1)}, bf16[4,8,384]{2,1,0:T(8,128)(2,1)}, u32[]{:S(2)}) copy-start(bf16[4,8,384]{2,1,0:T(8,128)(2,1)} %get-tuple-element.26) | copy-start | bytes 73732
  55.3 15.2 %all-to-all-start = ((bf16[8,8,4224]{2,1,0:T(8,128)(2,1)}), bf16[8,8,4224]{2,1,0:T(8,128)(2,1)S(1)}, u32[]{:S(2)}, u32[]{:S(2)}) async-start(bf16[8,8,4224]{2,1,0:T(8,128)(2,1)} %get-tuple-element.27), calls=%async_computation | async-start | bytes 1081344 | tf_op jit(solution)/shard_map/all_to_all | solution.py:501
  60.6 64.5 %all-gather.4.cloned.1.call-start = ((), (), s32[]{:S(2)}) async-start(), calls=%async_computation.4 | async-start | bytes 2457600 | tf_op jit(solution)/shard_map/all_gather | solution.py:503
  70.5 0.8 copy-start.1
  97.2 30.9 %all-to-all-start.3 = ((bf16[8,4,8,4224]{3,2,1,0:T(8,128)(2,1)}), bf16[8,4,8,4224]{3,2,1,0:T(8,128)(2,1)S(1)}, u32[]{:S(2)}, u32[]{:S(2)}) async-start(bf16[8,4,8,4224]{3,2,1,0:T(8,128)(2,1)} %bitcast.16), calls=%async_computation.3 | async-start | bytes 4325376 | tf_op jit(solution)/shard_map/all_to_all | solution.py:511
  128.1 1.4 copy-start
Sparse Core Ops, SparseCore 0:
  31.3 49.5 all-gather.5
  82.5 42.5 all-gather.3

commit v8 on v7

--- a/solution.py
+++ b/solution.py
@@ -128,22 +128,26 @@
     freq = np.arange(KEEP) - ORIGIN
     angle = (n[:, None] * freq[None, :] % points) * (2.0 * np.pi / points)
     cosine, sine = np.cos(angle), np.sin(angle)
-    table = np.zeros((2, points, 2, 2, 2, HALF))
+    one = np.zeros((2, points, 2, HALF))
+    one[0, :, 0, :KEEP] = cosine
+    one[1, :, 0, :KEEP] = sine
+    one[0, :, 1, :KEEP] = -sine
+    one[1, :, 1, :KEEP] = cosine
+    two = np.zeros((2, 2, points, 2, 2, HALF))
     for item in range(2):
-        table[0, :, item, item, 0, :KEEP] = cosine
-        table[1, :, item, item, 0, :KEEP] = sine
-        table[0, :, item, item, 1, :KEEP] = -sine
-        table[1, :, item, item, 1, :KEEP] = cosine
-    table = table.reshape(2, points, 2, 4 * HALF)
-    halves = table.reshape(2, points // 2, 2, 2, 4 * HALF).transpose(0, 3, 2, 1, 4)
-    orders = [table.transpose(2, 0, 1, 3), table.transpose(0, 2, 1, 3), halves]
-    out = []
-    for order in orders:
-        order = order.reshape(4 * points, 4 * HALF)
-        high = order.astype(jnp.bfloat16)
-        low = (order - high.astype(np.float64)).astype(jnp.bfloat16)
-        out.append(np.concatenate([high, low]))
-    return np.stack(out)
+        two[:, item, :, item] = one
+
+    def parts(table):
+        high = table.astype(jnp.bfloat16)
+        return high, (table - high.astype(np.float64)).astype(jnp.bfloat16)
+
+    high, low = parts(one[..., :KEEP].reshape(2 * points, 2 * KEEP).T)
+    first = np.concatenate([high, high, low], 1)
+    second = np.concatenate(parts(two.reshape(4 * points, 4 * HALF)), 0)
+    halves = two[..., :ROWS_K].reshape(2, 2, points // 2, 2, 4 * ROWS_K).transpose(0, 1, 3, 2, 4)
+    high, low = parts(halves.reshape(4 * points, 4 * ROWS_K).T)
+    third = np.concatenate([high, high, low], 1)
+    return [jnp.asarray(table) for table in (first, second, third)]
 
 
 def split_parts(value):
@@ -159,14 +163,12 @@
         target[rows, (part + 2) * LANES : (part + 3) * LANES] = low
 
 
-def apply_table(stored, table):
-    high = table[: 2 * LANES]
-    both = jnp.concatenate([stored, stored[:, : 2 * LANES]], 1)
-    return jnp.dot(both, jnp.concatenate([high, high, table[2 * LANES :]], 0), preferred_element_type=jnp.float32)
-
-
-def parts_of(turned):
-    return turned[:KEEP], turned[HALF : HALF + KEEP]
+def doubled(stored):
+    return jnp.concatenate([stored, stored[:, : stored.shape[1] // 2]], 1)
+
+
+def contract_last(table, stored):
+    return lax.dot_general(table, doubled(stored), (((1,), (1,)), ((), ())), preferred_element_type=jnp.float32)
 
 
 def pack_pieces(pieces, width, source, rows, lane, out):
@@ -192,8 +194,8 @@
     return [odd * PARITY_LANES // LANES + tile for odd in range(2) for tile in range(first, last)]
 
 
-def spectrum_kernel(plan, points, first_band, owner_ref, cond_energy_ref, val_energy_ref, val_ref, cond_ref, table_ref,
-                    plain_ref, weighted_ref, cond_a, cond_b, middle, turned, last):
+def spectrum_kernel(plan, points, first_band, owner_ref, cond_energy_ref, val_energy_ref, val_ref, cond_ref, first_ref,
+                    second_ref, third_ref, plain_ref, weighted_ref, cond_a, cond_b, middle, turned, last):
     band = pl.program_id(0)
     planes = 8
     pairs = planes // 2
@@ -220,20 +222,20 @@
         other = pltpu.roll(wave, HALF, 1)
         density = jnp.where(low_lanes, wave, other) * cond_a[rows, :] + jnp.where(low_lanes, other, wave) * cond_b[rows, :]
         high, low = split_parts(density)
-        half = planes * points // 2
-        stored = jnp.concatenate([high[:half], high[half:], low[:half], low[half:]], 1)
-        field = apply_table(stored, table_ref[0])
-        for item in range(2):
-            both = [
-                parts_of(field[pair * 2 * points : (pair + 1) * 2 * points, item * LANES : (item + 1) * LANES].T)
-                for pair in range(pairs // 2)
+        field = contract_last(first_ref[...], jnp.concatenate([high, low], 1))
+        for begin in range(0, pairs, 2):
+            blocks = [
+                [field[part * KEEP : (part + 1) * KEEP, pair * LANES : (pair + 1) * LANES] for pair in (begin, begin + 1)]
+                for part in range(2)
             ]
-            at = pl.ds(pl.multiple_of((block * pairs + item * pairs // 2) * KEEP, 2 * KEEP), 2 * KEEP)
-            store_split(middle, at, list(zip(*both)))
+            at = pl.ds(pl.multiple_of((block * pairs + begin) * KEEP, 2 * KEEP), 2 * KEEP)
+            store_split(middle, at, blocks)
 
     def second_axis(block):
         rows = pl.ds(pl.multiple_of(block * pairs * KEEP, pairs * KEEP), pairs * KEEP)
-        field = apply_table(middle[rows, :], table_ref[1])
+        high = second_ref[: 2 * LANES]
+        table = jnp.concatenate([high, high, second_ref[2 * LANES :]], 0)
+        field = jnp.dot(doubled(middle[rows, :]), table, preferred_element_type=jnp.float32)
         for item in range(2):
             turned[item, rows, :] = field[:, item * LANES : (item + 1) * LANES]
 
@@ -258,7 +260,8 @@
                 for k3 in range(2)
                 for item in range(2)
             ]
-            both.append(parts_of(jnp.concatenate(items, 0).T))
+            turn = jnp.concatenate(items, 0).T
+            both.append((turn[:KEEP], turn[HALF : HALF + KEEP]))
         store_split(last, slice(begin // 2 * KEEP, (begin // 2 + 2) * KEEP), list(zip(*both)))
 
     bands = val_energy_ref.shape[0] * cond_energy_ref.shape[0]
@@ -266,18 +269,16 @@
     weight = -2.0 / (math.sqrt(bands) * jnp.full((1, LANES), gap, jnp.float32))
     slab = slab_tiles(plan)
     tiles = PARITY_LANES // LANES
-    for begin, end in ((0, tiles // 2), (tiles // 2, tiles)):
-        field = apply_table(last[begin * LANES : end * LANES, :], table_ref[2])
-        for odd in range(2):
-            for row in range(begin, end):
-                tile = odd * tiles + row
-                turn = field[(row - begin) * LANES : (row - begin + 1) * LANES, odd * LANES : (odd + 1) * LANES].T
-                for part in range(2):
-                    value = turn[part * HALF : part * HALF + ROWS_K]
-                    plain_ref[part, 0, :, tile * LANES : (tile + 1) * LANES] = value.astype(jnp.bfloat16)
-                    if tile in slab:
-                        lanes = slice(slab.index(tile) * LANES, (slab.index(tile) + 1) * LANES)
-                        weighted_ref[part, 0, :, lanes] = (weight * value).astype(jnp.bfloat16)
+    field = contract_last(third_ref[...], last[...])
+    for odd in range(2):
+        for part in range(2):
+            at = (odd * 2 + part) * ROWS_K
+            value = field[at : at + ROWS_K]
+            plain_ref[part, 0, :, odd * PARITY_LANES : (odd + 1) * PARITY_LANES] = value.astype(jnp.bfloat16)
+            for place, tile in enumerate(slab):
+                if tile // tiles == odd:
+                    inside = value[:, tile % tiles * LANES : (tile % tiles + 1) * LANES]
+                    weighted_ref[part, 0, :, place * LANES : (place + 1) * LANES] = (weight * inside).astype(jnp.bfloat16)
 
 
 def spectra(plan, val_wave, cond_wave, energies, first_band, count):
@@ -285,6 +286,7 @@
     depth = 2 * PARITY_LANES
     slab_depth = len(slab_tiles(plan)) * LANES
     grid_rows = points * points
+    tables = dft_tables(points)
     kernel = lambda *refs: spectrum_kernel(plan, points, first_band, *refs)
     return pl.pallas_call(
         kernel,
@@ -295,7 +297,7 @@
             pl.BlockSpec(memory_space=pltpu.SMEM),
             pl.BlockSpec((1, points, points, 2 * points), lambda v: (first_band + v, 0, 0, 0)),
             pl.BlockSpec((1, points, points, 2 * points), lambda v: (0, 0, 0, 0)),
-            pl.BlockSpec((3, 8 * points, 4 * HALF), lambda v: (0, 0, 0)),
+            *[pl.BlockSpec(table.shape, lambda v: (0, 0)) for table in tables],
         ],
         out_specs=[
             pl.BlockSpec((2, 1, ROWS_K, depth), lambda v: (0, v, 0, 0)),
@@ -315,7 +317,7 @@
         compiler_params=pltpu.CompilerParams(vmem_limit_bytes=VMEM_BYTES, dimension_semantics=("arbitrary",)),
         cost_estimate=pl.CostEstimate(flops=count, bytes_accessed=count, transcendentals=0),
         name="spectra",
-    )(*energies, val_wave, cond_wave, jnp.asarray(dft_tables(points)))
+    )(*energies, val_wave, cond_wave, *tables)
 
 
 def pack_kernel(plan, groups, place_ref, *refs):

time: 147 us -> 142 us (0.966)
  Pallas kernels: 65.2 us -> 60.2 us
    pallas_call x2, Pallas kernels: 38.1 us -> 33.1 us  [spectra(): pl.pallas_call(kernel, grid=(count,), in_specs=[pl.BlockSpec(memory_space...]
    all_gather x1, waiting for transfers between devices: 18 us -> 21.5 us  [on_device(): last = lax.all_gather(mine, 'row', axis=0, tiled=True)]
    all_to_all x1, waiting for transfers between devices: 3.04 us -> 0.01 us  [on_device(): lax.all_to_all(early, 'col', split_axis=0, concat_axis=0, tiled=True)]
  transfers between devices with their start and end apart: 4 -> 4, of which waited for: 3 -> 2; matrix products, arithmetic and copies ran while one was open for 5% -> 5% of each run, Pallas kernels for 21% -> 20%
where the time goes in v8:
time: 142 us
  Pallas kernels  60.2 us (42%)
  waiting for transfers between devices  27.2 us (19%)
  blocking collectives  21.1 us (15%)
  between operations  14.1 us (10%)
  starting transfers between devices  9.13 us (6%)
  local copies, waits for them, and re-layouts  9.11 us (6%)
    pallas_call x2, Pallas kernels, spectra(): pl.pallas_call(kernel, grid=(count,), in_specs=[pl.BlockSpec(memory_space...  33.1 us
    all_gather x1, waiting for transfers between devices, on_device(): last = lax.all_gather(mine, 'row', axis=0, tiled=True)  21.5 us
    pallas_call x2, Pallas kernels, put_in_order(): pl.pallas_call(order_kernel if left is None else product_kernel, grid=(PA...  14.6 us
    all_to_all x1, blocking collectives, on_device(): lax.all_to_all(jnp.broadcast_to(slab, (col_count, *slab.shape)), 'col', s...  10.7 us
    all_to_all x1, blocking collectives, on_device(): slab = lax.all_to_all(slab, 'row', split_axis=0, concat_axis=0, tiled=True)  10.4 us
    pallas_call x2, Pallas kernels, packed(): pl.pallas_call(kernel, in_specs=[vmem] * (1 + 2 * len(plains)), out_specs...  9.98 us
    all_to_all x1, waiting for transfers between devices, on_device(): lax.all_to_all(send, 'col', split_axis=0, concat_axis=0, tiled=True)  5.63 us
    all_to_all x1, starting transfers between devices, on_device(): lax.all_to_all(send, 'col', split_axis=0, concat_axis=0, tiled=True)  5.31 us
  transfers between devices with their start and end apart: 4, of which 2 were waited for; matrix products, arithmetic and copies ran while one was open for 5% of the time, Pallas kernels for 20%

profile of v8, /device:TPU:0, one launch (start us, length us, event | category | flops | bytes accessed | tf_op | source)
XLA Modules:
  0.0 141.7 jit_solution(15567634823844774751)
XLA Ops:
  6.5 0.0 all-gather.6.cloned.1.call-start
  7.2 16.5 %spectra.2 = (bf16[2,4,48,1792]{3,2,1,0:T(8,128)(2,1)}, bf16[2,4,48,768]{3,2,1,0:T(8,128)(2,1)}) custom-call(s32[1]{0:T(128)S(6)} %copy.24.refs_0_, f32[32]{0:T(128)} %refs_1_.3, f32[8]{0:T(128)} %refs_2_.3, bf16[8,64,64,128]{3,2,1,0:T(8,128)(2,1)} %refs_3_.3, bf16[1,64,64,128]{3,2,1,0:T(8,128)(2,1)} %refs_4_.2, bf16[80,384]{1,0:T(8,128)(2,1)} %constant.41.clone.refs_5_, ...), custom_call_target="tpu_custom_call" | custom-call | flops 4 | bytes 4 | tf_op jit(solution)/shard_map/spectra/pallas_call | solution.py:291
  23.7 5.0 %pack.2 = (bf16[8,8,4224]{2,1,0:T(8,128)(2,1)}, bf16[4,8,384]{2,1,0:T(8,128)(2,1)}) custom-call(s32[1,1280]{1,0:T(1,128)} %constant.44.clone.refs_0_, bf16[2,4,48,1792]{3,2,1,0:T(8,128)(2,1)} %get-tuple-element.18.refs_1_, bf16[2,4,48,768]{3,2,1,0:T(8,128)(2,1)} %get-tuple-element.19.refs_2_), custom_call_target="tpu_custom_call" | custom-call | flops 1 | bytes 1 | tf_op jit(solution)/shard_map/pack/pallas_call | solution.py:375
  28.7 0.0 all-gather.6.cloned.1.call-update
  28.7 16.6 %spectra.3 = (bf16[2,4,48,1792]{3,2,1,0:T(8,128)(2,1)}, bf16[2,4,48,768]{3,2,1,0:T(8,128)(2,1)}) custom-call(s32[1]{0:T(128)S(6)} %copy.24.refs_0_, f32[32]{0:T(128)} %refs_1_.3, f32[8]{0:T(128)} %refs_2_.3, bf16[8,64,64,128]{3,2,1,0:T(8,128)(2,1)} %refs_3_.3, bf16[1,64,64,128]{3,2,1,0:T(8,128)(2,1)} %refs_4_.2, bf16[80,384]{1,0:T(8,128)(2,1)} %constant.41.clone.refs_5_, ...), custom_call_target="tpu_custom_call" | custom-call | flops 4 | bytes 4 | tf_op jit(solution)/shard_map/spectra/pallas_call | solution.py:291
  45.3 0.0 copy-start.2
  45.3 5.0 %pack.3 = (bf16[8,8,4224]{2,1,0:T(8,128)(2,1)}, bf16[4,8,384]{2,1,0:T(8,128)(2,1)}) custom-call(s32[1,1280]{1,0:T(1,128)} %constant.44.clone.refs_0_, bf16[2,4,48,1792]{3,2,1,0:T(8,128)(2,1)} %get-tuple-element.24.refs_1_, bf16[2,4,48,768]{3,2,1,0:T(8,128)(2,1)} %get-tuple-element.25.refs_2_), custom_call_target="tpu_custom_call" | custom-call | flops 1 | bytes 1 | tf_op jit(solution)/shard_map/pack/pallas_call | solution.py:375
  50.3 0.0 copy-start.3
  50.3 5.3 %all-to-all-start = ((bf16[8,8,4224]{2,1,0:T(8,128)(2,1)}), bf16[8,8,4224]{2,1,0:T(8,128)(2,1)S(1)}, u32[]{:S(2)}, u32[]{:S(2)}) async-start(bf16[8,8,4224]{2,1,0:T(8,128)(2,1)} %get-tuple-element.27), calls=%async_computation | async-start | bytes 1081344 | tf_op jit(solution)/shard_map/all_to_all | solution.py:503
  55.6 0.0 all-gather.4.cloned.1.call-start
  55.6 0.8 dynamic_slice.18
  56.5 0.6 broadcast_in_dim.9.wanted_ref
  57.1 1.3 fusion.starts_ref
  58.4 1.5 %constant_dynamic-slice_fusion.1.ids_ref = s32[1,4224]{1,0:T(1,128)} fusion(s32[8,4224]{1,0:T(8,128)} %constant.39.clone, s32[]{:T(128)S(6)} %select_n.14), kind=kLoop, calls=%fused_computation.3 | loop fusion | bytes 33796 | tf_op jit(solution)/shard_map/dynamic_slice | solution.py:488
  59.9 5.6 %all-to-all-done = bf16[8,8,4224]{2,1,0:T(8,128)(2,1)S(1)} async-done(((bf16[8,8,4224]{2,1,0:T(8,128)(2,1)}), bf16[8,8,4224]{2,1,0:T(8,128)(2,1)S(1)}, u32[]{:S(2)}, u32[]{:S(2)}) %all-to-all-start) | async-done | bytes 540704 | tf_op jit(solution)/shard_map/all_to_all | solution.py:503
  65.5 0.0 copy-start.1
  65.5 0.8 copy-done.1
  66.3 4.7 %in_order.1 = bf16[64,3840]{1,0:T(8,128)(2,1)} custom-call(s32[3]{0:T(128)} %fusion.starts_ref, s32[1,4224]{1,0:T(1,128)} %constant_dynamic-slice_fusion.1.ids_ref, s32[1,3840]{1,0:T(1,128)} %broadcast_in_dim.9.wanted_ref, bf16[64,4224]{1,0:T(8,128)(2,1)} %bitcast.17), custom_call_target="tpu_custom_call" | custom-call | flops 1 | bytes 1 | tf_op jit(solution)/shard_map/in_order/pallas_call | solution.py:467
  71.0 0.0 all-gather.4.cloned.1.call-update
  71.0 0.0 copy-done.2
  71.1 0.0 copy-done.3
  71.1 10.4 %all_to_all.20 = bf16[4,2,8,384]{3,2,1,0:T(8,128)(2,1)S(1)} all-to-all(bf16[4,2,8,384]{3,2,1,0:T(8,128)(2,1)S(1)} %copy.21), channel_id=1, replica_groups=mesh['row'=4,'col'=8] {'row'}, dimensions={0} | all-to-all | bytes 98304 | tf_op jit(solution)/shard_map/all_to_all | solution.py:507
  81.5 10.7 %all_to_all.21 = bf16[8,4,2,8,384]{4,3,1,2,0:T(8,128)(2,1)S(1)} all-to-all(bf16[8,4,2,8,384]{4,3,1,2,0:T(8,128)(2,1)S(1)} %broadcast_in_dim.10), channel_id=1, replica_groups=mesh['row'=4,'col'=8] {'col'}, dimensions={0} | all-to-all | bytes 786432 | tf_op jit(solution)/shard_map/all_to_all | solution.py:508
  92.2 0.0 all-gather.6.cloned.1.call-done
  92.2 3.8 %all-to-all-start.3 = ((bf16[8,4,8,4224]{3,2,1,0:T(8,128)(2,1)}), bf16[8,4,8,4224]{3,2,1,0:T(8,128)(2,1)S(1)}, u32[]{:S(2)}, u32[]{:S(2)}) async-start(bf16[8,4,8,4224]{3,2,1,0:T(8,128)(2,1)} %bitcast.16), calls=%async_computation.3 | async-start | bytes 4325376 | tf_op jit(solution)/shard_map/all_to_all | solution.py:513
  96.0 1.3 dynamic_slice.20
  97.4 1.2 constant_dynamic-slice_fusion.refs_1_
  98.7 0.8 pad_maximum_fusion
  99.5 2.6 %left_side.1.left_ref = bf16[512,512]{1,0:T(8,128)(2,1)} custom-call(bf16[512,384]{1,0:T(8,128)(2,1)} %bitcast.18, s32[1,384]{1,0:T(1,128)} %constant_dynamic-slice_fusion.refs_1_, s32[1,256]{1,0:T(1,128)} %bitcast.23), custom_call_target="tpu_custom_call" | custom-call | flops 1 | bytes 1 | tf_op jit(solution)/shard_map/left_side/pallas_call | solution.py:415
  102.1 21.5 %all-gather.4.cloned.1.call-done.last_ref = bf16[256,3840]{1,0:T(8,128)(2,1)} async-done(((bf16[64,3840]{1,0:T(8,128)(2,1)}), bf16[256,3840]{1,0:T(8,128)(2,1)}) %all-gather.4.cloned.1.call-update) | async-done | bytes 1966096 | tf_op jit(solution)/shard_map/all_gather | solution.py:505
  123.6 0.0 all-to-all-done.3
  123.6 0.0 copy-start
  123.6 1.4 copy-done
  124.9 9.9 %product.1 = f32[2,256,3840]{2,1,0:T(8,128)} custom-call(s32[3]{0:T(128)} %fusion.starts_ref, s32[1,4224]{1,0:T(1,128)} %constant_dynamic-slice_fusion.1.ids_ref, s32[1,3840]{1,0:T(1,128)} %broadcast_in_dim.9.wanted_ref, bf16[256,4224]{1,0:T(8,128)(2,1)} %bitcast.15, bf16[512,512]{1,0:T(8,128)(2,1)} %left_side.1.left_ref, ...), custom_call_target="tpu_custom_call" | custom-call | flops 1 | bytes 1 | tf_op jit(solution)/shard_map/product/pallas_call | solution.py:467
  (7 shorter events, 0.1 us)
Async XLA Ops:
  6.5 85.7 %all-gather.6.cloned.1.call-start = ((), (), s32[]{:S(2)}) async-start(), calls=%async_computation.5 | async-start | bytes 2703360 | tf_op jit(solution)/shard_map/all_gather | solution.py:501
  45.3 25.8 %copy-start.2 = (bf16[4,8,384]{2,1,0:T(8,128)(2,1)S(1)}, bf16[4,8,384]{2,1,0:T(8,128)(2,1)}, u32[]{:S(2)}) copy-start(bf16[4,8,384]{2,1,0:T(8,128)(2,1)} %get-tuple-element.22) | copy-start | bytes 73732
  50.3 20.8 %copy-start.3 = (bf16[4,8,384]{2,1,0:T(8,128)(2,1)S(1)}, bf16[4,8,384]{2,1,0:T(8,128)(2,1)}, u32[]{:S(2)}) copy-start(bf16[4,8,384]{2,1,0:T(8,128)(2,1)} %get-tuple-element.26) | copy-start | bytes 73732
  50.3 15.2 %all-to-all-start = ((bf16[8,8,4224]{2,1,0:T(8,128)(2,1)}), bf16[8,8,4224]{2,1,0:T(8,128)(2,1)S(1)}, u32[]{:S(2)}, u32[]{:S(2)}) async-start(bf16[8,8,4224]{2,1,0:T(8,128)(2,1)} %get-tuple-element.27), calls=%async_computation | async-start | bytes 1081344 | tf_op jit(solution)/shard_map/all_to_all | solution.py:503
  55.6 68.0 %all-gather.4.cloned.1.call-start = ((), (), s32[]{:S(2)}) async-start(), calls=%async_computation.4 | async-start | bytes 2457600 | tf_op jit(solution)/shard_map/all_gather | solution.py:505
  65.5 0.8 copy-start.1
  92.2 31.3 %all-to-all-start.3 = ((bf16[8,4,8,4224]{3,2,1,0:T(8,128)(2,1)}), bf16[8,4,8,4224]{3,2,1,0:T(8,128)(2,1)S(1)}, u32[]{:S(2)}, u32[]{:S(2)}) async-start(bf16[8,4,8,4224]{3,2,1,0:T(8,128)(2,1)} %bitcast.16), calls=%async_computation.3 | async-start | bytes 4325376 | tf_op jit(solution)/shard_map/all_to_all | solution.py:513
  123.6 1.4 copy-start
Sparse Core Ops, SparseCore 0:
  28.8 50.1 all-gather.5
  80.6 42.9 all-gather.3

commit v9 on v8

--- a/solution.py
+++ b/solution.py
@@ -423,58 +423,61 @@
     )(slab, slab_ids, slab_wanted)
 
 
-def in_order(starts_ref, ids_ref, wanted_ref, panel_ref, hot):
+def order_kernel(starts_ref, ids_ref, wanted_ref, panel_ref, out_ref, hot):
     start = pl.multiple_of(starts_ref[pl.program_id(0)], LANES)
     wanted = wanted_ref[...]
     window = hot.shape[0]
     for begin in range(0, window, LANES):
         hot[begin : begin + LANES, :] = one_hot(ids_ref, pl.multiple_of(start + begin, LANES), wanted)
-    return jnp.dot(panel_ref[:, pl.ds(start, window)], hot[...], preferred_element_type=jnp.float32).astype(jnp.bfloat16)
-
-
-def order_kernel(starts_ref, ids_ref, wanted_ref, panel_ref, out_ref, hot):
-    out_ref[...] = in_order(starts_ref, ids_ref, wanted_ref, panel_ref, hot)
-
-
-def product_kernel(starts_ref, ids_ref, wanted_ref, panel_ref, left_ref, last_ref, out_ref, hot):
+    ordered = jnp.dot(panel_ref[:, pl.ds(start, window)], hot[...], preferred_element_type=jnp.float32)
+    out_ref[...] = ordered.astype(jnp.bfloat16)
+
+
+def put_in_order(plan, starts, ids, wanted, panel):
+    columns = wanted.shape[1]
+    block = columns // PARTS
+    whole = lambda array: pl.BlockSpec(array.shape, lambda n: (0,) * array.ndim)
+    return pl.pallas_call(
+        order_kernel,
+        grid=(PARTS,),
+        in_specs=[
+            pl.BlockSpec(memory_space=pltpu.SMEM),
+            whole(ids),
+            pl.BlockSpec((1, block), lambda n: (0, n)),
+            whole(panel),
+        ],
+        out_specs=pl.BlockSpec((panel.shape[0], block), lambda n: (0, n)),
+        out_shape=jax.ShapeDtypeStruct((panel.shape[0], columns), jnp.bfloat16),
+        scratch_shapes=[pltpu.VMEM((plan["window"], block), jnp.bfloat16)],
+        compiler_params=pltpu.CompilerParams(vmem_limit_bytes=VMEM_BYTES, dimension_semantics=("arbitrary",)),
+        cost_estimate=pl.CostEstimate(flops=1, bytes_accessed=1, transcendentals=0),
+        name="in_order",
+    )(starts, ids, wanted, panel)
+
+
+def product_kernel(left_ref, *refs):
+    *ordered, out_ref = refs
     rows = out_ref.shape[1]
-    right = jnp.concatenate([in_order(starts_ref, ids_ref, wanted_ref, panel_ref, hot), last_ref[...]], 0)
+    right = jnp.concatenate([part[...] for part in ordered], 0)
     chi = jnp.dot(left_ref[...], right, preferred_element_type=jnp.float32)
     out_ref[0] = chi[:rows]
     out_ref[1] = chi[rows:]
 
 
-def put_in_order(plan, starts, ids, wanted, panel, left=None, last=None):
-    columns = wanted.shape[1]
-    block = columns // PARTS
-    whole = lambda array: pl.BlockSpec(array.shape, lambda n: (0,) * array.ndim)
-    in_specs = [
-        pl.BlockSpec(memory_space=pltpu.SMEM),
-        whole(ids),
-        pl.BlockSpec((1, block), lambda n: (0, n)),
-        whole(panel),
-    ]
-    operands = [starts, ids, wanted, panel]
-    if left is None:
-        out_spec = pl.BlockSpec((panel.shape[0], block), lambda n: (0, n))
-        out_shape = jax.ShapeDtypeStruct((panel.shape[0], columns), jnp.bfloat16)
-    else:
-        rows = left.shape[0] // 2
-        in_specs += [whole(left), pl.BlockSpec((last.shape[0], block), lambda n: (0, n))]
-        operands += [left, last]
-        out_spec = pl.BlockSpec((2, rows, block), lambda n: (0, 0, n))
-        out_shape = jax.ShapeDtypeStruct((2, rows, columns), jnp.float32)
+def product(left, ordered):
+    rows, columns = left.shape[0] // 2, ordered[0].shape[1]
+    block = columns // (2 * PARTS) // LANES * LANES
     return pl.pallas_call(
-        order_kernel if left is None else product_kernel,
-        grid=(PARTS,),
-        in_specs=in_specs,
-        out_specs=out_spec,
-        out_shape=out_shape,
-        scratch_shapes=[pltpu.VMEM((plan["window"], block), jnp.bfloat16)],
+        product_kernel,
+        grid=(pl.cdiv(columns, block),),
+        in_specs=[pl.BlockSpec(left.shape, lambda n: (0, 0))]
+        + [pl.BlockSpec((part.shape[0], block), lambda n: (0, n)) for part in ordered],
+        out_specs=pl.BlockSpec((2, rows, block), lambda n: (0, 0, n)),
+        out_shape=jax.ShapeDtypeStruct((2, rows, columns), jnp.float32),
         compiler_params=pltpu.CompilerParams(vmem_limit_bytes=VMEM_BYTES, dimension_semantics=("arbitrary",)),
         cost_estimate=pl.CostEstimate(flops=1, bytes_accessed=1, transcendentals=0),
-        name="in_order" if left is None else "product",
-    )(*operands)
+        name="product",
+    )(left, *ordered)
 
 
 def on_device(val_wave, cond_wave, val_energy, cond_energy, band_owner, grid_map):
@@ -498,20 +501,22 @@
         slabs.append(slab)
         if part == 0:
             send, cond_wave = lax.optimization_barrier((send, cond_wave))
-            early = lax.all_gather(send, "row", axis=1)
+            early = lax.all_gather(send, "row", axis=0)
         else:
             mine = lax.all_to_all(send, "col", split_axis=0, concat_axis=0, tiled=True).reshape(-1, plan["lanes"])
             mine = put_in_order(plan, starts, ids, wanted, mine)
             last = lax.all_gather(mine, "row", axis=0, tiled=True)
     slab, _ = lax.optimization_barrier((jnp.stack(slabs, 1), mine))
     slab = lax.all_to_all(slab, "row", split_axis=0, concat_axis=0, tiled=True)
+    early, slab = lax.optimization_barrier((early, slab))
+    early = lax.all_to_all(early, "col", split_axis=1, concat_axis=1, tiled=True)
+    early = early.transpose(1, 0, 2, 3).reshape(-1, plan["lanes"])
+    early, slab = lax.optimization_barrier((early, slab))
     slab = lax.all_to_all(jnp.broadcast_to(slab, (col_count, *slab.shape)), "col", split_axis=0, concat_axis=0)
-    early, slab = lax.optimization_barrier((early, slab))
     slab = [slab[:, :, 0], slab[:, :, 1].transpose(1, 0, 2, 3)]
     slab = jnp.stack([part.reshape(-1, plan["slab_lanes"]) for part in slab]).reshape(-1, plan["slab_lanes"])
     left = left_side(2 * chunk, slab, slab_ids, slab_wanted)
-    early = lax.all_to_all(early, "col", split_axis=0, concat_axis=0, tiled=True).reshape(-1, plan["lanes"])
-    return put_in_order(plan, starts, ids, wanted, early, left, last)
+    return product(left, [put_in_order(plan, starts, ids, wanted, early), last])
 
 
 def solution(mesh):

time: 142 us -> 147 us (1.035)
  waiting for transfers between devices: 27.2 us -> 5.72 us
  blocking collectives: 21.1 us -> 40.8 us
  Pallas kernels: 60.2 us -> 65.2 us
    all_gather x1, waiting for transfers between devices: 21.5 us -> 0.01 us  [on_device(): last = lax.all_gather(mine, 'row', axis=0, tiled=True)]
    all_to_all x1, blocking collectives: 10.7 us -> 30.5 us  [on_device(): lax.all_to_all(early, 'col', split_axis=1, concat_axis=1, tiled=True)]
    pallas_call x2 -> x3, Pallas kernels: 14.6 us -> 19.6 us  [the longest x2 11.7 us: put_in_order(): pl.pallas_call(order_kernel, grid=(PARTS,), in_specs=[pl.BlockSpec(memory...]
    optimization_barrier x1 -> x2, local copies, waits for them, and re-layouts: 0.04 us -> 1.76 us  [on_device(): early, slab = lax.optimization_barrier((early, slab))]
  transfers between devices with their start and end apart: 4 -> 4, of which waited for: 2 -> 1; matrix products, arithmetic and copies ran while one was open for 5% -> 7% of each run, Pallas kernels for 20% -> 25%
where the time goes in v9:
time: 147 us; the launch traced here: 146 us
  Pallas kernels  65.2 us (44%)
  blocking collectives  40.8 us (28%)
  between operations  14.1 us (10%)
  local copies, waits for them, and re-layouts  10.2 us (7%)
  starting transfers between devices  8.99 us (6%)
  waiting for transfers between devices  5.72 us (4%)
    pallas_call x2, Pallas kernels, spectra(): pl.pallas_call(kernel, grid=(count,), in_specs=[pl.BlockSpec(memory_space...  33.1 us
    all_to_all x1, blocking collectives, on_device(): lax.all_to_all(early, 'col', split_axis=1, concat_axis=1, tiled=True)  30.5 us
    pallas_call x2, Pallas kernels, put_in_order(): pl.pallas_call(order_kernel, grid=(PARTS,), in_specs=[pl.BlockSpec(memory...  11.7 us
    all_to_all x1, blocking collectives, on_device(): slab = lax.all_to_all(slab, 'row', split_axis=0, concat_axis=0, tiled=True)  10.4 us
    pallas_call x2, Pallas kernels, packed(): pl.pallas_call(kernel, in_specs=[vmem] * (1 + 2 * len(plains)), out_specs...  9.94 us
    pallas_call x1, Pallas kernels, product(): pl.pallas_call(product_kernel, grid=(pl.cdiv(columns, block),), in_specs=...  7.87 us
    all_to_all x1, waiting for transfers between devices, on_device(): lax.all_to_all(send, 'col', split_axis=0, concat_axis=0, tiled=True)  5.68 us
    all_to_all x1, starting transfers between devices, on_device(): lax.all_to_all(send, 'col', split_axis=0, concat_axis=0, tiled=True)  5.32 us
  transfers between devices with their start and end apart: 4, of which 1 were waited for; matrix products, arithmetic and copies ran while one was open for 7% of the time, Pallas kernels for 25%

profile of v9, /device:TPU:0, one launch (start us, length us, event | category | flops | bytes accessed | tf_op | source)
XLA Modules:
  0.0 145.9 jit_solution(361196583346272839)
XLA Ops:
  6.5 0.0 all-gather.6.cloned.1.call-start
  7.2 16.5 %spectra.2 = (bf16[2,4,48,1792]{3,2,1,0:T(8,128)(2,1)}, bf16[2,4,48,768]{3,2,1,0:T(8,128)(2,1)}) custom-call(s32[1]{0:T(128)S(6)} %copy.28.refs_0_, f32[32]{0:T(128)} %refs_1_.3, f32[8]{0:T(128)} %refs_2_.3, bf16[8,64,64,128]{3,2,1,0:T(8,128)(2,1)} %refs_3_.3, bf16[1,64,64,128]{3,2,1,0:T(8,128)(2,1)} %refs_4_.2, bf16[80,384]{1,0:T(8,128)(2,1)} %constant.41.clone.refs_5_, ...), custom_call_target="tpu_custom_call" | custom-call | flops 4 | bytes 4 | tf_op jit(solution)/shard_map/spectra/pallas_call | solution.py:291
  23.7 5.0 %pack.2 = (bf16[8,8,4224]{2,1,0:T(8,128)(2,1)}, bf16[4,8,384]{2,1,0:T(8,128)(2,1)}) custom-call(s32[1,1280]{1,0:T(1,128)} %constant.44.clone.refs_0_, bf16[2,4,48,1792]{3,2,1,0:T(8,128)(2,1)} %get-tuple-element.20.refs_1_, bf16[2,4,48,768]{3,2,1,0:T(8,128)(2,1)} %get-tuple-element.21.refs_2_), custom_call_target="tpu_custom_call" | custom-call | flops 1 | bytes 1 | tf_op jit(solution)/shard_map/pack/pallas_call | solution.py:375
  28.7 0.0 all-gather.6.cloned.1.call-update
  28.7 16.6 %spectra.3 = (bf16[2,4,48,1792]{3,2,1,0:T(8,128)(2,1)}, bf16[2,4,48,768]{3,2,1,0:T(8,128)(2,1)}) custom-call(s32[1]{0:T(128)S(6)} %copy.28.refs_0_, f32[32]{0:T(128)} %refs_1_.3, f32[8]{0:T(128)} %refs_2_.3, bf16[8,64,64,128]{3,2,1,0:T(8,128)(2,1)} %refs_3_.3, bf16[1,64,64,128]{3,2,1,0:T(8,128)(2,1)} %refs_4_.2, bf16[80,384]{1,0:T(8,128)(2,1)} %constant.41.clone.refs_5_, ...), custom_call_target="tpu_custom_call" | custom-call | flops 4 | bytes 4 | tf_op jit(solution)/shard_map/spectra/pallas_call | solution.py:291
  45.3 0.0 copy-start.1
  45.3 5.0 %pack.3 = (bf16[8,8,4224]{2,1,0:T(8,128)(2,1)}, bf16[4,8,384]{2,1,0:T(8,128)(2,1)}) custom-call(s32[1,1280]{1,0:T(1,128)} %constant.44.clone.refs_0_, bf16[2,4,48,1792]{3,2,1,0:T(8,128)(2,1)} %get-tuple-element.26.refs_1_, bf16[2,4,48,768]{3,2,1,0:T(8,128)(2,1)} %get-tuple-element.27.refs_2_), custom_call_target="tpu_custom_call" | custom-call | flops 1 | bytes 1 | tf_op jit(solution)/shard_map/pack/pallas_call | solution.py:375
  50.2 0.0 copy-start.2
  50.3 5.3 %all-to-all-start = ((bf16[8,8,4224]{2,1,0:T(8,128)(2,1)}), bf16[8,8,4224]{2,1,0:T(8,128)(2,1)S(1)}, u32[]{:S(2)}, u32[]{:S(2)}) async-start(bf16[8,8,4224]{2,1,0:T(8,128)(2,1)} %get-tuple-element.29), calls=%async_computation | async-start | bytes 1081344 | tf_op jit(solution)/shard_map/all_to_all | solution.py:506
  55.6 0.0 all-gather.4.cloned.1.call-start
  55.6 0.8 dynamic_slice.18
  56.4 0.6 broadcast_in_dim.9.wanted_ref
  57.1 1.2 fusion.starts_ref
  58.3 1.5 %constant_dynamic-slice_fusion.1.ids_ref = s32[1,4224]{1,0:T(1,128)} fusion(s32[8,4224]{1,0:T(8,128)} %constant.39.clone, s32[]{:T(128)S(6)} %select_n.14), kind=kLoop, calls=%fused_computation.3 | loop fusion | bytes 33796 | tf_op jit(solution)/shard_map/dynamic_slice | solution.py:491
  59.8 5.7 %all-to-all-done = bf16[8,8,4224]{2,1,0:T(8,128)(2,1)S(1)} async-done(((bf16[8,8,4224]{2,1,0:T(8,128)(2,1)}), bf16[8,8,4224]{2,1,0:T(8,128)(2,1)S(1)}, u32[]{:S(2)}, u32[]{:S(2)}) %all-to-all-start) | async-done | bytes 540704 | tf_op jit(solution)/shard_map/all_to_all | solution.py:506
  65.5 0.0 copy-start
  65.5 0.8 copy-done
  66.3 4.7 %in_order.2 = bf16[64,3840]{1,0:T(8,128)(2,1)} custom-call(s32[3]{0:T(128)} %fusion.starts_ref, s32[1,4224]{1,0:T(1,128)} %constant_dynamic-slice_fusion.1.ids_ref, s32[1,3840]{1,0:T(1,128)} %broadcast_in_dim.9.wanted_ref, bf16[64,4224]{1,0:T(8,128)(2,1)} %bitcast.19), custom_call_target="tpu_custom_call" | custom-call | flops 1 | bytes 1 | tf_op jit(solution)/shard_map/in_order/pallas_call | solution.py:440
  71.0 0.0 all-gather.4.cloned.1.call-update
  71.0 0.0 copy-done.1
  71.0 0.0 copy-done.2
  71.1 10.4 %all_to_all.20 = bf16[4,2,8,384]{3,2,1,0:T(8,128)(2,1)S(1)} all-to-all(bf16[4,2,8,384]{3,2,1,0:T(8,128)(2,1)S(1)} %copy.23), channel_id=1, replica_groups=mesh['row'=4,'col'=8] {'row'}, dimensions={0} | all-to-all | bytes 98304 | tf_op jit(solution)/shard_map/all_to_all | solution.py:510
  81.5 0.0 all-gather.6.cloned.1.call-done
  81.5 1.8 %copy.24 = bf16[4,8,8,4224]{3,2,0,1:T(8,128)(2,1)S(1)} copy(bf16[4,8,8,4224]{3,2,1,0:T(8,128)(2,1)} %bitcast.18) | data formatting | bytes 4325376 | tf_op jit(solution)/shard_map/optimization_barrier | solution.py:511
  83.2 30.5 %all_to_all.21 = bf16[4,8,8,4224]{3,2,0,1:T(8,128)(2,1)} all-to-all(bf16[4,8,8,4224]{3,2,0,1:T(8,128)(2,1)S(1)} %copy.24), channel_id=1, replica_groups=mesh['row'=4,'col'=8] {'col'}, dimensions={1} | all-to-all | bytes 4325376 | tf_op jit(solution)/shard_map/all_to_all | solution.py:512
  113.7 0.8 broadcast_in_dim.10
  114.5 3.6 %all-to-all-start.3 = ((bf16[8,4,2,8,384]{4,3,1,2,0:T(8,128)(2,1)}), bf16[8,4,2,8,384]{4,3,1,2,0:T(8,128)(2,1)S(1)}, u32[]{:S(2)}, u32[]{:S(2)}) async-start(bf16[8,4,2,8,384]{4,3,1,2,0:T(8,128)(2,1)} %broadcast_in_dim.10), calls=%async_computation.3 | async-start | bytes 786432 | tf_op jit(solution)/shard_map/all_to_all | solution.py:515
  118.1 1.3 dynamic_slice.20
  119.4 1.3 constant_dynamic-slice_fusion.refs_1_
  120.7 7.0 %in_order.3.refs_0_ = bf16[256,3840]{1,0:T(8,128)(2,1)} custom-call(s32[3]{0:T(128)} %fusion.starts_ref, s32[1,4224]{1,0:T(1,128)} %constant_dynamic-slice_fusion.1.ids_ref, s32[1,3840]{1,0:T(1,128)} %broadcast_in_dim.9.wanted_ref, bf16[256,4224]{1,0:T(8,128)(2,1)} %bitcast.17), custom_call_target="tpu_custom_call" | custom-call | flops 1 | bytes 1 | tf_op jit(solution)/shard_map/in_order/pallas_call | solution.py:440
  127.7 0.0 all-to-all-done.3
  127.8 0.8 pad_maximum_fusion
  128.6 2.5 %left_side.1.left_ref = bf16[512,512]{1,0:T(8,128)(2,1)} custom-call(bf16[512,384]{1,0:T(8,128)(2,1)} %bitcast.20, s32[1,384]{1,0:T(1,128)} %constant_dynamic-slice_fusion.refs_1_, s32[1,256]{1,0:T(1,128)} %bitcast.25), custom_call_target="tpu_custom_call" | custom-call | flops 1 | bytes 1 | tf_op jit(solution)/shard_map/left_side/pallas_call | solution.py:415
  131.2 0.0 all-gather.4.cloned.1.call-done.refs_1_
  131.2 7.9 %product.1 = f32[2,256,3840]{2,1,0:T(8,128)} custom-call(bf16[512,512]{1,0:T(8,128)(2,1)} %left_side.1.left_ref, bf16[256,3840]{1,0:T(8,128)(2,1)} %in_order.3.refs_0_, bf16[256,3840]{1,0:T(8,128)(2,1)} %all-gather.4.cloned.1.call-done.refs_1_), custom_call_target="tpu_custom_call" | custom-call | flops 1 | bytes 1 | tf_op jit(solution)/shard_map/product/pallas_call | solution.py:470
  (5 shorter events, 0.1 us)
Async XLA Ops:
  6.5 74.9 %all-gather.6.cloned.1.call-start = ((), (), s32[]{:S(2)}) async-start(), calls=%async_computation.5 | async-start | bytes 2703360 | tf_op jit(solution)/shard_map/all_gather | solution.py:504
  45.3 25.8 %copy-start.1 = (bf16[4,8,384]{2,1,0:T(8,128)(2,1)S(1)}, bf16[4,8,384]{2,1,0:T(8,128)(2,1)}, u32[]{:S(2)}) copy-start(bf16[4,8,384]{2,1,0:T(8,128)(2,1)} %get-tuple-element.24) | copy-start | bytes 73732
  50.2 20.8 %copy-start.2 = (bf16[4,8,384]{2,1,0:T(8,128)(2,1)S(1)}, bf16[4,8,384]{2,1,0:T(8,128)(2,1)}, u32[]{:S(2)}) copy-start(bf16[4,8,384]{2,1,0:T(8,128)(2,1)} %get-tuple-element.28) | copy-start | bytes 73732
  50.3 15.2 %all-to-all-start = ((bf16[8,8,4224]{2,1,0:T(8,128)(2,1)}), bf16[8,8,4224]{2,1,0:T(8,128)(2,1)S(1)}, u32[]{:S(2)}, u32[]{:S(2)}) async-start(bf16[8,8,4224]{2,1,0:T(8,128)(2,1)} %get-tuple-element.29), calls=%async_computation | async-start | bytes 1081344 | tf_op jit(solution)/shard_map/all_to_all | solution.py:506
  55.6 75.6 %all-gather.4.cloned.1.call-start = ((), (), s32[]{:S(2)}) async-start(), calls=%async_computation.4 | async-start | bytes 2457600 | tf_op jit(solution)/shard_map/all_gather | solution.py:508
  65.5 0.8 copy-start
  114.5 13.3 %all-to-all-start.3 = ((bf16[8,4,2,8,384]{4,3,1,2,0:T(8,128)(2,1)}), bf16[8,4,2,8,384]{4,3,1,2,0:T(8,128)(2,1)S(1)}, u32[]{:S(2)}, u32[]{:S(2)}) async-start(bf16[8,4,2,8,384]{4,3,1,2,0:T(8,128)(2,1)} %broadcast_in_dim.10), calls=%async_computation.3 | async-start | bytes 786432 | tf_op jit(solution)/shard_map/all_to_all | solution.py:515
Sparse Core Ops, SparseCore 0:
  28.8 50.0 all-gather.5
  80.5 42.9 all-gather.3

commit v10 on v9

--- a/solution.py
+++ b/solution.py
@@ -13,7 +13,6 @@
 VMEM_BYTES = 56 * 1024 * 1024
 HALF = 64
 KEEP = 40
-ROWS_K = 48
 ORIGIN = KEEP // 2
 PARITY_LANES = 896
 PARTS = 3
@@ -144,8 +143,8 @@
     high, low = parts(one[..., :KEEP].reshape(2 * points, 2 * KEEP).T)
     first = np.concatenate([high, high, low], 1)
     second = np.concatenate(parts(two.reshape(4 * points, 4 * HALF)), 0)
-    halves = two[..., :ROWS_K].reshape(2, 2, points // 2, 2, 4 * ROWS_K).transpose(0, 1, 3, 2, 4)
-    high, low = parts(halves.reshape(4 * points, 4 * ROWS_K).T)
+    halves = two[..., :KEEP].reshape(2, 2, points // 2, 2, 4 * KEEP).transpose(0, 1, 3, 2, 4)
+    high, low = parts(halves.reshape(4 * points, 4 * KEEP).T)
     third = np.concatenate([high, high, low], 1)
     return [jnp.asarray(table) for table in (first, second, third)]
 
@@ -194,8 +193,9 @@
     return [odd * PARITY_LANES // LANES + tile for odd in range(2) for tile in range(first, last)]
 
 
-def spectrum_kernel(plan, points, first_band, owner_ref, cond_energy_ref, val_energy_ref, val_ref, cond_ref, first_ref,
-                    second_ref, third_ref, plain_ref, weighted_ref, cond_a, cond_b, middle, turned, last):
+def spectrum_kernel(plan, points, first_band, count, owner_ref, cond_energy_ref, val_energy_ref, val_ref, cond_ref, place_ref, first_ref,
+                    second_ref, third_ref, send_ref, slab_ref, cond_a, cond_b, middle, turned, last, sorter, plain_rows, weighted_rows,
+                    plain_sorted, weighted_sorted):
     band = pl.program_id(0)
     planes = 8
     pairs = planes // 2
@@ -239,11 +239,16 @@
         for item in range(2):
             turned[item, rows, :] = field[:, item * LANES : (item + 1) * LANES]
 
+    turns = points // planes // 2 - 1
+    piece = sorter.shape[0] // (count * turns)
     first_axis(0)
     first_axis(1)
 
-    @pl.loop(1, points // planes // 2)
+    @pl.loop(1, turns + 1)
     def _(turn):
+        begin = pl.multiple_of((band * turns + turn - 1) * piece, 16)
+        at = lax.broadcasted_iota(jnp.int32, (piece, sorter.shape[1]), 0) + begin
+        sorter[pl.ds(begin, piece), :] = jnp.where(at == place_ref[...], 1.0, 0.0).astype(jnp.bfloat16)
         for part in range(2):
             second_axis(2 * turn - 2 + part)
         for part in range(2):
@@ -270,24 +275,60 @@
     slab = slab_tiles(plan)
     tiles = PARITY_LANES // LANES
     field = contract_last(third_ref[...], last[...])
+    band_rows = pl.ds(pl.multiple_of(band * 2 * KEEP, 2 * KEEP), 2 * KEEP)
     for odd in range(2):
-        for part in range(2):
-            at = (odd * 2 + part) * ROWS_K
-            value = field[at : at + ROWS_K]
-            plain_ref[part, 0, :, odd * PARITY_LANES : (odd + 1) * PARITY_LANES] = value.astype(jnp.bfloat16)
-            for place, tile in enumerate(slab):
-                if tile // tiles == odd:
-                    inside = value[:, tile % tiles * LANES : (tile % tiles + 1) * LANES]
-                    weighted_ref[part, 0, :, place * LANES : (place + 1) * LANES] = (weight * inside).astype(jnp.bfloat16)
+        value = field[odd * 2 * KEEP : (odd + 1) * 2 * KEEP]
+        plain_rows[band_rows, odd * PARITY_LANES : (odd + 1) * PARITY_LANES] = value.astype(jnp.bfloat16)
+        for place, tile in enumerate(slab):
+            if tile // tiles == odd:
+                inside = value[:, tile % tiles * LANES : (tile % tiles + 1) * LANES]
+                weighted_rows[band_rows, place * LANES : (place + 1) * LANES] = (weight * inside).astype(jnp.bfloat16)
+
+    @pl.when(band == count - 1)
+    def _():
+        def sort_rows(rows, which, target):
+            value = jnp.dot(rows, which, preferred_element_type=jnp.float32)
+            for tile in range(target.shape[0]):
+                target[tile] = value[:, tile * LANES : (tile + 1) * LANES]
+
+        which = [sorter[tile * LANES : (tile + 1) * LANES, : weighted_sorted.shape[0] * LANES] for tile in slab]
+        sort_rows(plain_rows[...], sorter[: 2 * PARITY_LANES, :], plain_sorted)
+        sort_rows(weighted_rows[...], jnp.concatenate(which, 0), weighted_sorted)
+
+        def plain_at(index, tile):
+            return plain_sorted[tile, pl.ds(index, 2 * count, stride=KEEP), :]
+
+        def weighted_at(index, tile):
+            return weighted_sorted[tile, pl.ds(index, 2 * count, stride=KEEP), :]
+
+        for block, bucket in enumerate(plan["buckets"]):
+
+            def keep(tile, value):
+                send_ref[block, :, tile * LANES : (tile + 1) * LANES] = value.astype(jnp.bfloat16)
+
+            pack_pieces(bucket.pieces, plan["lanes"], plain_at, 2 * count, lane, keep)
+        for block, bucket in enumerate(plan["slabs"]):
+
+            def keep_slab(tile, value):
+                slab_ref[block, :, tile * LANES : (tile + 1) * LANES] = value.astype(jnp.bfloat16)
+
+            pack_pieces(bucket.pieces, plan["slab_lanes"], weighted_at, 2 * count, lane, keep_slab)
 
 
 def spectra(plan, val_wave, cond_wave, energies, first_band, count):
     points = val_wave.shape[1]
-    depth = 2 * PARITY_LANES
+    turns = points // 16 - 1
+    depth = round_up(-(-2 * PARITY_LANES // (count * turns)), 16) * count * turns
+    columns = round_up(plan["column_place"].shape[0], 256)
+    slab_columns = round_up(plan["slab_columns"], LANES)
     slab_depth = len(slab_tiles(plan)) * LANES
+    place = np.full((1, columns), -1, np.int32)
+    place[0, : plan["column_place"].shape[0]] = plan["column_place"]
     grid_rows = points * points
     tables = dft_tables(points)
-    kernel = lambda *refs: spectrum_kernel(plan, points, first_band, *refs)
+    send_shape = (len(plan["buckets"]), 2 * count, plan["lanes"])
+    slab_shape = (len(plan["slabs"]), 2 * count, plan["slab_lanes"])
+    kernel = lambda *refs: spectrum_kernel(plan, points, first_band, count, *refs)
     return pl.pallas_call(
         kernel,
         grid=(count,),
@@ -297,95 +338,27 @@
             pl.BlockSpec(memory_space=pltpu.SMEM),
             pl.BlockSpec((1, points, points, 2 * points), lambda v: (first_band + v, 0, 0, 0)),
             pl.BlockSpec((1, points, points, 2 * points), lambda v: (0, 0, 0, 0)),
+            pl.BlockSpec((1, columns), lambda v: (0, 0)),
             *[pl.BlockSpec(table.shape, lambda v: (0, 0)) for table in tables],
         ],
-        out_specs=[
-            pl.BlockSpec((2, 1, ROWS_K, depth), lambda v: (0, v, 0, 0)),
-            pl.BlockSpec((2, 1, ROWS_K, slab_depth), lambda v: (0, v, 0, 0)),
-        ],
-        out_shape=[
-            jax.ShapeDtypeStruct((2, count, ROWS_K, depth), jnp.bfloat16),
-            jax.ShapeDtypeStruct((2, count, ROWS_K, slab_depth), jnp.bfloat16),
-        ],
+        out_specs=[pl.BlockSpec(send_shape, lambda v: (0, 0, 0)), pl.BlockSpec(slab_shape, lambda v: (0, 0, 0))],
+        out_shape=[jax.ShapeDtypeStruct(send_shape, jnp.bfloat16), jax.ShapeDtypeStruct(slab_shape, jnp.bfloat16)],
         scratch_shapes=[
             pltpu.VMEM((grid_rows, LANES), jnp.float32),
             pltpu.VMEM((grid_rows, LANES), jnp.float32),
             pltpu.VMEM((points // 2 * KEEP, 4 * LANES), jnp.bfloat16),
             pltpu.VMEM((2, points // 2 * KEEP, LANES), jnp.float32),
             pltpu.VMEM((PARITY_LANES, 4 * LANES), jnp.bfloat16),
+            pltpu.VMEM((depth, columns), jnp.bfloat16),
+            pltpu.VMEM((2 * count * KEEP, 2 * PARITY_LANES), jnp.bfloat16),
+            pltpu.VMEM((2 * count * KEEP, slab_depth), jnp.bfloat16),
+            pltpu.VMEM((columns // LANES, 2 * count * KEEP, LANES), jnp.float32),
+            pltpu.VMEM((slab_columns // LANES, 2 * count * KEEP, LANES), jnp.float32),
         ],
         compiler_params=pltpu.CompilerParams(vmem_limit_bytes=VMEM_BYTES, dimension_semantics=("arbitrary",)),
-        cost_estimate=pl.CostEstimate(flops=count, bytes_accessed=count, transcendentals=0),
+        cost_estimate=pl.CostEstimate(flops=1, bytes_accessed=1, transcendentals=0),
         name="spectra",
-    )(*energies, val_wave, cond_wave, *tables)
-
-
-def pack_kernel(plan, groups, place_ref, *refs):
-    plains, weighteds = refs[:groups], refs[groups : 2 * groups]
-    send_ref, slab_ref, sorter, plain_sorted, weighted_sorted = refs[2 * groups :]
-    depth, columns = sorter.shape
-    count = 2 * sum(plain.shape[1] for plain in plains)
-    lane = lax.broadcasted_iota(jnp.int32, (1, LANES), 1)
-    for begin in range(0, depth, LANES):
-        at = lax.broadcasted_iota(jnp.int32, (LANES, columns), 0) + begin
-        sorter[begin : begin + LANES, :] = jnp.where(at == place_ref[...], 1.0, 0.0).astype(jnp.bfloat16)
-
-    def sort_rows(parts, which, target):
-        rows = jnp.concatenate([part[n] for n in range(2) for part in parts], 0)
-        rows = rows.reshape(count * ROWS_K, rows.shape[2])
-        value = jnp.dot(rows, which, preferred_element_type=jnp.float32)
-        for tile in range(target.shape[0]):
-            target[tile] = value[:, tile * LANES : (tile + 1) * LANES]
-
-    slab = [sorter[tile * LANES : (tile + 1) * LANES, : weighted_sorted.shape[0] * LANES] for tile in slab_tiles(plan)]
-    sort_rows(plains, sorter[...], plain_sorted)
-    sort_rows(weighteds, jnp.concatenate(slab, 0), weighted_sorted)
-
-    def plain_at(index, tile):
-        return plain_sorted[tile, pl.ds(index, count, stride=ROWS_K), :]
-
-    def weighted_at(index, tile):
-        return weighted_sorted[tile, pl.ds(index, count, stride=ROWS_K), :]
-
-    for block, bucket in enumerate(plan["buckets"]):
-
-        def keep(tile, value):
-            send_ref[block, :, tile * LANES : (tile + 1) * LANES] = value.astype(jnp.bfloat16)
-
-        pack_pieces(bucket.pieces, plan["lanes"], plain_at, count, lane, keep)
-    for block, bucket in enumerate(plan["slabs"]):
-
-        def keep_slab(tile, value):
-            slab_ref[block, :, tile * LANES : (tile + 1) * LANES] = value.astype(jnp.bfloat16)
-
-        pack_pieces(bucket.pieces, plan["slab_lanes"], weighted_at, count, lane, keep_slab)
-
-
-def packed(plan, plains, weighteds):
-    depth = plains[0].shape[3]
-    count = 2 * sum(plain.shape[1] for plain in plains)
-    columns = round_up(plan["column_place"].shape[0], 256)
-    slab_columns = round_up(plan["slab_columns"], LANES)
-    place = np.full((1, columns), -1, np.int32)
-    place[0, : plan["column_place"].shape[0]] = plan["column_place"]
-    kernel = lambda *refs: pack_kernel(plan, len(plains), *refs)
-    vmem = pl.BlockSpec(memory_space=pltpu.VMEM)
-    send_shape = (len(plan["buckets"]), count, plan["lanes"])
-    slab_shape = (len(plan["slabs"]), count, plan["slab_lanes"])
-    return pl.pallas_call(
-        kernel,
-        in_specs=[vmem] * (1 + 2 * len(plains)),
-        out_specs=[vmem] * 2,
-        out_shape=[jax.ShapeDtypeStruct(send_shape, jnp.bfloat16), jax.ShapeDtypeStruct(slab_shape, jnp.bfloat16)],
-        scratch_shapes=[
-            pltpu.VMEM((depth, columns), jnp.bfloat16),
-            pltpu.VMEM((columns // LANES, count * ROWS_K, LANES), jnp.float32),
-            pltpu.VMEM((slab_columns // LANES, count * ROWS_K, LANES), jnp.float32),
-        ],
-        compiler_params=pltpu.CompilerParams(vmem_limit_bytes=VMEM_BYTES),
-        cost_estimate=pl.CostEstimate(flops=1, bytes_accessed=1, transcendentals=0),
-        name="pack",
-    )(jnp.asarray(place), *plains, *weighteds)
+    )(*energies, val_wave, cond_wave, jnp.asarray(place), *tables)
 
 
 def one_hot(ids_ref, begin, wanted):
@@ -394,26 +367,26 @@
     return jnp.where(ids == wanted, 1.0, 0.0).astype(jnp.bfloat16)
 
 
-def left_kernel(group, slab_ref, slab_ids_ref, slab_wanted_ref, left_ref):
+def left_kernel(slab_ref, slab_ids_ref, slab_wanted_ref, left_ref):
     rows = slab_wanted_ref.shape[1]
     choice = jnp.concatenate(
         [one_hot(slab_ids_ref, begin, slab_wanted_ref[...]) for begin in range(0, slab_ids_ref.shape[1], LANES)], 0
     )
     chosen = jnp.dot(slab_ref[...], choice, preferred_element_type=jnp.float32)
     lane = lax.broadcasted_iota(jnp.int32, (1, LANES), 1)
-    real_lanes = lane % group < group // 2
+    real_lanes = lane % 2 == 0
     for begin in range(0, chosen.shape[0], LANES):
         turned = chosen[begin : begin + LANES].T
-        after = pltpu.roll(turned, LANES - group // 2, 1)
-        before = pltpu.roll(turned, group // 2, 1)
+        after = pltpu.roll(turned, LANES - 1, 1)
+        before = pltpu.roll(turned, 1, 1)
         left_ref[:rows, begin : begin + LANES] = turned.astype(jnp.bfloat16)
         left_ref[rows:, begin : begin + LANES] = jnp.where(real_lanes, after, -before).astype(jnp.bfloat16)
 
 
-def left_side(group, slab, slab_ids, slab_wanted):
+def left_side(slab, slab_ids, slab_wanted):
     vmem = pl.BlockSpec(memory_space=pltpu.VMEM)
     return pl.pallas_call(
-        lambda *refs: left_kernel(group, *refs),
+        left_kernel,
         in_specs=[vmem] * 3,
         out_specs=vmem,
         out_shape=jax.ShapeDtypeStruct((2 * slab_wanted.shape[1], slab.shape[0]), jnp.bfloat16),
@@ -496,26 +469,23 @@
     energies = (band_owner, cond_energy, val_energy)
     slabs = []
     for part in range(2):
-        plain, weighted = spectra(plan, val_wave, cond_wave, energies, part * chunk, chunk)
-        send, slab = packed(plan, [plain], [weighted])
+        send, slab = spectra(plan, val_wave, cond_wave, energies, part * chunk, chunk)
         slabs.append(slab)
         if part == 0:
             send, cond_wave = lax.optimization_barrier((send, cond_wave))
-            early = lax.all_gather(send, "row", axis=0)
+            early = lax.all_gather(send, "row", axis=1)
         else:
             mine = lax.all_to_all(send, "col", split_axis=0, concat_axis=0, tiled=True).reshape(-1, plan["lanes"])
             mine = put_in_order(plan, starts, ids, wanted, mine)
             last = lax.all_gather(mine, "row", axis=0, tiled=True)
     slab, _ = lax.optimization_barrier((jnp.stack(slabs, 1), mine))
     slab = lax.all_to_all(slab, "row", split_axis=0, concat_axis=0, tiled=True)
+    slab = lax.all_to_all(jnp.broadcast_to(slab, (col_count, *slab.shape)), "col", split_axis=0, concat_axis=0)
     early, slab = lax.optimization_barrier((early, slab))
-    early = lax.all_to_all(early, "col", split_axis=1, concat_axis=1, tiled=True)
-    early = early.transpose(1, 0, 2, 3).reshape(-1, plan["lanes"])
-    early, slab = lax.optimization_barrier((early, slab))
-    slab = lax.all_to_all(jnp.broadcast_to(slab, (col_count, *slab.shape)), "col", split_axis=0, concat_axis=0)
     slab = [slab[:, :, 0], slab[:, :, 1].transpose(1, 0, 2, 3)]
     slab = jnp.stack([part.reshape(-1, plan["slab_lanes"]) for part in slab]).reshape(-1, plan["slab_lanes"])
-    left = left_side(2 * chunk, slab, slab_ids, slab_wanted)
+    left = left_side(slab, slab_ids, slab_wanted)
+    early = lax.all_to_all(early, "col", split_axis=0, concat_axis=0, tiled=True).reshape(-1, plan["lanes"])
     return product(left, [put_in_order(plan, starts, ids, wanted, early), last])
 
 

time: 147 us -> 142 us (0.966)
  waiting for transfers between devices: 5.72 us -> 26.9 us
  blocking collectives: 40.8 us -> 21.6 us
  Pallas kernels: 65.2 us -> 59.5 us
    all_to_all x1, waiting for transfers between devices: 0.01 us -> 21.2 us  [on_device(): lax.all_to_all(early, 'col', split_axis=0, concat_axis=0, tiled=True)]
    all_to_all x1, blocking collectives: 30.5 us -> 11 us  [on_device(): lax.all_to_all(jnp.broadcast_to(slab, (col_count, *slab.shape)), 'col', s...]
    pallas_call x3 -> x1, Pallas kernels: 12.5 us -> 2.56 us  [left_side(): pl.pallas_call(left_kernel, in_specs=[vmem] * 3, out_specs=vmem, out_shap...]
    pallas_call x2, Pallas kernels: 33.1 us -> 37.3 us  [spectra(): pl.pallas_call(kernel, grid=(count,), in_specs=[pl.BlockSpec(memory_space...]
    optimization_barrier x2 -> x1, local copies, waits for them, and re-layouts: 1.76 us -> 0.04 us  [on_device(): early, slab = lax.optimization_barrier((early, slab))]
  transfers between devices with their start and end apart: 4 -> 4, of which waited for: 1 -> 2; matrix products, arithmetic and copies ran while one was open for 7% -> 5% of each run, Pallas kernels for 25% -> 23%
where the time goes in v10:
time: 142 us; the launch traced here: 141 us
  Pallas kernels  59.5 us (42%)
  waiting for transfers between devices  26.9 us (19%)
  blocking collectives  21.6 us (15%)
  between operations  14.1 us (10%)
  local copies, waits for them, and re-layouts  9.05 us (6%)
  starting transfers between devices  8.96 us (6%)
    pallas_call x2, Pallas kernels, spectra(): pl.pallas_call(kernel, grid=(count,), in_specs=[pl.BlockSpec(memory_space...  37.3 us
    all_to_all x1, waiting for transfers between devices, on_device(): lax.all_to_all(early, 'col', split_axis=0, concat_axis=0, tiled=True)  21.2 us
    pallas_call x2, Pallas kernels, put_in_order(): pl.pallas_call(order_kernel, grid=(PARTS,), in_specs=[pl.BlockSpec(memory...  11.8 us
    all_to_all x1, blocking collectives, on_device(): lax.all_to_all(jnp.broadcast_to(slab, (col_count, *slab.shape)), 'col', s...  11 us
    all_to_all x1, blocking collectives, on_device(): slab = lax.all_to_all(slab, 'row', split_axis=0, concat_axis=0, tiled=True)  10.6 us
    pallas_call x1, Pallas kernels, product(): pl.pallas_call(product_kernel, grid=(pl.cdiv(columns, block),), in_specs=...  7.88 us
    all_to_all x1, waiting for transfers between devices, on_device(): lax.all_to_all(send, 'col', split_axis=0, concat_axis=0, tiled=True)  5.72 us
    all_to_all x1, starting transfers between devices, on_device(): lax.all_to_all(send, 'col', split_axis=0, concat_axis=0, tiled=True)  5.31 us
  transfers between devices with their start and end apart: 4, of which 2 were waited for; matrix products, arithmetic and copies ran while one was open for 5% of the time, Pallas kernels for 23%

profile of v10, /device:TPU:0, one launch (start us, length us, event | category | flops | bytes accessed | tf_op | source)
XLA Modules:
  0.0 141.0 jit_solution(7656313061516463285)
XLA Ops:
  6.5 0.0 all-gather.6.cloned.1.call-start
  7.2 18.7 %spectra.2 = (bf16[8,8,4224]{2,1,0:T(8,128)(2,1)}, bf16[4,8,384]{2,1,0:T(8,128)(2,1)}) custom-call(s32[1]{0:T(128)S(6)} %copy.24.refs_0_, f32[32]{0:T(128)} %refs_1_.3, f32[8]{0:T(128)} %refs_2_.3, bf16[8,64,64,128]{3,2,1,0:T(8,128)(2,1)} %refs_3_.3, bf16[1,64,64,128]{3,2,1,0:T(8,128)(2,1)} %refs_4_.2, s32[1,1280]{1,0:T(1,128)} %constant.44.clone.refs_5_, ...), custom_call_target="tpu_custom_call" | custom-call | flops 1 | bytes 1 | tf_op jit(solution)/shard_map/spectra/pallas_call | solution.py:332
  25.8 0.0 all-gather.6.cloned.1.call-update
  25.9 18.7 %spectra.3 = (bf16[8,8,4224]{2,1,0:T(8,128)(2,1)}, bf16[4,8,384]{2,1,0:T(8,128)(2,1)}) custom-call(s32[1]{0:T(128)S(6)} %copy.24.refs_0_, f32[32]{0:T(128)} %refs_1_.3, f32[8]{0:T(128)} %refs_2_.3, bf16[8,64,64,128]{3,2,1,0:T(8,128)(2,1)} %refs_3_.3, bf16[1,64,64,128]{3,2,1,0:T(8,128)(2,1)} %refs_4_.2, s32[1,1280]{1,0:T(1,128)} %constant.44.clone.refs_5_, ...), custom_call_target="tpu_custom_call" | custom-call | flops 1 | bytes 1 | tf_op jit(solution)/shard_map/spectra/pallas_call | solution.py:332
  44.5 0.0 copy-start.2
  44.5 0.0 copy-start.3
  44.5 5.3 %all-to-all-start = ((bf16[8,8,4224]{2,1,0:T(8,128)(2,1)}), bf16[8,8,4224]{2,1,0:T(8,128)(2,1)S(1)}, u32[]{:S(2)}, u32[]{:S(2)}) async-start(bf16[8,8,4224]{2,1,0:T(8,128)(2,1)} %get-tuple-element.19), calls=%async_computation | async-start | bytes 1081344 | tf_op jit(solution)/shard_map/all_to_all | solution.py:478
  49.8 0.0 all-gather.4.cloned.1.call-start
  49.9 0.8 dynamic_slice.18
  50.7 0.6 broadcast_in_dim.9.wanted_ref
  51.3 1.2 fusion.starts_ref
  52.5 1.5 %constant_dynamic-slice_fusion.1.ids_ref = s32[1,4224]{1,0:T(1,128)} fusion(s32[8,4224]{1,0:T(8,128)} %constant.39.clone, s32[]{:T(128)S(6)} %select_n.14), kind=kLoop, calls=%fused_computation.3 | loop fusion | bytes 33796 | tf_op jit(solution)/shard_map/dynamic_slice | solution.py:464
  54.0 5.7 %all-to-all-done = bf16[8,8,4224]{2,1,0:T(8,128)(2,1)S(1)} async-done(((bf16[8,8,4224]{2,1,0:T(8,128)(2,1)}), bf16[8,8,4224]{2,1,0:T(8,128)(2,1)S(1)}, u32[]{:S(2)}, u32[]{:S(2)}) %all-to-all-start) | async-done | bytes 540704 | tf_op jit(solution)/shard_map/all_to_all | solution.py:478
  59.8 0.0 copy-start.1
  59.8 0.8 copy-done.1
  60.6 4.7 %in_order.2 = bf16[64,3840]{1,0:T(8,128)(2,1)} custom-call(s32[3]{0:T(128)} %fusion.starts_ref, s32[1,4224]{1,0:T(1,128)} %constant_dynamic-slice_fusion.1.ids_ref, s32[1,3840]{1,0:T(1,128)} %broadcast_in_dim.9.wanted_ref, bf16[64,4224]{1,0:T(8,128)(2,1)} %bitcast.17), custom_call_target="tpu_custom_call" | custom-call | flops 1 | bytes 1 | tf_op jit(solution)/shard_map/in_order/pallas_call | solution.py:413
  65.3 0.0 all-gather.4.cloned.1.call-update
  65.3 0.0 copy-done.2
  65.3 0.0 copy-done.3
  65.3 10.6 %all_to_all.20 = bf16[4,2,8,384]{3,2,1,0:T(8,128)(2,1)S(1)} all-to-all(bf16[4,2,8,384]{3,2,1,0:T(8,128)(2,1)S(1)} %copy.21), channel_id=1, replica_groups=mesh['row'=4,'col'=8] {'row'}, dimensions={0} | all-to-all | bytes 98304 | tf_op jit(solution)/shard_map/all_to_all | solution.py:482
  76.0 11.0 %all_to_all.21 = bf16[8,4,2,8,384]{4,3,1,2,0:T(8,128)(2,1)S(1)} all-to-all(bf16[8,4,2,8,384]{4,3,1,2,0:T(8,128)(2,1)S(1)} %broadcast_in_dim.10), channel_id=1, replica_groups=mesh['row'=4,'col'=8] {'col'}, dimensions={0} | all-to-all | bytes 786432 | tf_op jit(solution)/shard_map/all_to_all | solution.py:483
  87.0 0.0 all-gather.6.cloned.1.call-done
  87.0 3.6 %all-to-all-start.3 = ((bf16[8,4,8,4224]{3,2,1,0:T(8,128)(2,1)}), bf16[8,4,8,4224]{3,2,1,0:T(8,128)(2,1)S(1)}, u32[]{:S(2)}, u32[]{:S(2)}) async-start(bf16[8,4,8,4224]{3,2,1,0:T(8,128)(2,1)} %bitcast.16), calls=%async_computation.3 | async-start | bytes 4325376 | tf_op jit(solution)/shard_map/all_to_all | solution.py:488
  90.6 1.3 dynamic_slice.20
  92.0 1.3 constant_dynamic-slice_fusion.slab_ids_ref
  93.4 0.8 pad_maximum_fusion
  94.1 2.6 %left_side.1.left_ref = bf16[512,512]{1,0:T(8,128)(2,1)} custom-call(bf16[512,384]{1,0:T(8,128)(2,1)} %bitcast.18, s32[1,384]{1,0:T(1,128)} %constant_dynamic-slice_fusion.slab_ids_ref, s32[1,256]{1,0:T(1,128)} %bitcast.23), custom_call_target="tpu_custom_call" | custom-call | flops 1 | bytes 1 | tf_op jit(solution)/shard_map/left_side/pallas_call | solution.py:388
  96.7 21.2 %all-to-all-done.3 = bf16[8,4,8,4224]{3,2,1,0:T(8,128)(2,1)S(1)} async-done(((bf16[8,4,8,4224]{3,2,1,0:T(8,128)(2,1)}), bf16[8,4,8,4224]{3,2,1,0:T(8,128)(2,1)S(1)}, u32[]{:S(2)}, u32[]{:S(2)}) %all-to-all-start.3) | async-done | bytes 2162720 | tf_op jit(solution)/shard_map/all_to_all | solution.py:488
  117.9 0.0 copy-start
  117.9 1.3 copy-done
  119.2 7.1 %in_order.3.refs_0_ = bf16[256,3840]{1,0:T(8,128)(2,1)} custom-call(s32[3]{0:T(128)} %fusion.starts_ref, s32[1,4224]{1,0:T(1,128)} %constant_dynamic-slice_fusion.1.ids_ref, s32[1,3840]{1,0:T(1,128)} %broadcast_in_dim.9.wanted_ref, bf16[256,4224]{1,0:T(8,128)(2,1)} %bitcast.15), custom_call_target="tpu_custom_call" | custom-call | flops 1 | bytes 1 | tf_op jit(solution)/shard_map/in_order/pallas_call | solution.py:413
  126.3 0.0 all-gather.4.cloned.1.call-done.refs_1_
  126.3 7.9 %product.1 = f32[2,256,3840]{2,1,0:T(8,128)} custom-call(bf16[512,512]{1,0:T(8,128)(2,1)} %left_side.1.left_ref, bf16[256,3840]{1,0:T(8,128)(2,1)} %in_order.3.refs_0_, bf16[256,3840]{1,0:T(8,128)(2,1)} %all-gather.4.cloned.1.call-done.refs_1_), custom_call_target="tpu_custom_call" | custom-call | flops 1 | bytes 1 | tf_op jit(solution)/shard_map/product/pallas_call | solution.py:443
  (7 shorter events, 0.1 us)
Async XLA Ops:
  6.5 80.5 %all-gather.6.cloned.1.call-start = ((), (), s32[]{:S(2)}) async-start(), calls=%async_computation.5 | async-start | bytes 2703360 | tf_op jit(solution)/shard_map/all_gather | solution.py:476
  44.5 20.8 %copy-start.2 = (bf16[4,8,384]{2,1,0:T(8,128)(2,1)S(1)}, bf16[4,8,384]{2,1,0:T(8,128)(2,1)}, u32[]{:S(2)}) copy-start(bf16[4,8,384]{2,1,0:T(8,128)(2,1)} %get-tuple-element.16) | copy-start | bytes 73732
  44.5 20.8 %copy-start.3 = (bf16[4,8,384]{2,1,0:T(8,128)(2,1)S(1)}, bf16[4,8,384]{2,1,0:T(8,128)(2,1)}, u32[]{:S(2)}) copy-start(bf16[4,8,384]{2,1,0:T(8,128)(2,1)} %get-tuple-element.18) | copy-start | bytes 73732
  44.5 15.2 %all-to-all-start = ((bf16[8,8,4224]{2,1,0:T(8,128)(2,1)}), bf16[8,8,4224]{2,1,0:T(8,128)(2,1)S(1)}, u32[]{:S(2)}, u32[]{:S(2)}) async-start(bf16[8,8,4224]{2,1,0:T(8,128)(2,1)} %get-tuple-element.19), calls=%async_computation | async-start | bytes 1081344 | tf_op jit(solution)/shard_map/all_to_all | solution.py:478
  49.8 76.5 %all-gather.4.cloned.1.call-start = ((), (), s32[]{:S(2)}) async-start(), calls=%async_computation.4 | async-start | bytes 2457600 | tf_op jit(solution)/shard_map/all_gather | solution.py:480
  59.8 0.8 copy-start.1
  87.0 30.9 %all-to-all-start.3 = ((bf16[8,4,8,4224]{3,2,1,0:T(8,128)(2,1)}), bf16[8,4,8,4224]{3,2,1,0:T(8,128)(2,1)S(1)}, u32[]{:S(2)}, u32[]{:S(2)}) async-start(bf16[8,4,8,4224]{3,2,1,0:T(8,128)(2,1)} %bitcast.16), calls=%async_computation.3 | async-start | bytes 4325376 | tf_op jit(solution)/shard_map/all_to_all | solution.py:488
  117.9 1.3 copy-start
Sparse Core Ops, SparseCore 0:
  26.0 50.5 all-gather.5
  78.1 42.7 all-gather.3

commit v11 on v10

--- a/solution.py
+++ b/solution.py
@@ -197,8 +197,9 @@
                     second_ref, third_ref, send_ref, slab_ref, cond_a, cond_b, middle, turned, last, sorter, plain_rows, weighted_rows,
                     plain_sorted, weighted_sorted):
     band = pl.program_id(0)
-    planes = 8
+    planes = 16
     pairs = planes // 2
+    blocks = points // planes
     lane = lax.broadcasted_iota(jnp.int32, (1, LANES), 1)
     low_lanes = lane < HALF
 
@@ -239,23 +240,18 @@
         for item in range(2):
             turned[item, rows, :] = field[:, item * LANES : (item + 1) * LANES]
 
-    turns = points // planes // 2 - 1
-    piece = sorter.shape[0] // (count * turns)
+    piece = sorter.shape[0] // (count * (blocks - 1))
     first_axis(0)
-    first_axis(1)
-
-    @pl.loop(1, turns + 1)
+
+    @pl.loop(1, blocks)
     def _(turn):
-        begin = pl.multiple_of((band * turns + turn - 1) * piece, 16)
+        begin = pl.multiple_of((band * (blocks - 1) + turn - 1) * piece, 16)
         at = lax.broadcasted_iota(jnp.int32, (piece, sorter.shape[1]), 0) + begin
         sorter[pl.ds(begin, piece), :] = jnp.where(at == place_ref[...], 1.0, 0.0).astype(jnp.bfloat16)
-        for part in range(2):
-            second_axis(2 * turn - 2 + part)
-        for part in range(2):
-            first_axis(2 * turn + part)
-
-    second_axis(points // planes - 2)
-    second_axis(points // planes - 1)
+        second_axis(turn - 1)
+        first_axis(turn)
+
+    second_axis(blocks - 1)
 
     for begin in range(0, KEEP, 4):
         both = []
@@ -439,7 +435,7 @@
 
 def product(left, ordered):
     rows, columns = left.shape[0] // 2, ordered[0].shape[1]
-    block = columns // (2 * PARTS) // LANES * LANES
+    block = 6 * LANES
     return pl.pallas_call(
         product_kernel,
         grid=(pl.cdiv(columns, block),),
@@ -476,8 +472,7 @@
             early = lax.all_gather(send, "row", axis=1)
         else:
             mine = lax.all_to_all(send, "col", split_axis=0, concat_axis=0, tiled=True).reshape(-1, plan["lanes"])
-            mine = put_in_order(plan, starts, ids, wanted, mine)
-            last = lax.all_gather(mine, "row", axis=0, tiled=True)
+            last = lax.all_gather(put_in_order(plan, starts, ids, wanted, mine), "row", axis=0, tiled=True)
     slab, _ = lax.optimization_barrier((jnp.stack(slabs, 1), mine))
     slab = lax.all_to_all(slab, "row", split_axis=0, concat_axis=0, tiled=True)
     slab = lax.all_to_all(jnp.broadcast_to(slab, (col_count, *slab.shape)), "col", split_axis=0, concat_axis=0)

time: 142 us -> 144 us (1.014)
  Pallas kernels: 59.5 us -> 62.2 us
    pallas_call x2, Pallas kernels: 37.3 us -> 40.3 us  [spectra(): pl.pallas_call(kernel, grid=(count,), in_specs=[pl.BlockSpec(memory_space...]
  transfers between devices with their start and end apart: 4 -> 4, of which waited for: 2 -> 2; matrix products, arithmetic and copies ran while one was open for 5% -> 5% of each run, Pallas kernels for 23% -> 24%
where the time goes in v11:
time: 144 us; the launch traced here: 143 us
  Pallas kernels  62.2 us (43%)
  waiting for transfers between devices  26.9 us (19%)
  blocking collectives  21.1 us (15%)
  between operations  14.1 us (10%)
  local copies, waits for them, and re-layouts  9.05 us (6%)
  starting transfers between devices  8.96 us (6%)
    pallas_call x2, Pallas kernels, spectra(): pl.pallas_call(kernel, grid=(count,), in_specs=[pl.BlockSpec(memory_space...  40.3 us
    all_to_all x1, waiting for transfers between devices, on_device(): lax.all_to_all(early, 'col', split_axis=0, concat_axis=0, tiled=True)  21.2 us
    pallas_call x2, Pallas kernels, put_in_order(): pl.pallas_call(order_kernel, grid=(PARTS,), in_specs=[pl.BlockSpec(memory...  11.8 us
    all_to_all x1, blocking collectives, on_device(): lax.all_to_all(jnp.broadcast_to(slab, (col_count, *slab.shape)), 'col', s...  10.7 us
    all_to_all x1, blocking collectives, on_device(): slab = lax.all_to_all(slab, 'row', split_axis=0, concat_axis=0, tiled=True)  10.4 us
    pallas_call x1, Pallas kernels, product(): pl.pallas_call(product_kernel, grid=(pl.cdiv(columns, block),), in_specs=...  7.65 us
    all_to_all x1, waiting for transfers between devices, on_device(): lax.all_to_all(send, 'col', split_axis=0, concat_axis=0, tiled=True)  5.72 us
    all_to_all x1, starting transfers between devices, on_device(): lax.all_to_all(send, 'col', split_axis=0, concat_axis=0, tiled=True)  5.31 us
  transfers between devices with their start and end apart: 4, of which 2 were waited for; matrix products, arithmetic and copies ran while one was open for 5% of the time, Pallas kernels for 24%

profile of v11, /device:TPU:0, one launch (start us, length us, event | category | flops | bytes accessed | tf_op | source)
XLA Modules:
  0.0 143.2 jit_solution(6661019464309619867)
XLA Ops:
  6.5 0.0 all-gather.6.cloned.1.call-start
  7.2 20.1 %spectra.2 = (bf16[8,8,4224]{2,1,0:T(8,128)(2,1)}, bf16[4,8,384]{2,1,0:T(8,128)(2,1)}) custom-call(s32[1]{0:T(128)S(6)} %copy.24.refs_0_, f32[32]{0:T(128)} %refs_1_.3, f32[8]{0:T(128)} %refs_2_.3, bf16[8,64,64,128]{3,2,1,0:T(8,128)(2,1)} %refs_3_.3, bf16[1,64,64,128]{3,2,1,0:T(8,128)(2,1)} %refs_4_.2, s32[1,1280]{1,0:T(1,128)} %constant.44.clone.refs_5_, ...), custom_call_target="tpu_custom_call" | custom-call | flops 1 | bytes 1 | tf_op jit(solution)/shard_map/spectra/pallas_call | solution.py:328
  27.3 0.0 all-gather.6.cloned.1.call-update
  27.3 20.1 %spectra.3 = (bf16[8,8,4224]{2,1,0:T(8,128)(2,1)}, bf16[4,8,384]{2,1,0:T(8,128)(2,1)}) custom-call(s32[1]{0:T(128)S(6)} %copy.24.refs_0_, f32[32]{0:T(128)} %refs_1_.3, f32[8]{0:T(128)} %refs_2_.3, bf16[8,64,64,128]{3,2,1,0:T(8,128)(2,1)} %refs_3_.3, bf16[1,64,64,128]{3,2,1,0:T(8,128)(2,1)} %refs_4_.2, s32[1,1280]{1,0:T(1,128)} %constant.44.clone.refs_5_, ...), custom_call_target="tpu_custom_call" | custom-call | flops 1 | bytes 1 | tf_op jit(solution)/shard_map/spectra/pallas_call | solution.py:328
  47.5 0.0 copy-start.2
  47.5 0.0 copy-start.3
  47.5 5.3 %all-to-all-start = ((bf16[8,8,4224]{2,1,0:T(8,128)(2,1)}), bf16[8,8,4224]{2,1,0:T(8,128)(2,1)S(1)}, u32[]{:S(2)}, u32[]{:S(2)}) async-start(bf16[8,8,4224]{2,1,0:T(8,128)(2,1)} %get-tuple-element.19), calls=%async_computation | async-start | bytes 1081344 | tf_op jit(solution)/shard_map/all_to_all | solution.py:474
  52.8 0.0 all-gather.4.cloned.1.call-start
  52.8 0.8 dynamic_slice.20
  53.6 0.6 broadcast_in_dim.11.wanted_ref
  54.3 1.2 fusion.starts_ref
  55.5 1.5 %constant_dynamic-slice_fusion.ids_ref = s32[1,4224]{1,0:T(1,128)} fusion(s32[8,4224]{1,0:T(8,128)} %constant.39.clone, s32[]{:T(128)S(6)} %select_n.16), kind=kLoop, calls=%fused_computation.2 | loop fusion | bytes 33796 | tf_op jit(solution)/shard_map/dynamic_slice | solution.py:460
  57.0 5.7 %all-to-all-done = bf16[8,8,4224]{2,1,0:T(8,128)(2,1)S(1)} async-done(((bf16[8,8,4224]{2,1,0:T(8,128)(2,1)}), bf16[8,8,4224]{2,1,0:T(8,128)(2,1)S(1)}, u32[]{:S(2)}, u32[]{:S(2)}) %all-to-all-start) | async-done | bytes 540704 | tf_op jit(solution)/shard_map/all_to_all | solution.py:474
  62.7 0.0 copy-start.1
  62.7 0.8 copy-done.1
  63.5 4.7 %in_order.3 = bf16[64,3840]{1,0:T(8,128)(2,1)} custom-call(s32[3]{0:T(128)} %fusion.starts_ref, s32[1,4224]{1,0:T(1,128)} %constant_dynamic-slice_fusion.ids_ref, s32[1,3840]{1,0:T(1,128)} %broadcast_in_dim.11.wanted_ref, bf16[64,4224]{1,0:T(8,128)(2,1)} %bitcast.17), custom_call_target="tpu_custom_call" | custom-call | flops 1 | bytes 1 | tf_op jit(solution)/shard_map/in_order/pallas_call | solution.py:409
  68.2 0.0 all-gather.4.cloned.1.call-update
  68.2 0.0 copy-done.2
  68.3 0.0 copy-done.3
  68.3 10.4 %all_to_all.20 = bf16[4,2,8,384]{3,2,1,0:T(8,128)(2,1)S(1)} all-to-all(bf16[4,2,8,384]{3,2,1,0:T(8,128)(2,1)S(1)} %copy.21), channel_id=1, replica_groups=mesh['row'=4,'col'=8] {'row'}, dimensions={0} | all-to-all | bytes 98304 | tf_op jit(solution)/shard_map/all_to_all | solution.py:477
  78.7 10.7 %all_to_all.21 = bf16[8,4,2,8,384]{4,3,1,2,0:T(8,128)(2,1)S(1)} all-to-all(bf16[8,4,2,8,384]{4,3,1,2,0:T(8,128)(2,1)S(1)} %broadcast_in_dim.9), channel_id=1, replica_groups=mesh['row'=4,'col'=8] {'col'}, dimensions={0} | all-to-all | bytes 786432 | tf_op jit(solution)/shard_map/all_to_all | solution.py:478
  89.5 0.0 all-gather.6.cloned.1.call-done
  89.5 3.6 %all-to-all-start.3 = ((bf16[8,4,8,4224]{3,2,1,0:T(8,128)(2,1)}), bf16[8,4,8,4224]{3,2,1,0:T(8,128)(2,1)S(1)}, u32[]{:S(2)}, u32[]{:S(2)}) async-start(bf16[8,4,8,4224]{3,2,1,0:T(8,128)(2,1)} %bitcast.16), calls=%async_computation.3 | async-start | bytes 4325376 | tf_op jit(solution)/shard_map/all_to_all | solution.py:483
  93.1 1.3 dynamic_slice.17
  94.4 1.3 constant_dynamic-slice_fusion.2.slab_ids_ref
  95.8 0.8 pad_maximum_fusion
  96.6 2.6 %left_side.1.left_ref = bf16[512,512]{1,0:T(8,128)(2,1)} custom-call(bf16[512,384]{1,0:T(8,128)(2,1)} %bitcast.18, s32[1,384]{1,0:T(1,128)} %constant_dynamic-slice_fusion.2.slab_ids_ref, s32[1,256]{1,0:T(1,128)} %bitcast.23), custom_call_target="tpu_custom_call" | custom-call | flops 1 | bytes 1 | tf_op jit(solution)/shard_map/left_side/pallas_call | solution.py:384
  99.2 21.2 %all-to-all-done.3 = bf16[8,4,8,4224]{3,2,1,0:T(8,128)(2,1)S(1)} async-done(((bf16[8,4,8,4224]{3,2,1,0:T(8,128)(2,1)}), bf16[8,4,8,4224]{3,2,1,0:T(8,128)(2,1)S(1)}, u32[]{:S(2)}, u32[]{:S(2)}) %all-to-all-start.3) | async-done | bytes 2162720 | tf_op jit(solution)/shard_map/all_to_all | solution.py:483
  120.3 0.0 copy-start
  120.3 1.3 copy-done
  121.7 7.1 %in_order.2.refs_0_ = bf16[256,3840]{1,0:T(8,128)(2,1)} custom-call(s32[3]{0:T(128)} %fusion.starts_ref, s32[1,4224]{1,0:T(1,128)} %constant_dynamic-slice_fusion.ids_ref, s32[1,3840]{1,0:T(1,128)} %broadcast_in_dim.11.wanted_ref, bf16[256,4224]{1,0:T(8,128)(2,1)} %bitcast.15), custom_call_target="tpu_custom_call" | custom-call | flops 1 | bytes 1 | tf_op jit(solution)/shard_map/in_order/pallas_call | solution.py:409
  128.7 0.0 all-gather.4.cloned.1.call-done.refs_1_
  128.7 7.6 %product.1 = f32[2,256,3840]{2,1,0:T(8,128)} custom-call(bf16[512,512]{1,0:T(8,128)(2,1)} %left_side.1.left_ref, bf16[256,3840]{1,0:T(8,128)(2,1)} %in_order.2.refs_0_, bf16[256,3840]{1,0:T(8,128)(2,1)} %all-gather.4.cloned.1.call-done.refs_1_), custom_call_target="tpu_custom_call" | custom-call | flops 1 | bytes 1 | tf_op jit(solution)/shard_map/product/pallas_call | solution.py:439
  (7 shorter events, 0.1 us)
Async XLA Ops:
  6.5 82.9 %all-gather.6.cloned.1.call-start = ((), (), s32[]{:S(2)}) async-start(), calls=%async_computation.5 | async-start | bytes 2703360 | tf_op jit(solution)/shard_map/all_gather | solution.py:472
  47.5 20.8 %copy-start.2 = (bf16[4,8,384]{2,1,0:T(8,128)(2,1)S(1)}, bf16[4,8,384]{2,1,0:T(8,128)(2,1)}, u32[]{:S(2)}) copy-start(bf16[4,8,384]{2,1,0:T(8,128)(2,1)} %get-tuple-element.16) | copy-start | bytes 73732
  47.5 20.8 %copy-start.3 = (bf16[4,8,384]{2,1,0:T(8,128)(2,1)S(1)}, bf16[4,8,384]{2,1,0:T(8,128)(2,1)}, u32[]{:S(2)}) copy-start(bf16[4,8,384]{2,1,0:T(8,128)(2,1)} %get-tuple-element.18) | copy-start | bytes 73732
  47.5 15.2 %all-to-all-start = ((bf16[8,8,4224]{2,1,0:T(8,128)(2,1)}), bf16[8,8,4224]{2,1,0:T(8,128)(2,1)S(1)}, u32[]{:S(2)}, u32[]{:S(2)}) async-start(bf16[8,8,4224]{2,1,0:T(8,128)(2,1)} %get-tuple-element.19), calls=%async_computation | async-start | bytes 1081344 | tf_op jit(solution)/shard_map/all_to_all | solution.py:474
  52.8 76.0 %all-gather.4.cloned.1.call-start = ((), (), s32[]{:S(2)}) async-start(), calls=%async_computation.4 | async-start | bytes 2457600 | tf_op jit(solution)/shard_map/all_gather | solution.py:475
  62.7 0.8 copy-start.1
  89.5 30.9 %all-to-all-start.3 = ((bf16[8,4,8,4224]{3,2,1,0:T(8,128)(2,1)}), bf16[8,4,8,4224]{3,2,1,0:T(8,128)(2,1)S(1)}, u32[]{:S(2)}, u32[]{:S(2)}) async-start(bf16[8,4,8,4224]{3,2,1,0:T(8,128)(2,1)} %bitcast.16), calls=%async_computation.3 | async-start | bytes 4325376 | tf_op jit(solution)/shard_map/all_to_all | solution.py:483
  120.3 1.3 copy-start
Sparse Core Ops, SparseCore 0:
  27.5 50.4 all-gather.5
  79.5 42.6 all-gather.3

commit v12 on v10

--- a/solution.py
+++ b/solution.py
@@ -197,7 +197,7 @@
                     second_ref, third_ref, send_ref, slab_ref, cond_a, cond_b, middle, turned, last, sorter, plain_rows, weighted_rows,
                     plain_sorted, weighted_sorted):
     band = pl.program_id(0)
-    planes = 8
+    planes = 4
     pairs = planes // 2
     lane = lax.broadcasted_iota(jnp.int32, (1, LANES), 1)
     low_lanes = lane < HALF
@@ -232,17 +232,17 @@
             store_split(middle, at, blocks)
 
     def second_axis(block):
-        rows = pl.ds(pl.multiple_of(block * pairs * KEEP, pairs * KEEP), pairs * KEEP)
+        rows = pl.ds(pl.multiple_of(block * 4 * KEEP, 4 * KEEP), 4 * KEEP)
         high = second_ref[: 2 * LANES]
         table = jnp.concatenate([high, high, second_ref[2 * LANES :]], 0)
         field = jnp.dot(doubled(middle[rows, :]), table, preferred_element_type=jnp.float32)
         for item in range(2):
             turned[item, rows, :] = field[:, item * LANES : (item + 1) * LANES]
 
-    turns = points // planes // 2 - 1
+    turns = points // 16 - 1
     piece = sorter.shape[0] // (count * turns)
-    first_axis(0)
-    first_axis(1)
+    for part in range(4):
+        first_axis(part)
 
     @pl.loop(1, turns + 1)
     def _(turn):
@@ -251,11 +251,11 @@
         sorter[pl.ds(begin, piece), :] = jnp.where(at == place_ref[...], 1.0, 0.0).astype(jnp.bfloat16)
         for part in range(2):
             second_axis(2 * turn - 2 + part)
-        for part in range(2):
-            first_axis(2 * turn + part)
-
-    second_axis(points // planes - 2)
-    second_axis(points // planes - 1)
+        for part in range(4):
+            first_axis(4 * turn + part)
+
+    for part in range(2):
+        second_axis(2 * turns + part)
 
     for begin in range(0, KEEP, 4):
         both = []
@@ -361,18 +361,24 @@
     )(*energies, val_wave, cond_wave, jnp.asarray(place), *tables)
 
 
-def one_hot(ids_ref, begin, wanted):
-    ids = jnp.broadcast_to(ids_ref[:, pl.ds(begin, LANES)], (LANES, LANES)).T
+def one_hot(ids, wanted):
+    ids = jnp.broadcast_to(ids, (LANES, LANES)).T
     ids = jnp.concatenate([ids] * (wanted.shape[1] // LANES), 1)
     return jnp.where(ids == wanted, 1.0, 0.0).astype(jnp.bfloat16)
 
 
-def left_kernel(slab_ref, slab_ids_ref, slab_wanted_ref, left_ref):
-    rows = slab_wanted_ref.shape[1]
-    choice = jnp.concatenate(
-        [one_hot(slab_ids_ref, begin, slab_wanted_ref[...]) for begin in range(0, slab_ids_ref.shape[1], LANES)], 0
+def left_kernel(row_count, place_ref, slab_ref, ids_ref, wanted_ref, left_ref):
+    rows = wanted_ref.shape[1]
+    col_count = slab_ref.shape[0]
+    group = slab_ref.shape[1] // (2 * row_count)
+    order = [(col, 2 * row) for col in range(col_count) for row in range(row_count)]
+    order += [(col, 2 * row + 1) for row in range(row_count) for col in range(col_count)]
+    slab = [slab_ref[col, at * group : (at + 1) * group, :].astype(jnp.float32) for col, at in order]
+    ids = ids_ref[0]
+    choice = [one_hot(ids[:, begin : begin + LANES], wanted_ref[...]) for begin in range(0, ids.shape[1], LANES)]
+    chosen = jnp.dot(
+        jnp.concatenate(slab, 0).astype(jnp.bfloat16), jnp.concatenate(choice, 0), preferred_element_type=jnp.float32
     )
-    chosen = jnp.dot(slab_ref[...], choice, preferred_element_type=jnp.float32)
     lane = lax.broadcasted_iota(jnp.int32, (1, LANES), 1)
     real_lanes = lane % 2 == 0
     for begin in range(0, chosen.shape[0], LANES):
@@ -383,49 +389,67 @@
         left_ref[rows:, begin : begin + LANES] = jnp.where(real_lanes, after, -before).astype(jnp.bfloat16)
 
 
-def left_side(slab, slab_ids, slab_wanted):
-    vmem = pl.BlockSpec(memory_space=pltpu.VMEM)
+def left_side(plan, place, points_map, slab):
+    pairs = slab.shape[0] * slab.shape[1]
+    ids = jnp.asarray(plan["slab_ids"])[:, None]
     return pl.pallas_call(
-        left_kernel,
-        in_specs=[vmem] * 3,
-        out_specs=vmem,
-        out_shape=jax.ShapeDtypeStruct((2 * slab_wanted.shape[1], slab.shape[0]), jnp.bfloat16),
+        lambda *refs: left_kernel(ids.shape[0], *refs),
+        grid_spec=pltpu.PrefetchScalarGridSpec(
+            num_scalar_prefetch=1,
+            grid=(1,),
+            in_specs=[
+                pl.BlockSpec(slab.shape, lambda n, place: (0, 0, 0)),
+                pl.BlockSpec((1, *ids.shape[1:]), lambda n, place: (place[1], 0, 0)),
+                pl.BlockSpec((1, ROWS_DEV), lambda n, place: (0, place[1])),
+            ],
+            out_specs=pl.BlockSpec((2 * ROWS_DEV, pairs), lambda n, place: (0, 0)),
+        ),
+        out_shape=jax.ShapeDtypeStruct((2 * ROWS_DEV, pairs), jnp.bfloat16),
         compiler_params=pltpu.CompilerParams(vmem_limit_bytes=VMEM_BYTES),
         cost_estimate=pl.CostEstimate(flops=1, bytes_accessed=1, transcendentals=0),
         name="left_side",
-    )(slab, slab_ids, slab_wanted)
-
-
-def order_kernel(starts_ref, ids_ref, wanted_ref, panel_ref, out_ref, hot):
-    start = pl.multiple_of(starts_ref[pl.program_id(0)], LANES)
+    )(place, slab, ids, points_map)
+
+
+def order_kernel(window_starts, place_ref, ids_ref, wanted_ref, panel_ref, out_ref, hot):
+    part = pl.program_id(0)
+    col = place_ref[0]
+    start = 0
+    for block, starts in enumerate(window_starts):
+        for n, value in enumerate(starts):
+            start = jnp.where((col == block) & (part == n), int(value), start)
+    start = pl.multiple_of(start, LANES)
     wanted = wanted_ref[...]
     window = hot.shape[0]
     for begin in range(0, window, LANES):
-        hot[begin : begin + LANES, :] = one_hot(ids_ref, pl.multiple_of(start + begin, LANES), wanted)
+        ids = ids_ref[0, :, pl.ds(pl.multiple_of(start + begin, LANES), LANES)]
+        hot[begin : begin + LANES, :] = one_hot(ids, wanted)
     ordered = jnp.dot(panel_ref[:, pl.ds(start, window)], hot[...], preferred_element_type=jnp.float32)
     out_ref[...] = ordered.astype(jnp.bfloat16)
 
 
-def put_in_order(plan, starts, ids, wanted, panel):
-    columns = wanted.shape[1]
+def put_in_order(plan, place, points_map, panel):
+    columns = points_map.shape[1] // len(plan["buckets"])
     block = columns // PARTS
-    whole = lambda array: pl.BlockSpec(array.shape, lambda n: (0,) * array.ndim)
+    ids = jnp.asarray(plan["ids"])[:, None]
     return pl.pallas_call(
-        order_kernel,
-        grid=(PARTS,),
-        in_specs=[
-            pl.BlockSpec(memory_space=pltpu.SMEM),
-            whole(ids),
-            pl.BlockSpec((1, block), lambda n: (0, n)),
-            whole(panel),
-        ],
-        out_specs=pl.BlockSpec((panel.shape[0], block), lambda n: (0, n)),
+        lambda *refs: order_kernel(plan["starts"].tolist(), *refs),
+        grid_spec=pltpu.PrefetchScalarGridSpec(
+            num_scalar_prefetch=1,
+            grid=(PARTS,),
+            in_specs=[
+                pl.BlockSpec((1, *ids.shape[1:]), lambda n, place: (place[0], 0, 0)),
+                pl.BlockSpec((1, block), lambda n, place: (0, place[0] * PARTS + n)),
+                pl.BlockSpec(panel.shape, lambda n, place: (0, 0)),
+            ],
+            out_specs=pl.BlockSpec((panel.shape[0], block), lambda n, place: (0, n)),
+            scratch_shapes=[pltpu.VMEM((plan["window"], block), jnp.bfloat16)],
+        ),
         out_shape=jax.ShapeDtypeStruct((panel.shape[0], columns), jnp.bfloat16),
-        scratch_shapes=[pltpu.VMEM((plan["window"], block), jnp.bfloat16)],
         compiler_params=pltpu.CompilerParams(vmem_limit_bytes=VMEM_BYTES, dimension_semantics=("arbitrary",)),
         cost_estimate=pl.CostEstimate(flops=1, bytes_accessed=1, transcendentals=0),
         name="in_order",
-    )(starts, ids, wanted, panel)
+    )(place, ids, points_map, panel)
 
 
 def product_kernel(left_ref, *refs):
@@ -439,7 +463,7 @@
 
 def product(left, ordered):
     rows, columns = left.shape[0] // 2, ordered[0].shape[1]
-    block = columns // (2 * PARTS) // LANES * LANES
+    block = 6 * LANES
     return pl.pallas_call(
         product_kernel,
         grid=(pl.cdiv(columns, block),),
@@ -459,12 +483,8 @@
     col_count = lax.axis_size("col")
     col, row = lax.axis_index("col"), lax.axis_index("row")
     plan = make_plan(points, grid_map.shape[0], col_count, ROWS_DEV * row_count, row_count)
-    width = grid_map.shape[0] // col_count
-    starts = lax.dynamic_index_in_dim(jnp.asarray(plan["starts"]), col, 0, keepdims=False)
-    ids = lax.dynamic_slice(jnp.asarray(plan["ids"]), (col, 0), (1, plan["lanes"]))
-    slab_ids = lax.dynamic_slice(jnp.asarray(plan["slab_ids"]), (row, 0), (1, plan["slab_lanes"]))
-    wanted = lax.dynamic_slice(grid_map, (col * width,), (width,))[None]
-    slab_wanted = lax.dynamic_slice(grid_map, (row * ROWS_DEV,), (ROWS_DEV,))[None]
+    place = jnp.stack([col, row]).astype(jnp.int32)
+    points_map = grid_map[None]
     chunk = bands // 2
     energies = (band_owner, cond_energy, val_energy)
     slabs = []
@@ -476,17 +496,17 @@
             early = lax.all_gather(send, "row", axis=1)
         else:
             mine = lax.all_to_all(send, "col", split_axis=0, concat_axis=0, tiled=True).reshape(-1, plan["lanes"])
-            mine = put_in_order(plan, starts, ids, wanted, mine)
+            mine = put_in_order(plan, place, points_map, mine)
             last = lax.all_gather(mine, "row", axis=0, tiled=True)
-    slab, _ = lax.optimization_barrier((jnp.stack(slabs, 1), mine))
-    slab = lax.all_to_all(slab, "row", split_axis=0, concat_axis=0, tiled=True)
-    slab = lax.all_to_all(jnp.broadcast_to(slab, (col_count, *slab.shape)), "col", split_axis=0, concat_axis=0)
+    slab, _ = lax.optimization_barrier((jnp.concatenate(slabs, 1), mine))
+    slab = lax.all_to_all(slab, "row", split_axis=0, concat_axis=0, tiled=True).reshape(-1, plan["slab_lanes"])
+    slab = jnp.broadcast_to(slab, (col_count, *slab.shape))
     early, slab = lax.optimization_barrier((early, slab))
-    slab = [slab[:, :, 0], slab[:, :, 1].transpose(1, 0, 2, 3)]
-    slab = jnp.stack([part.reshape(-1, plan["slab_lanes"]) for part in slab]).reshape(-1, plan["slab_lanes"])
-    left = left_side(slab, slab_ids, slab_wanted)
     early = lax.all_to_all(early, "col", split_axis=0, concat_axis=0, tiled=True).reshape(-1, plan["lanes"])
-    return product(left, [put_in_order(plan, starts, ids, wanted, early), last])
+    early, slab = lax.optimization_barrier((early, slab))
+    slab = lax.all_to_all(slab, "col", split_axis=0, concat_axis=0, tiled=True)
+    early = put_in_order(plan, place, points_map, early)
+    return product(left_side(plan, place, points_map, slab), [early, last])
 
 
 def solution(mesh):

time: 142 us -> 141 us (level)
  blocking collectives: 21.6 us -> 42 us
  waiting for transfers between devices: 26.9 us -> 9.77 us
  local copies, waits for them, and re-layouts: 9.05 us -> 2.33 us
  Pallas kernels: 59.5 us -> 62.4 us
    all_to_all x1, waiting for transfers between devices: 21.2 us -> 0.51 us  [on_device(): slab = lax.all_to_all(slab, 'col', split_axis=0, concat_axis=0, tiled=True)]
    all_to_all x2, blocking collectives: 21.6 us -> 42 us  [the longest x1 31.6 us: on_device(): lax.all_to_all(early, 'col', split_axis=0, concat_axis=0, tiled=True)]
    dynamic_slice x4 -> x0, local copies, waits for them, and re-layouts: 4.95 us -> none  [the longest x1 1.51 us: on_device(): lax.dynamic_slice(jnp.asarray(plan['ids']), (col, 0), (1, plan['lanes']))]
    all_to_all x1, waiting for transfers between devices: 5.72 us -> 9.23 us  [on_device(): lax.all_to_all(send, 'col', split_axis=0, concat_axis=0, tiled=True)]
    pallas_call x3, Pallas kernels: 14.3 us -> 16.4 us  [the longest x2 13.1 us: put_in_order(): pl.pallas_call(lambda *refs: order_kernel(plan['starts'].tolist(), *refs)...]
  transfers between devices with their start and end apart: 4 -> 4, of which waited for: 2 -> 2; matrix products, arithmetic and copies ran while one was open for 5% -> 1% of each run, Pallas kernels for 23% -> 25%
where the time goes in v12:
time: 141 us; the launch traced here: 140 us
  Pallas kernels  62.4 us (44%)
  blocking collectives  42 us (30%)
  between operations  14.1 us (10%)
  waiting for transfers between devices  9.77 us (7%)
  starting transfers between devices  8.81 us (6%)
  local copies, waits for them, and re-layouts  2.33 us (2%)
    pallas_call x2, Pallas kernels, spectra(): pl.pallas_call(kernel, grid=(count,), in_specs=[pl.BlockSpec(memory_space...  38.4 us
    all_to_all x1, blocking collectives, on_device(): lax.all_to_all(early, 'col', split_axis=0, concat_axis=0, tiled=True)  31.6 us
    pallas_call x2, Pallas kernels, put_in_order(): pl.pallas_call(lambda *refs: order_kernel(plan['starts'].tolist(), *refs)...  13.1 us
    all_to_all x1, blocking collectives, on_device(): lax.all_to_all(slab, 'row', split_axis=0, concat_axis=0, tiled=True)  10.4 us
    all_to_all x1, waiting for transfers between devices, on_device(): lax.all_to_all(send, 'col', split_axis=0, concat_axis=0, tiled=True)  9.23 us
    pallas_call x1, Pallas kernels, product(): pl.pallas_call(product_kernel, grid=(pl.cdiv(columns, block),), in_specs=...  7.64 us
    all_to_all x1, starting transfers between devices, on_device(): lax.all_to_all(send, 'col', split_axis=0, concat_axis=0, tiled=True)  5.32 us
    all_to_all x1, starting transfers between devices, on_device(): slab = lax.all_to_all(slab, 'col', split_axis=0, concat_axis=0, tiled=True)  3.45 us
  transfers between devices with their start and end apart: 4, of which 2 were waited for; matrix products, arithmetic and copies ran while one was open for 1% of the time, Pallas kernels for 25%

profile of v12, /device:TPU:0, one launch (start us, length us, event | category | flops | bytes accessed | tf_op | source)
XLA Modules:
  0.0 140.1 jit_solution(5004116044962757636)
XLA Ops:
  6.5 0.0 all-gather.6.cloned.1.call-start
  7.2 19.2 %spectra.2 = (bf16[8,8,4224]{2,1,0:T(8,128)(2,1)}, bf16[4,8,384]{2,1,0:T(8,128)(2,1)}) custom-call(s32[1]{0:T(128)S(6)} %copy.17.refs_0_, f32[32]{0:T(128)} %refs_1_.3, f32[8]{0:T(128)} %refs_2_.3, bf16[8,64,64,128]{3,2,1,0:T(8,128)(2,1)} %refs_3_.3, bf16[1,64,64,128]{3,2,1,0:T(8,128)(2,1)} %refs_4_.2, s32[1,1280]{1,0:T(1,128)} %constant.23.clone.refs_5_, ...), custom_call_target="tpu_custom_call" | custom-call | flops 1 | bytes 1 | tf_op jit(solution)/shard_map/spectra/pallas_call | solution.py:332
  26.4 0.0 all-gather.6.cloned.1.call-update
  26.4 19.2 %spectra.3 = (bf16[8,8,4224]{2,1,0:T(8,128)(2,1)}, bf16[4,8,384]{2,1,0:T(8,128)(2,1)}) custom-call(s32[1]{0:T(128)S(6)} %copy.17.refs_0_, f32[32]{0:T(128)} %refs_1_.3, f32[8]{0:T(128)} %refs_2_.3, bf16[8,64,64,128]{3,2,1,0:T(8,128)(2,1)} %refs_3_.3, bf16[1,64,64,128]{3,2,1,0:T(8,128)(2,1)} %refs_4_.2, s32[1,1280]{1,0:T(1,128)} %constant.23.clone.refs_5_, ...), custom_call_target="tpu_custom_call" | custom-call | flops 1 | bytes 1 | tf_op jit(solution)/shard_map/spectra/pallas_call | solution.py:332
  45.7 0.0 copy-start.2
  45.7 0.0 copy-start.3
  45.7 5.3 %all-to-all-start = ((bf16[8,8,4224]{2,1,0:T(8,128)(2,1)}), bf16[8,8,4224]{2,1,0:T(8,128)(2,1)S(1)}, u32[]{:S(2)}, u32[]{:S(2)}) async-start(bf16[8,8,4224]{2,1,0:T(8,128)(2,1)} %get-tuple-element.21), calls=%async_computation | async-start | bytes 1081344 | tf_op jit(solution)/shard_map/all_to_all | solution.py:498
  51.0 0.0 all-gather.4.cloned.1.call-start
  51.0 0.6 pad_add_fusion.refs_0_
  51.7 9.2 %all-to-all-done = bf16[8,8,4224]{2,1,0:T(8,128)(2,1)S(1)} async-done(((bf16[8,8,4224]{2,1,0:T(8,128)(2,1)}), bf16[8,8,4224]{2,1,0:T(8,128)(2,1)S(1)}, u32[]{:S(2)}, u32[]{:S(2)}) %all-to-all-start) | async-done | bytes 540704 | tf_op jit(solution)/shard_map/all_to_all | solution.py:498
  60.9 0.0 copy-start
  60.9 0.8 copy-done
  61.7 5.4 %in_order.2 = bf16[64,3840]{1,0:T(8,128)(2,1)} custom-call(s32[2]{0:T(128)} %pad_add_fusion.refs_0_, s32[8,1,4224]{2,1,0:T(1,128)} %constant.28.refs_1_, s32[1,30720]{1,0:T(1,128)} %bitcast.10, bf16[64,4224]{1,0:T(8,128)(2,1)} %bitcast.9), custom_call_target="tpu_custom_call" | custom-call | flops 1 | bytes 1 | tf_op jit(solution)/shard_map/in_order/pallas_call | solution.py:435
  67.1 0.0 all-gather.4.cloned.1.call-update
  67.1 0.0 copy-done.2
  67.1 0.0 copy-done.3
  67.2 10.4 %all_to_all.20 = bf16[4,16,384]{2,1,0:T(8,128)(2,1)S(1)} all-to-all(bf16[4,16,384]{2,1,0:T(8,128)(2,1)S(1)} %pad_maximum_fusion), channel_id=1, replica_groups=mesh['row'=4,'col'=8] {'row'}, dimensions={0} | all-to-all | bytes 98304 | tf_op jit(solution)/shard_map/all_to_all | solution.py:502
  77.5 0.0 all-gather.6.cloned.1.call-done
  77.5 0.8 broadcast_in_dim.15
  78.3 31.6 %all_to_all.21 = bf16[8,4,8,4224]{3,2,1,0:T(8,128)(2,1)} all-to-all(bf16[8,4,8,4224]{3,2,1,0:T(8,128)(2,1)} %bitcast.8), channel_id=1, replica_groups=mesh['row'=4,'col'=8] {'col'}, dimensions={0} | all-to-all | bytes 4325376 | tf_op jit(solution)/shard_map/all_to_all | solution.py:505
  109.9 3.5 %all-to-all-start.3 = ((bf16[8,64,384]{2,1,0:T(8,128)(2,1)}), bf16[8,64,384]{2,1,0:T(8,128)(2,1)S(1)}, u32[]{:S(2)}, u32[]{:S(2)}) async-start(bf16[8,64,384]{2,1,0:T(8,128)(2,1)} %broadcast_in_dim.15), calls=%async_computation.3 | async-start | bytes 786432 | tf_op jit(solution)/shard_map/all_to_all | solution.py:507
  113.4 7.8 %in_order.3.refs_0_ = bf16[256,3840]{1,0:T(8,128)(2,1)} custom-call(s32[2]{0:T(128)} %pad_add_fusion.refs_0_, s32[8,1,4224]{2,1,0:T(1,128)} %constant.28.refs_1_, s32[1,30720]{1,0:T(1,128)} %bitcast.11, bf16[256,4224]{1,0:T(8,128)(2,1)} %bitcast.7), custom_call_target="tpu_custom_call" | custom-call | flops 1 | bytes 1 | tf_op jit(solution)/shard_map/in_order/pallas_call | solution.py:435
  121.2 0.5 all-to-all-done.3.refs_1_
  121.7 0.0 copy-start.1
  121.7 0.7 copy-done.1
  122.4 3.2 %left_side.1.left_ref = bf16[512,512]{1,0:T(8,128)(2,1)} custom-call(s32[2]{0:T(128)} %pad_add_fusion.refs_0_, bf16[8,64,384]{2,1,0:T(8,128)(2,1)} %copy-done.1, s32[4,1,384]{2,1,0:T(1,128)} %constant.29.refs_2_, s32[1,30720]{1,0:T(1,128)} %bitcast.12), custom_call_target="tpu_custom_call" | custom-call | flops 1 | bytes 1 | tf_op jit(solution)/shard_map/left_side/pallas_call | solution.py:395
  125.6 0.0 all-gather.4.cloned.1.call-done.refs_1_
  125.6 7.6 %product.1 = f32[2,256,3840]{2,1,0:T(8,128)} custom-call(bf16[512,512]{1,0:T(8,128)(2,1)} %left_side.1.left_ref, bf16[256,3840]{1,0:T(8,128)(2,1)} %in_order.3.refs_0_, bf16[256,3840]{1,0:T(8,128)(2,1)} %all-gather.4.cloned.1.call-done.refs_1_), custom_call_target="tpu_custom_call" | custom-call | flops 1 | bytes 1 | tf_op jit(solution)/shard_map/product/pallas_call | solution.py:467
  (1 shorter events, 0.0 us)
Async XLA Ops:
  6.5 71.0 %all-gather.6.cloned.1.call-start = ((), (), s32[]{:S(2)}) async-start(), calls=%async_computation.5 | async-start | bytes 2703360 | tf_op jit(solution)/shard_map/all_gather | solution.py:496
  45.7 21.5 %copy-start.2 = (bf16[4,8,384]{2,1,0:T(8,128)(2,1)S(1)}, bf16[4,8,384]{2,1,0:T(8,128)(2,1)}, u32[]{:S(2)}) copy-start(bf16[4,8,384]{2,1,0:T(8,128)(2,1)} %get-tuple-element.18) | copy-start | bytes 73732
  45.7 21.5 %copy-start.3 = (bf16[4,8,384]{2,1,0:T(8,128)(2,1)S(1)}, bf16[4,8,384]{2,1,0:T(8,128)(2,1)}, u32[]{:S(2)}) copy-start(bf16[4,8,384]{2,1,0:T(8,128)(2,1)} %get-tuple-element.20) | copy-start | bytes 73732
  45.7 15.2 %all-to-all-start = ((bf16[8,8,4224]{2,1,0:T(8,128)(2,1)}), bf16[8,8,4224]{2,1,0:T(8,128)(2,1)S(1)}, u32[]{:S(2)}, u32[]{:S(2)}) async-start(bf16[8,8,4224]{2,1,0:T(8,128)(2,1)} %get-tuple-element.21), calls=%async_computation | async-start | bytes 1081344 | tf_op jit(solution)/shard_map/all_to_all | solution.py:498
  51.0 74.7 %all-gather.4.cloned.1.call-start = ((), (), s32[]{:S(2)}) async-start(), calls=%async_computation.4 | async-start | bytes 2457600 | tf_op jit(solution)/shard_map/all_gather | solution.py:500
  60.9 0.8 copy-start
  109.9 11.7 %all-to-all-start.3 = ((bf16[8,64,384]{2,1,0:T(8,128)(2,1)}), bf16[8,64,384]{2,1,0:T(8,128)(2,1)S(1)}, u32[]{:S(2)}, u32[]{:S(2)}) async-start(bf16[8,64,384]{2,1,0:T(8,128)(2,1)} %broadcast_in_dim.15), calls=%async_computation.3 | async-start | bytes 786432 | tf_op jit(solution)/shard_map/all_to_all | solution.py:507
  121.7 0.7 copy-start.1
Sparse Core Ops, SparseCore 0:
  26.6 50.0 all-gather.5
  78.2 43.0 all-gather.3

commit v13 on v12

--- a/solution.py
+++ b/solution.py
@@ -141,11 +141,11 @@
         return high, (table - high.astype(np.float64)).astype(jnp.bfloat16)
 
     high, low = parts(one[..., :KEEP].reshape(2 * points, 2 * KEEP).T)
-    first = np.concatenate([high, high, low], 1)
+    first = np.block([[high, high], [low, np.zeros_like(low)]])
     second = np.concatenate(parts(two.reshape(4 * points, 4 * HALF)), 0)
     halves = two[..., :KEEP].reshape(2, 2, points // 2, 2, 4 * KEEP).transpose(0, 1, 3, 2, 4)
     high, low = parts(halves.reshape(4 * points, 4 * KEEP).T)
-    third = np.concatenate([high, high, low], 1)
+    third = np.block([[high, high], [low, np.zeros_like(low)]])
     return [jnp.asarray(table) for table in (first, second, third)]
 
 
@@ -167,7 +167,9 @@
 
 
 def contract_last(table, stored):
-    return lax.dot_general(table, doubled(stored), (((1,), (1,)), ((), ())), preferred_element_type=jnp.float32)
+    both = lax.dot_general(table, stored, (((1,), (1,)), ((), ())), preferred_element_type=jnp.float32)
+    rows = both.shape[0] // 2
+    return both[:rows] + both[rows:]
 
 
 def pack_pieces(pieces, width, source, rows, lane, out):
@@ -197,7 +199,7 @@
                     second_ref, third_ref, send_ref, slab_ref, cond_a, cond_b, middle, turned, last, sorter, plain_rows, weighted_rows,
                     plain_sorted, weighted_sorted):
     band = pl.program_id(0)
-    planes = 4
+    planes = 8
     pairs = planes // 2
     lane = lax.broadcasted_iota(jnp.int32, (1, LANES), 1)
     low_lanes = lane < HALF
@@ -241,7 +243,7 @@
 
     turns = points // 16 - 1
     piece = sorter.shape[0] // (count * turns)
-    for part in range(4):
+    for part in range(2):
         first_axis(part)
 
     @pl.loop(1, turns + 1)
@@ -251,8 +253,8 @@
         sorter[pl.ds(begin, piece), :] = jnp.where(at == place_ref[...], 1.0, 0.0).astype(jnp.bfloat16)
         for part in range(2):
             second_axis(2 * turn - 2 + part)
-        for part in range(4):
-            first_axis(4 * turn + part)
+        for part in range(2):
+            first_axis(2 * turn + part)
 
     for part in range(2):
         second_axis(2 * turns + part)
@@ -411,14 +413,8 @@
     )(place, slab, ids, points_map)
 
 
-def order_kernel(window_starts, place_ref, ids_ref, wanted_ref, panel_ref, out_ref, hot):
-    part = pl.program_id(0)
-    col = place_ref[0]
-    start = 0
-    for block, starts in enumerate(window_starts):
-        for n, value in enumerate(starts):
-            start = jnp.where((col == block) & (part == n), int(value), start)
-    start = pl.multiple_of(start, LANES)
+def order_kernel(place_ref, starts_ref, ids_ref, wanted_ref, panel_ref, out_ref, hot):
+    start = pl.multiple_of(starts_ref[place_ref[0] * PARTS + pl.program_id(0)], LANES)
     wanted = wanted_ref[...]
     window = hot.shape[0]
     for begin in range(0, window, LANES):
@@ -433,23 +429,23 @@
     block = columns // PARTS
     ids = jnp.asarray(plan["ids"])[:, None]
     return pl.pallas_call(
-        lambda *refs: order_kernel(plan["starts"].tolist(), *refs),
+        order_kernel,
         grid_spec=pltpu.PrefetchScalarGridSpec(
-            num_scalar_prefetch=1,
+            num_scalar_prefetch=2,
             grid=(PARTS,),
             in_specs=[
-                pl.BlockSpec((1, *ids.shape[1:]), lambda n, place: (place[0], 0, 0)),
-                pl.BlockSpec((1, block), lambda n, place: (0, place[0] * PARTS + n)),
-                pl.BlockSpec(panel.shape, lambda n, place: (0, 0)),
+                pl.BlockSpec((1, *ids.shape[1:]), lambda n, place, starts: (place[0], 0, 0)),
+                pl.BlockSpec((1, block), lambda n, place, starts: (0, place[0] * PARTS + n)),
+                pl.BlockSpec(panel.shape, lambda n, place, starts: (0, 0)),
             ],
-            out_specs=pl.BlockSpec((panel.shape[0], block), lambda n, place: (0, n)),
+            out_specs=pl.BlockSpec((panel.shape[0], block), lambda n, place, starts: (0, n)),
             scratch_shapes=[pltpu.VMEM((plan["window"], block), jnp.bfloat16)],
         ),
         out_shape=jax.ShapeDtypeStruct((panel.shape[0], columns), jnp.bfloat16),
         compiler_params=pltpu.CompilerParams(vmem_limit_bytes=VMEM_BYTES, dimension_semantics=("arbitrary",)),
         cost_estimate=pl.CostEstimate(flops=1, bytes_accessed=1, transcendentals=0),
         name="in_order",
-    )(place, ids, points_map, panel)
+    )(place, jnp.asarray(plan["starts"].reshape(-1)), ids, points_map, panel)
 
 
 def product_kernel(left_ref, *refs):

time: 141 us -> 139 us (0.986)
  Pallas kernels: 62.4 us -> 59.7 us
    pallas_call x2, Pallas kernels: 38.4 us -> 35.8 us  [spectra(): pl.pallas_call(kernel, grid=(count,), in_specs=[pl.BlockSpec(memory_space...]
  transfers between devices with their start and end apart: 4 -> 4, of which waited for: 2 -> 3; matrix products, arithmetic and copies ran while one was open for 1% -> 1% of each run, Pallas kernels for 25% -> 25%
where the time goes in v13:
time: 139 us
  Pallas kernels  59.7 us (43%)
  blocking collectives  42.3 us (30%)
  between operations  14.1 us (10%)
  waiting for transfers between devices  10.7 us (8%)
  starting transfers between devices  8.81 us (6%)
  local copies, waits for them, and re-layouts  2.33 us (2%)
    pallas_call x2, Pallas kernels, spectra(): pl.pallas_call(kernel, grid=(count,), in_specs=[pl.BlockSpec(memory_space...  35.8 us
    all_to_all x1, blocking collectives, on_device(): lax.all_to_all(early, 'col', split_axis=0, concat_axis=0, tiled=True)  31.6 us
    pallas_call x2, Pallas kernels, put_in_order(): pl.pallas_call(order_kernel, grid_spec=pltpu.PrefetchScalarGridSpec(num_s...  13.1 us
    all_to_all x1, blocking collectives, on_device(): lax.all_to_all(slab, 'row', split_axis=0, concat_axis=0, tiled=True)  10.7 us
    all_to_all x1, waiting for transfers between devices, on_device(): lax.all_to_all(send, 'col', split_axis=0, concat_axis=0, tiled=True)  9.23 us
    pallas_call x1, Pallas kernels, product(): pl.pallas_call(product_kernel, grid=(pl.cdiv(columns, block),), in_specs=...  7.64 us
    all_to_all x1, starting transfers between devices, on_device(): lax.all_to_all(send, 'col', split_axis=0, concat_axis=0, tiled=True)  5.32 us
    all_to_all x1, starting transfers between devices, on_device(): slab = lax.all_to_all(slab, 'col', split_axis=0, concat_axis=0, tiled=True)  3.45 us
  transfers between devices with their start and end apart: 4, of which 3 were waited for; matrix products, arithmetic and copies ran while one was open for 1% of the time, Pallas kernels for 25%

profile of v13, /device:TPU:0, one launch (start us, length us, event | category | flops | bytes accessed | tf_op | source)
XLA Modules:
  0.0 138.7 jit_solution(12300032335396062321)
XLA Ops:
  6.5 0.0 all-gather.6.cloned.1.call-start
  7.2 17.9 %spectra.2 = (bf16[8,8,4224]{2,1,0:T(8,128)(2,1)}, bf16[4,8,384]{2,1,0:T(8,128)(2,1)}) custom-call(s32[1]{0:T(128)S(6)} %copy.19.refs_0_, f32[32]{0:T(128)} %refs_1_.3, f32[8]{0:T(128)} %refs_2_.3, bf16[8,64,64,128]{3,2,1,0:T(8,128)(2,1)} %refs_3_.3, bf16[1,64,64,128]{3,2,1,0:T(8,128)(2,1)} %refs_4_.2, s32[1,1280]{1,0:T(1,128)} %constant.25.clone.refs_5_, ...), custom_call_target="tpu_custom_call" | custom-call | flops 1 | bytes 1 | tf_op jit(solution)/shard_map/spectra/pallas_call | solution.py:334
  25.1 0.0 all-gather.6.cloned.1.call-update
  25.1 17.9 %spectra.3 = (bf16[8,8,4224]{2,1,0:T(8,128)(2,1)}, bf16[4,8,384]{2,1,0:T(8,128)(2,1)}) custom-call(s32[1]{0:T(128)S(6)} %copy.19.refs_0_, f32[32]{0:T(128)} %refs_1_.3, f32[8]{0:T(128)} %refs_2_.3, bf16[8,64,64,128]{3,2,1,0:T(8,128)(2,1)} %refs_3_.3, bf16[1,64,64,128]{3,2,1,0:T(8,128)(2,1)} %refs_4_.2, s32[1,1280]{1,0:T(1,128)} %constant.25.clone.refs_5_, ...), custom_call_target="tpu_custom_call" | custom-call | flops 1 | bytes 1 | tf_op jit(solution)/shard_map/spectra/pallas_call | solution.py:334
  43.0 0.0 copy-start.2
  43.0 0.0 copy-start.3
  43.0 5.3 %all-to-all-start = ((bf16[8,8,4224]{2,1,0:T(8,128)(2,1)}), bf16[8,8,4224]{2,1,0:T(8,128)(2,1)S(1)}, u32[]{:S(2)}, u32[]{:S(2)}) async-start(bf16[8,8,4224]{2,1,0:T(8,128)(2,1)} %get-tuple-element.21), calls=%async_computation | async-start | bytes 1081344 | tf_op jit(solution)/shard_map/all_to_all | solution.py:494
  48.3 0.0 all-gather.4.cloned.1.call-start
  48.4 0.6 pad_add_fusion.place_ref.refs_0_
  49.0 9.2 %all-to-all-done = bf16[8,8,4224]{2,1,0:T(8,128)(2,1)S(1)} async-done(((bf16[8,8,4224]{2,1,0:T(8,128)(2,1)}), bf16[8,8,4224]{2,1,0:T(8,128)(2,1)S(1)}, u32[]{:S(2)}, u32[]{:S(2)}) %all-to-all-start) | async-done | bytes 540704 | tf_op jit(solution)/shard_map/all_to_all | solution.py:494
  58.2 0.0 copy-start
  58.2 0.8 copy-done
  59.0 5.4 %in_order.2 = bf16[64,3840]{1,0:T(8,128)(2,1)} custom-call(s32[2]{0:T(128)} %pad_add_fusion.place_ref.refs_0_, s32[24]{0:T(128)} %constant.27.clone.starts_ref, s32[8,1,4224]{2,1,0:T(1,128)} %constant.31.ids_ref, s32[1,30720]{1,0:T(1,128)} %bitcast.10, bf16[64,4224]{1,0:T(8,128)(2,1)} %bitcast.8), custom_call_target="tpu_custom_call" | custom-call | flops 1 | bytes 1 | tf_op jit(solution)/shard_map/in_order/pallas_call | solution.py:431
  64.4 0.0 all-gather.4.cloned.1.call-update
  64.4 0.0 copy-done.2
  64.4 0.0 copy-done.3
  64.4 10.7 %all_to_all.20 = bf16[4,16,384]{2,1,0:T(8,128)(2,1)S(1)} all-to-all(bf16[4,16,384]{2,1,0:T(8,128)(2,1)S(1)} %pad_maximum_fusion), channel_id=1, replica_groups=mesh['row'=4,'col'=8] {'row'}, dimensions={0} | all-to-all | bytes 98304 | tf_op jit(solution)/shard_map/all_to_all | solution.py:498
  75.2 1.0 all-gather.6.cloned.1.call-done
  76.1 0.8 broadcast_in_dim.15
  76.9 31.6 %all_to_all.21 = bf16[8,4,8,4224]{3,2,1,0:T(8,128)(2,1)} all-to-all(bf16[8,4,8,4224]{3,2,1,0:T(8,128)(2,1)} %bitcast.9), channel_id=1, replica_groups=mesh['row'=4,'col'=8] {'col'}, dimensions={0} | all-to-all | bytes 4325376 | tf_op jit(solution)/shard_map/all_to_all | solution.py:501
  108.5 3.5 %all-to-all-start.3 = ((bf16[8,64,384]{2,1,0:T(8,128)(2,1)}), bf16[8,64,384]{2,1,0:T(8,128)(2,1)S(1)}, u32[]{:S(2)}, u32[]{:S(2)}) async-start(bf16[8,64,384]{2,1,0:T(8,128)(2,1)} %broadcast_in_dim.15), calls=%async_computation.3 | async-start | bytes 786432 | tf_op jit(solution)/shard_map/all_to_all | solution.py:503
  112.0 7.8 %in_order.3.refs_0_ = bf16[256,3840]{1,0:T(8,128)(2,1)} custom-call(s32[2]{0:T(128)} %pad_add_fusion.place_ref.refs_0_, s32[24]{0:T(128)} %constant.27.clone.starts_ref, s32[8,1,4224]{2,1,0:T(1,128)} %constant.31.ids_ref, s32[1,30720]{1,0:T(1,128)} %bitcast.11, bf16[256,4224]{1,0:T(8,128)(2,1)} %bitcast.7), custom_call_target="tpu_custom_call" | custom-call | flops 1 | bytes 1 | tf_op jit(solution)/shard_map/in_order/pallas_call | solution.py:431
  119.8 0.5 all-to-all-done.3.refs_1_
  120.3 0.0 copy-start.1
  120.3 0.7 copy-done.1
  121.0 3.2 %left_side.1.left_ref = bf16[512,512]{1,0:T(8,128)(2,1)} custom-call(s32[2]{0:T(128)} %pad_add_fusion.place_ref.refs_0_, bf16[8,64,384]{2,1,0:T(8,128)(2,1)} %copy-done.1, s32[4,1,384]{2,1,0:T(1,128)} %constant.32.refs_2_, s32[1,30720]{1,0:T(1,128)} %bitcast.12), custom_call_target="tpu_custom_call" | custom-call | flops 1 | bytes 1 | tf_op jit(solution)/shard_map/left_side/pallas_call | solution.py:397
  124.2 0.0 all-gather.4.cloned.1.call-done.refs_1_
  124.2 7.6 %product.1 = f32[2,256,3840]{2,1,0:T(8,128)} custom-call(bf16[512,512]{1,0:T(8,128)(2,1)} %left_side.1.left_ref, bf16[256,3840]{1,0:T(8,128)(2,1)} %in_order.3.refs_0_, bf16[256,3840]{1,0:T(8,128)(2,1)} %all-gather.4.cloned.1.call-done.refs_1_), custom_call_target="tpu_custom_call" | custom-call | flops 1 | bytes 1 | tf_op jit(solution)/shard_map/product/pallas_call | solution.py:463
  (1 shorter events, 0.0 us)
Async XLA Ops:
  6.5 69.6 %all-gather.6.cloned.1.call-start = ((), (), s32[]{:S(2)}) async-start(), calls=%async_computation.5 | async-start | bytes 2703360 | tf_op jit(solution)/shard_map/all_gather | solution.py:492
  43.0 21.4 %copy-start.2 = (bf16[4,8,384]{2,1,0:T(8,128)(2,1)S(1)}, bf16[4,8,384]{2,1,0:T(8,128)(2,1)}, u32[]{:S(2)}) copy-start(bf16[4,8,384]{2,1,0:T(8,128)(2,1)} %get-tuple-element.18) | copy-start | bytes 73732
  43.0 21.4 %copy-start.3 = (bf16[4,8,384]{2,1,0:T(8,128)(2,1)S(1)}, bf16[4,8,384]{2,1,0:T(8,128)(2,1)}, u32[]{:S(2)}) copy-start(bf16[4,8,384]{2,1,0:T(8,128)(2,1)} %get-tuple-element.20) | copy-start | bytes 73732
  43.0 15.2 %all-to-all-start = ((bf16[8,8,4224]{2,1,0:T(8,128)(2,1)}), bf16[8,8,4224]{2,1,0:T(8,128)(2,1)S(1)}, u32[]{:S(2)}, u32[]{:S(2)}) async-start(bf16[8,8,4224]{2,1,0:T(8,128)(2,1)} %get-tuple-element.21), calls=%async_computation | async-start | bytes 1081344 | tf_op jit(solution)/shard_map/all_to_all | solution.py:494
  48.3 75.9 %all-gather.4.cloned.1.call-start = ((), (), s32[]{:S(2)}) async-start(), calls=%async_computation.4 | async-start | bytes 2457600 | tf_op jit(solution)/shard_map/all_gather | solution.py:496
  58.2 0.8 copy-start
  108.5 11.7 %all-to-all-start.3 = ((bf16[8,64,384]{2,1,0:T(8,128)(2,1)}), bf16[8,64,384]{2,1,0:T(8,128)(2,1)S(1)}, u32[]{:S(2)}, u32[]{:S(2)}) async-start(bf16[8,64,384]{2,1,0:T(8,128)(2,1)} %broadcast_in_dim.15), calls=%async_computation.3 | async-start | bytes 786432 | tf_op jit(solution)/shard_map/all_to_all | solution.py:503
  120.3 0.7 copy-start.1
Sparse Core Ops, SparseCore 0:
  25.2 50.8 all-gather.5
  77.7 42.2 all-gather.3

commit v14 on v13

--- a/solution.py
+++ b/solution.py
@@ -15,7 +15,7 @@
 KEEP = 40
 ORIGIN = KEEP // 2
 PARITY_LANES = 896
-PARTS = 3
+PARTS = 5
 
 
 def round_up(value, step):
@@ -369,7 +369,7 @@
     return jnp.where(ids == wanted, 1.0, 0.0).astype(jnp.bfloat16)
 
 
-def left_kernel(row_count, place_ref, slab_ref, ids_ref, wanted_ref, left_ref):
+def make_left(row_count, slab_ref, ids_ref, wanted_ref, left):
     rows = wanted_ref.shape[1]
     col_count = slab_ref.shape[0]
     group = slab_ref.shape[1] // (2 * row_count)
@@ -387,30 +387,8 @@
         turned = chosen[begin : begin + LANES].T
         after = pltpu.roll(turned, LANES - 1, 1)
         before = pltpu.roll(turned, 1, 1)
-        left_ref[:rows, begin : begin + LANES] = turned.astype(jnp.bfloat16)
-        left_ref[rows:, begin : begin + LANES] = jnp.where(real_lanes, after, -before).astype(jnp.bfloat16)
-
-
-def left_side(plan, place, points_map, slab):
-    pairs = slab.shape[0] * slab.shape[1]
-    ids = jnp.asarray(plan["slab_ids"])[:, None]
-    return pl.pallas_call(
-        lambda *refs: left_kernel(ids.shape[0], *refs),
-        grid_spec=pltpu.PrefetchScalarGridSpec(
-            num_scalar_prefetch=1,
-            grid=(1,),
-            in_specs=[
-                pl.BlockSpec(slab.shape, lambda n, place: (0, 0, 0)),
-                pl.BlockSpec((1, *ids.shape[1:]), lambda n, place: (place[1], 0, 0)),
-                pl.BlockSpec((1, ROWS_DEV), lambda n, place: (0, place[1])),
-            ],
-            out_specs=pl.BlockSpec((2 * ROWS_DEV, pairs), lambda n, place: (0, 0)),
-        ),
-        out_shape=jax.ShapeDtypeStruct((2 * ROWS_DEV, pairs), jnp.bfloat16),
-        compiler_params=pltpu.CompilerParams(vmem_limit_bytes=VMEM_BYTES),
-        cost_estimate=pl.CostEstimate(flops=1, bytes_accessed=1, transcendentals=0),
-        name="left_side",
-    )(place, slab, ids, points_map)
+        left[:rows, begin : begin + LANES] = turned.astype(jnp.bfloat16)
+        left[rows:, begin : begin + LANES] = jnp.where(real_lanes, after, -before).astype(jnp.bfloat16)
 
 
 def order_kernel(place_ref, starts_ref, ids_ref, wanted_ref, panel_ref, out_ref, hot):
@@ -448,29 +426,43 @@
     )(place, jnp.asarray(plan["starts"].reshape(-1)), ids, points_map, panel)
 
 
-def product_kernel(left_ref, *refs):
-    *ordered, out_ref = refs
+def product_kernel(row_count, place_ref, slab_ref, ids_ref, wanted_ref, early_ref, last_ref, out_ref, left):
     rows = out_ref.shape[1]
-    right = jnp.concatenate([part[...] for part in ordered], 0)
-    chi = jnp.dot(left_ref[...], right, preferred_element_type=jnp.float32)
+
+    @pl.when(pl.program_id(0) == 0)
+    def _():
+        make_left(row_count, slab_ref, ids_ref, wanted_ref, left)
+
+    right = jnp.concatenate([early_ref[...], last_ref[...]], 0)
+    chi = jnp.dot(left[...], right, preferred_element_type=jnp.float32)
     out_ref[0] = chi[:rows]
     out_ref[1] = chi[rows:]
 
 
-def product(left, ordered):
-    rows, columns = left.shape[0] // 2, ordered[0].shape[1]
+def product(plan, place, points_map, slab, early, last):
+    pairs, columns = slab.shape[0] * slab.shape[1], early.shape[1]
     block = 6 * LANES
+    ids = jnp.asarray(plan["slab_ids"])[:, None]
     return pl.pallas_call(
-        product_kernel,
-        grid=(pl.cdiv(columns, block),),
-        in_specs=[pl.BlockSpec(left.shape, lambda n: (0, 0))]
-        + [pl.BlockSpec((part.shape[0], block), lambda n: (0, n)) for part in ordered],
-        out_specs=pl.BlockSpec((2, rows, block), lambda n: (0, 0, n)),
-        out_shape=jax.ShapeDtypeStruct((2, rows, columns), jnp.float32),
+        lambda *refs: product_kernel(ids.shape[0], *refs),
+        grid_spec=pltpu.PrefetchScalarGridSpec(
+            num_scalar_prefetch=1,
+            grid=(pl.cdiv(columns, block),),
+            in_specs=[
+                pl.BlockSpec(slab.shape, lambda n, place: (0, 0, 0)),
+                pl.BlockSpec((1, *ids.shape[1:]), lambda n, place: (place[1], 0, 0)),
+                pl.BlockSpec((1, ROWS_DEV), lambda n, place: (0, place[1])),
+                pl.BlockSpec((early.shape[0], block), lambda n, place: (0, n)),
+                pl.BlockSpec((last.shape[0], block), lambda n, place: (0, n)),
+            ],
+            out_specs=pl.BlockSpec((2, ROWS_DEV, block), lambda n, place: (0, 0, n)),
+            scratch_shapes=[pltpu.VMEM((2 * ROWS_DEV, pairs), jnp.bfloat16)],
+        ),
+        out_shape=jax.ShapeDtypeStruct((2, ROWS_DEV, columns), jnp.float32),
         compiler_params=pltpu.CompilerParams(vmem_limit_bytes=VMEM_BYTES, dimension_semantics=("arbitrary",)),
         cost_estimate=pl.CostEstimate(flops=1, bytes_accessed=1, transcendentals=0),
         name="product",
-    )(left, *ordered)
+    )(place, slab, ids, points_map, early, last)
 
 
 def on_device(val_wave, cond_wave, val_energy, cond_energy, band_owner, grid_map):
@@ -502,7 +494,7 @@
     early, slab = lax.optimization_barrier((early, slab))
     slab = lax.all_to_all(slab, "col", split_axis=0, concat_axis=0, tiled=True)
     early = put_in_order(plan, place, points_map, early)
-    return product(left_side(plan, place, points_map, slab), [early, last])
+    return product(plan, place, points_map, slab, early, last)
 
 
 def solution(mesh):

time: 139 us -> 138 us (level)
    pallas_call x2 -> x1, Pallas kernels: 10.9 us -> 9.13 us  [product(): pl.pallas_call(lambda *refs: product_kernel(ids.shape[0], *refs), grid_sp...]
  transfers between devices with their start and end apart: 4 -> 4, of which waited for: 3 -> 4; matrix products, arithmetic and copies ran while one was open for 1% -> 1% of each run, Pallas kernels for 25% -> 23%
where the time goes in v14:
time: 138 us; the launch traced here: 137 us
  Pallas kernels  58.4 us (42%)
  blocking collectives  42.2 us (31%)
  between operations  14.1 us (10%)
  waiting for transfers between devices  10.6 us (8%)
  starting transfers between devices  8.81 us (6%)
  local copies, waits for them, and re-layouts  2.33 us (2%)
    pallas_call x2, Pallas kernels, spectra(): pl.pallas_call(kernel, grid=(count,), in_specs=[pl.BlockSpec(memory_space...  36.3 us
    all_to_all x1, blocking collectives, on_device(): lax.all_to_all(early, 'col', split_axis=0, concat_axis=0, tiled=True)  31.6 us
    pallas_call x2, Pallas kernels, put_in_order(): pl.pallas_call(order_kernel, grid_spec=pltpu.PrefetchScalarGridSpec(num_s...  13 us
    all_to_all x1, blocking collectives, on_device(): lax.all_to_all(slab, 'row', split_axis=0, concat_axis=0, tiled=True)  10.6 us
    all_to_all x1, waiting for transfers between devices, on_device(): lax.all_to_all(send, 'col', split_axis=0, concat_axis=0, tiled=True)  9.23 us
    pallas_call x1, Pallas kernels, product(): pl.pallas_call(lambda *refs: product_kernel(ids.shape[0], *refs), grid_sp...  9.13 us
    all_to_all x1, starting transfers between devices, on_device(): lax.all_to_all(send, 'col', split_axis=0, concat_axis=0, tiled=True)  5.32 us
    all_to_all x1, starting transfers between devices, on_device(): slab = lax.all_to_all(slab, 'col', split_axis=0, concat_axis=0, tiled=True)  3.45 us
  transfers between devices with their start and end apart: 4, of which 4 were waited for; matrix products, arithmetic and copies ran while one was open for 1% of the time, Pallas kernels for 23%

profile of v14, /device:TPU:0, one launch (start us, length us, event | category | flops | bytes accessed | tf_op | source)
XLA Modules:
  0.0 137.2 jit_solution(10787288374328664690)
XLA Ops:
  6.5 0.0 all-gather.6.cloned.1.call-start
  7.2 18.2 %spectra.2 = (bf16[8,8,4224]{2,1,0:T(8,128)(2,1)}, bf16[4,8,384]{2,1,0:T(8,128)(2,1)}) custom-call(s32[1]{0:T(128)S(6)} %copy.19.refs_0_, f32[32]{0:T(128)} %refs_1_.3, f32[8]{0:T(128)} %refs_2_.3, bf16[8,64,64,128]{3,2,1,0:T(8,128)(2,1)} %refs_3_.3, bf16[1,64,64,128]{3,2,1,0:T(8,128)(2,1)} %refs_4_.2, s32[1,1280]{1,0:T(1,128)} %constant.25.clone.refs_5_, ...), custom_call_target="tpu_custom_call" | custom-call | flops 1 | bytes 1 | tf_op jit(solution)/shard_map/spectra/pallas_call | solution.py:334
  25.3 0.0 all-gather.6.cloned.1.call-update
  25.4 18.2 %spectra.3 = (bf16[8,8,4224]{2,1,0:T(8,128)(2,1)}, bf16[4,8,384]{2,1,0:T(8,128)(2,1)}) custom-call(s32[1]{0:T(128)S(6)} %copy.19.refs_0_, f32[32]{0:T(128)} %refs_1_.3, f32[8]{0:T(128)} %refs_2_.3, bf16[8,64,64,128]{3,2,1,0:T(8,128)(2,1)} %refs_3_.3, bf16[1,64,64,128]{3,2,1,0:T(8,128)(2,1)} %refs_4_.2, s32[1,1280]{1,0:T(1,128)} %constant.25.clone.refs_5_, ...), custom_call_target="tpu_custom_call" | custom-call | flops 1 | bytes 1 | tf_op jit(solution)/shard_map/spectra/pallas_call | solution.py:334
  43.5 0.0 copy-start.2
  43.5 0.0 copy-start.3
  43.5 5.3 %all-to-all-start = ((bf16[8,8,4224]{2,1,0:T(8,128)(2,1)}), bf16[8,8,4224]{2,1,0:T(8,128)(2,1)S(1)}, u32[]{:S(2)}, u32[]{:S(2)}) async-start(bf16[8,8,4224]{2,1,0:T(8,128)(2,1)} %get-tuple-element.21), calls=%async_computation | async-start | bytes 1081344 | tf_op jit(solution)/shard_map/all_to_all | solution.py:486
  48.9 0.0 all-gather.4.cloned.1.call-start
  48.9 0.6 pad_add_fusion.place_ref.refs_0_
  49.5 9.2 %all-to-all-done = bf16[8,8,4224]{2,1,0:T(8,128)(2,1)S(1)} async-done(((bf16[8,8,4224]{2,1,0:T(8,128)(2,1)}), bf16[8,8,4224]{2,1,0:T(8,128)(2,1)S(1)}, u32[]{:S(2)}, u32[]{:S(2)}) %all-to-all-start) | async-done | bytes 540704 | tf_op jit(solution)/shard_map/all_to_all | solution.py:486
  58.8 0.0 copy-start
  58.8 0.8 copy-done
  59.6 5.6 %in_order.2 = bf16[64,3840]{1,0:T(8,128)(2,1)} custom-call(s32[2]{0:T(128)} %pad_add_fusion.place_ref.refs_0_, s32[40]{0:T(128)} %constant.27.clone.starts_ref, s32[8,1,4224]{2,1,0:T(1,128)} %constant.31.ids_ref, s32[1,30720]{1,0:T(1,128)} %bitcast.10, bf16[64,4224]{1,0:T(8,128)(2,1)} %bitcast.8), custom_call_target="tpu_custom_call" | custom-call | flops 1 | bytes 1 | tf_op jit(solution)/shard_map/in_order/pallas_call | solution.py:409
  65.2 0.0 all-gather.4.cloned.1.call-update
  65.2 0.0 copy-done.2
  65.2 0.0 copy-done.3
  65.2 10.6 %all_to_all.20 = bf16[4,16,384]{2,1,0:T(8,128)(2,1)S(1)} all-to-all(bf16[4,16,384]{2,1,0:T(8,128)(2,1)S(1)} %pad_maximum_fusion), channel_id=1, replica_groups=mesh['row'=4,'col'=8] {'row'}, dimensions={0} | all-to-all | bytes 98304 | tf_op jit(solution)/shard_map/all_to_all | solution.py:490
  75.8 0.5 all-gather.6.cloned.1.call-done
  76.3 0.8 broadcast_in_dim.15
  77.1 31.6 %all_to_all.21 = bf16[8,4,8,4224]{3,2,1,0:T(8,128)(2,1)} all-to-all(bf16[8,4,8,4224]{3,2,1,0:T(8,128)(2,1)} %bitcast.9), channel_id=1, replica_groups=mesh['row'=4,'col'=8] {'col'}, dimensions={0} | all-to-all | bytes 4325376 | tf_op jit(solution)/shard_map/all_to_all | solution.py:493
  108.7 3.5 %all-to-all-start.3 = ((bf16[8,64,384]{2,1,0:T(8,128)(2,1)}), bf16[8,64,384]{2,1,0:T(8,128)(2,1)S(1)}, u32[]{:S(2)}, u32[]{:S(2)}) async-start(bf16[8,64,384]{2,1,0:T(8,128)(2,1)} %broadcast_in_dim.15), calls=%async_computation.3 | async-start | bytes 786432 | tf_op jit(solution)/shard_map/all_to_all | solution.py:495
  112.2 7.4 %in_order.3.refs_4_ = bf16[256,3840]{1,0:T(8,128)(2,1)} custom-call(s32[2]{0:T(128)} %pad_add_fusion.place_ref.refs_0_, s32[40]{0:T(128)} %constant.27.clone.starts_ref, s32[8,1,4224]{2,1,0:T(1,128)} %constant.31.ids_ref, s32[1,30720]{1,0:T(1,128)} %bitcast.11, bf16[256,4224]{1,0:T(8,128)(2,1)} %bitcast.7), custom_call_target="tpu_custom_call" | custom-call | flops 1 | bytes 1 | tf_op jit(solution)/shard_map/in_order/pallas_call | solution.py:409
  119.5 0.7 all-gather.4.cloned.1.call-done.refs_5_
  120.3 0.2 all-to-all-done.3.refs_1_
  120.4 0.0 copy-start.1
  120.4 0.7 copy-done.1
  121.2 9.1 %product.1 = f32[2,256,3840]{2,1,0:T(8,128)} custom-call(s32[2]{0:T(128)} %pad_add_fusion.place_ref.refs_0_, bf16[8,64,384]{2,1,0:T(8,128)(2,1)} %copy-done.1, s32[4,1,384]{2,1,0:T(1,128)} %constant.32.refs_2_, s32[1,30720]{1,0:T(1,128)} %bitcast.12, bf16[256,3840]{1,0:T(8,128)(2,1)} %in_order.3.refs_4_, bf16[256,3840]{1,0:T(8,128)(2,1)} %all-gather.4.cloned.1.call-done.refs_5_), custom_call_target="tpu_custom_call" | custom-call | flops 1 | bytes 1 | tf_op jit(solution)/shard_map/product/pallas_call | solution.py:446
  (1 shorter events, 0.0 us)
Async XLA Ops:
  6.5 69.8 %all-gather.6.cloned.1.call-start = ((), (), s32[]{:S(2)}) async-start(), calls=%async_computation.5 | async-start | bytes 2703360 | tf_op jit(solution)/shard_map/all_gather | solution.py:484
  43.5 21.7 %copy-start.2 = (bf16[4,8,384]{2,1,0:T(8,128)(2,1)S(1)}, bf16[4,8,384]{2,1,0:T(8,128)(2,1)}, u32[]{:S(2)}) copy-start(bf16[4,8,384]{2,1,0:T(8,128)(2,1)} %get-tuple-element.18) | copy-start | bytes 73732
  43.5 21.7 %copy-start.3 = (bf16[4,8,384]{2,1,0:T(8,128)(2,1)S(1)}, bf16[4,8,384]{2,1,0:T(8,128)(2,1)}, u32[]{:S(2)}) copy-start(bf16[4,8,384]{2,1,0:T(8,128)(2,1)} %get-tuple-element.20) | copy-start | bytes 73732
  43.5 15.2 %all-to-all-start = ((bf16[8,8,4224]{2,1,0:T(8,128)(2,1)}), bf16[8,8,4224]{2,1,0:T(8,128)(2,1)S(1)}, u32[]{:S(2)}, u32[]{:S(2)}) async-start(bf16[8,8,4224]{2,1,0:T(8,128)(2,1)} %get-tuple-element.21), calls=%async_computation | async-start | bytes 1081344 | tf_op jit(solution)/shard_map/all_to_all | solution.py:486
  48.9 71.4 %all-gather.4.cloned.1.call-start = ((), (), s32[]{:S(2)}) async-start(), calls=%async_computation.4 | async-start | bytes 2457600 | tf_op jit(solution)/shard_map/all_gather | solution.py:488
  58.8 0.8 copy-start
  108.7 11.7 %all-to-all-start.3 = ((bf16[8,64,384]{2,1,0:T(8,128)(2,1)}), bf16[8,64,384]{2,1,0:T(8,128)(2,1)S(1)}, u32[]{:S(2)}, u32[]{:S(2)}) async-start(bf16[8,64,384]{2,1,0:T(8,128)(2,1)} %broadcast_in_dim.15), calls=%async_computation.3 | async-start | bytes 786432 | tf_op jit(solution)/shard_map/all_to_all | solution.py:495
  120.4 0.7 copy-start.1
Sparse Core Ops, SparseCore 0:
  25.5 50.7 all-gather.5
  77.9 42.3 all-gather.3

commit v15 on v14

--- a/solution.py
+++ b/solution.py
@@ -14,8 +14,7 @@
 HALF = 64
 KEEP = 40
 ORIGIN = KEEP // 2
-PARITY_LANES = 896
-PARTS = 5
+PARTS = 3
 
 
 def round_up(value, step):
@@ -38,8 +37,23 @@
     return first.reshape(-1)[order], second.reshape(-1)[order], length[order]
 
 
-def column_place(index_2, index_3):
-    return index_3 % 2 * PARITY_LANES + index_3 // 2 * KEEP + index_2
+class Columns:
+    def __init__(self, top):
+        self.windows = []
+        offset = 0
+        for begin in range(0, KEEP, 4):
+            nearest = min(abs(index - ORIGIN) for index in range(begin, begin + 4))
+            reach = math.isqrt(max(top - nearest * nearest, 0))
+            low = (ORIGIN - reach) // 8 * 8
+            high = min(round_up(ORIGIN + reach + 1, 8), KEEP)
+            self.windows.append((low, high, offset))
+            offset += 2 * (high - low)
+        self.used = offset
+        self.parity = round_up(offset, 2 * LANES)
+
+    def place(self, index_2, index_3):
+        low, high, offset = np.array(self.windows)[index_3 // 4].T
+        return index_3 % 2 * self.parity + offset + index_3 // 2 % 2 * (high - low) + index_2 - low
 
 
 class Bucket:
@@ -98,6 +112,9 @@
     buckets = [Bucket(length_ranges(cumulative, n * width, step, PARTS), column_length) for n in range(blocks)]
     slabs = [Bucket(length_ranges(cumulative, n * slab_width, slab_width, 1), column_length) for n in range(slab_blocks)]
     slab_top = shell(slab - 1)
+    columns = Columns(shell(total - 1))
+    place = columns.place(column_2 + ORIGIN, column_3 + ORIGIN)
+    slab_columns = int(np.searchsorted(column_length, slab_top, side="right"))
     lanes = round_up(max(bucket.size for bucket in buckets), LANES)
     slab_lanes = round_up(max(bucket.size for bucket in slabs), LANES)
     windows = np.zeros((blocks, PARTS, 2), np.int64)
@@ -110,15 +127,16 @@
     return dict(
         buckets=buckets,
         slabs=slabs,
-        slab_columns=int(np.searchsorted(column_length, slab_top, side="right")),
-        slab_edge=math.isqrt(slab_top),
+        slab_columns=slab_columns,
+        slab_tiles=sorted({int(value) for value in place[:slab_columns] // LANES}),
+        columns=columns,
         lanes=lanes,
         slab_lanes=slab_lanes,
         window=window,
         starts=np.minimum(windows[..., 0], lanes - window).astype(np.int32),
         ids=np.stack([bucket.ids(column_2, column_3, points, lanes) for bucket in buckets]),
         slab_ids=np.stack([bucket.ids(column_2, column_3, points, slab_lanes) for bucket in slabs]),
-        column_place=column_place(column_2 + ORIGIN, column_3 + ORIGIN).astype(np.int32),
+        column_place=place.astype(np.int32),
     )
 
 
@@ -189,16 +207,11 @@
         out(tile, value)
 
 
-def slab_tiles(plan):
-    first = (ORIGIN - plan["slab_edge"]) // 2 * KEEP // LANES
-    last = round_up(((ORIGIN + plan["slab_edge"]) // 2 + 1) * KEEP, LANES) // LANES
-    return [odd * PARITY_LANES // LANES + tile for odd in range(2) for tile in range(first, last)]
-
-
 def spectrum_kernel(plan, points, first_band, count, owner_ref, cond_energy_ref, val_energy_ref, val_ref, cond_ref, place_ref, first_ref,
                     second_ref, third_ref, send_ref, slab_ref, cond_a, cond_b, middle, turned, last, sorter, plain_rows, weighted_rows,
                     plain_sorted, weighted_sorted):
     band = pl.program_id(0)
+    columns = plan["columns"]
     planes = 8
     pairs = planes // 2
     lane = lax.broadcasted_iota(jnp.int32, (1, LANES), 1)
@@ -216,7 +229,7 @@
             cond_a[rows, :] = wave * scale
             cond_b[rows, :] = pltpu.roll(wave, HALF, 1) * sign
 
-        last[KEEP * KEEP // 2 :, :] = jnp.zeros((last.shape[0] - KEEP * KEEP // 2, 4 * LANES), jnp.bfloat16)
+        last[columns.used :, :] = jnp.zeros((columns.parity - columns.used, 4 * LANES), jnp.bfloat16)
 
     def first_axis(block):
         rows = pl.ds(pl.multiple_of(block * planes * points, planes * points), planes * points)
@@ -259,7 +272,7 @@
     for part in range(2):
         second_axis(2 * turns + part)
 
-    for begin in range(0, KEEP, 4):
+    for begin, (low, high, offset) in zip(range(0, KEEP, 4), columns.windows):
         both = []
         for pair in range(2):
             items = [
@@ -268,19 +281,19 @@
                 for item in range(2)
             ]
             turn = jnp.concatenate(items, 0).T
-            both.append((turn[:KEEP], turn[HALF : HALF + KEEP]))
-        store_split(last, slice(begin // 2 * KEEP, (begin // 2 + 2) * KEEP), list(zip(*both)))
+            both.append((turn[low:high], turn[HALF + low : HALF + high]))
+        store_split(last, slice(offset, offset + 2 * (high - low)), list(zip(*both)))
 
     bands = val_energy_ref.shape[0] * cond_energy_ref.shape[0]
     gap = cond_energy_ref[owner_ref[0]] - val_energy_ref[first_band + band]
     weight = -2.0 / (math.sqrt(bands) * jnp.full((1, LANES), gap, jnp.float32))
-    slab = slab_tiles(plan)
-    tiles = PARITY_LANES // LANES
+    slab = plan["slab_tiles"]
+    tiles = columns.parity // LANES
     field = contract_last(third_ref[...], last[...])
     band_rows = pl.ds(pl.multiple_of(band * 2 * KEEP, 2 * KEEP), 2 * KEEP)
     for odd in range(2):
         value = field[odd * 2 * KEEP : (odd + 1) * 2 * KEEP]
-        plain_rows[band_rows, odd * PARITY_LANES : (odd + 1) * PARITY_LANES] = value.astype(jnp.bfloat16)
+        plain_rows[band_rows, odd * columns.parity : (odd + 1) * columns.parity] = value.astype(jnp.bfloat16)
         for place, tile in enumerate(slab):
             if tile // tiles == odd:
                 inside = value[:, tile % tiles * LANES : (tile % tiles + 1) * LANES]
@@ -294,7 +307,7 @@
                 target[tile] = value[:, tile * LANES : (tile + 1) * LANES]
 
         which = [sorter[tile * LANES : (tile + 1) * LANES, : weighted_sorted.shape[0] * LANES] for tile in slab]
-        sort_rows(plain_rows[...], sorter[: 2 * PARITY_LANES, :], plain_sorted)
+        sort_rows(plain_rows[...], sorter[: 2 * columns.parity, :], plain_sorted)
         sort_rows(weighted_rows[...], jnp.concatenate(which, 0), weighted_sorted)
 
         def plain_at(index, tile):
@@ -320,10 +333,11 @@
 def spectra(plan, val_wave, cond_wave, energies, first_band, count):
     points = val_wave.shape[1]
     turns = points // 16 - 1
-    depth = round_up(-(-2 * PARITY_LANES // (count * turns)), 16) * count * turns
+    parity = plan["columns"].parity
+    depth = round_up(-(-2 * parity // (count * turns)), 16) * count * turns
     columns = round_up(plan["column_place"].shape[0], 256)
     slab_columns = round_up(plan["slab_columns"], LANES)
-    slab_depth = len(slab_tiles(plan)) * LANES
+    slab_depth = len(plan["slab_tiles"]) * LANES
     place = np.full((1, columns), -1, np.int32)
     place[0, : plan["column_place"].shape[0]] = plan["column_place"]
     grid_rows = points * points
@@ -350,9 +364,9 @@
             pltpu.VMEM((grid_rows, LANES), jnp.float32),
             pltpu.VMEM((points // 2 * KEEP, 4 * LANES), jnp.bfloat16),
             pltpu.VMEM((2, points // 2 * KEEP, LANES), jnp.float32),
-            pltpu.VMEM((PARITY_LANES, 4 * LANES), jnp.bfloat16),
+            pltpu.VMEM((parity, 4 * LANES), jnp.bfloat16),
             pltpu.VMEM((depth, columns), jnp.bfloat16),
-            pltpu.VMEM((2 * count * KEEP, 2 * PARITY_LANES), jnp.bfloat16),
+            pltpu.VMEM((2 * count * KEEP, 2 * parity), jnp.bfloat16),
             pltpu.VMEM((2 * count * KEEP, slab_depth), jnp.bfloat16),
             pltpu.VMEM((columns // LANES, 2 * count * KEEP, LANES), jnp.float32),
             pltpu.VMEM((slab_columns // LANES, 2 * count * KEEP, LANES), jnp.float32),

time: 138 us -> 137 us (level)
  transfers between devices with their start and end apart: 4 -> 4, of which waited for: 4 -> 4; matrix products, arithmetic and copies ran while one was open for 1% -> 1% of each run, Pallas kernels for 23% -> 22%
where the time goes in v15:
time: 137 us
  Pallas kernels  57.4 us (42%)
  blocking collectives  42.8 us (31%)
  between operations  14.1 us (10%)
  waiting for transfers between devices  10.6 us (8%)
  starting transfers between devices  8.8 us (6%)
  local copies, waits for them, and re-layouts  2.33 us (2%)
    pallas_call x2, Pallas kernels, spectra(): pl.pallas_call(kernel, grid=(count,), in_specs=[pl.BlockSpec(memory_space...  35.2 us
    all_to_all x1, blocking collectives, on_device(): lax.all_to_all(early, 'col', split_axis=0, concat_axis=0, tiled=True)  31.6 us
    pallas_call x2, Pallas kernels, put_in_order(): pl.pallas_call(order_kernel, grid_spec=pltpu.PrefetchScalarGridSpec(num_s...  13.1 us
    all_to_all x1, blocking collectives, on_device(): lax.all_to_all(slab, 'row', split_axis=0, concat_axis=0, tiled=True)  11.1 us
    all_to_all x1, waiting for transfers between devices, on_device(): lax.all_to_all(send, 'col', split_axis=0, concat_axis=0, tiled=True)  9.23 us
    pallas_call x1, Pallas kernels, product(): pl.pallas_call(lambda *refs: product_kernel(ids.shape[0], *refs), grid_sp...  9.13 us
    all_to_all x1, starting transfers between devices, on_device(): lax.all_to_all(send, 'col', split_axis=0, concat_axis=0, tiled=True)  5.31 us
    all_to_all x1, starting transfers between devices, on_device(): slab = lax.all_to_all(slab, 'col', split_axis=0, concat_axis=0, tiled=True)  3.45 us
  transfers between devices with their start and end apart: 4, of which 4 were waited for; matrix products, arithmetic and copies ran while one was open for 1% of the time, Pallas kernels for 22%

profile of v15, /device:TPU:0, one launch (start us, length us, event | category | flops | bytes accessed | tf_op | source)
XLA Modules:
  0.0 136.7 jit_solution(2474420227782457411)
XLA Ops:
  6.5 0.0 all-gather.6.cloned.1.call-start
  7.2 17.6 %spectra.2 = (bf16[8,8,4224]{2,1,0:T(8,128)(2,1)}, bf16[4,8,384]{2,1,0:T(8,128)(2,1)}) custom-call(s32[1]{0:T(128)S(6)} %copy.19.refs_0_, f32[32]{0:T(128)} %refs_1_.3, f32[8]{0:T(128)} %refs_2_.3, bf16[8,64,64,128]{3,2,1,0:T(8,128)(2,1)} %refs_3_.3, bf16[1,64,64,128]{3,2,1,0:T(8,128)(2,1)} %refs_4_.2, s32[1,1280]{1,0:T(1,128)} %constant.25.clone.refs_5_, ...), custom_call_target="tpu_custom_call" | custom-call | flops 1 | bytes 1 | tf_op jit(solution)/shard_map/spectra/pallas_call | solution.py:348
  24.8 0.0 all-gather.6.cloned.1.call-update
  24.8 17.6 %spectra.3 = (bf16[8,8,4224]{2,1,0:T(8,128)(2,1)}, bf16[4,8,384]{2,1,0:T(8,128)(2,1)}) custom-call(s32[1]{0:T(128)S(6)} %copy.19.refs_0_, f32[32]{0:T(128)} %refs_1_.3, f32[8]{0:T(128)} %refs_2_.3, bf16[8,64,64,128]{3,2,1,0:T(8,128)(2,1)} %refs_3_.3, bf16[1,64,64,128]{3,2,1,0:T(8,128)(2,1)} %refs_4_.2, s32[1,1280]{1,0:T(1,128)} %constant.25.clone.refs_5_, ...), custom_call_target="tpu_custom_call" | custom-call | flops 1 | bytes 1 | tf_op jit(solution)/shard_map/spectra/pallas_call | solution.py:348
  42.4 0.0 copy-start.2
  42.4 0.0 copy-start.3
  42.4 5.3 %all-to-all-start = ((bf16[8,8,4224]{2,1,0:T(8,128)(2,1)}), bf16[8,8,4224]{2,1,0:T(8,128)(2,1)S(1)}, u32[]{:S(2)}, u32[]{:S(2)}) async-start(bf16[8,8,4224]{2,1,0:T(8,128)(2,1)} %get-tuple-element.21), calls=%async_computation | async-start | bytes 1081344 | tf_op jit(solution)/shard_map/all_to_all | solution.py:500
  47.7 0.0 all-gather.4.cloned.1.call-start
  47.8 0.6 pad_add_fusion.place_ref.refs_0_
  48.4 9.2 %all-to-all-done = bf16[8,8,4224]{2,1,0:T(8,128)(2,1)S(1)} async-done(((bf16[8,8,4224]{2,1,0:T(8,128)(2,1)}), bf16[8,8,4224]{2,1,0:T(8,128)(2,1)S(1)}, u32[]{:S(2)}, u32[]{:S(2)}) %all-to-all-start) | async-done | bytes 540704 | tf_op jit(solution)/shard_map/all_to_all | solution.py:500
  57.6 0.0 copy-start
  57.6 0.8 copy-done
  58.4 5.4 %in_order.2 = bf16[64,3840]{1,0:T(8,128)(2,1)} custom-call(s32[2]{0:T(128)} %pad_add_fusion.place_ref.refs_0_, s32[24]{0:T(128)} %constant.27.clone.starts_ref, s32[8,1,4224]{2,1,0:T(1,128)} %constant.31.ids_ref, s32[1,30720]{1,0:T(1,128)} %bitcast.10, bf16[64,4224]{1,0:T(8,128)(2,1)} %bitcast.8), custom_call_target="tpu_custom_call" | custom-call | flops 1 | bytes 1 | tf_op jit(solution)/shard_map/in_order/pallas_call | solution.py:423
  63.8 0.0 all-gather.4.cloned.1.call-update
  63.8 0.0 copy-done.2
  63.8 0.0 copy-done.3
  63.9 11.1 %all_to_all.20 = bf16[4,16,384]{2,1,0:T(8,128)(2,1)S(1)} all-to-all(bf16[4,16,384]{2,1,0:T(8,128)(2,1)S(1)} %pad_maximum_fusion), channel_id=1, replica_groups=mesh['row'=4,'col'=8] {'row'}, dimensions={0} | all-to-all | bytes 98304 | tf_op jit(solution)/shard_map/all_to_all | solution.py:504
  75.0 0.9 all-gather.6.cloned.1.call-done
  75.9 0.8 broadcast_in_dim.15
  76.7 31.6 %all_to_all.21 = bf16[8,4,8,4224]{3,2,1,0:T(8,128)(2,1)} all-to-all(bf16[8,4,8,4224]{3,2,1,0:T(8,128)(2,1)} %bitcast.9), channel_id=1, replica_groups=mesh['row'=4,'col'=8] {'col'}, dimensions={0} | all-to-all | bytes 4325376 | tf_op jit(solution)/shard_map/all_to_all | solution.py:507
  108.3 3.5 %all-to-all-start.3 = ((bf16[8,64,384]{2,1,0:T(8,128)(2,1)}), bf16[8,64,384]{2,1,0:T(8,128)(2,1)S(1)}, u32[]{:S(2)}, u32[]{:S(2)}) async-start(bf16[8,64,384]{2,1,0:T(8,128)(2,1)} %broadcast_in_dim.15), calls=%async_computation.3 | async-start | bytes 786432 | tf_op jit(solution)/shard_map/all_to_all | solution.py:509
  111.8 7.8 %in_order.3.refs_4_ = bf16[256,3840]{1,0:T(8,128)(2,1)} custom-call(s32[2]{0:T(128)} %pad_add_fusion.place_ref.refs_0_, s32[24]{0:T(128)} %constant.27.clone.starts_ref, s32[8,1,4224]{2,1,0:T(1,128)} %constant.31.ids_ref, s32[1,30720]{1,0:T(1,128)} %bitcast.11, bf16[256,4224]{1,0:T(8,128)(2,1)} %bitcast.7), custom_call_target="tpu_custom_call" | custom-call | flops 1 | bytes 1 | tf_op jit(solution)/shard_map/in_order/pallas_call | solution.py:423
  119.5 0.2 all-gather.4.cloned.1.call-done.refs_5_
  119.7 0.3 all-to-all-done.3.refs_1_
  120.0 0.0 copy-start.1
  120.0 0.7 copy-done.1
  120.8 9.1 %product.1 = f32[2,256,3840]{2,1,0:T(8,128)} custom-call(s32[2]{0:T(128)} %pad_add_fusion.place_ref.refs_0_, bf16[8,64,384]{2,1,0:T(8,128)(2,1)} %copy-done.1, s32[4,1,384]{2,1,0:T(1,128)} %constant.32.refs_2_, s32[1,30720]{1,0:T(1,128)} %bitcast.12, bf16[256,3840]{1,0:T(8,128)(2,1)} %in_order.3.refs_4_, bf16[256,3840]{1,0:T(8,128)(2,1)} %all-gather.4.cloned.1.call-done.refs_5_), custom_call_target="tpu_custom_call" | custom-call | flops 1 | bytes 1 | tf_op jit(solution)/shard_map/product/pallas_call | solution.py:460
  (1 shorter events, 0.0 us)
Async XLA Ops:
  6.5 69.3 %all-gather.6.cloned.1.call-start = ((), (), s32[]{:S(2)}) async-start(), calls=%async_computation.5 | async-start | bytes 2703360 | tf_op jit(solution)/shard_map/all_gather | solution.py:498
  42.4 21.4 %copy-start.2 = (bf16[4,8,384]{2,1,0:T(8,128)(2,1)S(1)}, bf16[4,8,384]{2,1,0:T(8,128)(2,1)}, u32[]{:S(2)}) copy-start(bf16[4,8,384]{2,1,0:T(8,128)(2,1)} %get-tuple-element.18) | copy-start | bytes 73732
  42.4 21.4 %copy-start.3 = (bf16[4,8,384]{2,1,0:T(8,128)(2,1)S(1)}, bf16[4,8,384]{2,1,0:T(8,128)(2,1)}, u32[]{:S(2)}) copy-start(bf16[4,8,384]{2,1,0:T(8,128)(2,1)} %get-tuple-element.20) | copy-start | bytes 73732
  42.4 15.2 %all-to-all-start = ((bf16[8,8,4224]{2,1,0:T(8,128)(2,1)}), bf16[8,8,4224]{2,1,0:T(8,128)(2,1)S(1)}, u32[]{:S(2)}, u32[]{:S(2)}) async-start(bf16[8,8,4224]{2,1,0:T(8,128)(2,1)} %get-tuple-element.21), calls=%async_computation | async-start | bytes 1081344 | tf_op jit(solution)/shard_map/all_to_all | solution.py:500
  47.7 72.0 %all-gather.4.cloned.1.call-start = ((), (), s32[]{:S(2)}) async-start(), calls=%async_computation.4 | async-start | bytes 2457600 | tf_op jit(solution)/shard_map/all_gather | solution.py:502
  57.6 0.8 copy-start
  108.3 11.7 %all-to-all-start.3 = ((bf16[8,64,384]{2,1,0:T(8,128)(2,1)}), bf16[8,64,384]{2,1,0:T(8,128)(2,1)S(1)}, u32[]{:S(2)}, u32[]{:S(2)}) async-start(bf16[8,64,384]{2,1,0:T(8,128)(2,1)} %broadcast_in_dim.15), calls=%async_computation.3 | async-start | bytes 786432 | tf_op jit(solution)/shard_map/all_to_all | solution.py:509
  120.0 0.7 copy-start.1
Sparse Core Ops, SparseCore 0:
  24.9 50.9 all-gather.5
  77.4 42.2 all-gather.3

commit v16 on v15

--- a/solution.py
+++ b/solution.py
@@ -222,20 +222,20 @@
         scale = 1.0 / float(points) ** 1.5
         sign = jnp.where(low_lanes, scale, -scale)
 
-        @pl.loop(0, points // planes)
+        @pl.loop(0, points // planes, unroll=4)
         def _(block):
             rows = pl.ds(pl.multiple_of(block * planes * points, planes * points), planes * points)
             wave = cond_ref[0, pl.ds(block * planes, planes)].reshape(planes * points, LANES).astype(jnp.float32)
-            cond_a[rows, :] = wave * scale
-            cond_b[rows, :] = pltpu.roll(wave, HALF, 1) * sign
+            other = pltpu.roll(wave, HALF, 1)
+            cond_a[rows, :] = jnp.where(low_lanes, wave, other) * sign
+            cond_b[rows, :] = jnp.where(low_lanes, other, wave) * scale
 
         last[columns.used :, :] = jnp.zeros((columns.parity - columns.used, 4 * LANES), jnp.bfloat16)
 
     def first_axis(block):
         rows = pl.ds(pl.multiple_of(block * planes * points, planes * points), planes * points)
         wave = val_ref[0, pl.ds(block * planes, planes)].reshape(planes * points, LANES).astype(jnp.float32)
-        other = pltpu.roll(wave, HALF, 1)
-        density = jnp.where(low_lanes, wave, other) * cond_a[rows, :] + jnp.where(low_lanes, other, wave) * cond_b[rows, :]
+        density = wave * cond_a[rows, :] + pltpu.roll(wave, HALF, 1) * cond_b[rows, :]
         high, low = split_parts(density)
         field = contract_last(first_ref[...], jnp.concatenate([high, low], 1))
         for begin in range(0, pairs, 2):
@@ -390,18 +390,24 @@
     order = [(col, 2 * row) for col in range(col_count) for row in range(row_count)]
     order += [(col, 2 * row + 1) for row in range(row_count) for col in range(col_count)]
     slab = [slab_ref[col, at * group : (at + 1) * group, :].astype(jnp.float32) for col, at in order]
-    ids = ids_ref[0]
-    choice = [one_hot(ids[:, begin : begin + LANES], wanted_ref[...]) for begin in range(0, ids.shape[1], LANES)]
-    chosen = jnp.dot(
-        jnp.concatenate(slab, 0).astype(jnp.bfloat16), jnp.concatenate(choice, 0), preferred_element_type=jnp.float32
+    wanted = [
+        jnp.broadcast_to(wanted_ref[:, begin : begin + LANES], (LANES, LANES)).T for begin in range(0, rows, LANES)
+    ]
+    wanted = jnp.concatenate([jnp.concatenate(wanted, 0)] * (ids_ref.shape[2] // LANES), 1)
+    choice = jnp.where(wanted == ids_ref[0], 1.0, 0.0).astype(jnp.bfloat16)
+    chosen = lax.dot_general(
+        choice,
+        jnp.concatenate(slab, 0).astype(jnp.bfloat16),
+        (((1,), (1,)), ((), ())),
+        preferred_element_type=jnp.float32,
     )
     lane = lax.broadcasted_iota(jnp.int32, (1, LANES), 1)
     real_lanes = lane % 2 == 0
-    for begin in range(0, chosen.shape[0], LANES):
-        turned = chosen[begin : begin + LANES].T
-        after = pltpu.roll(turned, LANES - 1, 1)
-        before = pltpu.roll(turned, 1, 1)
-        left[:rows, begin : begin + LANES] = turned.astype(jnp.bfloat16)
+    for begin in range(0, chosen.shape[1], LANES):
+        part = chosen[:, begin : begin + LANES]
+        after = pltpu.roll(part, LANES - 1, 1)
+        before = pltpu.roll(part, 1, 1)
+        left[:rows, begin : begin + LANES] = part.astype(jnp.bfloat16)
         left[rows:, begin : begin + LANES] = jnp.where(real_lanes, after, -before).astype(jnp.bfloat16)
 
 

time: 137 us -> 137 us (level)
  no operation moved by 1% of the time
where the time goes in v16:
time: 137 us; the launch traced here: 136 us
  Pallas kernels  57 us (42%)
  blocking collectives  42.8 us (31%)
  between operations  14.1 us (10%)
  waiting for transfers between devices  10.7 us (8%)
  starting transfers between devices  8.81 us (6%)
  local copies, waits for them, and re-layouts  2.33 us (2%)
    pallas_call x2, Pallas kernels, spectra(): pl.pallas_call(kernel, grid=(count,), in_specs=[pl.BlockSpec(memory_space...  34.9 us
    all_to_all x1, blocking collectives, on_device(): lax.all_to_all(early, 'col', split_axis=0, concat_axis=0, tiled=True)  31.6 us
    pallas_call x2, Pallas kernels, put_in_order(): pl.pallas_call(order_kernel, grid_spec=pltpu.PrefetchScalarGridSpec(num_s...  13.1 us
    all_to_all x1, blocking collectives, on_device(): lax.all_to_all(slab, 'row', split_axis=0, concat_axis=0, tiled=True)  11.2 us
    all_to_all x1, waiting for transfers between devices, on_device(): lax.all_to_all(send, 'col', split_axis=0, concat_axis=0, tiled=True)  9.23 us
    pallas_call x1, Pallas kernels, product(): pl.pallas_call(lambda *refs: product_kernel(ids.shape[0], *refs), grid_sp...  8.91 us
    all_to_all x1, starting transfers between devices, on_device(): lax.all_to_all(send, 'col', split_axis=0, concat_axis=0, tiled=True)  5.31 us
    all_to_all x1, starting transfers between devices, on_device(): slab = lax.all_to_all(slab, 'col', split_axis=0, concat_axis=0, tiled=True)  3.45 us
  transfers between devices with their start and end apart: 4, of which 4 were waited for; matrix products, arithmetic and copies ran while one was open for 1% of the time, Pallas kernels for 22%

profile of v16, /device:TPU:0, one launch (start us, length us, event | category | flops | bytes accessed | tf_op | source)
XLA Modules:
  0.0 136.3 jit_solution(4731761251596440098)
XLA Ops:
  6.5 0.0 all-gather.6.cloned.1.call-start
  7.2 17.5 %spectra.2 = (bf16[8,8,4224]{2,1,0:T(8,128)(2,1)}, bf16[4,8,384]{2,1,0:T(8,128)(2,1)}) custom-call(s32[1]{0:T(128)S(6)} %copy.19.refs_0_, f32[32]{0:T(128)} %refs_1_.3, f32[8]{0:T(128)} %refs_2_.3, bf16[8,64,64,128]{3,2,1,0:T(8,128)(2,1)} %refs_3_.3, bf16[1,64,64,128]{3,2,1,0:T(8,128)(2,1)} %refs_4_.2, s32[1,1280]{1,0:T(1,128)} %constant.25.clone.refs_5_, ...), custom_call_target="tpu_custom_call" | custom-call | flops 1 | bytes 1 | tf_op jit(solution)/shard_map/spectra/pallas_call | solution.py:348
  24.7 0.0 all-gather.6.cloned.1.call-update
  24.7 17.5 %spectra.3 = (bf16[8,8,4224]{2,1,0:T(8,128)(2,1)}, bf16[4,8,384]{2,1,0:T(8,128)(2,1)}) custom-call(s32[1]{0:T(128)S(6)} %copy.19.refs_0_, f32[32]{0:T(128)} %refs_1_.3, f32[8]{0:T(128)} %refs_2_.3, bf16[8,64,64,128]{3,2,1,0:T(8,128)(2,1)} %refs_3_.3, bf16[1,64,64,128]{3,2,1,0:T(8,128)(2,1)} %refs_4_.2, s32[1,1280]{1,0:T(1,128)} %constant.25.clone.refs_5_, ...), custom_call_target="tpu_custom_call" | custom-call | flops 1 | bytes 1 | tf_op jit(solution)/shard_map/spectra/pallas_call | solution.py:348
  42.1 0.0 copy-start.2
  42.1 0.0 copy-start.3
  42.1 5.3 %all-to-all-start = ((bf16[8,8,4224]{2,1,0:T(8,128)(2,1)}), bf16[8,8,4224]{2,1,0:T(8,128)(2,1)S(1)}, u32[]{:S(2)}, u32[]{:S(2)}) async-start(bf16[8,8,4224]{2,1,0:T(8,128)(2,1)} %get-tuple-element.21), calls=%async_computation | async-start | bytes 1081344 | tf_op jit(solution)/shard_map/all_to_all | solution.py:506
  47.5 0.0 all-gather.4.cloned.1.call-start
  47.5 0.6 pad_add_fusion.place_ref.refs_0_
  48.2 9.2 %all-to-all-done = bf16[8,8,4224]{2,1,0:T(8,128)(2,1)S(1)} async-done(((bf16[8,8,4224]{2,1,0:T(8,128)(2,1)}), bf16[8,8,4224]{2,1,0:T(8,128)(2,1)S(1)}, u32[]{:S(2)}, u32[]{:S(2)}) %all-to-all-start) | async-done | bytes 540704 | tf_op jit(solution)/shard_map/all_to_all | solution.py:506
  57.4 0.0 copy-start
  57.4 0.8 copy-done
  58.2 5.4 %in_order.2 = bf16[64,3840]{1,0:T(8,128)(2,1)} custom-call(s32[2]{0:T(128)} %pad_add_fusion.place_ref.refs_0_, s32[24]{0:T(128)} %constant.27.clone.starts_ref, s32[8,1,4224]{2,1,0:T(1,128)} %constant.31.ids_ref, s32[1,30720]{1,0:T(1,128)} %bitcast.10, bf16[64,4224]{1,0:T(8,128)(2,1)} %bitcast.8), custom_call_target="tpu_custom_call" | custom-call | flops 1 | bytes 1 | tf_op jit(solution)/shard_map/in_order/pallas_call | solution.py:429
  63.5 0.0 all-gather.4.cloned.1.call-update
  63.6 0.0 copy-done.2
  63.6 0.0 copy-done.3
  63.6 11.2 %all_to_all.20 = bf16[4,16,384]{2,1,0:T(8,128)(2,1)S(1)} all-to-all(bf16[4,16,384]{2,1,0:T(8,128)(2,1)S(1)} %pad_maximum_fusion), channel_id=1, replica_groups=mesh['row'=4,'col'=8] {'row'}, dimensions={0} | all-to-all | bytes 98304 | tf_op jit(solution)/shard_map/all_to_all | solution.py:510
  74.8 0.9 all-gather.6.cloned.1.call-done
  75.7 0.8 broadcast_in_dim.15
  76.5 31.6 %all_to_all.21 = bf16[8,4,8,4224]{3,2,1,0:T(8,128)(2,1)} all-to-all(bf16[8,4,8,4224]{3,2,1,0:T(8,128)(2,1)} %bitcast.9), channel_id=1, replica_groups=mesh['row'=4,'col'=8] {'col'}, dimensions={0} | all-to-all | bytes 4325376 | tf_op jit(solution)/shard_map/all_to_all | solution.py:513
  108.1 3.5 %all-to-all-start.3 = ((bf16[8,64,384]{2,1,0:T(8,128)(2,1)}), bf16[8,64,384]{2,1,0:T(8,128)(2,1)S(1)}, u32[]{:S(2)}, u32[]{:S(2)}) async-start(bf16[8,64,384]{2,1,0:T(8,128)(2,1)} %broadcast_in_dim.15), calls=%async_computation.3 | async-start | bytes 786432 | tf_op jit(solution)/shard_map/all_to_all | solution.py:515
  111.6 7.8 %in_order.3.refs_4_ = bf16[256,3840]{1,0:T(8,128)(2,1)} custom-call(s32[2]{0:T(128)} %pad_add_fusion.place_ref.refs_0_, s32[24]{0:T(128)} %constant.27.clone.starts_ref, s32[8,1,4224]{2,1,0:T(1,128)} %constant.31.ids_ref, s32[1,30720]{1,0:T(1,128)} %bitcast.11, bf16[256,4224]{1,0:T(8,128)(2,1)} %bitcast.7), custom_call_target="tpu_custom_call" | custom-call | flops 1 | bytes 1 | tf_op jit(solution)/shard_map/in_order/pallas_call | solution.py:429
  119.3 0.3 all-gather.4.cloned.1.call-done.refs_5_
  119.6 0.2 all-to-all-done.3.refs_1_
  119.8 0.0 copy-start.1
  119.8 0.7 copy-done.1
  120.6 8.9 %product.1 = f32[2,256,3840]{2,1,0:T(8,128)} custom-call(s32[2]{0:T(128)} %pad_add_fusion.place_ref.refs_0_, bf16[8,64,384]{2,1,0:T(8,128)(2,1)} %copy-done.1, s32[4,1,384]{2,1,0:T(1,128)} %constant.32.refs_2_, s32[1,30720]{1,0:T(1,128)} %bitcast.12, bf16[256,3840]{1,0:T(8,128)(2,1)} %in_order.3.refs_4_, bf16[256,3840]{1,0:T(8,128)(2,1)} %all-gather.4.cloned.1.call-done.refs_5_), custom_call_target="tpu_custom_call" | custom-call | flops 1 | bytes 1 | tf_op jit(solution)/shard_map/product/pallas_call | solution.py:466
  (1 shorter events, 0.0 us)
Async XLA Ops:
  6.5 69.1 %all-gather.6.cloned.1.call-start = ((), (), s32[]{:S(2)}) async-start(), calls=%async_computation.5 | async-start | bytes 2703360 | tf_op jit(solution)/shard_map/all_gather | solution.py:504
  42.1 21.4 %copy-start.2 = (bf16[4,8,384]{2,1,0:T(8,128)(2,1)S(1)}, bf16[4,8,384]{2,1,0:T(8,128)(2,1)}, u32[]{:S(2)}) copy-start(bf16[4,8,384]{2,1,0:T(8,128)(2,1)} %get-tuple-element.18) | copy-start | bytes 73732
  42.1 21.4 %copy-start.3 = (bf16[4,8,384]{2,1,0:T(8,128)(2,1)S(1)}, bf16[4,8,384]{2,1,0:T(8,128)(2,1)}, u32[]{:S(2)}) copy-start(bf16[4,8,384]{2,1,0:T(8,128)(2,1)} %get-tuple-element.20) | copy-start | bytes 73732
  42.1 15.2 %all-to-all-start = ((bf16[8,8,4224]{2,1,0:T(8,128)(2,1)}), bf16[8,8,4224]{2,1,0:T(8,128)(2,1)S(1)}, u32[]{:S(2)}, u32[]{:S(2)}) async-start(bf16[8,8,4224]{2,1,0:T(8,128)(2,1)} %get-tuple-element.21), calls=%async_computation | async-start | bytes 1081344 | tf_op jit(solution)/shard_map/all_to_all | solution.py:506
  47.5 72.1 %all-gather.4.cloned.1.call-start = ((), (), s32[]{:S(2)}) async-start(), calls=%async_computation.4 | async-start | bytes 2457600 | tf_op jit(solution)/shard_map/all_gather | solution.py:508
  57.4 0.8 copy-start
  108.1 11.7 %all-to-all-start.3 = ((bf16[8,64,384]{2,1,0:T(8,128)(2,1)}), bf16[8,64,384]{2,1,0:T(8,128)(2,1)S(1)}, u32[]{:S(2)}, u32[]{:S(2)}) async-start(bf16[8,64,384]{2,1,0:T(8,128)(2,1)} %broadcast_in_dim.15), calls=%async_computation.3 | async-start | bytes 786432 | tf_op jit(solution)/shard_map/all_to_all | solution.py:515
  119.8 0.7 copy-start.1
Sparse Core Ops, SparseCore 0:
  24.8 50.8 all-gather.5
  77.2 42.2 all-gather.3

commit v17 on v16

--- a/solution.py
+++ b/solution.py
@@ -246,8 +246,8 @@
             at = pl.ds(pl.multiple_of((block * pairs + begin) * KEEP, 2 * KEEP), 2 * KEEP)
             store_split(middle, at, blocks)
 
-    def second_axis(block):
-        rows = pl.ds(pl.multiple_of(block * 4 * KEEP, 4 * KEEP), 4 * KEEP)
+    def second_axis(turn):
+        rows = pl.ds(pl.multiple_of(turn * 8 * KEEP, 8 * KEEP), 8 * KEEP)
         high = second_ref[: 2 * LANES]
         table = jnp.concatenate([high, high, second_ref[2 * LANES :]], 0)
         field = jnp.dot(doubled(middle[rows, :]), table, preferred_element_type=jnp.float32)
@@ -264,13 +264,11 @@
         begin = pl.multiple_of((band * turns + turn - 1) * piece, 16)
         at = lax.broadcasted_iota(jnp.int32, (piece, sorter.shape[1]), 0) + begin
         sorter[pl.ds(begin, piece), :] = jnp.where(at == place_ref[...], 1.0, 0.0).astype(jnp.bfloat16)
-        for part in range(2):
-            second_axis(2 * turn - 2 + part)
+        second_axis(turn - 1)
         for part in range(2):
             first_axis(2 * turn + part)
 
-    for part in range(2):
-        second_axis(2 * turns + part)
+    second_axis(turns)
 
     for begin, (low, high, offset) in zip(range(0, KEEP, 4), columns.windows):
         both = []

time: 137 us -> 138 us (level)
  Pallas kernels: 57 us -> 58.7 us
    pallas_call x2, Pallas kernels: 34.9 us -> 36.7 us  [spectra(): pl.pallas_call(kernel, grid=(count,), in_specs=[pl.BlockSpec(memory_space...]
  transfers between devices with their start and end apart: 4 -> 4, of which waited for: 4 -> 4; matrix products, arithmetic and copies ran while one was open for 1% -> 1% of each run, Pallas kernels for 22% -> 23%
where the time goes in v17:
time: 138 us; the launch traced here: 137 us
  Pallas kernels  58.7 us (43%)
  blocking collectives  42.2 us (31%)
  between operations  14.1 us (10%)
  waiting for transfers between devices  10.4 us (8%)
  starting transfers between devices  8.81 us (6%)
  local copies, waits for them, and re-layouts  2.33 us (2%)
    pallas_call x2, Pallas kernels, spectra(): pl.pallas_call(kernel, grid=(count,), in_specs=[pl.BlockSpec(memory_space...  36.7 us
    all_to_all x1, blocking collectives, on_device(): lax.all_to_all(early, 'col', split_axis=0, concat_axis=0, tiled=True)  31.6 us
    pallas_call x2, Pallas kernels, put_in_order(): pl.pallas_call(order_kernel, grid_spec=pltpu.PrefetchScalarGridSpec(num_s...  13.1 us
    all_to_all x1, blocking collectives, on_device(): lax.all_to_all(slab, 'row', split_axis=0, concat_axis=0, tiled=True)  10.6 us
    all_to_all x1, waiting for transfers between devices, on_device(): lax.all_to_all(send, 'col', split_axis=0, concat_axis=0, tiled=True)  9.23 us
    pallas_call x1, Pallas kernels, product(): pl.pallas_call(lambda *refs: product_kernel(ids.shape[0], *refs), grid_sp...  8.91 us
    all_to_all x1, starting transfers between devices, on_device(): lax.all_to_all(send, 'col', split_axis=0, concat_axis=0, tiled=True)  5.31 us
    all_to_all x1, starting transfers between devices, on_device(): slab = lax.all_to_all(slab, 'col', split_axis=0, concat_axis=0, tiled=True)  3.45 us
  transfers between devices with their start and end apart: 4, of which 4 were waited for; matrix products, arithmetic and copies ran while one was open for 1% of the time, Pallas kernels for 23%

profile of v17, /device:TPU:0, one launch (start us, length us, event | category | flops | bytes accessed | tf_op | source)
XLA Modules:
  0.0 137.2 jit_solution(8344262619516542508)
XLA Ops:
  6.5 0.0 all-gather.6.cloned.1.call-start
  7.2 18.3 %spectra.2 = (bf16[8,8,4224]{2,1,0:T(8,128)(2,1)}, bf16[4,8,384]{2,1,0:T(8,128)(2,1)}) custom-call(s32[1]{0:T(128)S(6)} %copy.19.refs_0_, f32[32]{0:T(128)} %refs_1_.3, f32[8]{0:T(128)} %refs_2_.3, bf16[8,64,64,128]{3,2,1,0:T(8,128)(2,1)} %refs_3_.3, bf16[1,64,64,128]{3,2,1,0:T(8,128)(2,1)} %refs_4_.2, s32[1,1280]{1,0:T(1,128)} %constant.25.clone.refs_5_, ...), custom_call_target="tpu_custom_call" | custom-call | flops 1 | bytes 1 | tf_op jit(solution)/shard_map/spectra/pallas_call | solution.py:346
  25.5 0.0 all-gather.6.cloned.1.call-update
  25.6 18.3 %spectra.3 = (bf16[8,8,4224]{2,1,0:T(8,128)(2,1)}, bf16[4,8,384]{2,1,0:T(8,128)(2,1)}) custom-call(s32[1]{0:T(128)S(6)} %copy.19.refs_0_, f32[32]{0:T(128)} %refs_1_.3, f32[8]{0:T(128)} %refs_2_.3, bf16[8,64,64,128]{3,2,1,0:T(8,128)(2,1)} %refs_3_.3, bf16[1,64,64,128]{3,2,1,0:T(8,128)(2,1)} %refs_4_.2, s32[1,1280]{1,0:T(1,128)} %constant.25.clone.refs_5_, ...), custom_call_target="tpu_custom_call" | custom-call | flops 1 | bytes 1 | tf_op jit(solution)/shard_map/spectra/pallas_call | solution.py:346
  43.9 0.0 copy-start.2
  43.9 0.0 copy-start.3
  43.9 5.3 %all-to-all-start = ((bf16[8,8,4224]{2,1,0:T(8,128)(2,1)}), bf16[8,8,4224]{2,1,0:T(8,128)(2,1)S(1)}, u32[]{:S(2)}, u32[]{:S(2)}) async-start(bf16[8,8,4224]{2,1,0:T(8,128)(2,1)} %get-tuple-element.21), calls=%async_computation | async-start | bytes 1081344 | tf_op jit(solution)/shard_map/all_to_all | solution.py:504
  49.2 0.0 all-gather.4.cloned.1.call-start
  49.3 0.6 pad_add_fusion.place_ref.refs_0_
  49.9 9.2 %all-to-all-done = bf16[8,8,4224]{2,1,0:T(8,128)(2,1)S(1)} async-done(((bf16[8,8,4224]{2,1,0:T(8,128)(2,1)}), bf16[8,8,4224]{2,1,0:T(8,128)(2,1)S(1)}, u32[]{:S(2)}, u32[]{:S(2)}) %all-to-all-start) | async-done | bytes 540704 | tf_op jit(solution)/shard_map/all_to_all | solution.py:504
  59.1 0.0 copy-start
  59.1 0.8 copy-done
  59.9 5.4 %in_order.2 = bf16[64,3840]{1,0:T(8,128)(2,1)} custom-call(s32[2]{0:T(128)} %pad_add_fusion.place_ref.refs_0_, s32[24]{0:T(128)} %constant.27.clone.starts_ref, s32[8,1,4224]{2,1,0:T(1,128)} %constant.31.ids_ref, s32[1,30720]{1,0:T(1,128)} %bitcast.10, bf16[64,4224]{1,0:T(8,128)(2,1)} %bitcast.8), custom_call_target="tpu_custom_call" | custom-call | flops 1 | bytes 1 | tf_op jit(solution)/shard_map/in_order/pallas_call | solution.py:427
  65.3 0.0 all-gather.4.cloned.1.call-update
  65.3 0.0 copy-done.2
  65.3 0.0 copy-done.3
  65.4 10.6 %all_to_all.20 = bf16[4,16,384]{2,1,0:T(8,128)(2,1)S(1)} all-to-all(bf16[4,16,384]{2,1,0:T(8,128)(2,1)S(1)} %pad_maximum_fusion), channel_id=1, replica_groups=mesh['row'=4,'col'=8] {'row'}, dimensions={0} | all-to-all | bytes 98304 | tf_op jit(solution)/shard_map/all_to_all | solution.py:508
  76.0 0.6 all-gather.6.cloned.1.call-done
  76.6 0.8 broadcast_in_dim.15
  77.4 31.6 %all_to_all.21 = bf16[8,4,8,4224]{3,2,1,0:T(8,128)(2,1)} all-to-all(bf16[8,4,8,4224]{3,2,1,0:T(8,128)(2,1)} %bitcast.9), channel_id=1, replica_groups=mesh['row'=4,'col'=8] {'col'}, dimensions={0} | all-to-all | bytes 4325376 | tf_op jit(solution)/shard_map/all_to_all | solution.py:511
  109.0 3.5 %all-to-all-start.3 = ((bf16[8,64,384]{2,1,0:T(8,128)(2,1)}), bf16[8,64,384]{2,1,0:T(8,128)(2,1)S(1)}, u32[]{:S(2)}, u32[]{:S(2)}) async-start(bf16[8,64,384]{2,1,0:T(8,128)(2,1)} %broadcast_in_dim.15), calls=%async_computation.3 | async-start | bytes 786432 | tf_op jit(solution)/shard_map/all_to_all | solution.py:513
  112.5 7.8 %in_order.3.refs_4_ = bf16[256,3840]{1,0:T(8,128)(2,1)} custom-call(s32[2]{0:T(128)} %pad_add_fusion.place_ref.refs_0_, s32[24]{0:T(128)} %constant.27.clone.starts_ref, s32[8,1,4224]{2,1,0:T(1,128)} %constant.31.ids_ref, s32[1,30720]{1,0:T(1,128)} %bitcast.11, bf16[256,4224]{1,0:T(8,128)(2,1)} %bitcast.7), custom_call_target="tpu_custom_call" | custom-call | flops 1 | bytes 1 | tf_op jit(solution)/shard_map/in_order/pallas_call | solution.py:427
  120.2 0.3 all-gather.4.cloned.1.call-done.refs_5_
  120.5 0.3 all-to-all-done.3.refs_1_
  120.7 0.0 copy-start.1
  120.7 0.7 copy-done.1
  121.5 8.9 %product.1 = f32[2,256,3840]{2,1,0:T(8,128)} custom-call(s32[2]{0:T(128)} %pad_add_fusion.place_ref.refs_0_, bf16[8,64,384]{2,1,0:T(8,128)(2,1)} %copy-done.1, s32[4,1,384]{2,1,0:T(1,128)} %constant.32.refs_2_, s32[1,30720]{1,0:T(1,128)} %bitcast.12, bf16[256,3840]{1,0:T(8,128)(2,1)} %in_order.3.refs_4_, bf16[256,3840]{1,0:T(8,128)(2,1)} %all-gather.4.cloned.1.call-done.refs_5_), custom_call_target="tpu_custom_call" | custom-call | flops 1 | bytes 1 | tf_op jit(solution)/shard_map/product/pallas_call | solution.py:464
  (1 shorter events, 0.0 us)
Async XLA Ops:
  6.5 70.0 %all-gather.6.cloned.1.call-start = ((), (), s32[]{:S(2)}) async-start(), calls=%async_computation.5 | async-start | bytes 2703360 | tf_op jit(solution)/shard_map/all_gather | solution.py:502
  43.9 21.4 %copy-start.2 = (bf16[4,8,384]{2,1,0:T(8,128)(2,1)S(1)}, bf16[4,8,384]{2,1,0:T(8,128)(2,1)}, u32[]{:S(2)}) copy-start(bf16[4,8,384]{2,1,0:T(8,128)(2,1)} %get-tuple-element.18) | copy-start | bytes 73732
  43.9 21.4 %copy-start.3 = (bf16[4,8,384]{2,1,0:T(8,128)(2,1)S(1)}, bf16[4,8,384]{2,1,0:T(8,128)(2,1)}, u32[]{:S(2)}) copy-start(bf16[4,8,384]{2,1,0:T(8,128)(2,1)} %get-tuple-element.20) | copy-start | bytes 73732
  43.9 15.2 %all-to-all-start = ((bf16[8,8,4224]{2,1,0:T(8,128)(2,1)}), bf16[8,8,4224]{2,1,0:T(8,128)(2,1)S(1)}, u32[]{:S(2)}, u32[]{:S(2)}) async-start(bf16[8,8,4224]{2,1,0:T(8,128)(2,1)} %get-tuple-element.21), calls=%async_computation | async-start | bytes 1081344 | tf_op jit(solution)/shard_map/all_to_all | solution.py:504
  49.2 71.2 %all-gather.4.cloned.1.call-start = ((), (), s32[]{:S(2)}) async-start(), calls=%async_computation.4 | async-start | bytes 2457600 | tf_op jit(solution)/shard_map/all_gather | solution.py:506
  59.1 0.8 copy-start
  109.0 11.7 %all-to-all-start.3 = ((bf16[8,64,384]{2,1,0:T(8,128)(2,1)}), bf16[8,64,384]{2,1,0:T(8,128)(2,1)S(1)}, u32[]{:S(2)}, u32[]{:S(2)}) async-start(bf16[8,64,384]{2,1,0:T(8,128)(2,1)} %broadcast_in_dim.15), calls=%async_computation.3 | async-start | bytes 786432 | tf_op jit(solution)/shard_map/all_to_all | solution.py:513
  120.7 0.7 copy-start.1
Sparse Core Ops, SparseCore 0:
  25.7 50.8 all-gather.5
  78.1 42.2 all-gather.3

commit v18 on v16

--- a/solution.py
+++ b/solution.py
@@ -288,27 +288,33 @@
     gap = cond_energy_ref[owner_ref[0]] - val_energy_ref[first_band + band]
     weight = -2.0 / (math.sqrt(bands) * jnp.full((1, LANES), gap, jnp.float32))
     slab = plan["slab_tiles"]
-    tiles = columns.parity // LANES
-    field = contract_last(third_ref[...], last[...])
     band_rows = pl.ds(pl.multiple_of(band * 2 * KEEP, 2 * KEEP), 2 * KEEP)
-    for odd in range(2):
-        value = field[odd * 2 * KEEP : (odd + 1) * 2 * KEEP]
-        plain_rows[band_rows, odd * columns.parity : (odd + 1) * columns.parity] = value.astype(jnp.bfloat16)
-        for place, tile in enumerate(slab):
-            if tile // tiles == odd:
-                inside = value[:, tile % tiles * LANES : (tile % tiles + 1) * LANES]
-                weighted_rows[band_rows, place * LANES : (place + 1) * LANES] = (weight * inside).astype(jnp.bfloat16)
+    for begin in range(0, columns.parity, 2 * LANES):
+        field = contract_last(third_ref[...], last[begin : begin + 2 * LANES, :])
+        for odd in range(2):
+            value = field[odd * 2 * KEEP : (odd + 1) * 2 * KEEP]
+            first = odd * columns.parity + begin
+            plain_rows[band_rows, first : first + 2 * LANES] = value.astype(jnp.bfloat16)
+            for place, tile in enumerate(slab):
+                at = tile * LANES - first
+                if 0 <= at < 2 * LANES:
+                    inside = (weight * value[:, at : at + LANES]).astype(jnp.bfloat16)
+                    weighted_rows[band_rows, place * LANES : (place + 1) * LANES] = inside
 
     @pl.when(band == count - 1)
     def _():
         def sort_rows(rows, which, target):
-            value = jnp.dot(rows, which, preferred_element_type=jnp.float32)
-            for tile in range(target.shape[0]):
-                target[tile] = value[:, tile * LANES : (tile + 1) * LANES]
-
-        which = [sorter[tile * LANES : (tile + 1) * LANES, : weighted_sorted.shape[0] * LANES] for tile in slab]
-        sort_rows(plain_rows[...], sorter[: 2 * columns.parity, :], plain_sorted)
-        sort_rows(weighted_rows[...], jnp.concatenate(which, 0), weighted_sorted)
+            for tile in range(0, target.shape[0], 2):
+                lanes = slice(tile * LANES, (tile + 2) * LANES)
+                value = jnp.dot(rows, which(lanes), preferred_element_type=jnp.float32)
+                target[tile] = value[:, :LANES]
+                target[tile + 1] = value[:, LANES:]
+
+        def slab_places(lanes):
+            return jnp.concatenate([sorter[tile * LANES : (tile + 1) * LANES, lanes] for tile in slab], 0)
+
+        sort_rows(plain_rows[...], lambda lanes: sorter[: 2 * columns.parity, lanes], plain_sorted)
+        sort_rows(weighted_rows[...], slab_places, weighted_sorted)
 
         def plain_at(index, tile):
             return plain_sorted[tile, pl.ds(index, 2 * count, stride=KEEP), :]
@@ -336,7 +342,7 @@
     parity = plan["columns"].parity
     depth = round_up(-(-2 * parity // (count * turns)), 16) * count * turns
     columns = round_up(plan["column_place"].shape[0], 256)
-    slab_columns = round_up(plan["slab_columns"], LANES)
+    slab_columns = round_up(plan["slab_columns"], 2 * LANES)
     slab_depth = len(plan["slab_tiles"]) * LANES
     place = np.full((1, columns), -1, np.int32)
     place[0, : plan["column_place"].shape[0]] = plan["column_place"]
@@ -413,13 +419,14 @@
 
 def order_kernel(place_ref, starts_ref, ids_ref, wanted_ref, panel_ref, out_ref, hot):
     start = pl.multiple_of(starts_ref[place_ref[0] * PARTS + pl.program_id(0)], LANES)
-    wanted = wanted_ref[...]
     window = hot.shape[0]
-    for begin in range(0, window, LANES):
-        ids = ids_ref[0, :, pl.ds(pl.multiple_of(start + begin, LANES), LANES)]
-        hot[begin : begin + LANES, :] = one_hot(ids, wanted)
-    ordered = jnp.dot(panel_ref[:, pl.ds(start, window)], hot[...], preferred_element_type=jnp.float32)
-    out_ref[...] = ordered.astype(jnp.bfloat16)
+    for column in range(0, hot.shape[1], 2 * LANES):
+        lanes = slice(column, min(column + 2 * LANES, hot.shape[1]))
+        for begin in range(0, window, LANES):
+            ids = ids_ref[0, :, pl.ds(pl.multiple_of(start + begin, LANES), LANES)]
+            hot[begin : begin + LANES, lanes] = one_hot(ids, wanted_ref[:, lanes])
+        ordered = jnp.dot(panel_ref[:, pl.ds(start, window)], hot[:, lanes], preferred_element_type=jnp.float32)
+        out_ref[:, lanes] = ordered.astype(jnp.bfloat16)
 
 
 def put_in_order(plan, place, points_map, panel):
@@ -453,10 +460,12 @@
     def _():
         make_left(row_count, slab_ref, ids_ref, wanted_ref, left)
 
-    right = jnp.concatenate([early_ref[...], last_ref[...]], 0)
-    chi = jnp.dot(left[...], right, preferred_element_type=jnp.float32)
-    out_ref[0] = chi[:rows]
-    out_ref[1] = chi[rows:]
+    for begin in range(0, out_ref.shape[2], 2 * LANES):
+        lanes = slice(begin, begin + 2 * LANES)
+        right = jnp.concatenate([early_ref[:, lanes], last_ref[:, lanes]], 0)
+        for part in range(2):
+            half = left[part * rows : (part + 1) * rows, :]
+            out_ref[part, :, lanes] = jnp.dot(half, right, preferred_element_type=jnp.float32)
 
 
 def product(plan, place, points_map, slab, early, last):

time: 137 us -> 137 us (level)
  Pallas kernels: 57 us -> 58.5 us
    pallas_call x2, Pallas kernels: 13.1 us -> 14.7 us  [put_in_order(): pl.pallas_call(order_kernel, grid_spec=pltpu.PrefetchScalarGridSpec(num_s...]
  transfers between devices with their start and end apart: 4 -> 4, of which waited for: 4 -> 3; matrix products, arithmetic and copies ran while one was open for 1% -> 1% of each run, Pallas kernels for 22% -> 24%
where the time goes in v18:
time: 137 us; the launch traced here: 136 us
  Pallas kernels  58.5 us (43%)
  blocking collectives  42 us (31%)
  between operations  14.1 us (10%)
  waiting for transfers between devices  9.79 us (7%)
  starting transfers between devices  8.81 us (6%)
  local copies, waits for them, and re-layouts  2.33 us (2%)
    pallas_call x2, Pallas kernels, spectra(): pl.pallas_call(kernel, grid=(count,), in_specs=[pl.BlockSpec(memory_space...  34.9 us
    all_to_all x1, blocking collectives, on_device(): lax.all_to_all(early, 'col', split_axis=0, concat_axis=0, tiled=True)  31.6 us
    pallas_call x2, Pallas kernels, put_in_order(): pl.pallas_call(order_kernel, grid_spec=pltpu.PrefetchScalarGridSpec(num_s...  14.7 us
    all_to_all x1, blocking collectives, on_device(): lax.all_to_all(slab, 'row', split_axis=0, concat_axis=0, tiled=True)  10.4 us
    all_to_all x1, waiting for transfers between devices, on_device(): lax.all_to_all(send, 'col', split_axis=0, concat_axis=0, tiled=True)  9.23 us
    pallas_call x1, Pallas kernels, product(): pl.pallas_call(lambda *refs: product_kernel(ids.shape[0], *refs), grid_sp...  8.91 us
    all_to_all x1, starting transfers between devices, on_device(): lax.all_to_all(send, 'col', split_axis=0, concat_axis=0, tiled=True)  5.31 us
    all_to_all x1, starting transfers between devices, on_device(): slab = lax.all_to_all(slab, 'col', split_axis=0, concat_axis=0, tiled=True)  3.45 us
  transfers between devices with their start and end apart: 4, of which 3 were waited for; matrix products, arithmetic and copies ran while one was open for 1% of the time, Pallas kernels for 24%

profile of v18, /device:TPU:0, one launch (start us, length us, event | category | flops | bytes accessed | tf_op | source)
XLA Modules:
  0.0 136.2 jit_solution(11142538340549636822)
XLA Ops:
  6.5 0.0 all-gather.6.cloned.1.call-start
  7.2 17.5 %spectra.2 = (bf16[8,8,4224]{2,1,0:T(8,128)(2,1)}, bf16[4,8,384]{2,1,0:T(8,128)(2,1)}) custom-call(s32[1]{0:T(128)S(6)} %copy.19.refs_0_, f32[32]{0:T(128)} %refs_1_.3, f32[8]{0:T(128)} %refs_2_.3, bf16[8,64,64,128]{3,2,1,0:T(8,128)(2,1)} %refs_3_.3, bf16[1,64,64,128]{3,2,1,0:T(8,128)(2,1)} %refs_4_.2, s32[1,1280]{1,0:T(1,128)} %constant.25.clone.refs_5_, ...), custom_call_target="tpu_custom_call" | custom-call | flops 1 | bytes 1 | tf_op jit(solution)/shard_map/spectra/pallas_call | solution.py:354
  24.7 0.0 all-gather.6.cloned.1.call-update
  24.7 17.5 %spectra.3 = (bf16[8,8,4224]{2,1,0:T(8,128)(2,1)}, bf16[4,8,384]{2,1,0:T(8,128)(2,1)}) custom-call(s32[1]{0:T(128)S(6)} %copy.19.refs_0_, f32[32]{0:T(128)} %refs_1_.3, f32[8]{0:T(128)} %refs_2_.3, bf16[8,64,64,128]{3,2,1,0:T(8,128)(2,1)} %refs_3_.3, bf16[1,64,64,128]{3,2,1,0:T(8,128)(2,1)} %refs_4_.2, s32[1,1280]{1,0:T(1,128)} %constant.25.clone.refs_5_, ...), custom_call_target="tpu_custom_call" | custom-call | flops 1 | bytes 1 | tf_op jit(solution)/shard_map/spectra/pallas_call | solution.py:354
  42.1 0.0 copy-start.2
  42.2 0.0 copy-start.3
  42.2 5.3 %all-to-all-start = ((bf16[8,8,4224]{2,1,0:T(8,128)(2,1)}), bf16[8,8,4224]{2,1,0:T(8,128)(2,1)S(1)}, u32[]{:S(2)}, u32[]{:S(2)}) async-start(bf16[8,8,4224]{2,1,0:T(8,128)(2,1)} %get-tuple-element.21), calls=%async_computation | async-start | bytes 1081344 | tf_op jit(solution)/shard_map/all_to_all | solution.py:515
  47.5 0.0 all-gather.4.cloned.1.call-start
  47.5 0.6 pad_add_fusion.place_ref.refs_0_
  48.2 9.2 %all-to-all-done = bf16[8,8,4224]{2,1,0:T(8,128)(2,1)S(1)} async-done(((bf16[8,8,4224]{2,1,0:T(8,128)(2,1)}), bf16[8,8,4224]{2,1,0:T(8,128)(2,1)S(1)}, u32[]{:S(2)}, u32[]{:S(2)}) %all-to-all-start) | async-done | bytes 540704 | tf_op jit(solution)/shard_map/all_to_all | solution.py:515
  57.4 0.0 copy-start
  57.4 0.8 copy-done
  58.2 6.9 %in_order.2 = bf16[64,3840]{1,0:T(8,128)(2,1)} custom-call(s32[2]{0:T(128)} %pad_add_fusion.place_ref.refs_0_, s32[24]{0:T(128)} %constant.27.clone.starts_ref, s32[8,1,4224]{2,1,0:T(1,128)} %constant.31.ids_ref, s32[1,30720]{1,0:T(1,128)} %bitcast.10, bf16[64,4224]{1,0:T(8,128)(2,1)} %bitcast.8), custom_call_target="tpu_custom_call" | custom-call | flops 1 | bytes 1 | tf_op jit(solution)/shard_map/in_order/pallas_call | solution.py:436
  65.1 0.0 all-gather.4.cloned.1.call-update
  65.1 0.0 copy-done.2
  65.1 0.0 copy-done.3
  65.2 10.4 %all_to_all.20 = bf16[4,16,384]{2,1,0:T(8,128)(2,1)S(1)} all-to-all(bf16[4,16,384]{2,1,0:T(8,128)(2,1)S(1)} %pad_maximum_fusion), channel_id=1, replica_groups=mesh['row'=4,'col'=8] {'row'}, dimensions={0} | all-to-all | bytes 98304 | tf_op jit(solution)/shard_map/all_to_all | solution.py:519
  75.5 0.0 all-gather.6.cloned.1.call-done
  75.5 0.8 broadcast_in_dim.15
  76.3 31.6 %all_to_all.21 = bf16[8,4,8,4224]{3,2,1,0:T(8,128)(2,1)} all-to-all(bf16[8,4,8,4224]{3,2,1,0:T(8,128)(2,1)} %bitcast.9), channel_id=1, replica_groups=mesh['row'=4,'col'=8] {'col'}, dimensions={0} | all-to-all | bytes 4325376 | tf_op jit(solution)/shard_map/all_to_all | solution.py:522
  108.0 3.5 %all-to-all-start.3 = ((bf16[8,64,384]{2,1,0:T(8,128)(2,1)}), bf16[8,64,384]{2,1,0:T(8,128)(2,1)S(1)}, u32[]{:S(2)}, u32[]{:S(2)}) async-start(bf16[8,64,384]{2,1,0:T(8,128)(2,1)} %broadcast_in_dim.15), calls=%async_computation.3 | async-start | bytes 786432 | tf_op jit(solution)/shard_map/all_to_all | solution.py:524
  111.4 7.7 %in_order.3.refs_4_ = bf16[256,3840]{1,0:T(8,128)(2,1)} custom-call(s32[2]{0:T(128)} %pad_add_fusion.place_ref.refs_0_, s32[24]{0:T(128)} %constant.27.clone.starts_ref, s32[8,1,4224]{2,1,0:T(1,128)} %constant.31.ids_ref, s32[1,30720]{1,0:T(1,128)} %bitcast.11, bf16[256,4224]{1,0:T(8,128)(2,1)} %bitcast.7), custom_call_target="tpu_custom_call" | custom-call | flops 1 | bytes 1 | tf_op jit(solution)/shard_map/in_order/pallas_call | solution.py:436
  119.2 0.4 all-gather.4.cloned.1.call-done.refs_5_
  119.6 0.1 all-to-all-done.3.refs_1_
  119.7 0.0 copy-start.1
  119.7 0.7 copy-done.1
  120.4 8.9 %product.1 = f32[2,256,3840]{2,1,0:T(8,128)} custom-call(s32[2]{0:T(128)} %pad_add_fusion.place_ref.refs_0_, bf16[8,64,384]{2,1,0:T(8,128)(2,1)} %copy-done.1, s32[4,1,384]{2,1,0:T(1,128)} %constant.32.refs_2_, s32[1,30720]{1,0:T(1,128)} %bitcast.12, bf16[256,3840]{1,0:T(8,128)(2,1)} %in_order.3.refs_4_, bf16[256,3840]{1,0:T(8,128)(2,1)} %all-gather.4.cloned.1.call-done.refs_5_), custom_call_target="tpu_custom_call" | custom-call | flops 1 | bytes 1 | tf_op jit(solution)/shard_map/product/pallas_call | solution.py:475
  (1 shorter events, 0.0 us)
Async XLA Ops:
  6.5 69.0 %all-gather.6.cloned.1.call-start = ((), (), s32[]{:S(2)}) async-start(), calls=%async_computation.5 | async-start | bytes 2703360 | tf_op jit(solution)/shard_map/all_gather | solution.py:513
  42.1 23.0 %copy-start.2 = (bf16[4,8,384]{2,1,0:T(8,128)(2,1)S(1)}, bf16[4,8,384]{2,1,0:T(8,128)(2,1)}, u32[]{:S(2)}) copy-start(bf16[4,8,384]{2,1,0:T(8,128)(2,1)} %get-tuple-element.18) | copy-start | bytes 73732
  42.2 23.0 %copy-start.3 = (bf16[4,8,384]{2,1,0:T(8,128)(2,1)S(1)}, bf16[4,8,384]{2,1,0:T(8,128)(2,1)}, u32[]{:S(2)}) copy-start(bf16[4,8,384]{2,1,0:T(8,128)(2,1)} %get-tuple-element.20) | copy-start | bytes 73732
  42.2 15.2 %all-to-all-start = ((bf16[8,8,4224]{2,1,0:T(8,128)(2,1)}), bf16[8,8,4224]{2,1,0:T(8,128)(2,1)S(1)}, u32[]{:S(2)}, u32[]{:S(2)}) async-start(bf16[8,8,4224]{2,1,0:T(8,128)(2,1)} %get-tuple-element.21), calls=%async_computation | async-start | bytes 1081344 | tf_op jit(solution)/shard_map/all_to_all | solution.py:515
  47.5 72.1 %all-gather.4.cloned.1.call-start = ((), (), s32[]{:S(2)}) async-start(), calls=%async_computation.4 | async-start | bytes 2457600 | tf_op jit(solution)/shard_map/all_gather | solution.py:517
  57.4 0.8 copy-start
  108.0 11.7 %all-to-all-start.3 = ((bf16[8,64,384]{2,1,0:T(8,128)(2,1)}), bf16[8,64,384]{2,1,0:T(8,128)(2,1)S(1)}, u32[]{:S(2)}, u32[]{:S(2)}) async-start(bf16[8,64,384]{2,1,0:T(8,128)(2,1)} %broadcast_in_dim.15), calls=%async_computation.3 | async-start | bytes 786432 | tf_op jit(solution)/shard_map/all_to_all | solution.py:524
  119.7 0.7 copy-start.1
Sparse Core Ops, SparseCore 0:
  24.8 50.5 all-gather.5
  77.0 42.5 all-gather.3

commit v19 on v18

--- a/solution.py
+++ b/solution.py
@@ -419,14 +419,13 @@
 
 def order_kernel(place_ref, starts_ref, ids_ref, wanted_ref, panel_ref, out_ref, hot):
     start = pl.multiple_of(starts_ref[place_ref[0] * PARTS + pl.program_id(0)], LANES)
+    wanted = wanted_ref[...]
     window = hot.shape[0]
-    for column in range(0, hot.shape[1], 2 * LANES):
-        lanes = slice(column, min(column + 2 * LANES, hot.shape[1]))
-        for begin in range(0, window, LANES):
-            ids = ids_ref[0, :, pl.ds(pl.multiple_of(start + begin, LANES), LANES)]
-            hot[begin : begin + LANES, lanes] = one_hot(ids, wanted_ref[:, lanes])
-        ordered = jnp.dot(panel_ref[:, pl.ds(start, window)], hot[:, lanes], preferred_element_type=jnp.float32)
-        out_ref[:, lanes] = ordered.astype(jnp.bfloat16)
+    for begin in range(0, window, LANES):
+        ids = ids_ref[0, :, pl.ds(pl.multiple_of(start + begin, LANES), LANES)]
+        hot[begin : begin + LANES, :] = one_hot(ids, wanted)
+    ordered = jnp.dot(panel_ref[:, pl.ds(start, window)], hot[...], preferred_element_type=jnp.float32)
+    out_ref[...] = ordered.astype(jnp.bfloat16)
 
 
 def put_in_order(plan, place, points_map, panel):
@@ -517,9 +516,9 @@
             last = lax.all_gather(mine, "row", axis=0, tiled=True)
     slab, _ = lax.optimization_barrier((jnp.concatenate(slabs, 1), mine))
     slab = lax.all_to_all(slab, "row", split_axis=0, concat_axis=0, tiled=True).reshape(-1, plan["slab_lanes"])
-    slab = jnp.broadcast_to(slab, (col_count, *slab.shape))
     early, slab = lax.optimization_barrier((early, slab))
     early = lax.all_to_all(early, "col", split_axis=0, concat_axis=0, tiled=True).reshape(-1, plan["lanes"])
+    slab = jnp.broadcast_to(slab, (col_count, *slab.shape))
     early, slab = lax.optimization_barrier((early, slab))
     slab = lax.all_to_all(slab, "col", split_axis=0, concat_axis=0, tiled=True)
     early = put_in_order(plan, place, points_map, early)

time: 137 us -> 137 us (level)
  Pallas kernels: 58.5 us -> 57 us
    pallas_call x2, Pallas kernels: 14.7 us -> 13.1 us  [put_in_order(): pl.pallas_call(order_kernel, grid_spec=pltpu.PrefetchScalarGridSpec(num_s...]
  transfers between devices with their start and end apart: 4 -> 4, of which waited for: 3 -> 4; matrix products, arithmetic and copies ran while one was open for 1% -> 1% of each run, Pallas kernels for 24% -> 22%
where the time goes in v19:
time: 137 us; the launch traced here: 136 us
  Pallas kernels  57 us (42%)
  blocking collectives  42.8 us (31%)
  between operations  14.1 us (10%)
  waiting for transfers between devices  10.7 us (8%)
  starting transfers between devices  8.81 us (6%)
  local copies, waits for them, and re-layouts  2.33 us (2%)
    pallas_call x2, Pallas kernels, spectra(): pl.pallas_call(kernel, grid=(count,), in_specs=[pl.BlockSpec(memory_space...  34.9 us
    all_to_all x1, blocking collectives, on_device(): lax.all_to_all(early, 'col', split_axis=0, concat_axis=0, tiled=True)  31.6 us
    pallas_call x2, Pallas kernels, put_in_order(): pl.pallas_call(order_kernel, grid_spec=pltpu.PrefetchScalarGridSpec(num_s...  13.1 us
    all_to_all x1, blocking collectives, on_device(): lax.all_to_all(slab, 'row', split_axis=0, concat_axis=0, tiled=True)  11.2 us
    all_to_all x1, waiting for transfers between devices, on_device(): lax.all_to_all(send, 'col', split_axis=0, concat_axis=0, tiled=True)  9.23 us
    pallas_call x1, Pallas kernels, product(): pl.pallas_call(lambda *refs: product_kernel(ids.shape[0], *refs), grid_sp...  8.91 us
    all_to_all x1, starting transfers between devices, on_device(): lax.all_to_all(send, 'col', split_axis=0, concat_axis=0, tiled=True)  5.31 us
    all_to_all x1, starting transfers between devices, on_device(): slab = lax.all_to_all(slab, 'col', split_axis=0, concat_axis=0, tiled=True)  3.45 us
  transfers between devices with their start and end apart: 4, of which 4 were waited for; matrix products, arithmetic and copies ran while one was open for 1% of the time, Pallas kernels for 22%

profile of v19, /device:TPU:0, one launch (start us, length us, event | category | flops | bytes accessed | tf_op | source)
XLA Modules:
  0.0 136.3 jit_solution(655253795285526068)
XLA Ops:
  6.5 0.0 all-gather.6.cloned.1.call-start
  7.2 17.5 %spectra.2 = (bf16[8,8,4224]{2,1,0:T(8,128)(2,1)}, bf16[4,8,384]{2,1,0:T(8,128)(2,1)}) custom-call(s32[1]{0:T(128)S(6)} %copy.19.refs_0_, f32[32]{0:T(128)} %refs_1_.3, f32[8]{0:T(128)} %refs_2_.3, bf16[8,64,64,128]{3,2,1,0:T(8,128)(2,1)} %refs_3_.3, bf16[1,64,64,128]{3,2,1,0:T(8,128)(2,1)} %refs_4_.2, s32[1,1280]{1,0:T(1,128)} %constant.25.clone.refs_5_, ...), custom_call_target="tpu_custom_call" | custom-call | flops 1 | bytes 1 | tf_op jit(solution)/shard_map/spectra/pallas_call | solution.py:354
  24.7 0.0 all-gather.6.cloned.1.call-update
  24.7 17.5 %spectra.3 = (bf16[8,8,4224]{2,1,0:T(8,128)(2,1)}, bf16[4,8,384]{2,1,0:T(8,128)(2,1)}) custom-call(s32[1]{0:T(128)S(6)} %copy.19.refs_0_, f32[32]{0:T(128)} %refs_1_.3, f32[8]{0:T(128)} %refs_2_.3, bf16[8,64,64,128]{3,2,1,0:T(8,128)(2,1)} %refs_3_.3, bf16[1,64,64,128]{3,2,1,0:T(8,128)(2,1)} %refs_4_.2, s32[1,1280]{1,0:T(1,128)} %constant.25.clone.refs_5_, ...), custom_call_target="tpu_custom_call" | custom-call | flops 1 | bytes 1 | tf_op jit(solution)/shard_map/spectra/pallas_call | solution.py:354
  42.1 0.0 copy-start.2
  42.2 0.0 copy-start.3
  42.2 5.3 %all-to-all-start = ((bf16[8,8,4224]{2,1,0:T(8,128)(2,1)}), bf16[8,8,4224]{2,1,0:T(8,128)(2,1)S(1)}, u32[]{:S(2)}, u32[]{:S(2)}) async-start(bf16[8,8,4224]{2,1,0:T(8,128)(2,1)} %get-tuple-element.21), calls=%async_computation | async-start | bytes 1081344 | tf_op jit(solution)/shard_map/all_to_all | solution.py:514
  47.5 0.0 all-gather.4.cloned.1.call-start
  47.5 0.6 pad_add_fusion.place_ref.refs_0_
  48.2 9.2 %all-to-all-done = bf16[8,8,4224]{2,1,0:T(8,128)(2,1)S(1)} async-done(((bf16[8,8,4224]{2,1,0:T(8,128)(2,1)}), bf16[8,8,4224]{2,1,0:T(8,128)(2,1)S(1)}, u32[]{:S(2)}, u32[]{:S(2)}) %all-to-all-start) | async-done | bytes 540704 | tf_op jit(solution)/shard_map/all_to_all | solution.py:514
  57.4 0.0 copy-start
  57.4 0.8 copy-done
  58.2 5.4 %in_order.2 = bf16[64,3840]{1,0:T(8,128)(2,1)} custom-call(s32[2]{0:T(128)} %pad_add_fusion.place_ref.refs_0_, s32[24]{0:T(128)} %constant.27.clone.starts_ref, s32[8,1,4224]{2,1,0:T(1,128)} %constant.31.ids_ref, s32[1,30720]{1,0:T(1,128)} %bitcast.10, bf16[64,4224]{1,0:T(8,128)(2,1)} %bitcast.8), custom_call_target="tpu_custom_call" | custom-call | flops 1 | bytes 1 | tf_op jit(solution)/shard_map/in_order/pallas_call | solution.py:435
  63.5 0.0 all-gather.4.cloned.1.call-update
  63.6 0.0 copy-done.2
  63.6 0.0 copy-done.3
  63.6 11.2 %all_to_all.20 = bf16[4,16,384]{2,1,0:T(8,128)(2,1)S(1)} all-to-all(bf16[4,16,384]{2,1,0:T(8,128)(2,1)S(1)} %pad_maximum_fusion), channel_id=1, replica_groups=mesh['row'=4,'col'=8] {'row'}, dimensions={0} | all-to-all | bytes 98304 | tf_op jit(solution)/shard_map/all_to_all | solution.py:518
  74.8 0.9 all-gather.6.cloned.1.call-done
  75.7 31.6 %all_to_all.21 = bf16[8,4,8,4224]{3,2,1,0:T(8,128)(2,1)} all-to-all(bf16[8,4,8,4224]{3,2,1,0:T(8,128)(2,1)} %bitcast.9), channel_id=1, replica_groups=mesh['row'=4,'col'=8] {'col'}, dimensions={0} | all-to-all | bytes 4325376 | tf_op jit(solution)/shard_map/all_to_all | solution.py:520
  107.3 0.8 broadcast_in_dim.15
  108.1 3.5 %all-to-all-start.3 = ((bf16[8,64,384]{2,1,0:T(8,128)(2,1)}), bf16[8,64,384]{2,1,0:T(8,128)(2,1)S(1)}, u32[]{:S(2)}, u32[]{:S(2)}) async-start(bf16[8,64,384]{2,1,0:T(8,128)(2,1)} %broadcast_in_dim.15), calls=%async_computation.3 | async-start | bytes 786432 | tf_op jit(solution)/shard_map/all_to_all | solution.py:523
  111.6 7.8 %in_order.3.refs_4_ = bf16[256,3840]{1,0:T(8,128)(2,1)} custom-call(s32[2]{0:T(128)} %pad_add_fusion.place_ref.refs_0_, s32[24]{0:T(128)} %constant.27.clone.starts_ref, s32[8,1,4224]{2,1,0:T(1,128)} %constant.31.ids_ref, s32[1,30720]{1,0:T(1,128)} %bitcast.11, bf16[256,4224]{1,0:T(8,128)(2,1)} %bitcast.7), custom_call_target="tpu_custom_call" | custom-call | flops 1 | bytes 1 | tf_op jit(solution)/shard_map/in_order/pallas_call | solution.py:435
  119.3 0.3 all-gather.4.cloned.1.call-done.refs_5_
  119.6 0.2 all-to-all-done.3.refs_1_
  119.8 0.0 copy-start.1
  119.8 0.7 copy-done.1
  120.6 8.9 %product.1 = f32[2,256,3840]{2,1,0:T(8,128)} custom-call(s32[2]{0:T(128)} %pad_add_fusion.place_ref.refs_0_, bf16[8,64,384]{2,1,0:T(8,128)(2,1)} %copy-done.1, s32[4,1,384]{2,1,0:T(1,128)} %constant.32.refs_2_, s32[1,30720]{1,0:T(1,128)} %bitcast.12, bf16[256,3840]{1,0:T(8,128)(2,1)} %in_order.3.refs_4_, bf16[256,3840]{1,0:T(8,128)(2,1)} %all-gather.4.cloned.1.call-done.refs_5_), custom_call_target="tpu_custom_call" | custom-call | flops 1 | bytes 1 | tf_op jit(solution)/shard_map/product/pallas_call | solution.py:474
  (1 shorter events, 0.0 us)
Async XLA Ops:
  6.5 69.1 %all-gather.6.cloned.1.call-start = ((), (), s32[]{:S(2)}) async-start(), calls=%async_computation.5 | async-start | bytes 2703360 | tf_op jit(solution)/shard_map/all_gather | solution.py:512
  42.1 21.4 %copy-start.2 = (bf16[4,8,384]{2,1,0:T(8,128)(2,1)S(1)}, bf16[4,8,384]{2,1,0:T(8,128)(2,1)}, u32[]{:S(2)}) copy-start(bf16[4,8,384]{2,1,0:T(8,128)(2,1)} %get-tuple-element.18) | copy-start | bytes 73732
  42.2 21.4 %copy-start.3 = (bf16[4,8,384]{2,1,0:T(8,128)(2,1)S(1)}, bf16[4,8,384]{2,1,0:T(8,128)(2,1)}, u32[]{:S(2)}) copy-start(bf16[4,8,384]{2,1,0:T(8,128)(2,1)} %get-tuple-element.20) | copy-start | bytes 73732
  42.2 15.2 %all-to-all-start = ((bf16[8,8,4224]{2,1,0:T(8,128)(2,1)}), bf16[8,8,4224]{2,1,0:T(8,128)(2,1)S(1)}, u32[]{:S(2)}, u32[]{:S(2)}) async-start(bf16[8,8,4224]{2,1,0:T(8,128)(2,1)} %get-tuple-element.21), calls=%async_computation | async-start | bytes 1081344 | tf_op jit(solution)/shard_map/all_to_all | solution.py:514
  47.5 72.1 %all-gather.4.cloned.1.call-start = ((), (), s32[]{:S(2)}) async-start(), calls=%async_computation.4 | async-start | bytes 2457600 | tf_op jit(solution)/shard_map/all_gather | solution.py:516
  57.4 0.8 copy-start
  108.1 11.7 %all-to-all-start.3 = ((bf16[8,64,384]{2,1,0:T(8,128)(2,1)}), bf16[8,64,384]{2,1,0:T(8,128)(2,1)S(1)}, u32[]{:S(2)}, u32[]{:S(2)}) async-start(bf16[8,64,384]{2,1,0:T(8,128)(2,1)} %broadcast_in_dim.15), calls=%async_computation.3 | async-start | bytes 786432 | tf_op jit(solution)/shard_map/all_to_all | solution.py:523
  119.8 0.7 copy-start.1
Sparse Core Ops, SparseCore 0:
  24.8 50.8 all-gather.5
  77.2 42.2 all-gather.3

commit v20 on v19

--- a/solution.py
+++ b/solution.py
@@ -233,11 +233,14 @@
         last[columns.used :, :] = jnp.zeros((columns.parity - columns.used, 4 * LANES), jnp.bfloat16)
 
     def first_axis(block):
-        rows = pl.ds(pl.multiple_of(block * planes * points, planes * points), planes * points)
-        wave = val_ref[0, pl.ds(block * planes, planes)].reshape(planes * points, LANES).astype(jnp.float32)
-        density = wave * cond_a[rows, :] + pltpu.roll(wave, HALF, 1) * cond_b[rows, :]
-        high, low = split_parts(density)
-        field = contract_last(first_ref[...], jnp.concatenate([high, low], 1))
+        stored = []
+        for part in range(pairs):
+            at = block * planes + 2 * part
+            rows = pl.ds(pl.multiple_of(at * points, 2 * points), 2 * points)
+            wave = val_ref[0, pl.ds(at, 2)].reshape(2 * points, LANES).astype(jnp.float32)
+            density = wave * cond_a[rows, :] + pltpu.roll(wave, HALF, 1) * cond_b[rows, :]
+            stored.append(jnp.concatenate(split_parts(density), 1))
+        field = contract_last(first_ref[...], jnp.concatenate(stored, 0))
         for begin in range(0, pairs, 2):
             blocks = [
                 [field[part * KEEP : (part + 1) * KEEP, pair * LANES : (pair + 1) * LANES] for pair in (begin, begin + 1)]

time: 137 us -> 137 us (level)
  no operation moved by 1% of the time
where the time goes in v20:
time: 137 us; the launch traced here: 136 us
  Pallas kernels  57 us (42%)
  blocking collectives  42.8 us (31%)
  between operations  14.1 us (10%)
  waiting for transfers between devices  10.7 us (8%)
  starting transfers between devices  8.81 us (6%)
  local copies, waits for them, and re-layouts  2.33 us (2%)
    pallas_call x2, Pallas kernels, spectra(): pl.pallas_call(kernel, grid=(count,), in_specs=[pl.BlockSpec(memory_space...  34.9 us
    all_to_all x1, blocking collectives, on_device(): lax.all_to_all(early, 'col', split_axis=0, concat_axis=0, tiled=True)  31.6 us
    pallas_call x2, Pallas kernels, put_in_order(): pl.pallas_call(order_kernel, grid_spec=pltpu.PrefetchScalarGridSpec(num_s...  13.1 us
    all_to_all x1, blocking collectives, on_device(): lax.all_to_all(slab, 'row', split_axis=0, concat_axis=0, tiled=True)  11.2 us
    all_to_all x1, waiting for transfers between devices, on_device(): lax.all_to_all(send, 'col', split_axis=0, concat_axis=0, tiled=True)  9.23 us
    pallas_call x1, Pallas kernels, product(): pl.pallas_call(lambda *refs: product_kernel(ids.shape[0], *refs), grid_sp...  8.91 us
    all_to_all x1, starting transfers between devices, on_device(): lax.all_to_all(send, 'col', split_axis=0, concat_axis=0, tiled=True)  5.31 us
    all_to_all x1, starting transfers between devices, on_device(): slab = lax.all_to_all(slab, 'col', split_axis=0, concat_axis=0, tiled=True)  3.45 us
  transfers between devices with their start and end apart: 4, of which 4 were waited for; matrix products, arithmetic and copies ran while one was open for 1% of the time, Pallas kernels for 22%

profile of v20, /device:TPU:0, one launch (start us, length us, event | category | flops | bytes accessed | tf_op | source)
XLA Modules:
  0.0 136.3 jit_solution(655253795285526068)
XLA Ops:
  6.5 0.0 all-gather.6.cloned.1.call-start
  7.2 17.5 %spectra.2 = (bf16[8,8,4224]{2,1,0:T(8,128)(2,1)}, bf16[4,8,384]{2,1,0:T(8,128)(2,1)}) custom-call(s32[1]{0:T(128)S(6)} %copy.19.refs_0_, f32[32]{0:T(128)} %refs_1_.3, f32[8]{0:T(128)} %refs_2_.3, bf16[8,64,64,128]{3,2,1,0:T(8,128)(2,1)} %refs_3_.3, bf16[1,64,64,128]{3,2,1,0:T(8,128)(2,1)} %refs_4_.2, s32[1,1280]{1,0:T(1,128)} %constant.25.clone.refs_5_, ...), custom_call_target="tpu_custom_call" | custom-call | flops 1 | bytes 1 | tf_op jit(solution)/shard_map/spectra/pallas_call | solution.py:357
  24.7 0.0 all-gather.6.cloned.1.call-update
  24.7 17.5 %spectra.3 = (bf16[8,8,4224]{2,1,0:T(8,128)(2,1)}, bf16[4,8,384]{2,1,0:T(8,128)(2,1)}) custom-call(s32[1]{0:T(128)S(6)} %copy.19.refs_0_, f32[32]{0:T(128)} %refs_1_.3, f32[8]{0:T(128)} %refs_2_.3, bf16[8,64,64,128]{3,2,1,0:T(8,128)(2,1)} %refs_3_.3, bf16[1,64,64,128]{3,2,1,0:T(8,128)(2,1)} %refs_4_.2, s32[1,1280]{1,0:T(1,128)} %constant.25.clone.refs_5_, ...), custom_call_target="tpu_custom_call" | custom-call | flops 1 | bytes 1 | tf_op jit(solution)/shard_map/spectra/pallas_call | solution.py:357
  42.1 0.0 copy-start.2
  42.2 0.0 copy-start.3
  42.2 5.3 %all-to-all-start = ((bf16[8,8,4224]{2,1,0:T(8,128)(2,1)}), bf16[8,8,4224]{2,1,0:T(8,128)(2,1)S(1)}, u32[]{:S(2)}, u32[]{:S(2)}) async-start(bf16[8,8,4224]{2,1,0:T(8,128)(2,1)} %get-tuple-element.21), calls=%async_computation | async-start | bytes 1081344 | tf_op jit(solution)/shard_map/all_to_all | solution.py:517
  47.5 0.0 all-gather.4.cloned.1.call-start
  47.5 0.6 pad_add_fusion.place_ref.refs_0_
  48.2 9.2 %all-to-all-done = bf16[8,8,4224]{2,1,0:T(8,128)(2,1)S(1)} async-done(((bf16[8,8,4224]{2,1,0:T(8,128)(2,1)}), bf16[8,8,4224]{2,1,0:T(8,128)(2,1)S(1)}, u32[]{:S(2)}, u32[]{:S(2)}) %all-to-all-start) | async-done | bytes 540704 | tf_op jit(solution)/shard_map/all_to_all | solution.py:517
  57.4 0.0 copy-start
  57.4 0.8 copy-done
  58.2 5.4 %in_order.2 = bf16[64,3840]{1,0:T(8,128)(2,1)} custom-call(s32[2]{0:T(128)} %pad_add_fusion.place_ref.refs_0_, s32[24]{0:T(128)} %constant.27.clone.starts_ref, s32[8,1,4224]{2,1,0:T(1,128)} %constant.31.ids_ref, s32[1,30720]{1,0:T(1,128)} %bitcast.10, bf16[64,4224]{1,0:T(8,128)(2,1)} %bitcast.8), custom_call_target="tpu_custom_call" | custom-call | flops 1 | bytes 1 | tf_op jit(solution)/shard_map/in_order/pallas_call | solution.py:438
  63.5 0.0 all-gather.4.cloned.1.call-update
  63.6 0.0 copy-done.2
  63.6 0.0 copy-done.3
  63.6 11.2 %all_to_all.20 = bf16[4,16,384]{2,1,0:T(8,128)(2,1)S(1)} all-to-all(bf16[4,16,384]{2,1,0:T(8,128)(2,1)S(1)} %pad_maximum_fusion), channel_id=1, replica_groups=mesh['row'=4,'col'=8] {'row'}, dimensions={0} | all-to-all | bytes 98304 | tf_op jit(solution)/shard_map/all_to_all | solution.py:521
  74.8 0.9 all-gather.6.cloned.1.call-done
  75.7 31.6 %all_to_all.21 = bf16[8,4,8,4224]{3,2,1,0:T(8,128)(2,1)} all-to-all(bf16[8,4,8,4224]{3,2,1,0:T(8,128)(2,1)} %bitcast.9), channel_id=1, replica_groups=mesh['row'=4,'col'=8] {'col'}, dimensions={0} | all-to-all | bytes 4325376 | tf_op jit(solution)/shard_map/all_to_all | solution.py:523
  107.3 0.8 broadcast_in_dim.15
  108.1 3.5 %all-to-all-start.3 = ((bf16[8,64,384]{2,1,0:T(8,128)(2,1)}), bf16[8,64,384]{2,1,0:T(8,128)(2,1)S(1)}, u32[]{:S(2)}, u32[]{:S(2)}) async-start(bf16[8,64,384]{2,1,0:T(8,128)(2,1)} %broadcast_in_dim.15), calls=%async_computation.3 | async-start | bytes 786432 | tf_op jit(solution)/shard_map/all_to_all | solution.py:526
  111.6 7.8 %in_order.3.refs_4_ = bf16[256,3840]{1,0:T(8,128)(2,1)} custom-call(s32[2]{0:T(128)} %pad_add_fusion.place_ref.refs_0_, s32[24]{0:T(128)} %constant.27.clone.starts_ref, s32[8,1,4224]{2,1,0:T(1,128)} %constant.31.ids_ref, s32[1,30720]{1,0:T(1,128)} %bitcast.11, bf16[256,4224]{1,0:T(8,128)(2,1)} %bitcast.7), custom_call_target="tpu_custom_call" | custom-call | flops 1 | bytes 1 | tf_op jit(solution)/shard_map/in_order/pallas_call | solution.py:438
  119.3 0.3 all-gather.4.cloned.1.call-done.refs_5_
  119.6 0.2 all-to-all-done.3.refs_1_
  119.8 0.0 copy-start.1
  119.8 0.7 copy-done.1
  120.6 8.9 %product.1 = f32[2,256,3840]{2,1,0:T(8,128)} custom-call(s32[2]{0:T(128)} %pad_add_fusion.place_ref.refs_0_, bf16[8,64,384]{2,1,0:T(8,128)(2,1)} %copy-done.1, s32[4,1,384]{2,1,0:T(1,128)} %constant.32.refs_2_, s32[1,30720]{1,0:T(1,128)} %bitcast.12, bf16[256,3840]{1,0:T(8,128)(2,1)} %in_order.3.refs_4_, bf16[256,3840]{1,0:T(8,128)(2,1)} %all-gather.4.cloned.1.call-done.refs_5_), custom_call_target="tpu_custom_call" | custom-call | flops 1 | bytes 1 | tf_op jit(solution)/shard_map/product/pallas_call | solution.py:477
  (1 shorter events, 0.0 us)
Async XLA Ops:
  6.5 69.1 %all-gather.6.cloned.1.call-start = ((), (), s32[]{:S(2)}) async-start(), calls=%async_computation.5 | async-start | bytes 2703360 | tf_op jit(solution)/shard_map/all_gather | solution.py:515
  42.1 21.4 %copy-start.2 = (bf16[4,8,384]{2,1,0:T(8,128)(2,1)S(1)}, bf16[4,8,384]{2,1,0:T(8,128)(2,1)}, u32[]{:S(2)}) copy-start(bf16[4,8,384]{2,1,0:T(8,128)(2,1)} %get-tuple-element.18) | copy-start | bytes 73732
  42.2 21.4 %copy-start.3 = (bf16[4,8,384]{2,1,0:T(8,128)(2,1)S(1)}, bf16[4,8,384]{2,1,0:T(8,128)(2,1)}, u32[]{:S(2)}) copy-start(bf16[4,8,384]{2,1,0:T(8,128)(2,1)} %get-tuple-element.20) | copy-start | bytes 73732
  42.2 15.2 %all-to-all-start = ((bf16[8,8,4224]{2,1,0:T(8,128)(2,1)}), bf16[8,8,4224]{2,1,0:T(8,128)(2,1)S(1)}, u32[]{:S(2)}, u32[]{:S(2)}) async-start(bf16[8,8,4224]{2,1,0:T(8,128)(2,1)} %get-tuple-element.21), calls=%async_computation | async-start | bytes 1081344 | tf_op jit(solution)/shard_map/all_to_all | solution.py:517
  47.5 72.1 %all-gather.4.cloned.1.call-start = ((), (), s32[]{:S(2)}) async-start(), calls=%async_computation.4 | async-start | bytes 2457600 | tf_op jit(solution)/shard_map/all_gather | solution.py:519
  57.4 0.8 copy-start
  108.1 11.7 %all-to-all-start.3 = ((bf16[8,64,384]{2,1,0:T(8,128)(2,1)}), bf16[8,64,384]{2,1,0:T(8,128)(2,1)S(1)}, u32[]{:S(2)}, u32[]{:S(2)}) async-start(bf16[8,64,384]{2,1,0:T(8,128)(2,1)} %broadcast_in_dim.15), calls=%async_computation.3 | async-start | bytes 786432 | tf_op jit(solution)/shard_map/all_to_all | solution.py:526
  119.8 0.7 copy-start.1
Sparse Core Ops, SparseCore 0:
  24.8 50.8 all-gather.5
  77.2 42.2 all-gather.3
